TPU v7x, 32 devices: a whole 2x2x4 slice. The times are simulated.
32 devices in a mesh: lon: 4 (over z), lat: 2 (over y), ch: 4 (over x, core).
Axes of the slice: x: 2, y: 2, z: 4, core: 2. Of those that a mesh axis runs over, the one named last changes fastest.
Arguments:
- ocean_state: bfloat16 [300, 64, 512], P('ch', 'lat', 'lon'), may hold values from -6 to 6
- land_mask: int32 [64, 512], P('lat', 'lon'), may hold values 0 or 1
- out_grad: bfloat16 [300, 64, 512], P('ch', 'lat', 'lon'), may hold values from -6 to 6
- swath_offset: int32 [2, 4, 512], P('lat', 'lon'), may hold values from 0 to 4095
- swath_value: float32 [2, 4, 512], P('lat', 'lon'), may hold values from -8 to 8
- depth_kernel: float32 [3, 3, 300], P(None, None, 'ch'), may hold values from -2.5 to 2.5
- expand_weight: bfloat16 [300, 600], P(None, 'ch'), may hold values from -0.375 to 0.375
- expand_bias: float32 [600], P('ch'), may hold values from -3 to 3
- project_weight: bfloat16 [600, 300], P('ch'), may hold values from -0.25 to 0.25
Outputs:
- state_grad: bfloat16 [300, 64, 512], P('ch', 'lat', 'lon')
- expand_grad: float32 [300, 600], P(None, 'ch')
- project_grad: float32 [600, 300], P('ch')
- bias_grad: float32 [600], P('ch')
- kernel_grad: float32 [3, 3, 300], P(None, None, 'ch')
Inputs may be any that keep to these rules, and one draw needn't show every extreme that they name: `swath_offset`: position of a swath point in row-major order over the 32 x 128 cells of its device's block.
All inputs are finite; a program needn't handle non-finite values. No bound on the sum of `land_mask` on one device may be relied on, other than what follows from the above.
Results may differ from a plain program's by a relative error of at most 0.014.
Values may be sent and summed in bfloat16 or wider, within the bound.
No kernel may reach another device: no remote copies, remote signals or barrier semaphores. Data moves between devices by JAX's collectives and lax.ppermute only.
A program may use at most 64 MiB of HBM per device.

v0:
```python
import math

import jax
import jax.numpy as jnp
from jax import lax
from jax.sharding import PartitionSpec as P

DILATION_STEP = 2


def with_halo(block, sides, width):
    for axis, dim in sides:
        count = lax.axis_size(axis)
        forward = [(i, i + 1) for i in range(count - 1)]
        forward.append((count - 1, 0))
        backward = [(target, source) for source, target in forward]
        low = lax.ppermute(
            lax.slice_in_dim(block, block.shape[dim] - width, None, axis=dim), axis, forward
        )
        high = lax.ppermute(lax.slice_in_dim(block, 0, width, axis=dim), axis, backward)
        block = jnp.concatenate([low, block, high], axis=dim)
    return block


def extend(ocean_field):
    count_of_rows = ocean_field.shape[1]
    column_count = ocean_field.shape[2]
    halo_padded = with_halo(ocean_field, (("lon", 2), ("lat", 1)), DILATION_STEP)
    uppermost_rows = ocean_field[:, count_of_rows - DILATION_STEP :, :]
    gathered = lax.all_gather(uppermost_rows, "lon", axis=2, tiled=True)
    seam_mirrored = gathered[:, ::-1, ::-1]
    seam_mirrored = jnp.concatenate(
        [seam_mirrored[:, :, -DILATION_STEP:], seam_mirrored, seam_mirrored[:, :, :DILATION_STEP]],
        axis=2,
    )
    northern_border = lax.dynamic_slice_in_dim(
        seam_mirrored, lax.axis_index("lon") * column_count, column_count + 2 * DILATION_STEP, 2
    )
    latitude_index = lax.axis_index("lat")
    southern_boundary = halo_padded[:, :DILATION_STEP, :]
    southern_border = jnp.where(
        latitude_index == 0, jnp.zeros_like(southern_boundary), southern_boundary
    )
    northern_border = jnp.where(
        latitude_index == lax.axis_size("lat") - 1,
        northern_border,
        halo_padded[:, count_of_rows + DILATION_STEP :, :],
    )
    return jnp.concatenate(
        [
            southern_border,
            halo_padded[:, DILATION_STEP : count_of_rows + DILATION_STEP, :],
            northern_border,
        ],
        axis=1,
    )


def on_device(
    ocean_state,
    land_mask,
    out_grad,
    swath_offset,
    swath_value,
    depth_kernel,
    expand_weight,
    expand_bias,
    project_weight,
):
    channels_per_shard = ocean_state.shape[0]
    count_of_rows = ocean_state.shape[1]
    column_count = ocean_state.shape[2]
    cells = count_of_rows * column_count
    scale = 1.0 / math.sqrt(
        count_of_rows * lax.axis_size("lat") * column_count * lax.axis_size("lon")
    )
    mask_float = land_mask.astype(jnp.float32)[None]
    masked = ocean_state * land_mask.astype(jnp.bfloat16)[None]
    state_pad = extend(masked)
    forward = jnp.zeros((channels_per_shard, count_of_rows, column_count), jnp.float32)
    for row_offset in range(3):
        for column_offset in range(3):
            kernel_window = state_pad[
                :,
                DILATION_STEP * row_offset : DILATION_STEP * row_offset + count_of_rows,
                DILATION_STEP * column_offset : DILATION_STEP * column_offset + column_count,
            ]
            forward = forward + depth_kernel[row_offset, column_offset][
                :, None, None
            ] * kernel_window.astype(jnp.float32)
    conv_out = forward.astype(jnp.bfloat16)
    swath = (
        jnp.zeros((cells,), jnp.float32).at[swath_offset.reshape(-1)].add(swath_value.reshape(-1))
    )
    first_group = jnp.where(lax.axis_index("ch") == 0, 1.0, 0.0).astype(jnp.float32)
    cotan = (
        out_grad.astype(jnp.float32)
        .at[0]
        .add(first_group * swath.reshape(count_of_rows, column_count))
    )
    cotan = (cotan * mask_float).astype(jnp.bfloat16)
    conv_all, cotan_all = (
        lax.all_gather(conv_out, "ch", axis=0, tiled=True),
        lax.all_gather(cotan, "ch", axis=0, tiled=True),
    )
    conv_flat = conv_all.reshape(conv_all.shape[0], cells)
    cotan_flat = cotan_all.reshape(cotan_all.shape[0], cells)
    hidden = (
        jnp.dot(expand_weight.T, conv_flat, preferred_element_type=jnp.float32)
        + expand_bias[:, None]
    )
    activ, gelu_back = jax.vjp(jax.nn.gelu, hidden)
    act_grad = jnp.dot(project_weight, cotan_flat, preferred_element_type=jnp.float32)
    pre_grad = gelu_back(act_grad)[0].astype(jnp.bfloat16)
    project_part = (
        jnp.dot(activ.astype(jnp.bfloat16), cotan_flat.T, preferred_element_type=jnp.float32)
        * scale
    )
    expand_part = jnp.dot(conv_flat, pre_grad.T, preferred_element_type=jnp.float32) * scale
    bias_part = jnp.sum(pre_grad.astype(jnp.float32), axis=1) * scale
    summed = lax.psum_scatter(
        jnp.dot(expand_weight, pre_grad, preferred_element_type=jnp.float32).astype(jnp.bfloat16),
        "ch",
        scatter_dimension=0,
        tiled=True,
    )
    conv_grad = summed.reshape(channels_per_shard, count_of_rows, column_count)
    grad_pad = extend(conv_grad)
    grad_float = conv_grad.astype(jnp.float32)
    kernel_rows = []
    swapped_axes = jnp.zeros((channels_per_shard, count_of_rows, column_count), jnp.float32)
    for row_offset in range(3):
        kernel_cols = []
        for column_offset in range(3):
            kernel_window = state_pad[
                :,
                DILATION_STEP * row_offset : DILATION_STEP * row_offset + count_of_rows,
                DILATION_STEP * column_offset : DILATION_STEP * column_offset + column_count,
            ]
            kernel_cols.append(jnp.sum(grad_float * kernel_window.astype(jnp.float32), axis=(1, 2)))
            reverse_row = DILATION_STEP * (2 - row_offset)
            reverse_column = DILATION_STEP * (2 - column_offset)
            back_window = grad_pad[
                :,
                reverse_row : reverse_row + count_of_rows,
                reverse_column : reverse_column + column_count,
            ]
            swapped_axes = swapped_axes + depth_kernel[row_offset, column_offset][
                :, None, None
            ] * back_window.astype(jnp.float32)
        kernel_rows.append(jnp.stack(kernel_cols, axis=0))
    kernel_part = jnp.stack(kernel_rows, axis=0) * scale
    fold_adjustment = jnp.zeros((channels_per_shard, DILATION_STEP, column_count), jnp.float32)
    for column_offset in range(3):
        reverse_column = DILATION_STEP * (2 - column_offset)
        rim_window = grad_pad[
            :,
            count_of_rows + DILATION_STEP : count_of_rows + 2 * DILATION_STEP,
            reverse_column : reverse_column + column_count,
        ]
        weight_change = depth_kernel[2, 2 - column_offset] - depth_kernel[0, column_offset]
        fold_adjustment = fold_adjustment + weight_change[:, None, None] * rim_window.astype(
            jnp.float32
        )
    at_top = lax.axis_index("lat") == lax.axis_size("lat") - 1
    swapped_axes = swapped_axes.at[:, count_of_rows - DILATION_STEP :, :].add(
        jnp.where(at_top, fold_adjustment, jnp.zeros_like(fold_adjustment))
    )
    state_grad = (mask_float * (cotan.astype(jnp.float32) + swapped_axes)).astype(jnp.bfloat16)
    expand_grad, project_grad, bias_grad, kernel_grad = lax.psum(
        (expand_part, project_part, bias_part, kernel_part), ("lon", "lat")
    )
    return (state_grad, expand_grad, project_grad, bias_grad, kernel_grad)


def solution(mesh):
    return jax.shard_map(
        on_device,
        mesh=mesh,
        in_specs=(
            P("ch", "lat", "lon"),
            P("lat", "lon"),
            P("ch", "lat", "lon"),
            P("lat", "lon", None),
            P("lat", "lon", None),
            P(None, None, "ch"),
            P(None, "ch"),
            P("ch"),
            P("ch", None),
        ),
        out_specs=(
            P("ch", "lat", "lon"),
            P(None, "ch"),
            P("ch", None),
            P("ch"),
            P(None, None, "ch"),
        ),
        check_vma=False,
    )
```

profile of v0, /device:TPU:0, one launch (start us, length us, event | category | flops | bytes accessed | tf_op | source)
XLA Modules:
  0.0 203.8 jit_solution(1774880135024396246)
XLA Ops:
  10.0 3.4 %scatter_custom_fusion = f32[4096]{0:T(1024)S(1)} fusion(s32[512]{0:T(512)S(1)} %bitcast.100, f32[512]{0:T(512)} %bitcast.101, f32[]{:T(128)} %constant.86.clone.1), kind=kCustom, calls=%fused_computation.98 | custom fusion | flops 512 | bytes 16896 | tf_op jit(solution)/shard_map/scatter-add | solution.py:93
  16.0 5.1 %collective-permute-start.1 = (bf16[75,32,2]{0,1,2:T(8,128)(2,1)S(1)}, bf16[75,32,2]{0,1,2:T(8,128)(2,1)S(1)}, u32[]{:S(2)}, u32[]{:S(2)}) collective-permute-start(bf16[75,32,2]{0,1,2:T(8,128)(2,1)S(1)} %copy.31), channel_id=1, source_target_pairs={{8,0},{16,8},{24,16},{0,24},{9,1},{17,9},{25,17},{1,25},{10,2},{18... | collective-permute-start | bytes 28808 | tf_op jit(solution)/shard_map/ppermute | solution.py:20
  21.9 12.7 %all_gather.13 = bf16[75,2,512]{2,1,0:T(2,128)(2,1)S(1)} all-gather(bf16[75,2,128]{2,1,0:T(2,128)(2,1)S(1)} %slice.277), channel_id=1, replica_groups=mesh['lon'=4,'lat'=2,'ch'=4] {'lon'}, dimensions={2}, use_global_device_ids=true | all-gather | bytes 192000 | tf_op jit(solution)/shard_map/all_gather | solution.py:30
  37.4 1.6 collective-permute-start.2
  39.1 1.4 rev.6
  42.5 3.2 %collective-permute-done.3 = bf16[75,2,132]{2,1,0:T(2,128)(2,1)S(1)} collective-permute-done((bf16[75,2,132]{2,1,0:T(2,128)(2,1)S(1)}, bf16[75,2,132]{2,1,0:T(2,128)(2,1)S(1)}, u32[]{:S(2)}, u32[]{:S(2)}) %collective-permute-start.3) | collective-permute-done | bytes 39632 | tf_op jit(solution)/shard_map/ppermute | solution.py:20
  46.1 2.4 %maximum_maximum_fusion = (bf16[75,34,132]{2,1,0:T(8,128)(2,1)S(1)}, bf16[75,34,132]{2,1,0:T(8,128)(2,1)S(1)}) fusion(bf16[75,32,2]{2,1,0:T(8,128)(2,1)S(1)} %copy.33, bf16[75,32,128]{2,1,0:T(8,128)(2,1)S(1)} %broadcast_multiply_fusion, bf16[75,32,2]{2,1,0:T(8,128)(2,1)S(1)} %copy.32, bf16[75,2,132]{2,1,0:T(2,128)(2,1)S(1)} %broadcast_select_fusion.3, ...), kind=kLoop, calls=%fused_computation.27 | loop fusion | flops 5385600 | bytes 2059200 | tf_op jit(solution)/shard_map/concatenate | solution.py:49
  50.1 4.1 %fusion.19 = bf16[75,32,128]{2,1,0:T(8,128)(2,1)} fusion(bf16[75,32,128]{2,1,0:T(8,128)(2,1)S(1)} %broadcast_multiply_fusion, f32[75]{0:T(128)S(1)} %get-tuple-element.79, f32[75]{0:T(128)S(1)} %get-tuple-element.80, f32[75]{0:T(128)S(1)} %get-tuple-element.73, f32[75]{0:T(128)S(1)} %get-tuple-element.74, f32[75]{0:T(128)S(1)} %get-tuple-element.75, ...), kind=kLoop, calls=%fused_computation.49 | loop fusion | flops 10137600 | bytes 4937100 | tf_op jit(solution)/shard_map/convert_element_type | solution.py:91
  56.3 2.2 %pad.73 = bf16[304,32,128]{2,1,0:T(8,128)(2,1)S(1)} pad(bf16[300,32,128]{2,1,0:T(8,128)(2,1)} %all-gather.3.cloned.1.call-done, bf16[]{:T(256)} %constant.90.clone.1), padding=0_4x0_0x0_0 | pad | bytes 4947970
  59.7 16.8 %all-gather.5.cloned.1.call-done = bf16[300,32,128]{2,1,0:T(8,128)(2,1)} async-done(((bf16[75,32,128]{2,1,0:T(8,128)(2,1)}), bf16[300,32,128]{2,1,0:T(8,128)(2,1)}) %all-gather.5.cloned.1.call-update) | async-done | bytes 2457616 | tf_op jit(solution)/shard_map/all_gather | solution.py:103
  76.5 2.1 %pad.74 = bf16[304,32,128]{2,1,0:T(8,128)(2,1)S(1)} pad(bf16[300,32,128]{2,1,0:T(8,128)(2,1)} %all-gather.5.cloned.1.call-done, bf16[]{:T(256)} %constant.90.clone.1), padding=0_4x0_0x0_0 | pad | bytes 4947970
  80.7 1.9 fusion.34
  82.6 2.5 %convert_reduce_fusion = (f32[150]{0:T(256)S(1)}, bf16[150,4096]{1,0:T(8,128)(2,1)S(1)}) fusion(f32[150,4096]{1,0:T(8,128)S(1)} %fusion.1, bf16[300,4096]{1,0:T(8,128)(2,1)S(1)} %bitcast.90, bf16[150,300]{1,0:T(8,128)(2,1)S(1)} %copy-done.47), kind=kOutput, calls=%fused_computation.25 | convolution fusion | flops 382156640 | bytes 6234600 | tf_op jit(solution)/shard_map/dot_general | solution.py:113
  86.2 1.8 convolution_multiply_fusion
  88.0 2.2 %fusion.2 = bf16[300,4096]{1,0:T(8,128)(2,1)S(1)} fusion(bf16[150,4096]{1,0:T(8,128)(2,1)} %copy-done.11, bf16[300,150]{0,1:T(8,128)(2,1)S(1)} %copy-done), kind=kOutput, calls=%fused_computation.4 | convolution fusion | flops 369868800 | bytes 3776400 | tf_op jit(solution)/shard_map/dot_general | solution.py:122
  90.2 27.2 %fusion = bf16[80,4096]{1,0:T(8,128)(2,1)} fusion(bf16[300,4096]{1,0:T(8,128)(2,1)S(1)} %fusion.2), kind=kCustom, calls=%all-reduce-scatter | all-reduce-scatter fusion | flops 1310721 | bytes 3113472
  120.6 5.9 %concatenate.62 = bf16[95,4096]{1,0:T(8,128)(2,1)} concatenate(bf16[15,4096]{1,0:T(8,128)(2,1)S(1)} %collective-permute-done.8, bf16[80,4096]{1,0:T(8,128)(2,1)} %fusion), dimensions={0} | concatenate | bytes 1556480
  126.6 1.4 constant_dynamic-slice_fusion
  128.4 4.9 %fusion.28 = (f32[75]{0:T(128)}, f32[75]{0:T(128)}, f32[75]{0:T(128)}, f32[75]{0:T(128)}, f32[75]{0:T(128)}, /*index=5*/f32[75]{0:T(128)}, f32[75]{0:T(128)}, f32[75]{0:T(128)}, f32[75]{0:T(128)}) fusion(bf16[75,32,128]{2,1,0:T(8,128)(2,1)S(1)} %broadcast_multiply_fusion, bf16[75,32,2]{2,1,0:T(8,128)(2,1)S(1)} %copy-done.6, ...), kind=kLoop, calls=%fused_computation.58 | loop fusion | flops 10444125 | bytes 4937100 | tf_op jit(solution)/shard_map/reduce_sum | solution.py:140
  133.6 12.7 %all_gather.15 = bf16[75,2,512]{2,1,0:T(2,128)(2,1)S(1)} all-gather(bf16[75,2,128]{2,1,0:T(2,128)(2,1)S(1)} %slice.285), channel_id=1, replica_groups=mesh['lon'=4,'lat'=2,'ch'=4] {'lon'}, dimensions={2}, use_global_device_ids=true | all-gather | bytes 192000 | tf_op jit(solution)/shard_map/all_gather | solution.py:30
  148.0 2.0 collective-permute-start.4
  150.2 3.5 %collective-permute-done.4 = bf16[75,32,2]{0,1,2:T(8,128)(2,1)S(1)} collective-permute-done((bf16[75,32,2]{0,1,2:T(8,128)(2,1)S(1)}, bf16[75,32,2]{0,1,2:T(8,128)(2,1)S(1)}, u32[]{:S(2)}, u32[]{:S(2)}) %collective-permute-start.4) | collective-permute-done | bytes 9632 | tf_op jit(solution)/shard_map/ppermute | solution.py:17
  156.2 1.6 collective-permute-start.7
  157.8 1.4 rev.7
  159.9 18.7 %all-reduce.2 = (f32[150]{0:T(256)}, f32[3,3,75]{2,1,0:T(4,128)}) all-reduce(f32[150]{0:T(256)S(1)} %copy-done.33, f32[3,3,75]{2,1,0:T(4,128)S(1)} %maximum_multiply_fusion), channel_id=1, replica_groups=mesh['lon'=4,'lat'=2,'ch'=4] {'lon','lat'}, use_global_device_ids=true, to_apply=%region_5.6 | all-reduce | flops 825 | bytes 6600 | tf_op jit(solution)/shard_map/psum | solution.py:170
  178.5 1.4 collective-permute-start.6
  180.0 3.2 %collective-permute-done.6 = bf16[75,2,132]{2,1,0:T(2,128)(2,1)S(1)} collective-permute-done((bf16[75,2,132]{2,1,0:T(2,128)(2,1)S(1)}, bf16[75,2,132]{2,1,0:T(2,128)(2,1)S(1)}, u32[]{:S(2)}, u32[]{:S(2)}) %collective-permute-start.6) | collective-permute-done | bytes 39632 | tf_op jit(solution)/shard_map/ppermute | solution.py:20
  183.8 2.4 %pad_maximum_fusion.1 = (bf16[75,34,132]{2,1,0:T(8,128)(2,1)S(1)}, bf16[75,34,132]{2,1,0:T(8,128)(2,1)S(1)}) fusion(bf16[75,2,132]{2,1,0:T(2,128)(2,1)S(1)} %broadcast_select_fusion, bf16[75,32,2]{2,1,0:T(8,128)(2,1)S(1)} %copy.39, bf16[75,32,128]{2,1,0:T(8,128)(2,1)S(1)} %slice.299, bf16[75,32,2]{2,1,0:T(8,128)(2,1)S(1)} %copy.38, ...), kind=kLoop, calls=%fused_computation.29 | loop fusion | flops 5385600 | bytes 2059200 | tf_op jit(solution)/shard_map/concatenate | solution.py:49
  186.4 3.4 %fusion.24 = f32[75,32,128]{2,1,0:T(8,128)S(1)} fusion(bf16[75,32,128]{2,1,0:T(8,128)(2,1)S(1)} %slice.299, bf16[75,34,132]{2,1,0:T(8,128)(2,1)S(1)} %get-tuple-element.46, bf16[75,32,2]{2,1,0:T(8,128)(2,1)S(1)} %copy.38, bf16[75,32,2]{2,1,0:T(8,128)(2,1)S(1)} %copy.39, bf16[75,34,132]{2,1,0:T(8,128)(2,1)S(1)} %get-tuple-element.45, f32[75]{0:T(128)S(1)} %copy-done.29, ...), kind=kLoop, calls=%fused_computation.54 | loop fusion | flops 9830400 | bytes 5551500 | tf_op jit(solution)/shard_map/add | solution.py:148
  191.3 2.7 %all-reduce.6.cloned.1.call-done = (f32[300,150]{0,1:T(8,128)}, f32[150,300]{1,0:T(8,128)}) async-done(((f32[300,150]{0,1:T(8,128)}, f32[150,300]{1,0:T(8,128)}), (f32[300,150]{0,1:T(8,128)}, f32[150,300]{1,0:T(8,128)})) %all-reduce.6.cloned.1.call-update) | async-done | bytes 360016 | tf_op jit(solution)/shard_map/psum | solution.py:170
  194.0 1.6 copy.49
  195.7 1.6 copy.50
  (158 shorter events, 29.5 us)
Async XLA Ops:
  7.2 72.6 %copy-start = (bf16[300,150]{0,1:T(8,128)(2,1)S(1)}, bf16[300,150]{0,1:T(8,128)(2,1)}, u32[]{:S(2)}) copy-start(bf16[300,150]{0,1:T(8,128)(2,1)} %param.19) | copy-start | bytes 270004
  7.2 49.1 %all-gather.3.cloned.1.call-start = ((), (), s32[]{:S(2)}) async-start(), calls=%async_computation | async-start | bytes 3072000 | tf_op jit(solution)/shard_map/all_gather | solution.py:104
  14.4 62.1 %all-gather.5.cloned.1.call-start = ((), (), s32[]{:S(2)}) async-start(), calls=%async_computation.1 | async-start | bytes 3072000 | tf_op jit(solution)/shard_map/all_gather | solution.py:103
  16.0 19.9 %collective-permute-start.1 = (bf16[75,32,2]{0,1,2:T(8,128)(2,1)S(1)}, bf16[75,32,2]{0,1,2:T(8,128)(2,1)S(1)}, u32[]{:S(2)}, u32[]{:S(2)}) collective-permute-start(bf16[75,32,2]{0,1,2:T(8,128)(2,1)S(1)} %copy.31), channel_id=1, source_target_pairs={{8,0},{16,8},{24,16},{0,24},{9,1},{17,9},{25,17},{1,25},{10,2},{18... | collective-permute-start | bytes 28808 | tf_op jit(solution)/shard_map/ppermute | solution.py:20
  21.8 13.0 %collective-permute-start = (bf16[75,32,2]{0,1,2:T(8,128)(2,1)S(1)}, bf16[75,32,2]{0,1,2:T(8,128)(2,1)S(1)}, u32[]{:S(2)}, u32[]{:S(2)}) collective-permute-start(bf16[75,32,2]{0,1,2:T(8,128)(2,1)S(1)} %copy.30), channel_id=1, source_target_pairs={{0,8},{8,16},{16,24},{24,0},{1,9},{9,17},{17,25},{25,1},{2,10},{10... | collective-permute-start | bytes 28808 | tf_op jit(solution)/shard_map/ppermute | solution.py:17
  35.9 12.7 %copy-start.5 = (bf16[75,32,2]{2,1,0:T(8,128)(2,1)}, bf16[75,32,2]{2,1,0:T(8,128)(2,1)S(1)}, u32[]{:S(2)}) copy-start(bf16[75,32,2]{2,1,0:T(8,128)(2,1)S(1)} %copy.32) | copy-start | bytes 28804
  36.9 11.6 %copy-start.7 = (bf16[75,32,2]{2,1,0:T(8,128)(2,1)}, bf16[75,32,2]{2,1,0:T(8,128)(2,1)S(1)}, u32[]{:S(2)}) copy-start(bf16[75,32,2]{2,1,0:T(8,128)(2,1)S(1)} %copy.33) | copy-start | bytes 28804
  37.4 5.0 %collective-permute-start.2 = (bf16[75,2,132]{2,1,0:T(2,128)(2,1)S(1)}, bf16[75,2,132]{2,1,0:T(2,128)(2,1)S(1)}, u32[]{:S(2)}, u32[]{:S(2)}) collective-permute-start(bf16[75,2,132]{2,1,0:T(2,128)(2,1)S(1)} %get-tuple-element.51), channel_id=1, source_target_pairs={{0,4},{4,0},{1,5},{5,1},{2,6},{6,2},{3,7},{7,3},{8,12},{12,8},{9,1... | collective-permute-start | bytes 118808 | tf_op jit(solution)/shard_map/ppermute | solution.py:17
  39.0 9.5 %copy-start.16 = (f32[75]{0:T(128)}, f32[75]{0:T(128)S(1)}, u32[]{:S(2)}) copy-start(f32[75]{0:T(128)S(1)} %get-tuple-element.73) | copy-start | bytes 904
  39.0 9.5 %copy-start.18 = (f32[75]{0:T(128)}, f32[75]{0:T(128)S(1)}, u32[]{:S(2)}) copy-start(f32[75]{0:T(128)S(1)} %get-tuple-element.74) | copy-start | bytes 904
  39.0 9.5 %copy-start.20 = (f32[75]{0:T(128)}, f32[75]{0:T(128)S(1)}, u32[]{:S(2)}) copy-start(f32[75]{0:T(128)S(1)} %get-tuple-element.75) | copy-start | bytes 904
  39.0 9.5 %copy-start.22 = (f32[75]{0:T(128)}, f32[75]{0:T(128)S(1)}, u32[]{:S(2)}) copy-start(f32[75]{0:T(128)S(1)} %get-tuple-element.76) | copy-start | bytes 904
  39.0 9.5 %copy-start.24 = (f32[75]{0:T(128)}, f32[75]{0:T(128)S(1)}, u32[]{:S(2)}) copy-start(f32[75]{0:T(128)S(1)} %get-tuple-element.77) | copy-start | bytes 904
  39.1 9.5 %copy-start.26 = (f32[75]{0:T(128)}, f32[75]{0:T(128)S(1)}, u32[]{:S(2)}) copy-start(f32[75]{0:T(128)S(1)} %get-tuple-element.78) | copy-start | bytes 904
  39.1 9.5 %copy-start.28 = (f32[75]{0:T(128)}, f32[75]{0:T(128)S(1)}, u32[]{:S(2)}) copy-start(f32[75]{0:T(128)S(1)} %get-tuple-element.79) | copy-start | bytes 904
  39.1 9.5 %copy-start.30 = (f32[75]{0:T(128)}, f32[75]{0:T(128)S(1)}, u32[]{:S(2)}) copy-start(f32[75]{0:T(128)S(1)} %get-tuple-element.80) | copy-start | bytes 904
  41.2 4.4 %collective-permute-start.3 = (bf16[75,2,132]{2,1,0:T(2,128)(2,1)S(1)}, bf16[75,2,132]{2,1,0:T(2,128)(2,1)S(1)}, u32[]{:S(2)}, u32[]{:S(2)}) collective-permute-start(bf16[75,2,132]{2,1,0:T(2,128)(2,1)S(1)} %get-tuple-element.52), channel_id=1, source_target_pairs={{4,0},{0,4},{5,1},{1,5},{6,2},{2,6},{7,3},{3,7},{12,8},{8,12},{13,... | collective-permute-start | bytes 118808 | tf_op jit(solution)/shard_map/ppermute | solution.py:20
  54.3 139.7 %all-reduce.6.cloned.1.call-start = ((), (), s32[]{:S(2)}) async-start(), calls=%async_computation.2 | async-start | bytes 933888 | tf_op jit(solution)/shard_map/psum | solution.py:170
  118.3 2.3 %collective-permute-start.8 = (bf16[15,4096]{1,0:T(8,128)(2,1)S(1)}, bf16[15,4096]{1,0:T(8,128)(2,1)S(1)}, u32[]{:S(2)}, u32[]{:S(2)}) collective-permute-start(bf16[15,4096]{1,0:T(8,128)(2,1)S(1)} %slice.298), channel_id=1, source_target_pairs={{0,1},{1,2},{2,3},{4,5},{5,6},{6,7},{8,9},{9,10},{10,11},{12,13},{... | collective-permute-start | bytes 368648
  133.6 16.5 %copy-start.34 = (f32[75]{0:T(128)S(1)}, f32[75]{0:T(128)}, u32[]{:S(2)}) copy-start(f32[75]{0:T(128)} %get-tuple-element.35) | copy-start | bytes 904
  133.6 16.5 %copy-start.35 = (f32[75]{0:T(128)S(1)}, f32[75]{0:T(128)}, u32[]{:S(2)}) copy-start(f32[75]{0:T(128)} %get-tuple-element.36) | copy-start | bytes 904
  133.6 16.5 %copy-start.36 = (f32[75]{0:T(128)S(1)}, f32[75]{0:T(128)}, u32[]{:S(2)}) copy-start(f32[75]{0:T(128)} %get-tuple-element.37) | copy-start | bytes 904
  133.6 16.4 %copy-start.37 = (f32[75]{0:T(128)S(1)}, f32[75]{0:T(128)}, u32[]{:S(2)}) copy-start(f32[75]{0:T(128)} %get-tuple-element.56) | copy-start | bytes 904
  133.6 16.4 %copy-start.38 = (f32[75]{0:T(128)S(1)}, f32[75]{0:T(128)}, u32[]{:S(2)}) copy-start(f32[75]{0:T(128)} %get-tuple-element.57) | copy-start | bytes 904
  133.6 16.4 %copy-start.39 = (f32[75]{0:T(128)S(1)}, f32[75]{0:T(128)}, u32[]{:S(2)}) copy-start(f32[75]{0:T(128)} %get-tuple-element.58) | copy-start | bytes 904
  133.6 16.5 %copy-start.43 = (f32[75]{0:T(128)S(1)}, f32[75]{0:T(128)}, u32[]{:S(2)}) copy-start(f32[75]{0:T(128)} %get-tuple-element.53) | copy-start | bytes 904
  133.6 16.5 %copy-start.44 = (f32[75]{0:T(128)S(1)}, f32[75]{0:T(128)}, u32[]{:S(2)}) copy-start(f32[75]{0:T(128)} %get-tuple-element.54) | copy-start | bytes 904
  133.6 16.5 %copy-start.45 = (f32[75]{0:T(128)S(1)}, f32[75]{0:T(128)}, u32[]{:S(2)}) copy-start(f32[75]{0:T(128)} %get-tuple-element.55) | copy-start | bytes 904
  148.0 6.7 %collective-permute-start.5 = (bf16[75,32,2]{0,1,2:T(8,128)(2,1)S(1)}, bf16[75,32,2]{0,1,2:T(8,128)(2,1)S(1)}, u32[]{:S(2)}, u32[]{:S(2)}) collective-permute-start(bf16[75,32,2]{0,1,2:T(8,128)(2,1)S(1)} %copy.37), channel_id=1, source_target_pairs={{8,0},{16,8},{24,16},{0,24},{9,1},{17,9},{25,17},{1,25},{10,2},{18... | collective-permute-start | bytes 28808 | tf_op jit(solution)/shard_map/ppermute | solution.py:20
  148.0 5.6 %collective-permute-start.4 = (bf16[75,32,2]{0,1,2:T(8,128)(2,1)S(1)}, bf16[75,32,2]{0,1,2:T(8,128)(2,1)S(1)}, u32[]{:S(2)}, u32[]{:S(2)}) collective-permute-start(bf16[75,32,2]{0,1,2:T(8,128)(2,1)S(1)} %copy.36), channel_id=1, source_target_pairs={{0,8},{8,16},{16,24},{24,0},{1,9},{9,17},{17,25},{25,1},{2,10},{10... | collective-permute-start | bytes 28808 | tf_op jit(solution)/shard_map/ppermute | solution.py:17
  156.2 23.7 %collective-permute-start.7 = (bf16[75,2,132]{2,1,0:T(2,128)(2,1)S(1)}, bf16[75,2,132]{2,1,0:T(2,128)(2,1)S(1)}, u32[]{:S(2)}, u32[]{:S(2)}) collective-permute-start(bf16[75,2,132]{2,1,0:T(2,128)(2,1)S(1)} %get-tuple-element.48), channel_id=1, source_target_pairs={{0,4},{4,0},{1,5},{5,1},{2,6},{6,2},{3,7},{7,3},{8,12},{12,8},{9,1... | collective-permute-start | bytes 118808 | tf_op jit(solution)/shard_map/ppermute | solution.py:17
  178.5 4.7 %collective-permute-start.6 = (bf16[75,2,132]{2,1,0:T(2,128)(2,1)S(1)}, bf16[75,2,132]{2,1,0:T(2,128)(2,1)S(1)}, u32[]{:S(2)}, u32[]{:S(2)}) collective-permute-start(bf16[75,2,132]{2,1,0:T(2,128)(2,1)S(1)} %get-tuple-element.47), channel_id=1, source_target_pairs={{4,0},{0,4},{5,1},{1,5},{6,2},{2,6},{7,3},{3,7},{12,8},{8,12},{13,... | collective-permute-start | bytes 118808 | tf_op jit(solution)/shard_map/ppermute | solution.py:20
  (28 other events, 87.4 us)
Sparse Core Ops, SparseCore 0:
  14.5 27.3 all-gather.2
  54.4 22.0 all-gather.4
  119.8 74.1 all-reduce.5
where the time goes:
time: 205 us; the launch traced here: 204 us
  blocking collectives  71.3 us (35%)
  local copies, waits for them, and re-layouts  34.7 us (17%)
  waiting for transfers between devices  30.3 us (15%)
  other arithmetic  29 us (14%)
  between operations  15.3 us (7%)
  starting transfers between devices  13.9 us (7%)
  matrix products  9.26 us (5%)
    unnamed x1, blocking collectives  27.2 us
    all_gather x2, blocking collectives, extend(): gathered = lax.all_gather(uppermost_rows, 'lon', axis=2, tiled=True)  25.4 us
    unnamed x107, local copies, waits for them, and re-layouts  22.5 us
    psum x1, blocking collectives, on_device(): lax.psum((expand_part, project_part, bias_part, kernel_part), ('lon', 'la...  18.7 us
    all_gather x1, waiting for transfers between devices, on_device(): lax.all_gather(conv_out, 'ch', axis=0, tiled=True)  16.8 us
    ppermute x4, starting transfers between devices, with_halo(): lax.ppermute(lax.slice_in_dim(block, 0, width, axis=dim), axis, backward)  7.07 us
    ppermute x4, waiting for transfers between devices, with_halo(): lax.ppermute(lax.slice_in_dim(block, 0, width, axis=dim), axis, backward)  6.39 us
    ppermute x4, starting transfers between devices, with_halo(): lax.ppermute(lax.slice_in_dim(block, block.shape[dim] - width, None, axis...  5.22 us
  transfers between devices with their start and end apart: 12, of which 7 were waited for; matrix products, arithmetic and copies ran while one was open for 22% of the time, Pallas kernels for 0%

commit v1 on v0

v1 whole, which is shorter than its diff:
```python
import functools
import math

import jax
import jax.numpy as jnp
from jax import lax
from jax.experimental import pallas as pl
from jax.experimental.pallas import tpu as pltpu
from jax.sharding import PartitionSpec as P

DIL = 2
LANES = 128
BF = jnp.bfloat16
F32 = jnp.float32


def shape(dims, kind):
    return jax.ShapeDtypeStruct(dims, kind)


def call(kernel, outs, args, scratch=(), name=None, flops=0, moved=None):
    if moved is None:
        moved = sum(math.prod(a.shape) * a.dtype.itemsize for a in list(args) + list(outs))
    return pl.pallas_call(
        kernel,
        out_shape=tuple(outs),
        in_specs=[pl.BlockSpec(memory_space=pltpu.VMEM) for _ in args],
        out_specs=tuple(pl.BlockSpec(memory_space=pltpu.VMEM) for _ in outs),
        scratch_shapes=list(scratch),
        name=name,
        compiler_params=pltpu.CompilerParams(vmem_limit_bytes=48 * 1024 * 1024),
        cost_estimate=pl.CostEstimate(flops=flops, bytes_accessed=moved, transcendentals=0),
    )(*args)


def iota(dims, dim):
    return lax.broadcasted_iota(jnp.int32, dims, dim)


def aligned(index):
    return pl.multiple_of(index, 16)


def to_rows(block_ref, weight, scr, pad):
    channels, rows, cols = block_ref.shape

    def body(c, carry):
        value = block_ref[c].astype(F32)
        if weight is not None:
            value = value * weight
        scr[pl.ds(c, rows, stride=pad), :] = value
        return carry

    lax.fori_loop(0, channels, body, 0, unroll=5 if channels % 5 == 0 else 1)
    for c in range(channels, pad):
        scr[pl.ds(c, rows, stride=pad), :] = jnp.zeros((rows, cols), F32)


def pack_columns(value, ext_row, left, right):
    lane = iota(value.shape, 1)
    here = (lane == 2 * ext_row) | (lane == 2 * ext_row + 1)
    size = value.shape[1]
    left = jnp.where(here, pltpu.roll(value, (2 * ext_row) % size, 1), left)
    right = jnp.where(here, pltpu.roll(value, (2 * ext_row + 2) % size, 1), right)
    return left, right


def mirrored(value):
    size = value.shape[1]
    flip = (iota((size, size), 0) + iota((size, size), 1) == size - 1).astype(BF)
    return jnp.dot(value, flip, preferred_element_type=F32).astype(BF)


def emit_strips(read, rows, pad, swap, strips):
    if swap:
        strip_ref, fold_ref, left_ref, right_ref = strips
        at_bottom = lax.axis_index("lat") == 0
        for t in range(DIL):
            low, high = read(t), read(rows - DIL + t)
            strip_ref[t] = jnp.where(at_bottom, high.astype(F32), low.astype(F32)).astype(BF)
    else:
        down_ref, up_ref, fold_ref, left_ref, right_ref = strips
        for t in range(DIL):
            down_ref[t] = read(t)
            up_ref[t] = read(rows - DIL + t)
    for t in range(DIL):
        fold_ref[t] = mirrored(read(rows - 1 - t))
    left = jnp.zeros((pad, LANES), F32)
    right = jnp.zeros((pad, LANES), F32)
    for r in range(rows):
        left, right = pack_columns(read(r).astype(F32), r + DIL, left, right)
    left_ref[...] = left.astype(BF)
    right_ref[...] = right.astype(BF)


def strip_shapes(pad, swap):
    one = shape((DIL, pad, LANES), BF)
    packs = [shape((pad, LANES), BF)] * 2
    return ([one] if swap else [one, one]) + [one] + packs


def prepare_state(swap, state_ref, mask_ref, rows_ref, *rest):
    strips, scr = rest[:-1], rest[-1]
    rows, pad = rows_ref.shape[:2]
    to_rows(state_ref, mask_ref[...].astype(F32), scr, pad)
    for r in range(rows):
        rows_ref[r] = scr[r * pad : (r + 1) * pad, :].astype(BF)
    emit_strips(lambda r: rows_ref[r], rows, pad, swap, strips)


def prepare_cotan(grad_ref, mask_ref, offset_ref, value_ref, rows_ref, *rest):
    quarters, scr = rest[:-1], rest[-1]
    rows, pad, cols = rows_ref.shape
    me = lax.axis_index("ch")
    mask = mask_ref[...].astype(F32)
    to_rows(grad_ref, None, scr, pad)
    offset = offset_ref[...]
    points = offset.shape[1]
    value = value_ref[...]
    total = jnp.zeros((rows, cols), F32)
    row_hot = iota((rows, points), 0) == offset // cols
    col_hot = (iota((cols, points), 0) == offset % cols).astype(BF)
    for _ in range(3):
        part = value.astype(BF)
        value = value - part.astype(F32)
        lhs = jnp.where(row_hot, part.astype(F32), 0.0).astype(BF)
        total = total + lax.dot_general(
            lhs, col_hot, (((1,), (1,)), ((), ())), preferred_element_type=F32
        )
    total = jnp.where(me == 0, total, 0.0)
    first = scr[pl.ds(0, rows, stride=pad), :]
    scr[pl.ds(0, rows, stride=pad), :] = first + total
    for r in range(rows):
        rows_ref[r] = (scr[r * pad : (r + 1) * pad, :] * mask[r : r + 1, :]).astype(BF)
    part_rows = quarters[0].shape[0]
    for k, quarter in enumerate(quarters):
        quarter[...] = rows_ref[pl.ds((me ^ k) * part_rows, part_rows)]


def ring(count, step):
    return [(i, (i + step) % count) for i in range(count)]


def exchange_halo(strips, rows, pad, swap, name):
    n_lat, n_lon = lax.axis_size("lat"), lax.axis_size("lon")
    top = n_lat - 1
    fold_pairs = [
        (lon * n_lat + top, (n_lon - 1 - lon) * n_lat + top) for lon in range(n_lon)
    ]
    if swap:
        strip, fold, left, right = strips
        moved = [lax.ppermute(strip, "lat", [(0, 1), (1, 0)])]
    else:
        down, up, fold, left, right = strips
        moved = [
            lax.ppermute(up, "lat", [(i, i + 1) for i in range(n_lat - 1)]),
            lax.ppermute(down, "lat", [(i + 1, i) for i in range(n_lat - 1)]),
        ]
    fold = lax.ppermute(fold, ("lon", "lat"), fold_pairs)
    kernel = functools.partial(finish_columns, rows, swap)
    halo, left, right = call(
        kernel,
        [shape((2 * DIL, pad, LANES), BF)] + [shape((pad, LANES), BF)] * 2,
        [*moved, fold, left, right],
        name=name,
    )
    from_right = lax.ppermute(left, "lon", ring(n_lon, -1))
    from_left = lax.ppermute(right, "lon", ring(n_lon, 1))
    return halo, from_left, from_right


def finish_columns(rows, swap, *refs):
    if swap:
        strip_ref, fold_ref, left_ref, right_ref, halo_ref, left_out, right_out = refs
        low_ref = high_ref = strip_ref
    else:
        low_ref, high_ref, fold_ref, left_ref, right_ref, halo_ref, left_out, right_out = refs
    lat, count = lax.axis_index("lat"), lax.axis_size("lat")
    left, right = left_ref[...].astype(F32), right_ref[...].astype(F32)
    for t in range(DIL):
        south = jnp.where(lat == 0, 0.0, low_ref[t].astype(F32))
        north = jnp.where(lat == count - 1, fold_ref[t].astype(F32), high_ref[t].astype(F32))
        halo_ref[t] = south.astype(BF)
        halo_ref[DIL + t] = north.astype(BF)
        left, right = pack_columns(south, t, left, right)
        left, right = pack_columns(north, rows + DIL + t, left, right)
    left_out[...] = left.astype(BF)
    right_out[...] = right.astype(BF)


def shifted_rows(block_ref, halo_ref, left_ref, right_ref, group):
    rows = block_ref.shape[0]
    at = pl.ds(aligned(group * 16), 16)
    lane = iota((16, LANES), 1)
    left, right = left_ref[at, :].astype(F32), right_ref[at, :].astype(F32)
    for e in range(rows + 2 * DIL):
        if e < DIL:
            row = halo_ref[e, at, :]
        elif e < rows + DIL:
            row = block_ref[e - DIL, at, :]
        else:
            row = halo_ref[e - rows, at, :]
        row = row.astype(F32)
        west = jnp.where(
            lane < DIL, pltpu.roll(left, (-2 * e) % LANES, 1), pltpu.roll(row, DIL, 1)
        )
        east = jnp.where(
            lane >= LANES - DIL,
            pltpu.roll(right, (LANES - DIL - 2 * e) % LANES, 1),
            pltpu.roll(row, LANES - DIL, 1),
        )
        yield e, (west, row, east)


def stencil(block_ref, halo_ref, left_ref, right_ref, group, taps, north, emit):
    rows = block_ref.shape[0]
    sums = {}
    for e, shifts in shifted_rows(block_ref, halo_ref, left_ref, right_ref, group):
        for a in (2, 1, 0):
            r = e - DIL * a
            if not 0 <= r < rows:
                continue
            used = north if e >= rows + DIL else taps[a]
            term = used[0] * shifts[0] + used[1] * shifts[1] + used[2] * shifts[2]
            sums[r] = term if r not in sums else sums[r] + term
            if a == 2:
                emit(r, sums.pop(r))


def spread(tap_ref, group):
    values = tap_ref[pl.ds(aligned(group * 16), 16), :]
    return [
        [jnp.broadcast_to(values[:, 3 * a + b : 3 * a + b + 1], (16, LANES)) for b in range(3)]
        for a in range(3)
    ]


def conv_forward(ones_row, block_ref, halo_ref, left_ref, right_ref, tap_ref, *rest):
    quarters, scr = rest[:-1], rest[-1]
    pad = block_ref.shape[1]
    me = lax.axis_index("ch")

    def body(group, carry):
        taps = spread(tap_ref, group)
        is_one = iota((16, LANES), 0) + group * 16 == ones_row

        def emit(r, value):
            value = jnp.where(is_one, 1.0, value)
            scr[r, pl.ds(aligned(group * 16), 16), :] = value.astype(BF)

        stencil(block_ref, halo_ref, left_ref, right_ref, group, taps, taps[2], emit)
        return carry

    lax.fori_loop(0, pad // 16, body, 0)
    part_rows = quarters[0].shape[0]
    for k, quarter in enumerate(quarters):
        quarter[...] = scr[pl.ds((me ^ k) * part_rows, part_rows)]


def conv_adjoint(
    block_ref, halo_ref, left_ref, right_ref, tap_ref, cotan_ref, mask_ref, out_ref, scr
):
    rows, pad = block_ref.shape[:2]
    at_top = lax.axis_index("lat") == lax.axis_size("lat") - 1
    mask = mask_ref[...].astype(F32)

    def body(group, carry):
        taps = spread(tap_ref, group)
        back = [[taps[2 - a][2 - b] for b in range(3)] for a in range(3)]
        north = [jnp.where(at_top, taps[2][b], back[2][b]) for b in range(3)]

        def emit(r, value):
            cotan = cotan_ref[r, pl.ds(aligned(group * 16), 16), :].astype(F32)
            scr[pl.ds(pl.multiple_of(r * pad + group * 16, 16), 16), :] = (cotan + value) * mask[
                r : r + 1, :
            ]

        stencil(block_ref, halo_ref, left_ref, right_ref, group, back, north, emit)
        return carry

    lax.fori_loop(0, pad // 16, body, 0)

    def write(c, carry):
        out_ref[c] = scr[pl.ds(c, rows, stride=pad), :].astype(BF)
        return carry

    channels = out_ref.shape[0]
    lax.fori_loop(0, channels, write, 0, unroll=5 if channels % 5 == 0 else 1)


def collect_grad(swap, q0, q1, q2, q3, rows_ref, *strips):
    part_rows = q0.shape[0]
    rows, pad = rows_ref.shape[:2]
    me = lax.axis_index("ch")
    for k, quarter in enumerate((q0, q1, q2, q3)):
        rows_ref[pl.ds((me ^ k) * part_rows, part_rows)] = quarter[...]
    emit_strips(lambda r: rows_ref[r], rows, pad, swap, strips)


def kernel_gradient(grad_ref, block_ref, halo_ref, left_ref, right_ref, out_ref):
    rows, pad = grad_ref.shape[:2]

    def body(group, carry):
        at = pl.ds(aligned(group * 16), 16)
        sums = [[jnp.zeros((16, LANES), F32) for _ in range(3)] for _ in range(3)]
        for e, shifts in shifted_rows(block_ref, halo_ref, left_ref, right_ref, group):
            for a in range(3):
                r = e - DIL * a
                if 0 <= r < rows:
                    grad = grad_ref[r, at, :].astype(F32)
                    for b in range(3):
                        sums[a][b] = sums[a][b] + grad * shifts[b]
        lane = iota((16, LANES), 1)
        out = jnp.zeros((16, LANES), F32)
        for a in range(3):
            for b in range(3):
                total = jnp.sum(sums[a][b], axis=1, keepdims=True)
                out = jnp.where(lane == 3 * a + b, total, out)
        out_ref[at, :] = out
        return carry

    lax.fori_loop(0, pad // 16, body, 0)


def channel_of(slot, part, pad):
    block = sum((slot >= pad * b).astype(jnp.int32) for b in range(1, 4))
    inside = slot - block * pad
    return jnp.where((slot >= 0) & (slot < 4 * pad) & (inside < part), block * part + inside, -1)


def expand_slot(lane, pad):
    return jnp.where(lane < 4 * pad, lane, -1)


def project_slot(lane, pad, split):
    tail = 4 * pad - split
    low = LANES - tail
    return jnp.where(lane >= LANES, lane - LANES, jnp.where(lane >= low, lane - low + split, -1))


def pack_weights(part, pad, expand_ref, bias_ref, project_ref, out_ref):
    channels, hidden = expand_ref.shape
    wide = out_ref.shape[1]
    split = 4 * pad // LANES * LANES
    lane = iota((channels, wide), 1)
    row = iota((channels, wide), 0)
    pick_e = (channel_of(expand_slot(lane, pad), part, pad) == row).astype(BF)
    slot = jnp.where(lane >= split, project_slot(lane - split, pad, split), -1)
    pick_p = (channel_of(slot, part, pad) == row).astype(BF)
    bias = bias_ref[...]
    parts = jnp.zeros((16, hidden), F32)
    at = iota((16, hidden), 0)
    for k in range(3):
        piece = bias.astype(BF).astype(F32)
        bias = bias - piece
        parts = jnp.where(at == k, piece, parts)
    lane, row = iota((16, wide), 1), iota((16, wide), 0)
    pick_b = ((lane == row * pad + part) & (row < 3)).astype(BF)
    turned = (((0,), (0,)), ((), ()))
    packed = (
        lax.dot_general(expand_ref[...], pick_e, turned, preferred_element_type=F32)
        + lax.dot_general(parts.astype(BF), pick_b, turned, preferred_element_type=F32)
        + jnp.dot(project_ref[...], pick_p, preferred_element_type=F32)
    )
    rows = out_ref.shape[0]
    out_ref[0:hidden, :] = packed.astype(BF)
    out_ref[hidden:rows, :] = jnp.zeros((rows - hidden, wide), BF)


GELU_C = math.sqrt(2.0 / math.pi)


def mlp(*refs):
    xs, ys, ws = refs[0:4], refs[4:8], refs[8:12]
    grads, keep_ref, send_ref = refs[12:16], refs[16], refs[17]
    x_scr, y_scr, w_scr, t_scr, act_scr, pre_scr, cg_scr = refs[18:]
    part_rows, pad = xs[0].shape[:2]
    hid = ws[0].shape[0]
    split = 4 * pad // LANES * LANES
    depth = x_scr.shape[0]
    cells = x_scr.shape[1]
    me = lax.axis_index("ch")
    x_scr[4 * pad : depth, :] = jnp.zeros((depth - 4 * pad, cells), BF)
    y_scr[0 : depth - 4 * pad, :] = jnp.zeros((depth - 4 * pad, cells), BF)
    for k in range(4):
        block = me ^ k
        w_scr[k * hid : (k + 1) * hid, :] = ws[k][...]
        for r in range(part_rows):
            cols = slice(r * LANES, (r + 1) * LANES)
            x_scr[pl.ds(aligned(block * pad), pad), cols] = xs[k][r]
            for u in range(pad // 16):
                slot = block * pad + 16 * u
                to = jnp.where(slot < split, slot + LANES, slot - split + depth - 4 * pad)
                y_scr[pl.ds(aligned(to), 16), cols] = ys[k][r, 16 * u : 16 * (u + 1), :]
    t_scr[...] = jnp.transpose(w_scr[:, 0:depth])
    step = 256
    for start in range(0, cells, step):
        cols = slice(start, start + step)
        hidden = jnp.dot(w_scr[:, 0:depth], x_scr[:, cols], preferred_element_type=F32)
        act_grad = jnp.dot(w_scr[:, split : split + depth], y_scr[:, cols], preferred_element_type=F32)
        square = hidden * hidden
        tanh = jnp.tanh(GELU_C * hidden * (1.0 + 0.044715 * square))
        half = 0.5 * (1.0 + tanh)
        slope = half + (0.5 * GELU_C) * hidden * (1.0 - tanh * tanh) * (
            1.0 + (3 * 0.044715) * square
        )
        act_scr[:, cols] = (hidden * half).astype(BF)
        pre = (act_grad * slope).astype(BF)
        pre_scr[:, cols] = pre
        cg_scr[:, cols] = jnp.dot(t_scr[...], pre, preferred_element_type=F32).astype(BF)
    for k in range(4):
        for r in range(part_rows):
            grads[k][r] = cg_scr[
                pl.ds(aligned((me ^ k) * pad), pad), r * LANES : (r + 1) * LANES
            ]
    over_cells = (((1,), (1,)), ((), ()))
    expand = lax.dot_general(pre_scr[...], x_scr[...], over_cells, preferred_element_type=F32)
    project = lax.dot_general(act_scr[...], y_scr[...], over_cells, preferred_element_type=F32)
    shared = split // LANES
    tiles = [expand[:, t * LANES : (t + 1) * LANES] for t in range(shared)]
    tiles.append(expand[:, split : split + LANES] + project[:, 0:LANES])
    tiles += [project[:, t * LANES : (t + 1) * LANES] for t in range(1, shared + 1)]
    for k in range(4):
        to = send_ref if k % 2 else keep_ref
        for t, tile in enumerate(tiles):
            to[k // 2, t * hid : (t + 1) * hid, :] = tile[k * hid : (k + 1) * hid].astype(to.dtype)


def add_cores(keep_ref, got_ref, own_ref, y_ref, x_ref, xy_ref):
    half = own_ref.shape[0]
    lat = lax.axis_index("lat")
    here, there = pl.ds(aligned(lat * half), half), pl.ds(aligned((1 - lat) * half), half)

    def total(group, at):
        return keep_ref[group, at, :] + got_ref[group, at, :].astype(F32)

    own_ref[...] = total(0, here)
    y_ref[...] = total(0, there).astype(BF)
    x_ref[...] = total(1, here).astype(BF)
    xy_ref[...] = total(1, there).astype(BF)


def add_planes(own_ref, a_ref, b_ref, c_ref, keep_ref, *rest):
    sends, scr = rest[:-1], rest[-1]
    scr[...] = own_ref[...] + (
        a_ref[...].astype(F32) + b_ref[...].astype(F32) + c_ref[...].astype(F32)
    )
    piece = keep_ref.shape[0]
    step = piece - 16
    lon = lax.axis_index("lon")
    keep_ref[...] = scr[pl.ds(aligned(lon * step), piece), :]
    for k, send in enumerate(sends):
        send[...] = scr[pl.ds(aligned((lon ^ (k + 1)) * step), piece), :].astype(BF)


def add_lines(own_ref, a_ref, b_ref, c_ref, kernel_ref, out_ref):
    piece = own_ref.shape[0]
    out_ref[0:piece, :] = (
        own_ref[...] + (a_ref[...].astype(F32) + b_ref[...].astype(F32) + c_ref[...].astype(F32))
    ).astype(BF)
    out_ref[piece : out_ref.shape[0], :] = kernel_ref[...].astype(BF)


def join_lines(piece, p0, p1, p2, p3, out_ref, scr):
    step = piece - 16
    half = 4 * step + 16
    extra = out_ref.shape[0] - half
    lon = lax.axis_index("lon")
    for k, ref in enumerate((p0, p1, p2, p3)):
        place = lon ^ k
        out_ref[pl.ds(aligned(place * step), step), :] = ref[0:step, :]

        @pl.when(place == 3)
        def _():
            out_ref[4 * step : half, :] = ref[step:piece, :]

        scr[pl.ds(aligned(place * extra), extra), :] = ref[piece : piece + extra, :].astype(F32)
    total = scr[0:extra, :]
    for k in range(1, 4):
        total = total + scr[k * extra : (k + 1) * extra, :]
    out_ref[half : half + extra, :] = total.astype(BF)


def write_parameters(part, pad, scale, hid, own_ref, got_ref, *rest):
    expand_ref, project_ref, bias_ref, taps_ref, all_scr, turn_scr = rest
    half = all_scr.shape[0] // 2
    extra = own_ref.shape[0] - half
    lat = lax.axis_index("lat")
    all_scr[pl.ds(aligned(lat * half), half), :] = own_ref[0:half, :]
    all_scr[pl.ds(aligned((1 - lat) * half), half), :] = got_ref[0:half, :]
    unpack(part, pad, scale, hid, all_scr, expand_ref, project_ref, bias_ref)
    total = own_ref[half : half + extra, :].astype(F32) + got_ref[half : half + extra, :].astype(F32)
    write_taps(total, scale, taps_ref, turn_scr)


def write_taps(total, scale, taps_ref, turn_scr):
    turn_scr[...] = jnp.zeros(turn_scr.shape, F32)
    turn_scr[0 : total.shape[0], :] = total * scale
    taps_ref[...] = jnp.transpose(turn_scr[...])[0 : taps_ref.shape[0], 0 : taps_ref.shape[1]]


def unpack(part, pad, scale, hid, all_ref, expand_ref, project_ref, bias_ref):
    channels, hidden = expand_ref.shape
    split = 4 * pad // LANES * LANES
    shared = split // LANES
    tiles = [all_ref[t * hid : (t + 1) * hid, :] for t in range(2 * shared + 1)]
    depth = (shared + 1) * LANES
    expand = jnp.concatenate(tiles[: shared + 1], axis=1)
    project = jnp.concatenate(tiles[shared:], axis=1)
    lane, row = iota((channels, depth), 1), iota((channels, depth), 0)
    pick_e = (channel_of(expand_slot(lane, pad), part, pad) == row).astype(BF)
    pick_p = (channel_of(project_slot(lane, pad, split), part, pad) == row).astype(BF)
    pick_b = (iota((16, depth), 1) == part).astype(BF)
    last = (((1,), (1,)), ((), ()))
    dot = functools.partial(lax.dot_general, dimension_numbers=last, preferred_element_type=F32)
    expand_ref[...] = dot(pick_e, expand)[:, 0:hidden] * scale
    bias_ref[...] = dot(pick_b, expand)[0:1, 0:hidden] * scale
    project_ref[...] = dot(project, pick_p)[0:hidden, :] * scale


def unpack_whole(part, pad, scale, hid, all_ref, taps_in, expand_ref, project_ref, bias_ref, taps_ref, turn_scr):
    unpack(part, pad, scale, hid, all_ref, expand_ref, project_ref, bias_ref)
    write_taps(taps_in[...], scale, taps_ref, turn_scr)


def on_device(
    ocean_state,
    land_mask,
    out_grad,
    swath_offset,
    swath_value,
    depth_kernel,
    expand_weight,
    expand_bias,
    project_weight,
):
    part, rows, cols = ocean_state.shape
    n_lon, n_lat, n_ch = lax.axis_size("lon"), lax.axis_size("lat"), lax.axis_size("ch")
    channels, hidden = expand_weight.shape
    assert n_ch == 4 and cols == LANES and rows % n_ch == 0
    pad = (part + 16) // 16 * 16
    hid = (hidden + 15) // 16 * 16
    split = n_ch * pad // LANES * LANES
    tail = n_ch * pad - split
    assert tail == LANES // 2
    wide = 2 * n_ch * pad
    depth = split + LANES
    part_rows = rows // n_ch
    cells = part_rows * cols
    swap = n_lat == 2
    scale = 1.0 / math.sqrt(rows * n_lat * cols * n_lon)
    core = [(i, i ^ 1) for i in range(n_ch)]
    across = [(i, i ^ 2) for i in range(n_ch)]
    both = [(i, i ^ 3) for i in range(n_ch)]
    block = shape((rows, pad, cols), BF)
    quarter = shape((part_rows, pad, cols), BF)
    flat = pltpu.VMEM((rows * pad, cols), F32)

    masked, *strips = call(
        functools.partial(prepare_state, swap),
        [block] + strip_shapes(pad, swap),
        [ocean_state, land_mask],
        [flat],
        "state_rows",
    )
    weights = call(
        functools.partial(pack_weights, part, pad),
        [shape((hid, wide), BF)],
        [expand_weight, expand_bias.reshape(1, hidden), project_weight],
        (),
        "weight_rows",
    )[0]
    taps = jnp.pad(depth_kernel.reshape(9, part).T, ((0, pad - part), (0, LANES - 9)))
    cotan, *cotan_parts = call(
        prepare_cotan,
        [block] + [quarter] * 4,
        [out_grad, land_mask, swath_offset.reshape(1, -1), swath_value.reshape(1, -1)],
        [flat],
        "cotan_rows",
    )
    around = exchange_halo(strips, rows, pad, swap, "state_columns")

    def spread_parts(parts):
        return [
            parts[0],
            lax.ppermute(parts[1], "ch", core),
            lax.ppermute(parts[2], "ch", across),
            lax.ppermute(parts[3], "ch", both),
        ]

    weights_across = lax.ppermute(weights, "ch", across)
    all_weights = [
        weights,
        lax.ppermute(weights, "ch", core),
        weights_across,
        lax.ppermute(weights_across, "ch", core),
    ]
    all_cotan = spread_parts(cotan_parts)
    conv_parts = call(
        functools.partial(conv_forward, part),
        [quarter] * 4,
        [masked, *around, taps],
        [pltpu.VMEM((rows, pad, cols), BF)],
        "conv_forward",
    )
    all_conv = spread_parts(conv_parts)
    tile_rows = wide // LANES * hid
    *grad_parts, keep, send = call(
        mlp,
        [quarter] * 4 + [shape((2, tile_rows, LANES), F32), shape((2, tile_rows, LANES), BF)],
        [*all_conv, *all_cotan, *all_weights],
        [
            pltpu.VMEM((depth, cells), BF),
            pltpu.VMEM((depth, cells), BF),
            pltpu.VMEM((n_ch * hid, wide), BF),
            pltpu.VMEM((depth, n_ch * hid), BF),
            pltpu.VMEM((n_ch * hid, cells), BF),
            pltpu.VMEM((n_ch * hid, cells), BF),
            pltpu.VMEM((depth, cells), BF),
        ],
        "mlp",
        flops=10 * cells * depth * n_ch * hid,
    )
    got = lax.ppermute(send, "ch", core)
    grad_got = spread_parts(grad_parts)
    conv_grad, *grad_strips = call(
        functools.partial(collect_grad, swap),
        [block] + strip_shapes(pad, swap),
        grad_got,
        (),
        "grad_rows",
    )
    grad_around = exchange_halo(grad_strips, rows, pad, swap, "grad_columns")
    kernel_part = call(
        kernel_gradient,
        [shape((pad, LANES), F32)],
        [conv_grad, masked, *around],
        (),
        "kernel_gradient",
    )[0]
    state_grad = call(
        conv_adjoint,
        [shape((part, rows, cols), BF)],
        [conv_grad, *grad_around, taps, cotan, land_mask],
        [flat],
        "conv_adjoint",
    )[0]
    outs = [
        shape((channels, hidden), F32),
        shape((hidden, channels), F32),
        shape((1, hidden), F32),
        shape((9, part), F32),
    ]
    turn = pltpu.VMEM((LANES, LANES), F32)
    if n_lat == 2 and n_lon == 4 and tile_rows % 32 == 0 and (tile_rows // 2 - 16) % 64 == 0:
        half = tile_rows // 2
        step = (half - 16) // 4
        piece = step + 16
        mine, to_y, to_x, to_xy = call(
            add_cores,
            [shape((half, LANES), F32)] + [shape((half, LANES), BF)] * 3,
            [keep, got],
            (),
            "add_cores",
        )
        both_axes = [
            (lat * n_ch + i, (1 - lat) * n_ch + (i ^ 2)) for lat in range(n_lat) for i in range(n_ch)
        ]
        planes = [
            lax.ppermute(to_y, "lat", [(0, 1), (1, 0)]),
            lax.ppermute(to_x, "ch", across),
            lax.ppermute(to_xy, ("lat", "ch"), both_axes),
        ]
        own, *line_parts = call(
            add_planes,
            [shape((piece, LANES), F32)] + [shape((piece, LANES), BF)] * 3,
            [mine, *planes],
            [pltpu.VMEM((half, LANES), F32)],
            "add_planes",
        )
        turns = [[(i, i ^ k) for i in range(n_lon)] for k in range(4)]
        lines = [lax.ppermute(line_parts[k - 1], "lon", turns[k]) for k in (1, 2, 3)]
        summed = call(
            add_lines, [shape((piece + pad, LANES), BF)], [own, *lines, kernel_part], (), "add_lines"
        )[0]
        pieces = [summed] + [lax.ppermute(summed, "lon", turns[k]) for k in (1, 2, 3)]
        mine = call(
            functools.partial(join_lines, piece),
            [shape((half + pad, LANES), BF)],
            pieces,
            [pltpu.VMEM((4 * pad, LANES), F32)],
            "join_lines",
        )[0]
        other = lax.ppermute(mine, "lat", [(0, 1), (1, 0)])
        expand_grad, project_grad, bias_grad, kernel_grad = call(
            functools.partial(write_parameters, part, pad, scale, hid),
            outs,
            [mine, other],
            [pltpu.VMEM((tile_rows, LANES), BF), turn],
            "write_parameters",
        )
    else:
        total = keep + got.astype(F32)
        total = total[0] + lax.ppermute(total[1].astype(BF), "ch", across).astype(F32)
        total, kernel_sum = lax.psum((total, kernel_part), ("lon", "lat"))
        expand_grad, project_grad, bias_grad, kernel_grad = call(
            functools.partial(unpack_whole, part, pad, scale, hid),
            outs,
            [total.astype(BF), kernel_sum],
            [turn],
            "write_parameters",
        )
    return (
        state_grad,
        expand_grad,
        project_grad,
        bias_grad.reshape(hidden),
        kernel_grad.reshape(3, 3, part),
    )


def solution(mesh):
    return jax.shard_map(
        on_device,
        mesh=mesh,
        in_specs=(
            P("ch", "lat", "lon"),
            P("lat", "lon"),
            P("ch", "lat", "lon"),
            P("lat", "lon", None),
            P("lat", "lon", None),
            P(None, None, "ch"),
            P(None, "ch"),
            P("ch"),
            P("ch", None),
        ),
        out_specs=(
            P("ch", "lat", "lon"),
            P(None, "ch"),
            P("ch", None),
            P("ch"),
            P(None, None, "ch"),
        ),
        check_vma=False,
    )
```

time: 205 us -> 100 us (0.49)
  the two profiles are of different devices: /device:TPU:0 before, /device:TPU:28 now
where the time goes in v1:
time: 100 us; the launch traced here: 99.9 us
  waiting for transfers between devices  51.7 us (52%)
  starting transfers between devices  28.4 us (28%)
  Pallas kernels  15.5 us (16%)
  local copies, waits for them, and re-layouts  3.5 us (4%)
    pallas_call x15, Pallas kernels, call(): pl.pallas_call(kernel, out_shape=tuple(outs), in_specs=[pl.BlockSpec(memo...  15.5 us
    ppermute x2, waiting for transfers between devices, exchange_halo(): fold = lax.ppermute(fold, ('lon', 'lat'), fold_pairs)  9.97 us
    ppermute x2, waiting for transfers between devices, exchange_halo(): from_right = lax.ppermute(left, 'lon', ring(n_lon, -1))  8.93 us
    ppermute x1, waiting for transfers between devices, on_device(): lax.ppermute(to_x, 'ch', across)  7.75 us
    ppermute x2, starting transfers between devices, exchange_halo(): fold = lax.ppermute(fold, ('lon', 'lat'), fold_pairs)  5.48 us
    ppermute x2, waiting for transfers between devices, exchange_halo(): from_left = lax.ppermute(right, 'lon', ring(n_lon, 1))  5.42 us
    ppermute x3, waiting for transfers between devices, spread_parts(): lax.ppermute(parts[2], 'ch', across)  5.21 us
    ppermute x3, starting transfers between devices, on_device(): lax.ppermute(summed, 'lon', turns[k])  4.45 us
  transfers between devices with their start and end apart: 31, of which 15 were waited for; matrix products, arithmetic and copies ran while one was open for 0% of the time, Pallas kernels for 9%

profile of v1, /device:TPU:28, one launch (start us, length us, event | category | flops | bytes accessed | tf_op | source)
XLA Modules:
  0.0 99.9 jit_solution(17989334020297051376)
XLA Ops:
  0.7 1.1 %copy.18.expand_ref = bf16[300,150]{1,0:T(8,128)(2,1)S(1)} copy(bf16[300,150]{0,1:T(8,128)(2,1)} %param.15) | data formatting | bytes 180000 | tf_op args[6]
  3.0 1.6 %collective-permute-start.11 = (bf16[160,640]{1,0:T(8,128)(2,1)S(1)}, bf16[160,640]{1,0:T(8,128)(2,1)S(1)}, u32[]{:S(2)}, u32[]{:S(2)}) collective-permute-start(bf16[160,640]{1,0:T(8,128)(2,1)S(1)} %weight_rows.1.refs_8_), channel_id=1, source_target_pairs={{0,2},{1,3},{2,0},{3,1},{4,6},{5,7},{6,4},{7,5},{8,10},{9,11},{10,... | collective-permute-start | bytes 614408 | tf_op jit(solution)/shard_map/ppermute | solution.py:591
  4.6 1.0 state_rows.1
  7.7 1.3 %collective-permute-start.9 = (bf16[8,80,128]{2,1,0:T(8,128)(2,1)S(1)}, bf16[8,80,128]{2,1,0:T(8,128)(2,1)S(1)}, u32[]{:S(2)}, u32[]{:S(2)}) collective-permute-start(bf16[8,80,128]{2,1,0:T(8,128)(2,1)S(1)} %get-tuple-element.63), channel_id=1, source_target_pairs={{0,3},{1,2},{2,1},{3,0},{4,7},{5,6},{6,5},{7,4},{8,11},{9,10},{10,... | collective-permute-start | bytes 491528 | tf_op jit(solution)/shard_map/ppermute | solution.py:588
  9.6 2.1 %collective-permute-start.1 = (bf16[2,80,128]{2,1,0:T(8,128)(2,1)S(1)}, bf16[2,80,128]{2,1,0:T(8,128)(2,1)S(1)}, u32[]{:S(2)}, u32[]{:S(2)}) collective-permute-start(bf16[2,80,128]{2,1,0:T(8,128)(2,1)S(1)} %get-tuple-element.50), channel_id=1, source_target_pairs={{4,28},{12,20},{20,12},{28,4},{5,29},{13,21},{21,13},{29,5},{6,30}... | collective-permute-start | bytes 122888 | tf_op jit(solution)/shard_map/ppermute | solution.py:159
  11.8 5.7 %collective-permute-done.1.refs_1_ = bf16[2,80,128]{2,1,0:T(8,128)(2,1)S(1)} collective-permute-done((bf16[2,80,128]{2,1,0:T(8,128)(2,1)S(1)}, bf16[2,80,128]{2,1,0:T(8,128)(2,1)S(1)}, u32[]{:S(2)}, u32[]{:S(2)}) %collective-permute-start.1) | collective-permute-done | bytes 40992 | tf_op jit(solution)/shard_map/ppermute | solution.py:159
  17.7 3.7 %collective-permute-done.2.left_ref = bf16[80,128]{1,0:T(8,128)(2,1)S(1)} collective-permute-done((bf16[80,128]{1,0:T(8,128)(2,1)S(1)}, bf16[80,128]{1,0:T(8,128)(2,1)S(1)}, u32[]{:S(2)}, u32[]{:S(2)}) %collective-permute-start.2) | collective-permute-done | bytes 20512 | tf_op jit(solution)/shard_map/ppermute | solution.py:168
  21.4 5.6 %collective-permute-done.3.right_ref = bf16[80,128]{1,0:T(8,128)(2,1)S(1)} collective-permute-done((bf16[80,128]{1,0:T(8,128)(2,1)S(1)}, bf16[80,128]{1,0:T(8,128)(2,1)S(1)}, u32[]{:S(2)}, u32[]{:S(2)}) %collective-permute-start.3) | collective-permute-done | bytes 20512 | tf_op jit(solution)/shard_map/ppermute | solution.py:167
  27.6 1.6 %conv_forward.1 = (bf16[8,80,128]{2,1,0:T(8,128)(2,1)S(1)}, bf16[8,80,128]{2,1,0:T(8,128)(2,1)S(1)}, bf16[8,80,128]{2,1,0:T(8,128)(2,1)S(1)}, bf16[8,80,128]{2,1,0:T(8,128)(2,1)S(1)}) custom-call(bf16[32,80,128]{2,1,0:T(8,128)(2,1)S(1)} %get-tuple-element.48.block_ref, bf16[4,80,128]{2,1,0:T(8,128)(2,1)S(1)} %get-tuple-element.53.halo_ref, ...), custom_call_target="tpu_custom_call" | custom-call | bytes 1474560 | tf_op jit(solution)/shard_map/conv_forward/pallas_call | solution.py:24
  29.9 1.3 %collective-permute-start.6 = (bf16[8,80,128]{2,1,0:T(8,128)(2,1)S(1)}, bf16[8,80,128]{2,1,0:T(8,128)(2,1)S(1)}, u32[]{:S(2)}, u32[]{:S(2)}) collective-permute-start(bf16[8,80,128]{2,1,0:T(8,128)(2,1)S(1)} %get-tuple-element.59), channel_id=1, source_target_pairs={{0,3},{1,2},{2,1},{3,0},{4,7},{5,6},{6,5},{7,4},{8,11},{9,10},{10,... | collective-permute-start | bytes 491528 | tf_op jit(solution)/shard_map/ppermute | solution.py:588
  31.2 5.2 %collective-permute-done.5.refs_2_ = bf16[8,80,128]{2,1,0:T(8,128)(2,1)S(1)} collective-permute-done((bf16[8,80,128]{2,1,0:T(8,128)(2,1)S(1)}, bf16[8,80,128]{2,1,0:T(8,128)(2,1)S(1)}, u32[]{:S(2)}, u32[]{:S(2)}) %collective-permute-start.5) | collective-permute-done | bytes 163872 | tf_op jit(solution)/shard_map/ppermute | solution.py:587
  36.4 2.6 %collective-permute-done.6.refs_3_ = bf16[8,80,128]{2,1,0:T(8,128)(2,1)S(1)} collective-permute-done((bf16[8,80,128]{2,1,0:T(8,128)(2,1)S(1)}, bf16[8,80,128]{2,1,0:T(8,128)(2,1)S(1)}, u32[]{:S(2)}, u32[]{:S(2)}) %collective-permute-start.6) | collective-permute-done | bytes 163872 | tf_op jit(solution)/shard_map/ppermute | solution.py:588
  39.0 5.0 %mlp.1 = (bf16[8,80,128]{2,1,0:T(8,128)(2,1)S(1)}, bf16[8,80,128]{2,1,0:T(8,128)(2,1)S(1)}, bf16[8,80,128]{2,1,0:T(8,128)(2,1)S(1)}, bf16[8,80,128]{2,1,0:T(8,12...) custom-call(bf16[8,80,128]{2,1,0:T(8,128)(2,1)S(1)} %get-tuple-element.56.refs_0_, ...), custom_call_target="tpu_custom_call" | custom-call | flops 2516582400 | bytes 4014080 | tf_op jit(solution)/shard_map/mlp/pallas_call | solution.py:24
  44.3 1.5 %collective-permute-done.20.got_ref = bf16[2,800,128]{2,1,0:T(8,128)(2,1)S(1)} collective-permute-done((bf16[2,800,128]{2,1,0:T(8,128)(2,1)S(1)}, bf16[2,800,128]{2,1,0:T(8,128)(2,1)S(1)}, u32[]{:S(2)}, u32[]{:S(2)}) %collective-permute-start.20) | collective-permute-done | bytes 409632 | tf_op jit(solution)/shard_map/ppermute | solution.py:624
  46.8 1.0 %collective-permute-start.15 = (bf16[8,80,128]{2,1,0:T(8,128)(2,1)S(1)}, bf16[8,80,128]{2,1,0:T(8,128)(2,1)S(1)}, u32[]{:S(2)}, u32[]{:S(2)}) collective-permute-start(bf16[8,80,128]{2,1,0:T(8,128)(2,1)S(1)} %get-tuple-element.67), channel_id=1, source_target_pairs={{0,3},{1,2},{2,1},{3,0},{4,7},{5,6},{6,5},{7,4},{8,11},{9,10},{10,... | collective-permute-start | bytes 491528 | tf_op jit(solution)/shard_map/ppermute | solution.py:588
  48.4 2.6 %collective-permute-done.21.a_ref = bf16[400,128]{1,0:T(8,128)(2,1)S(1)} collective-permute-done((bf16[400,128]{1,0:T(8,128)(2,1)S(1)}, bf16[400,128]{1,0:T(8,128)(2,1)S(1)}, u32[]{:S(2)}, u32[]{:S(2)}) %collective-permute-start.21) | collective-permute-done | bytes 102432 | tf_op jit(solution)/shard_map/ppermute | solution.py:670
  51.3 7.7 %collective-permute-done.22.b_ref = bf16[400,128]{1,0:T(8,128)(2,1)S(1)} collective-permute-done((bf16[400,128]{1,0:T(8,128)(2,1)S(1)}, bf16[400,128]{1,0:T(8,128)(2,1)S(1)}, u32[]{:S(2)}, u32[]{:S(2)}) %collective-permute-start.22) | collective-permute-done | bytes 102432 | tf_op jit(solution)/shard_map/ppermute | solution.py:671
  59.0 2.9 %collective-permute-done.23.c_ref = bf16[400,128]{1,0:T(8,128)(2,1)S(1)} collective-permute-done((bf16[400,128]{1,0:T(8,128)(2,1)S(1)}, bf16[400,128]{1,0:T(8,128)(2,1)S(1)}, u32[]{:S(2)}, u32[]{:S(2)}) %collective-permute-start.23) | collective-permute-done | bytes 102432 | tf_op jit(solution)/shard_map/ppermute | solution.py:672
  62.7 3.7 %collective-permute-start.26 = (bf16[112,128]{1,0:T(8,128)(2,1)S(1)}, bf16[112,128]{1,0:T(8,128)(2,1)S(1)}, u32[]{:S(2)}, u32[]{:S(2)}) collective-permute-start(bf16[112,128]{1,0:T(8,128)(2,1)S(1)} %get-tuple-element.86), channel_id=1, source_target_pairs={{0,24},{8,16},{16,8},{24,0},{1,25},{9,17},{17,9},{25,1},{2,26},{10... | collective-permute-start | bytes 86024 | tf_op jit(solution)/shard_map/ppermute | solution.py:682
  66.9 1.7 %kernel_gradient.1.kernel_ref = f32[80,128]{1,0:T(8,128)S(1)} custom-call(bf16[32,80,128]{2,1,0:T(8,128)(2,1)S(1)} %get-tuple-element.68.block_ref.grad_ref, bf16[32,80,128]{2,1,0:T(8,128)(2,1)S(1)} %get-tuple-element.48.block_ref, bf16[4,80,128]{2,1,0:T(8,128)(2,1)S(1)} %get-tuple-element.53.halo_ref, bf16[80,128]{1,0:T(8,128)(2,1)S(1)} %collective-permute-done.2.left_ref, ...), custom_call_target="tpu_custom_call" | custom-call | bytes 1474560 | tf_op jit(solution)/shard_map/kernel_gradient/pallas_call | solution.py:24
  68.7 3.6 %collective-permute-start.29 = (bf16[192,128]{1,0:T(8,128)(2,1)S(1)}, bf16[192,128]{1,0:T(8,128)(2,1)S(1)}, u32[]{:S(2)}, u32[]{:S(2)}) collective-permute-start(bf16[192,128]{1,0:T(8,128)(2,1)S(1)} %add_lines.1.p0), channel_id=1, source_target_pairs={{0,24},{8,16},{16,8},{24,0},{1,25},{9,17},{17,9},{25,1},{2,26},{10... | collective-permute-start | bytes 147464 | tf_op jit(solution)/shard_map/ppermute | solution.py:686
  73.1 1.6 %collective-permute-done.29.p3 = bf16[192,128]{1,0:T(8,128)(2,1)S(1)} collective-permute-done((bf16[192,128]{1,0:T(8,128)(2,1)S(1)}, bf16[192,128]{1,0:T(8,128)(2,1)S(1)}, u32[]{:S(2)}, u32[]{:S(2)}) %collective-permute-start.29) | collective-permute-done | bytes 49184 | tf_op jit(solution)/shard_map/ppermute | solution.py:686
  74.7 2.6 %collective-permute-done.28.p2 = bf16[192,128]{1,0:T(8,128)(2,1)S(1)} collective-permute-done((bf16[192,128]{1,0:T(8,128)(2,1)S(1)}, bf16[192,128]{1,0:T(8,128)(2,1)S(1)}, u32[]{:S(2)}, u32[]{:S(2)}) %collective-permute-start.28) | collective-permute-done | bytes 49184 | tf_op jit(solution)/shard_map/ppermute | solution.py:686
  77.4 2.0 %collective-permute-start.16 = (bf16[2,80,128]{2,1,0:T(8,128)(2,1)S(1)}, bf16[2,80,128]{2,1,0:T(8,128)(2,1)S(1)}, u32[]{:S(2)}, u32[]{:S(2)}) collective-permute-start(bf16[2,80,128]{2,1,0:T(8,128)(2,1)S(1)} %get-tuple-element.69), channel_id=1, source_target_pairs={{0,4},{4,0},{1,5},{5,1},{2,6},{6,2},{3,7},{7,3},{8,12},{12,8},{9,1... | collective-permute-start | bytes 122888 | tf_op jit(solution)/shard_map/ppermute | solution.py:152
  79.4 3.4 %collective-permute-start.17 = (bf16[2,80,128]{2,1,0:T(8,128)(2,1)S(1)}, bf16[2,80,128]{2,1,0:T(8,128)(2,1)S(1)}, u32[]{:S(2)}, u32[]{:S(2)}) collective-permute-start(bf16[2,80,128]{2,1,0:T(8,128)(2,1)S(1)} %get-tuple-element.70), channel_id=1, source_target_pairs={{4,28},{12,20},{20,12},{28,4},{5,29},{13,21},{21,13},{29,5},{6,30}... | collective-permute-start | bytes 122888 | tf_op jit(solution)/shard_map/ppermute | solution.py:159
  82.8 4.3 %collective-permute-done.17.refs_1_ = bf16[2,80,128]{2,1,0:T(8,128)(2,1)S(1)} collective-permute-done((bf16[2,80,128]{2,1,0:T(8,128)(2,1)S(1)}, bf16[2,80,128]{2,1,0:T(8,128)(2,1)S(1)}, u32[]{:S(2)}, u32[]{:S(2)}) %collective-permute-start.17) | collective-permute-done | bytes 40992 | tf_op jit(solution)/shard_map/ppermute | solution.py:159
  87.2 1.6 %collective-permute-start.18 = (bf16[80,128]{1,0:T(8,128)(2,1)S(1)}, bf16[80,128]{1,0:T(8,128)(2,1)S(1)}, u32[]{:S(2)}, u32[]{:S(2)}) collective-permute-start(bf16[80,128]{1,0:T(8,128)(2,1)S(1)} %get-tuple-element.74), channel_id=1, source_target_pairs={{0,8},{8,16},{16,24},{24,0},{1,9},{9,17},{17,25},{25,1},{2,10},{10... | collective-permute-start | bytes 61448 | tf_op jit(solution)/shard_map/ppermute | solution.py:168
  89.3 1.8 %collective-permute-done.18.left_ref = bf16[80,128]{1,0:T(8,128)(2,1)S(1)} collective-permute-done((bf16[80,128]{1,0:T(8,128)(2,1)S(1)}, bf16[80,128]{1,0:T(8,128)(2,1)S(1)}, u32[]{:S(2)}, u32[]{:S(2)}) %collective-permute-start.18) | collective-permute-done | bytes 20512 | tf_op jit(solution)/shard_map/ppermute | solution.py:168
  91.1 3.4 %collective-permute-done.19.right_ref = bf16[80,128]{1,0:T(8,128)(2,1)S(1)} collective-permute-done((bf16[80,128]{1,0:T(8,128)(2,1)S(1)}, bf16[80,128]{1,0:T(8,128)(2,1)S(1)}, u32[]{:S(2)}, u32[]{:S(2)}) %collective-permute-start.19) | collective-permute-done | bytes 20512 | tf_op jit(solution)/shard_map/ppermute | solution.py:167
  94.4 3.0 %conv_adjoint.1 = bf16[75,32,128]{2,1,0:T(8,128)(2,1)} custom-call(bf16[32,80,128]{2,1,0:T(8,128)(2,1)S(1)} %get-tuple-element.68.block_ref.grad_ref, bf16[4,80,128]{2,1,0:T(8,128)(2,1)S(1)} %get-tuple-element.73.halo_ref, bf16[80,128]{1,0:T(8,128)(2,1)S(1)} %collective-permute-done.18.left_ref, bf16[80,128]{1,0:T(8,128)(2,1)S(1)} %collective-permute-done.19.right_ref, ...), custom_call_target="tpu_custom_call" | custom-call | bytes 2105344 | tf_op jit(solution)/shard_map/conv_adjoint/pallas_call | solution.py:24
  97.4 1.1 %write_parameters.1 = (f32[300,150]{1,0:T(8,128)S(1)}, f32[150,300]{1,0:T(8,128)}, f32[1,150]{1,0:T(1,128)}, f32[9,75]{1,0:T(8,128)S(1)}) custom-call(bf16[480,128]{1,0:T(8,128)(2,1)S(1)} %join_lines.1.own_ref, bf16[480,128]{1,0:T(8,128)(2,1)S(1)} %collective-permute-done.30.got_ref), custom_call_target="tpu_custom_call" | custom-call | bytes 609060 | tf_op jit(solution)/shard_map/write_parameters/pallas_call | solution.py:24
  98.5 0.8 copy.19
  (67 shorter events, 11.3 us)
Async XLA Ops:
  3.0 24.0 %collective-permute-start.11 = (bf16[160,640]{1,0:T(8,128)(2,1)S(1)}, bf16[160,640]{1,0:T(8,128)(2,1)S(1)}, u32[]{:S(2)}, u32[]{:S(2)}) collective-permute-start(bf16[160,640]{1,0:T(8,128)(2,1)S(1)} %weight_rows.1.refs_8_), channel_id=1, source_target_pairs={{0,2},{1,3},{2,0},{3,1},{4,6},{5,7},{6,4},{7,5},{8,10},{9,11},{10,... | collective-permute-start | bytes 614408 | tf_op jit(solution)/shard_map/ppermute | solution.py:591
  5.6 4.1 %collective-permute-start = (bf16[2,80,128]{2,1,0:T(8,128)(2,1)S(1)}, bf16[2,80,128]{2,1,0:T(8,128)(2,1)S(1)}, u32[]{:S(2)}, u32[]{:S(2)}) collective-permute-start(bf16[2,80,128]{2,1,0:T(8,128)(2,1)S(1)} %get-tuple-element.49), channel_id=1, source_target_pairs={{0,4},{4,0},{1,5},{5,1},{2,6},{6,2},{3,7},{7,3},{8,12},{12,8},{9,1... | collective-permute-start | bytes 122888 | tf_op jit(solution)/shard_map/ppermute | solution.py:152
  7.1 22.2 %collective-permute-start.7 = (bf16[8,80,128]{2,1,0:T(8,128)(2,1)S(1)}, bf16[8,80,128]{2,1,0:T(8,128)(2,1)S(1)}, u32[]{:S(2)}, u32[]{:S(2)}) collective-permute-start(bf16[8,80,128]{2,1,0:T(8,128)(2,1)S(1)} %get-tuple-element.61), channel_id=1, source_target_pairs={{0,1},{1,0},{2,3},{3,2},{4,5},{5,4},{6,7},{7,6},{8,9},{9,8},{10,11... | collective-permute-start | bytes 491528 | tf_op jit(solution)/shard_map/ppermute | solution.py:586
  7.1 22.2 %collective-permute-start.8 = (bf16[8,80,128]{2,1,0:T(8,128)(2,1)S(1)}, bf16[8,80,128]{2,1,0:T(8,128)(2,1)S(1)}, u32[]{:S(2)}, u32[]{:S(2)}) collective-permute-start(bf16[8,80,128]{2,1,0:T(8,128)(2,1)S(1)} %get-tuple-element.62), channel_id=1, source_target_pairs={{0,2},{1,3},{2,0},{3,1},{4,6},{5,7},{6,4},{7,5},{8,10},{9,11},{10,... | collective-permute-start | bytes 491528 | tf_op jit(solution)/shard_map/ppermute | solution.py:587
  7.7 22.2 %collective-permute-start.9 = (bf16[8,80,128]{2,1,0:T(8,128)(2,1)S(1)}, bf16[8,80,128]{2,1,0:T(8,128)(2,1)S(1)}, u32[]{:S(2)}, u32[]{:S(2)}) collective-permute-start(bf16[8,80,128]{2,1,0:T(8,128)(2,1)S(1)} %get-tuple-element.63), channel_id=1, source_target_pairs={{0,3},{1,2},{2,1},{3,0},{4,7},{5,6},{6,5},{7,4},{8,11},{9,10},{10,... | collective-permute-start | bytes 491528 | tf_op jit(solution)/shard_map/ppermute | solution.py:588
  9.6 7.8 %collective-permute-start.1 = (bf16[2,80,128]{2,1,0:T(8,128)(2,1)S(1)}, bf16[2,80,128]{2,1,0:T(8,128)(2,1)S(1)}, u32[]{:S(2)}, u32[]{:S(2)}) collective-permute-start(bf16[2,80,128]{2,1,0:T(8,128)(2,1)S(1)} %get-tuple-element.50), channel_id=1, source_target_pairs={{4,28},{12,20},{20,12},{28,4},{5,29},{13,21},{21,13},{29,5},{6,30}... | collective-permute-start | bytes 122888 | tf_op jit(solution)/shard_map/ppermute | solution.py:159
  17.4 10.1 %copy-start.7 = (f32[3,3,75]{2,1,0:T(4,128)S(1)}, f32[3,3,75]{2,1,0:T(4,128)}, u32[]{:S(2)}) copy-start(f32[3,3,75]{2,1,0:T(4,128)} %param.14) | copy-start | bytes 8104
  17.5 3.8 %collective-permute-start.2 = (bf16[80,128]{1,0:T(8,128)(2,1)S(1)}, bf16[80,128]{1,0:T(8,128)(2,1)S(1)}, u32[]{:S(2)}, u32[]{:S(2)}) collective-permute-start(bf16[80,128]{1,0:T(8,128)(2,1)S(1)} %get-tuple-element.54), channel_id=1, source_target_pairs={{0,8},{8,16},{16,24},{24,0},{1,9},{9,17},{17,25},{25,1},{2,10},{10... | collective-permute-start | bytes 61448 | tf_op jit(solution)/shard_map/ppermute | solution.py:168
  21.4 5.6 %collective-permute-start.3 = (bf16[80,128]{1,0:T(8,128)(2,1)S(1)}, bf16[80,128]{1,0:T(8,128)(2,1)S(1)}, u32[]{:S(2)}, u32[]{:S(2)}) collective-permute-start(bf16[80,128]{1,0:T(8,128)(2,1)S(1)} %get-tuple-element.55), channel_id=1, source_target_pairs={{0,24},{8,0},{16,8},{24,16},{1,25},{9,1},{17,9},{25,17},{2,26},{10... | collective-permute-start | bytes 61448 | tf_op jit(solution)/shard_map/ppermute | solution.py:167
  27.0 4.2 %collective-permute-start.10 = (bf16[160,640]{1,0:T(8,128)(2,1)S(1)}, bf16[160,640]{1,0:T(8,128)(2,1)S(1)}, u32[]{:S(2)}, u32[]{:S(2)}) collective-permute-start(bf16[160,640]{1,0:T(8,128)(2,1)S(1)} %weight_rows.1.refs_8_), channel_id=1, source_target_pairs={{0,1},{1,0},{2,3},{3,2},{4,5},{5,4},{6,7},{7,6},{8,9},{9,8},{10,11... | collective-permute-start | bytes 614408 | tf_op jit(solution)/shard_map/ppermute | solution.py:594
  27.0 12.0 %collective-permute-start.12 = (bf16[160,640]{1,0:T(8,128)(2,1)S(1)}, bf16[160,640]{1,0:T(8,128)(2,1)S(1)}, u32[]{:S(2)}, u32[]{:S(2)}) collective-permute-start(bf16[160,640]{1,0:T(8,128)(2,1)S(1)} %collective-permute-done.11.refs_10_), channel_id=1, source_target_pairs={{0,1},{1,0},{2,3},{3,2},{4,5},{5,4},{6,7},{7,6},{8,9},{9,8},{10,11... | collective-permute-start | bytes 614408 | tf_op jit(solution)/shard_map/ppermute | solution.py:596
  29.2 2.0 %collective-permute-start.4 = (bf16[8,80,128]{2,1,0:T(8,128)(2,1)S(1)}, bf16[8,80,128]{2,1,0:T(8,128)(2,1)S(1)}, u32[]{:S(2)}, u32[]{:S(2)}) collective-permute-start(bf16[8,80,128]{2,1,0:T(8,128)(2,1)S(1)} %get-tuple-element.57), channel_id=1, source_target_pairs={{0,1},{1,0},{2,3},{3,2},{4,5},{5,4},{6,7},{7,6},{8,9},{9,8},{10,11... | collective-permute-start | bytes 491528 | tf_op jit(solution)/shard_map/ppermute | solution.py:586
  29.3 7.1 %collective-permute-start.5 = (bf16[8,80,128]{2,1,0:T(8,128)(2,1)S(1)}, bf16[8,80,128]{2,1,0:T(8,128)(2,1)S(1)}, u32[]{:S(2)}, u32[]{:S(2)}) collective-permute-start(bf16[8,80,128]{2,1,0:T(8,128)(2,1)S(1)} %get-tuple-element.58), channel_id=1, source_target_pairs={{0,2},{1,3},{2,0},{3,1},{4,6},{5,7},{6,4},{7,5},{8,10},{9,11},{10,... | collective-permute-start | bytes 491528 | tf_op jit(solution)/shard_map/ppermute | solution.py:587
  29.9 9.1 %collective-permute-start.6 = (bf16[8,80,128]{2,1,0:T(8,128)(2,1)S(1)}, bf16[8,80,128]{2,1,0:T(8,128)(2,1)S(1)}, u32[]{:S(2)}, u32[]{:S(2)}) collective-permute-start(bf16[8,80,128]{2,1,0:T(8,128)(2,1)S(1)} %get-tuple-element.59), channel_id=1, source_target_pairs={{0,3},{1,2},{2,1},{3,0},{4,7},{5,6},{6,5},{7,4},{8,11},{9,10},{10,... | collective-permute-start | bytes 491528 | tf_op jit(solution)/shard_map/ppermute | solution.py:588
  44.0 1.8 %collective-permute-start.20 = (bf16[2,800,128]{2,1,0:T(8,128)(2,1)S(1)}, bf16[2,800,128]{2,1,0:T(8,128)(2,1)S(1)}, u32[]{:S(2)}, u32[]{:S(2)}) collective-permute-start(bf16[2,800,128]{2,1,0:T(8,128)(2,1)S(1)} %get-tuple-element.78), channel_id=1, source_target_pairs={{0,1},{1,0},{2,3},{3,2},{4,5},{5,4},{6,7},{7,6},{8,9},{9,8},{10,11... | collective-permute-start | bytes 1228808 | tf_op jit(solution)/shard_map/ppermute | solution.py:624
  45.9 5.1 %collective-permute-start.21 = (bf16[400,128]{1,0:T(8,128)(2,1)S(1)}, bf16[400,128]{1,0:T(8,128)(2,1)S(1)}, u32[]{:S(2)}, u32[]{:S(2)}) collective-permute-start(bf16[400,128]{1,0:T(8,128)(2,1)S(1)} %get-tuple-element.80), channel_id=1, source_target_pairs={{0,4},{4,0},{1,5},{5,1},{2,6},{6,2},{3,7},{7,3},{8,12},{12,8},{9,1... | collective-permute-start | bytes 307208 | tf_op jit(solution)/shard_map/ppermute | solution.py:670
  46.0 16.8 %collective-permute-start.13 = (bf16[8,80,128]{2,1,0:T(8,128)(2,1)S(1)}, bf16[8,80,128]{2,1,0:T(8,128)(2,1)S(1)}, u32[]{:S(2)}, u32[]{:S(2)}) collective-permute-start(bf16[8,80,128]{2,1,0:T(8,128)(2,1)S(1)} %get-tuple-element.65), channel_id=1, source_target_pairs={{0,1},{1,0},{2,3},{3,2},{4,5},{5,4},{6,7},{7,6},{8,9},{9,8},{10,11... | collective-permute-start | bytes 491528 | tf_op jit(solution)/shard_map/ppermute | solution.py:586
  46.3 20.2 %collective-permute-start.14 = (bf16[8,80,128]{2,1,0:T(8,128)(2,1)S(1)}, bf16[8,80,128]{2,1,0:T(8,128)(2,1)S(1)}, u32[]{:S(2)}, u32[]{:S(2)}) collective-permute-start(bf16[8,80,128]{2,1,0:T(8,128)(2,1)S(1)} %get-tuple-element.66), channel_id=1, source_target_pairs={{0,2},{1,3},{2,0},{3,1},{4,6},{5,7},{6,4},{7,5},{8,10},{9,11},{10,... | collective-permute-start | bytes 491528 | tf_op jit(solution)/shard_map/ppermute | solution.py:587
  46.8 19.6 %collective-permute-start.15 = (bf16[8,80,128]{2,1,0:T(8,128)(2,1)S(1)}, bf16[8,80,128]{2,1,0:T(8,128)(2,1)S(1)}, u32[]{:S(2)}, u32[]{:S(2)}) collective-permute-start(bf16[8,80,128]{2,1,0:T(8,128)(2,1)S(1)} %get-tuple-element.67), channel_id=1, source_target_pairs={{0,3},{1,2},{2,1},{3,0},{4,7},{5,6},{6,5},{7,4},{8,11},{9,10},{10,... | collective-permute-start | bytes 491528 | tf_op jit(solution)/shard_map/ppermute | solution.py:588
  47.9 11.2 %collective-permute-start.22 = (bf16[400,128]{1,0:T(8,128)(2,1)S(1)}, bf16[400,128]{1,0:T(8,128)(2,1)S(1)}, u32[]{:S(2)}, u32[]{:S(2)}) collective-permute-start(bf16[400,128]{1,0:T(8,128)(2,1)S(1)} %get-tuple-element.81), channel_id=1, source_target_pairs={{0,2},{1,3},{2,0},{3,1},{4,6},{5,7},{6,4},{7,5},{8,10},{9,11},{10,... | collective-permute-start | bytes 307208 | tf_op jit(solution)/shard_map/ppermute | solution.py:671
  51.0 10.9 %collective-permute-start.23 = (bf16[400,128]{1,0:T(8,128)(2,1)S(1)}, bf16[400,128]{1,0:T(8,128)(2,1)S(1)}, u32[]{:S(2)}, u32[]{:S(2)}) collective-permute-start(bf16[400,128]{1,0:T(8,128)(2,1)S(1)} %get-tuple-element.82), channel_id=1, source_target_pairs={{0,6},{1,7},{2,4},{3,5},{4,2},{5,3},{6,0},{7,1},{8,14},{9,15},{10,... | collective-permute-start | bytes 307208 | tf_op jit(solution)/shard_map/ppermute | solution.py:672
  62.0 6.6 %collective-permute-start.24 = (bf16[112,128]{1,0:T(8,128)(2,1)S(1)}, bf16[112,128]{1,0:T(8,128)(2,1)S(1)}, u32[]{:S(2)}, u32[]{:S(2)}) collective-permute-start(bf16[112,128]{1,0:T(8,128)(2,1)S(1)} %get-tuple-element.84), channel_id=1, source_target_pairs={{0,8},{8,0},{16,24},{24,16},{1,9},{9,1},{17,25},{25,17},{2,10},{10... | collective-permute-start | bytes 86024 | tf_op jit(solution)/shard_map/ppermute | solution.py:682
  62.1 6.6 %collective-permute-start.25 = (bf16[112,128]{1,0:T(8,128)(2,1)S(1)}, bf16[112,128]{1,0:T(8,128)(2,1)S(1)}, u32[]{:S(2)}, u32[]{:S(2)}) collective-permute-start(bf16[112,128]{1,0:T(8,128)(2,1)S(1)} %get-tuple-element.85), channel_id=1, source_target_pairs={{0,16},{8,24},{16,0},{24,8},{1,17},{9,25},{17,1},{25,9},{2,18},{10... | collective-permute-start | bytes 86024 | tf_op jit(solution)/shard_map/ppermute | solution.py:682
  62.7 5.9 %collective-permute-start.26 = (bf16[112,128]{1,0:T(8,128)(2,1)S(1)}, bf16[112,128]{1,0:T(8,128)(2,1)S(1)}, u32[]{:S(2)}, u32[]{:S(2)}) collective-permute-start(bf16[112,128]{1,0:T(8,128)(2,1)S(1)} %get-tuple-element.86), channel_id=1, source_target_pairs={{0,24},{8,16},{16,8},{24,0},{1,25},{9,17},{17,9},{25,1},{2,26},{10... | collective-permute-start | bytes 86024 | tf_op jit(solution)/shard_map/ppermute | solution.py:682
  68.7 6.0 %collective-permute-start.29 = (bf16[192,128]{1,0:T(8,128)(2,1)S(1)}, bf16[192,128]{1,0:T(8,128)(2,1)S(1)}, u32[]{:S(2)}, u32[]{:S(2)}) collective-permute-start(bf16[192,128]{1,0:T(8,128)(2,1)S(1)} %add_lines.1.p0), channel_id=1, source_target_pairs={{0,24},{8,16},{16,8},{24,0},{1,25},{9,17},{17,9},{25,1},{2,26},{10... | collective-permute-start | bytes 147464 | tf_op jit(solution)/shard_map/ppermute | solution.py:686
  72.3 5.0 %collective-permute-start.28 = (bf16[192,128]{1,0:T(8,128)(2,1)S(1)}, bf16[192,128]{1,0:T(8,128)(2,1)S(1)}, u32[]{:S(2)}, u32[]{:S(2)}) collective-permute-start(bf16[192,128]{1,0:T(8,128)(2,1)S(1)} %add_lines.1.p0), channel_id=1, source_target_pairs={{0,16},{8,24},{16,0},{24,8},{1,17},{9,25},{17,1},{25,9},{2,18},{10... | collective-permute-start | bytes 147464 | tf_op jit(solution)/shard_map/ppermute | solution.py:686
  72.3 5.0 %collective-permute-start.27 = (bf16[192,128]{1,0:T(8,128)(2,1)S(1)}, bf16[192,128]{1,0:T(8,128)(2,1)S(1)}, u32[]{:S(2)}, u32[]{:S(2)}) collective-permute-start(bf16[192,128]{1,0:T(8,128)(2,1)S(1)} %add_lines.1.p0), channel_id=1, source_target_pairs={{0,8},{8,0},{16,24},{24,16},{1,9},{9,1},{17,25},{25,17},{2,10},{10... | collective-permute-start | bytes 147464 | tf_op jit(solution)/shard_map/ppermute | solution.py:686
  77.4 20.0 %collective-permute-start.30 = (bf16[480,128]{1,0:T(8,128)(2,1)S(1)}, bf16[480,128]{1,0:T(8,128)(2,1)S(1)}, u32[]{:S(2)}, u32[]{:S(2)}) collective-permute-start(bf16[480,128]{1,0:T(8,128)(2,1)S(1)} %join_lines.1.own_ref), channel_id=1, source_target_pairs={{0,4},{4,0},{1,5},{5,1},{2,6},{6,2},{3,7},{7,3},{8,12},{12,8},{9,1... | collective-permute-start | bytes 368648 | tf_op jit(solution)/shard_map/ppermute | solution.py:694
  77.4 5.4 %collective-permute-start.16 = (bf16[2,80,128]{2,1,0:T(8,128)(2,1)S(1)}, bf16[2,80,128]{2,1,0:T(8,128)(2,1)S(1)}, u32[]{:S(2)}, u32[]{:S(2)}) collective-permute-start(bf16[2,80,128]{2,1,0:T(8,128)(2,1)S(1)} %get-tuple-element.69), channel_id=1, source_target_pairs={{0,4},{4,0},{1,5},{5,1},{2,6},{6,2},{3,7},{7,3},{8,12},{12,8},{9,1... | collective-permute-start | bytes 122888 | tf_op jit(solution)/shard_map/ppermute | solution.py:152
  79.4 7.7 %collective-permute-start.17 = (bf16[2,80,128]{2,1,0:T(8,128)(2,1)S(1)}, bf16[2,80,128]{2,1,0:T(8,128)(2,1)S(1)}, u32[]{:S(2)}, u32[]{:S(2)}) collective-permute-start(bf16[2,80,128]{2,1,0:T(8,128)(2,1)S(1)} %get-tuple-element.70), channel_id=1, source_target_pairs={{4,28},{12,20},{20,12},{28,4},{5,29},{13,21},{21,13},{29,5},{6,30}... | collective-permute-start | bytes 122888 | tf_op jit(solution)/shard_map/ppermute | solution.py:159
  87.2 3.8 %collective-permute-start.18 = (bf16[80,128]{1,0:T(8,128)(2,1)S(1)}, bf16[80,128]{1,0:T(8,128)(2,1)S(1)}, u32[]{:S(2)}, u32[]{:S(2)}) collective-permute-start(bf16[80,128]{1,0:T(8,128)(2,1)S(1)} %get-tuple-element.74), channel_id=1, source_target_pairs={{0,8},{8,16},{16,24},{24,0},{1,9},{9,17},{17,25},{25,1},{2,10},{10... | collective-permute-start | bytes 61448 | tf_op jit(solution)/shard_map/ppermute | solution.py:168
  88.9 5.6 %collective-permute-start.19 = (bf16[80,128]{1,0:T(8,128)(2,1)S(1)}, bf16[80,128]{1,0:T(8,128)(2,1)S(1)}, u32[]{:S(2)}, u32[]{:S(2)}) collective-permute-start(bf16[80,128]{1,0:T(8,128)(2,1)S(1)} %get-tuple-element.75), channel_id=1, source_target_pairs={{0,24},{8,0},{16,8},{24,16},{1,25},{9,1},{17,9},{25,17},{2,26},{10... | collective-permute-start | bytes 61448 | tf_op jit(solution)/shard_map/ppermute | solution.py:167
  (7 other events, 15.5 us)

commit v2 on v1

--- a/solution.py
+++ b/solution.py
@@ -10,6 +10,7 @@
 
 DIL = 2
 LANES = 128
+RIDE = 96
 BF = jnp.bfloat16
 F32 = jnp.float32
 
@@ -18,17 +19,27 @@
     return jax.ShapeDtypeStruct(dims, kind)
 
 
-def call(kernel, outs, args, scratch=(), name=None, flops=0, moved=None):
-    if moved is None:
-        moved = sum(math.prod(a.shape) * a.dtype.itemsize for a in list(args) + list(outs))
+def call(kernel, outs, args, scratch=(), name=None, flops=0, aliases=None, far=False, after=()):
+    count = len(args)
+    if after:
+        body, args = kernel, [*args, *after]
+
+        def kernel(*refs):
+            body(*refs[:count], *refs[len(args) :])
+
+    if far:
+        args = [pltpu.with_memory_space_constraint(a, pltpu.HBM) for a in args]
+    spaces = [pltpu.HBM if far else pl.ANY if i >= count else pltpu.VMEM for i in range(len(args))]
+    moved = sum(math.prod(a.shape) * a.dtype.itemsize for a in list(args) + list(outs))
     return pl.pallas_call(
         kernel,
         out_shape=tuple(outs),
-        in_specs=[pl.BlockSpec(memory_space=pltpu.VMEM) for _ in args],
+        in_specs=[pl.BlockSpec(memory_space=space) for space in spaces],
         out_specs=tuple(pl.BlockSpec(memory_space=pltpu.VMEM) for _ in outs),
         scratch_shapes=list(scratch),
+        input_output_aliases=aliases or {},
         name=name,
-        compiler_params=pltpu.CompilerParams(vmem_limit_bytes=48 * 1024 * 1024),
+        compiler_params=pltpu.CompilerParams(vmem_limit_bytes=24 * 1024 * 1024),
         cost_estimate=pl.CostEstimate(flops=flops, bytes_accessed=moved, transcendentals=0),
     )(*args)
 
@@ -108,8 +119,19 @@
     emit_strips(lambda r: rows_ref[r], rows, pad, swap, strips)
 
 
-def prepare_cotan(grad_ref, mask_ref, offset_ref, value_ref, rows_ref, *rest):
-    quarters, scr = rest[:-1], rest[-1]
+def prepare_cotan(part, *refs):
+    rows_ref, own_ref, core_ref, far_ref, taps_ref, mask_ref, state_ref = refs[9:16]
+    scr, weights_scr, turn_scr, sems = refs[16:20]
+    grad_ref, offset_ref, value_ref = refs[20:23]
+    held = (grad_ref, mask_ref, offset_ref, value_ref, *refs[23:27], state_ref)
+    copies = [pltpu.make_async_copy(refs[k], held[k], sems.at[k]) for k in range(9)]
+    for k in (4, 5, 6, 7, 0, 1, 2, 3, 8):
+        copies[k].start()
+    for k in range(4, 8):
+        copies[k].wait()
+    pack_weights(part, rows_ref.shape[1], *held[4:8], weights_scr, taps_ref, turn_scr)
+    for k in range(0, 4):
+        copies[k].wait()
     rows, pad, cols = rows_ref.shape
     me = lax.axis_index("ch")
     mask = mask_ref[...].astype(F32)
@@ -132,16 +154,28 @@
     scr[pl.ds(0, rows, stride=pad), :] = first + total
     for r in range(rows):
         rows_ref[r] = (scr[r * pad : (r + 1) * pad, :] * mask[r : r + 1, :]).astype(BF)
-    part_rows = quarters[0].shape[0]
-    for k, quarter in enumerate(quarters):
-        quarter[...] = rows_ref[pl.ds((me ^ k) * part_rows, part_rows)]
+    tiles = weights_scr.shape[1] // LANES
+    hid = weights_scr.shape[0]
+    for to in (own_ref, core_ref, far_ref):
+        for t in range(tiles):
+            to[t * hid : (t + 1) * hid, :] = weights_scr[:, t * LANES : (t + 1) * LANES]
+    count = (own_ref.shape[0] - tiles * hid) // pad
+    for k, (to, slot) in enumerate(((own_ref, 0), (core_ref, 0), (far_ref, 0), (far_ref, 1))):
+        for r in range(count):
+            at = tiles * hid + (slot * count + r) * pad
+            to[at : at + pad, :] = rows_ref[(me ^ k) * count + r]
+    copies[8].wait()
+
+
+def relay(in_ref, out_ref):
+    del in_ref, out_ref
 
 
 def ring(count, step):
     return [(i, (i + step) % count) for i in range(count)]
 
 
-def exchange_halo(strips, rows, pad, swap, name):
+def exchange_halo(strips, rows, pad, swap, name, riding=()):
     n_lat, n_lon = lax.axis_size("lat"), lax.axis_size("lon")
     top = n_lat - 1
     fold_pairs = [
@@ -157,11 +191,11 @@
             lax.ppermute(down, "lat", [(i + 1, i) for i in range(n_lat - 1)]),
         ]
     fold = lax.ppermute(fold, ("lon", "lat"), fold_pairs)
-    kernel = functools.partial(finish_columns, rows, swap)
+    kernel = functools.partial(finish_columns, rows, swap, len(riding) > 0)
     halo, left, right = call(
         kernel,
         [shape((2 * DIL, pad, LANES), BF)] + [shape((pad, LANES), BF)] * 2,
-        [*moved, fold, left, right],
+        [*riding, *moved, fold, left, right],
         name=name,
     )
     from_right = lax.ppermute(left, "lon", ring(n_lon, -1))
@@ -169,7 +203,9 @@
     return halo, from_left, from_right
 
 
-def finish_columns(rows, swap, *refs):
+def finish_columns(rows, swap, riding, *refs):
+    if riding:
+        ride_ref, *refs = refs
     if swap:
         strip_ref, fold_ref, left_ref, right_ref, halo_ref, left_out, right_out = refs
         low_ref = high_ref = strip_ref
@@ -184,6 +220,9 @@
         halo_ref[DIL + t] = north.astype(BF)
         left, right = pack_columns(south, t, left, right)
         left, right = pack_columns(north, rows + DIL + t, left, right)
+    if riding:
+        ride = pltpu.roll(ride_ref[...].astype(F32), RIDE, 1)
+        left, right = left + ride, right + ride
     left_out[...] = left.astype(BF)
     right_out[...] = right.astype(BF)
 
@@ -238,7 +277,6 @@
 def conv_forward(ones_row, block_ref, halo_ref, left_ref, right_ref, tap_ref, *rest):
     quarters, scr = rest[:-1], rest[-1]
     pad = block_ref.shape[1]
-    me = lax.axis_index("ch")
 
     def body(group, carry):
         taps = spread(tap_ref, group)
@@ -252,9 +290,10 @@
         return carry
 
     lax.fori_loop(0, pad // 16, body, 0)
-    part_rows = quarters[0].shape[0]
+    me = lax.axis_index("ch")
+    count = quarters[0].shape[0]
     for k, quarter in enumerate(quarters):
-        quarter[...] = scr[pl.ds((me ^ k) * part_rows, part_rows)]
+        quarter[...] = scr[pl.ds((me ^ k) * count, count)]
 
 
 def conv_adjoint(
@@ -316,7 +355,7 @@
             for b in range(3):
                 total = jnp.sum(sums[a][b], axis=1, keepdims=True)
                 out = jnp.where(lane == 3 * a + b, total, out)
-        out_ref[at, :] = out
+        out_ref[at, :] = out.astype(BF)
         return carry
 
     lax.fori_loop(0, pad // 16, body, 0)
@@ -338,8 +377,12 @@
     return jnp.where(lane >= LANES, lane - LANES, jnp.where(lane >= low, lane - low + split, -1))
 
 
-def pack_weights(part, pad, expand_ref, bias_ref, project_ref, out_ref):
-    channels, hidden = expand_ref.shape
+def pack_weights(part, pad, expand_ref, bias_ref, project_ref, kernel_ref, out_ref, taps_ref, turn_scr):
+    hidden, channels = expand_ref.shape
+    turn_scr[...] = jnp.zeros(turn_scr.shape, F32)
+    for a in range(3):
+        turn_scr[3 * a : 3 * a + 3, 0:part] = kernel_ref[a]
+    taps_ref[...] = jnp.transpose(turn_scr[...])[0:pad, :]
     wide = out_ref.shape[1]
     split = 4 * pad // LANES * LANES
     lane = iota((channels, wide), 1)
@@ -358,7 +401,7 @@
     pick_b = ((lane == row * pad + part) & (row < 3)).astype(BF)
     turned = (((0,), (0,)), ((), ()))
     packed = (
-        lax.dot_general(expand_ref[...], pick_e, turned, preferred_element_type=F32)
+        jnp.dot(expand_ref[...], pick_e, preferred_element_type=F32)
         + lax.dot_general(parts.astype(BF), pick_b, turned, preferred_element_type=F32)
         + jnp.dot(project_ref[...], pick_p, preferred_element_type=F32)
     )
@@ -370,52 +413,67 @@
 GELU_C = math.sqrt(2.0 / math.pi)
 
 
-def mlp(*refs):
-    xs, ys, ws = refs[0:4], refs[4:8], refs[8:12]
-    grads, keep_ref, send_ref = refs[12:16], refs[16], refs[17]
-    x_scr, y_scr, w_scr, t_scr, act_scr, pre_scr, cg_scr = refs[18:]
-    part_rows, pad = xs[0].shape[:2]
-    hid = ws[0].shape[0]
+def activation_gradient(*refs):
+    parts = refs[0:4]
+    act_ref, y_scr, w_scr, t_scr = refs[4:]
+    me = lax.axis_index("ch")
+    tiles = w_scr.shape[1] // LANES
+    hid = w_scr.shape[0] // 4
+    depth, cells = y_scr.shape
+    part_rows = cells // LANES
+    pad = (parts[0].shape[0] - tiles * hid) // part_rows
     split = 4 * pad // LANES * LANES
-    depth = x_scr.shape[0]
-    cells = x_scr.shape[1]
-    me = lax.axis_index("ch")
-    x_scr[4 * pad : depth, :] = jnp.zeros((depth - 4 * pad, cells), BF)
     y_scr[0 : depth - 4 * pad, :] = jnp.zeros((depth - 4 * pad, cells), BF)
-    for k in range(4):
+    for k, ref in enumerate(parts):
+        for t in range(tiles):
+            w_scr[k * hid : (k + 1) * hid, t * LANES : (t + 1) * LANES] = ref[
+                t * hid : (t + 1) * hid, :
+            ]
         block = me ^ k
-        w_scr[k * hid : (k + 1) * hid, :] = ws[k][...]
+        start = tiles * hid + (part_rows * pad if k == 3 else 0)
         for r in range(part_rows):
             cols = slice(r * LANES, (r + 1) * LANES)
-            x_scr[pl.ds(aligned(block * pad), pad), cols] = xs[k][r]
             for u in range(pad // 16):
                 slot = block * pad + 16 * u
                 to = jnp.where(slot < split, slot + LANES, slot - split + depth - 4 * pad)
-                y_scr[pl.ds(aligned(to), 16), cols] = ys[k][r, 16 * u : 16 * (u + 1), :]
+                at = start + r * pad + 16 * u
+                y_scr[pl.ds(aligned(to), 16), cols] = ref[at : at + 16, :]
     t_scr[...] = jnp.transpose(w_scr[:, 0:depth])
     step = 256
     for start in range(0, cells, step):
         cols = slice(start, start + step)
-        hidden = jnp.dot(w_scr[:, 0:depth], x_scr[:, cols], preferred_element_type=F32)
-        act_grad = jnp.dot(w_scr[:, split : split + depth], y_scr[:, cols], preferred_element_type=F32)
+        act_ref[:, cols] = jnp.dot(
+            w_scr[:, split : split + depth], y_scr[:, cols], preferred_element_type=F32
+        )
+
+
+def hidden_gradient(*refs):
+    xs, (act_ref, y_ref, w_ref) = refs[0:4], refs[4:7]
+    pre_ref, keep_ref, send_ref, x_scr, value_scr = refs[7:]
+    part_rows, pad = xs[0].shape[:2]
+    hid = w_ref.shape[0] // 4
+    split = 4 * pad // LANES * LANES
+    depth, cells = x_scr.shape
+    me = lax.axis_index("ch")
+    x_scr[4 * pad : depth, :] = jnp.zeros((depth - 4 * pad, cells), BF)
+    for k in range(4):
+        for r in range(part_rows):
+            x_scr[pl.ds(aligned((me ^ k) * pad), pad), r * LANES : (r + 1) * LANES] = xs[k][r]
+    step = 256
+    for start in range(0, cells, step):
+        cols = slice(start, start + step)
+        hidden = jnp.dot(w_ref[:, 0:depth], x_scr[:, cols], preferred_element_type=F32)
         square = hidden * hidden
         tanh = jnp.tanh(GELU_C * hidden * (1.0 + 0.044715 * square))
         half = 0.5 * (1.0 + tanh)
         slope = half + (0.5 * GELU_C) * hidden * (1.0 - tanh * tanh) * (
             1.0 + (3 * 0.044715) * square
         )
-        act_scr[:, cols] = (hidden * half).astype(BF)
-        pre = (act_grad * slope).astype(BF)
-        pre_scr[:, cols] = pre
-        cg_scr[:, cols] = jnp.dot(t_scr[...], pre, preferred_element_type=F32).astype(BF)
-    for k in range(4):
-        for r in range(part_rows):
-            grads[k][r] = cg_scr[
-                pl.ds(aligned((me ^ k) * pad), pad), r * LANES : (r + 1) * LANES
-            ]
+        value_scr[:, cols] = (hidden * half).astype(BF)
+        pre_ref[:, cols] = (act_ref[:, cols] * slope).astype(BF)
     over_cells = (((1,), (1,)), ((), ()))
-    expand = lax.dot_general(pre_scr[...], x_scr[...], over_cells, preferred_element_type=F32)
-    project = lax.dot_general(act_scr[...], y_scr[...], over_cells, preferred_element_type=F32)
+    expand = lax.dot_general(pre_ref[...], x_scr[...], over_cells, preferred_element_type=F32)
+    project = lax.dot_general(value_scr[...], y_ref[...], over_cells, preferred_element_type=F32)
     shared = split // LANES
     tiles = [expand[:, t * LANES : (t + 1) * LANES] for t in range(shared)]
     tiles.append(expand[:, split : split + LANES] + project[:, 0:LANES])
@@ -426,81 +484,92 @@
             to[k // 2, t * hid : (t + 1) * hid, :] = tile[k * hid : (k + 1) * hid].astype(to.dtype)
 
 
-def add_cores(keep_ref, got_ref, own_ref, y_ref, x_ref, xy_ref):
-    half = own_ref.shape[0]
-    lat = lax.axis_index("lat")
-    here, there = pl.ds(aligned(lat * half), half), pl.ds(aligned((1 - lat) * half), half)
-
-    def total(group, at):
-        return keep_ref[group, at, :] + got_ref[group, at, :].astype(F32)
-
-    own_ref[...] = total(0, here)
-    y_ref[...] = total(0, there).astype(BF)
-    x_ref[...] = total(1, here).astype(BF)
-    xy_ref[...] = total(1, there).astype(BF)
-
-
-def add_planes(own_ref, a_ref, b_ref, c_ref, keep_ref, *rest):
-    sends, scr = rest[:-1], rest[-1]
-    scr[...] = own_ref[...] + (
-        a_ref[...].astype(F32) + b_ref[...].astype(F32) + c_ref[...].astype(F32)
-    )
-    piece = keep_ref.shape[0]
-    step = piece - 16
-    lon = lax.axis_index("lon")
-    keep_ref[...] = scr[pl.ds(aligned(lon * step), piece), :]
-    for k, send in enumerate(sends):
-        send[...] = scr[pl.ds(aligned((lon ^ (k + 1)) * step), piece), :].astype(BF)
-
-
-def add_lines(own_ref, a_ref, b_ref, c_ref, kernel_ref, out_ref):
-    piece = own_ref.shape[0]
-    out_ref[0:piece, :] = (
-        own_ref[...] + (a_ref[...].astype(F32) + b_ref[...].astype(F32) + c_ref[...].astype(F32))
+def conv_gradient(pre_ref, t_ref, *rest):
+    outs, scr = rest[:-1], rest[-1]
+    part_rows, pad = outs[0].shape[:2]
+    me = lax.axis_index("ch")
+    step = 256
+    for start in range(0, pre_ref.shape[1], step):
+        cols = slice(start, start + step)
+        scr[:, cols] = jnp.dot(t_ref[...], pre_ref[:, cols], preferred_element_type=F32).astype(BF)
+    for k, to in enumerate(outs):
+        for r in range(part_rows):
+            to[r] = scr[pl.ds(aligned((me ^ k) * pad), pad), r * LANES : (r + 1) * LANES]
+
+
+def add_cores(keep_ref, got_ref, own_ref, *sends):
+    piece = own_ref.shape[1]
+    step = piece - 32
+    place = 2 * lax.axis_index("lat") + lax.axis_index("lon") % 2
+    for k in range(4):
+        at = pl.ds(pl.multiple_of((place ^ k) * step, 32), piece)
+        for group in range(2):
+            total = keep_ref[group, at, :] + got_ref[group, at, :].astype(F32)
+            to = sends[k - 1] if k else own_ref
+            to[group] = total.astype(to.dtype)
+
+
+def add_pieces(own_ref, a_ref, b_ref, c_ref, mine_ref, other_ref):
+    for group, to in enumerate((mine_ref, other_ref)):
+        total = own_ref[group] + (
+            a_ref[group].astype(F32) + b_ref[group].astype(F32) + c_ref[group].astype(F32)
+        )
+        to[...] = total.astype(to.dtype)
+
+
+def add_across(mine_ref, got_ref, out_ref):
+    out_ref[...] = (mine_ref[...] + got_ref[...].astype(F32)).astype(BF)
+
+
+def finish_pieces(mine_ref, line_ref, kernel_ref, left_ref, right_ref, out_ref):
+    piece = mine_ref.shape[0]
+    out_ref[0:piece, :] = (mine_ref[...].astype(F32) + line_ref[...].astype(F32)).astype(BF)
+    even = lax.axis_index("lon") % 2 == 0
+    other = jnp.where(even, left_ref[...].astype(F32), right_ref[...].astype(F32))
+    other = pltpu.roll(other, LANES - RIDE + 16, 1)
+    lane = iota(other.shape, 1)
+    here = kernel_ref[...].astype(F32)
+    out_ref[piece : out_ref.shape[0], :] = jnp.where(
+        lane < 16, here, jnp.where(lane < 32, other, 0.0)
     ).astype(BF)
-    out_ref[piece : out_ref.shape[0], :] = kernel_ref[...].astype(BF)
-
-
-def join_lines(piece, p0, p1, p2, p3, out_ref, scr):
-    step = piece - 16
-    half = 4 * step + 16
-    extra = out_ref.shape[0] - half
-    lon = lax.axis_index("lon")
+
+
+def write_parameters(part, pad, scale, hid, p0, p1, p2, p3, *rest):
+    expand_ref, project_ref, bias_ref, taps_ref, all_scr, taps_scr, turn_scr = rest
+    piece = p0.shape[0] - pad
+    step = piece - 32
+    place = 2 * lax.axis_index("lat") + lax.axis_index("lon") % 2
     for k, ref in enumerate((p0, p1, p2, p3)):
-        place = lon ^ k
-        out_ref[pl.ds(aligned(place * step), step), :] = ref[0:step, :]
-
-        @pl.when(place == 3)
+        to = place ^ k
+        all_scr[pl.ds(pl.multiple_of(to * step, 32), step), :] = ref[0:step, :]
+
+        @pl.when(to == 3)
         def _():
-            out_ref[4 * step : half, :] = ref[step:piece, :]
-
-        scr[pl.ds(aligned(place * extra), extra), :] = ref[piece : piece + extra, :].astype(F32)
-    total = scr[0:extra, :]
-    for k in range(1, 4):
-        total = total + scr[k * extra : (k + 1) * extra, :]
-    out_ref[half : half + extra, :] = total.astype(BF)
-
-
-def write_parameters(part, pad, scale, hid, own_ref, got_ref, *rest):
-    expand_ref, project_ref, bias_ref, taps_ref, all_scr, turn_scr = rest
-    half = all_scr.shape[0] // 2
-    extra = own_ref.shape[0] - half
-    lat = lax.axis_index("lat")
-    all_scr[pl.ds(aligned(lat * half), half), :] = own_ref[0:half, :]
-    all_scr[pl.ds(aligned((1 - lat) * half), half), :] = got_ref[0:half, :]
+            all_scr[4 * step : 4 * step + 32, :] = ref[step:piece, :]
+
+        lat, lon = lax.axis_index("lat") ^ (k >> 1), lax.axis_index("lon") ^ (k & 1)
+        taps = ref[piece : piece + pad, :].astype(F32)
+        taps_scr[pl.ds(aligned((4 * lat + lon) * pad), pad), :] = taps
+        taps_scr[pl.ds(aligned((4 * lat + (lon ^ 3)) * pad), pad), :] = pltpu.roll(
+            taps, LANES - 16, 1
+        )
     unpack(part, pad, scale, hid, all_scr, expand_ref, project_ref, bias_ref)
-    total = own_ref[half : half + extra, :].astype(F32) + got_ref[half : half + extra, :].astype(F32)
+    total = taps_scr[0:pad, :]
+    for k in range(1, 8):
+        total = total + taps_scr[k * pad : (k + 1) * pad, :]
     write_taps(total, scale, taps_ref, turn_scr)
 
 
 def write_taps(total, scale, taps_ref, turn_scr):
     turn_scr[...] = jnp.zeros(turn_scr.shape, F32)
     turn_scr[0 : total.shape[0], :] = total * scale
-    taps_ref[...] = jnp.transpose(turn_scr[...])[0 : taps_ref.shape[0], 0 : taps_ref.shape[1]]
+    turned = jnp.transpose(turn_scr[...])
+    for a in range(3):
+        taps_ref[a] = turned[3 * a : 3 * a + 3, 0 : taps_ref.shape[2]]
 
 
 def unpack(part, pad, scale, hid, all_ref, expand_ref, project_ref, bias_ref):
-    channels, hidden = expand_ref.shape
+    hidden, channels = expand_ref.shape
     split = 4 * pad // LANES * LANES
     shared = split // LANES
     tiles = [all_ref[t * hid : (t + 1) * hid, :] for t in range(2 * shared + 1)]
@@ -513,7 +582,7 @@
     pick_b = (iota((16, depth), 1) == part).astype(BF)
     last = (((1,), (1,)), ((), ()))
     dot = functools.partial(lax.dot_general, dimension_numbers=last, preferred_element_type=F32)
-    expand_ref[...] = dot(pick_e, expand)[:, 0:hidden] * scale
+    expand_ref[...] = dot(expand, pick_e)[0:hidden, :] * scale
     bias_ref[...] = dot(pick_b, expand)[0:1, 0:hidden] * scale
     project_ref[...] = dot(project, pick_p)[0:hidden, :] * scale
 
@@ -551,51 +620,56 @@
     scale = 1.0 / math.sqrt(rows * n_lat * cols * n_lon)
     core = [(i, i ^ 1) for i in range(n_ch)]
     across = [(i, i ^ 2) for i in range(n_ch)]
-    both = [(i, i ^ 3) for i in range(n_ch)]
     block = shape((rows, pad, cols), BF)
     quarter = shape((part_rows, pad, cols), BF)
     flat = pltpu.VMEM((rows * pad, cols), F32)
 
+    turn = pltpu.VMEM((LANES, LANES), F32)
+    def spread_parts(parts):
+        return [parts[0]] + [
+            lax.ppermute(parts[k], "ch", [(i, i ^ k) for i in range(n_ch)]) for k in (3, 2, 1)
+        ][::-1]
+
+    tile_rows = wide // LANES * hid
+    near_rows, far_rows = tile_rows + part_rows * pad, tile_rows + 2 * part_rows * pad
+    prepared = [
+        out_grad,
+        land_mask,
+        swath_offset.reshape(1, -1),
+        swath_value.reshape(1, -1),
+        expand_weight.T,
+        expand_bias.reshape(1, hidden),
+        project_weight,
+        depth_kernel,
+        ocean_state,
+    ]
+    cotan, own, to_core, to_far, taps, land_mask, ocean_state = call(
+        functools.partial(prepare_cotan, part),
+        [
+            block,
+            shape((near_rows, LANES), BF),
+            shape((near_rows, LANES), BF),
+            shape((far_rows, LANES), BF),
+            shape((pad, LANES), F32),
+            shape(land_mask.shape, land_mask.dtype),
+            shape(ocean_state.shape, ocean_state.dtype),
+        ],
+        prepared,
+        [flat, pltpu.VMEM((hid, wide), BF), turn, pltpu.SemaphoreType.DMA((9,))]
+        + [pltpu.VMEM(prepared[k].shape, prepared[k].dtype) for k in (0, 2, 3, 4, 5, 6, 7)],
+        "cotan_rows",
+        far=True,
+    )
     masked, *strips = call(
         functools.partial(prepare_state, swap),
         [block] + strip_shapes(pad, swap),
         [ocean_state, land_mask],
         [flat],
         "state_rows",
-    )
-    weights = call(
-        functools.partial(pack_weights, part, pad),
-        [shape((hid, wide), BF)],
-        [expand_weight, expand_bias.reshape(1, hidden), project_weight],
-        (),
-        "weight_rows",
-    )[0]
-    taps = jnp.pad(depth_kernel.reshape(9, part).T, ((0, pad - part), (0, LANES - 9)))
-    cotan, *cotan_parts = call(
-        prepare_cotan,
-        [block] + [quarter] * 4,
-        [out_grad, land_mask, swath_offset.reshape(1, -1), swath_value.reshape(1, -1)],
-        [flat],
-        "cotan_rows",
+        after=[taps],
     )
     around = exchange_halo(strips, rows, pad, swap, "state_columns")
-
-    def spread_parts(parts):
-        return [
-            parts[0],
-            lax.ppermute(parts[1], "ch", core),
-            lax.ppermute(parts[2], "ch", across),
-            lax.ppermute(parts[3], "ch", both),
-        ]
-
-    weights_across = lax.ppermute(weights, "ch", across)
-    all_weights = [
-        weights,
-        lax.ppermute(weights, "ch", core),
-        weights_across,
-        lax.ppermute(weights_across, "ch", core),
-    ]
-    all_cotan = spread_parts(cotan_parts)
+    from_far = lax.ppermute(to_far, "ch", across)
     conv_parts = call(
         functools.partial(conv_forward, part),
         [quarter] * 4,
@@ -604,40 +678,98 @@
         "conv_forward",
     )
     all_conv = spread_parts(conv_parts)
-    tile_rows = wide // LANES * hid
-    *grad_parts, keep, send = call(
-        mlp,
-        [quarter] * 4 + [shape((2, tile_rows, LANES), F32), shape((2, tile_rows, LANES), BF)],
-        [*all_conv, *all_cotan, *all_weights],
+    from_far = call(
+        relay, [from_far], [from_far], (), "cotan_relay", aliases={0: 0}, after=around[1:]
+    )[0]
+    passed = lax.ppermute(from_far, "ch", core)
+    act_grad, cotan_all, weights_all, weights_turned = call(
+        activation_gradient,
         [
-            pltpu.VMEM((depth, cells), BF),
-            pltpu.VMEM((depth, cells), BF),
-            pltpu.VMEM((n_ch * hid, wide), BF),
-            pltpu.VMEM((depth, n_ch * hid), BF),
-            pltpu.VMEM((n_ch * hid, cells), BF),
-            pltpu.VMEM((n_ch * hid, cells), BF),
-            pltpu.VMEM((depth, cells), BF),
+            shape((n_ch * hid, cells), F32),
+            shape((depth, cells), BF),
+            shape((n_ch * hid, wide), BF),
+            shape((depth, n_ch * hid), BF),
         ],
-        "mlp",
-        flops=10 * cells * depth * n_ch * hid,
+        [own, lax.ppermute(to_core, "ch", core), from_far, passed],
+        (),
+        "activation_gradient",
+    )
+    pre_grad, keep, send = call(
+        hidden_gradient,
+        [
+            shape((n_ch * hid, cells), BF),
+            shape((2, tile_rows, LANES), F32),
+            shape((2, tile_rows, LANES), BF),
+        ],
+        [*all_conv, act_grad, cotan_all, weights_all],
+        [pltpu.VMEM((depth, cells), BF), pltpu.VMEM((n_ch * hid, cells), BF)],
+        "hidden_gradient",
     )
     got = lax.ppermute(send, "ch", core)
+    grad_parts = call(
+        conv_gradient,
+        [quarter] * 4,
+        [pre_grad, weights_turned],
+        [pltpu.VMEM((depth, cells), BF)],
+        "conv_gradient",
+    )
     grad_got = spread_parts(grad_parts)
+    staged = n_lat == 2 and n_lon == 4 and tile_rows % 32 == 0
+    if staged:
+        step = (tile_rows - 32) // 128 * 32
+        piece = step + 32
+        assert 3 * step + piece == tile_rows
+        mine, *sends = call(
+            add_cores,
+            [shape((2, piece, LANES), F32)] + [shape((2, piece, LANES), BF)] * 3,
+            [keep, got],
+            (),
+            "add_cores",
+            after=grad_got[1:2],
+        )
+
+        def turn_plane(k):
+            pairs = []
+            for lon in range(n_lon):
+                for lat in range(n_lat):
+                    pairs.append((lon * n_lat + lat, (lon ^ (k & 1)) * n_lat + (lat ^ (k >> 1))))
+            return pairs
+
+        def over_plane(values):
+            return [lax.ppermute(values[k - 1], ("lon", "lat"), turn_plane(k)) for k in (1, 2, 3)]
+
+        mine, other = call(
+            add_pieces,
+            [shape((piece, LANES), F32), shape((piece, LANES), BF)],
+            [mine, *over_plane(sends)],
+            (),
+            "add_pieces",
+        )
     conv_grad, *grad_strips = call(
         functools.partial(collect_grad, swap),
         [block] + strip_shapes(pad, swap),
         grad_got,
         (),
         "grad_rows",
-    )
-    grad_around = exchange_halo(grad_strips, rows, pad, swap, "grad_columns")
+        after=[other] if staged else [],
+    )
+    if staged:
+        mine = call(
+            add_across,
+            [shape((piece, LANES), BF)],
+            [mine, lax.ppermute(other, "ch", across)],
+            (),
+            "add_across",
+        )[0]
     kernel_part = call(
         kernel_gradient,
-        [shape((pad, LANES), F32)],
+        [shape((pad, LANES), BF)],
         [conv_grad, masked, *around],
         (),
         "kernel_gradient",
+        after=[mine] if staged else [],
     )[0]
+    grad_around = exchange_halo(grad_strips, rows, pad, swap, "grad_columns", [kernel_part])
     state_grad = call(
         conv_adjoint,
         [shape((part, rows, cols), BF)],
@@ -646,63 +778,36 @@
         "conv_adjoint",
     )[0]
     outs = [
-        shape((channels, hidden), F32),
+        shape((hidden, channels), F32),
         shape((hidden, channels), F32),
         shape((1, hidden), F32),
-        shape((9, part), F32),
+        shape((3, 3, part), F32),
     ]
-    turn = pltpu.VMEM((LANES, LANES), F32)
-    if n_lat == 2 and n_lon == 4 and tile_rows % 32 == 0 and (tile_rows // 2 - 16) % 64 == 0:
-        half = tile_rows // 2
-        step = (half - 16) // 4
-        piece = step + 16
-        mine, to_y, to_x, to_xy = call(
-            add_cores,
-            [shape((half, LANES), F32)] + [shape((half, LANES), BF)] * 3,
-            [keep, got],
+    if staged:
+        far_lon = [(lon, lon ^ 2) for lon in range(n_lon)]
+        summed = call(
+            finish_pieces,
+            [shape((piece + pad, LANES), BF)],
+            [
+                mine,
+                lax.ppermute(mine, "lon", far_lon),
+                kernel_part,
+                *grad_around[1:],
+            ],
             (),
-            "add_cores",
-        )
-        both_axes = [
-            (lat * n_ch + i, (1 - lat) * n_ch + (i ^ 2)) for lat in range(n_lat) for i in range(n_ch)
-        ]
-        planes = [
-            lax.ppermute(to_y, "lat", [(0, 1), (1, 0)]),
-            lax.ppermute(to_x, "ch", across),
-            lax.ppermute(to_xy, ("lat", "ch"), both_axes),
-        ]
-        own, *line_parts = call(
-            add_planes,
-            [shape((piece, LANES), F32)] + [shape((piece, LANES), BF)] * 3,
-            [mine, *planes],
-            [pltpu.VMEM((half, LANES), F32)],
-            "add_planes",
-        )
-        turns = [[(i, i ^ k) for i in range(n_lon)] for k in range(4)]
-        lines = [lax.ppermute(line_parts[k - 1], "lon", turns[k]) for k in (1, 2, 3)]
-        summed = call(
-            add_lines, [shape((piece + pad, LANES), BF)], [own, *lines, kernel_part], (), "add_lines"
+            "finish_pieces",
         )[0]
-        pieces = [summed] + [lax.ppermute(summed, "lon", turns[k]) for k in (1, 2, 3)]
-        mine = call(
-            functools.partial(join_lines, piece),
-            [shape((half + pad, LANES), BF)],
-            pieces,
-            [pltpu.VMEM((4 * pad, LANES), F32)],
-            "join_lines",
-        )[0]
-        other = lax.ppermute(mine, "lat", [(0, 1), (1, 0)])
         expand_grad, project_grad, bias_grad, kernel_grad = call(
             functools.partial(write_parameters, part, pad, scale, hid),
             outs,
-            [mine, other],
-            [pltpu.VMEM((tile_rows, LANES), BF), turn],
+            [summed, *over_plane([summed] * 3)],
+            [pltpu.VMEM((tile_rows, LANES), BF), pltpu.VMEM((8 * pad, LANES), F32), turn],
             "write_parameters",
         )
     else:
         total = keep + got.astype(F32)
         total = total[0] + lax.ppermute(total[1].astype(BF), "ch", across).astype(F32)
-        total, kernel_sum = lax.psum((total, kernel_part), ("lon", "lat"))
+        total, kernel_sum = lax.psum((total, kernel_part.astype(F32)), ("lon", "lat"))
         expand_grad, project_grad, bias_grad, kernel_grad = call(
             functools.partial(unpack_whole, part, pad, scale, hid),
             outs,
@@ -712,10 +817,10 @@
         )
     return (
         state_grad,
-        expand_grad,
+        expand_grad.T,
         project_grad,
         bias_grad.reshape(hidden),
-        kernel_grad.reshape(3, 3, part),
+        kernel_grad,
     )
 
 

time: 100 us -> 73.9 us (0.74)
  the two profiles are of different devices: /device:TPU:28 before, /device:TPU:0 now
where the time goes in v2:
time: 73.9 us; the launch traced here: 73.7 us
  starting transfers between devices  32.9 us (45%)
  waiting for transfers between devices  22.4 us (30%)
  Pallas kernels  17.6 us (24%)
  between operations  0.79 us (1%)
    pallas_call x17, Pallas kernels, call(): pl.pallas_call(kernel, out_shape=tuple(outs), in_specs=[pl.BlockSpec(memo...  17.6 us
    ppermute x6, starting transfers between devices, over_plane(): lax.ppermute(values[k - 1], ('lon', 'lat'), turn_plane(k))  10.1 us
    ppermute x6, waiting for transfers between devices, spread_parts(): lax.ppermute(parts[k], 'ch', [(i, i ^ k) for i in range(n_ch)])  9.58 us
    ppermute x6, waiting for transfers between devices, over_plane(): lax.ppermute(values[k - 1], ('lon', 'lat'), turn_plane(k))  5.7 us
    ppermute x2, starting transfers between devices, exchange_halo(): from_right = lax.ppermute(left, 'lon', ring(n_lon, -1))  4.4 us
    ppermute x2, waiting for transfers between devices, exchange_halo(): from_left = lax.ppermute(right, 'lon', ring(n_lon, 1))  3.61 us
    ppermute x2, starting transfers between devices, exchange_halo(): from_left = lax.ppermute(right, 'lon', ring(n_lon, 1))  3.35 us
    ppermute x2, starting transfers between devices, exchange_halo(): moved = [lax.ppermute(strip, 'lat', [(0, 1), (1, 0)])]  3.29 us
  transfers between devices with their start and end apart: 26, of which 14 were waited for; matrix products, arithmetic and copies ran while one was open for 0% of the time, Pallas kernels for 13%

profile of v2, /device:TPU:0, one launch (start us, length us, event | category | flops | bytes accessed | tf_op | source)
XLA Modules:
  0.0 73.7 jit_solution(11938248833509848443)
XLA Ops:
  0.6 2.6 %cotan_rows.1 = (bf16[32,80,128]{2,1,0:T(8,128)(2,1)S(1)}, bf16[1440,128]{1,0:T(8,128)(2,1)S(1)}, bf16[1440,128]{1,0:T(8,128)(2,1)S(1)}, bf16[2080,128]{1,0:T(8,...) custom-call(bf16[75,32,128]{2,1,0:T(8,128)(2,1)} %refs_0_.1, ...), custom_call_target="tpu_custom_call" | custom-call | bytes 4029444 | tf_op jit(solution)/shard_map/cotan_rows/pallas_call | solution.py:34
  3.2 3.0 %collective-permute-start.8 = (bf16[2080,128]{1,0:T(8,128)(2,1)S(1)}, bf16[2080,128]{1,0:T(8,128)(2,1)S(1)}, u32[]{:S(2)}, u32[]{:S(2)}) collective-permute-start(bf16[2080,128]{1,0:T(8,128)(2,1)S(1)} %get-tuple-element.70), channel_id=1, source_target_pairs={{0,2},{1,3},{2,0},{3,1},{4,6},{5,7},{6,4},{7,5},{8,10},{9,11},{10,... | collective-permute-start | bytes 1597448 | tf_op jit(solution)/shard_map/ppermute | solution.py:672
  6.2 1.0 %state_rows.1 = (bf16[32,80,128]{2,1,0:T(8,128)(2,1)S(1)}, bf16[2,80,128]{2,1,0:T(8,128)(2,1)S(1)}, bf16[2,80,128]{2,1,0:T(8,128)(2,1)S(1)}, bf16[80,128]{1,0:T(8,128)(2,1)S(1)}, bf16[80,128]{1,0:T(8,128)(2,1)S(1)}) custom-call(bf16[75,32,128]{2,1,0:T(8,128)(2,1)S(1)} %get-tuple-element.53.refs_0_, s32[32,128]{1,0:T(8,128)S(1)} %get-tuple-element.54.refs_1_.mask_ref, ...), custom_call_target="tpu_custom_call" | custom-call | bytes 1449984 | tf_op jit(solution)/shard_map/state_rows/pallas_call | solution.py:34
  7.2 1.6 %collective-permute-start = (bf16[2,80,128]{2,1,0:T(8,128)(2,1)S(1)}, bf16[2,80,128]{2,1,0:T(8,128)(2,1)S(1)}, u32[]{:S(2)}, u32[]{:S(2)}) collective-permute-start(bf16[2,80,128]{2,1,0:T(8,128)(2,1)S(1)} %get-tuple-element.57), channel_id=1, source_target_pairs={{0,4},{4,0},{1,5},{5,1},{2,6},{6,2},{3,7},{7,3},{8,12},{12,8},{9,1... | collective-permute-start | bytes 122888 | tf_op jit(solution)/shard_map/ppermute | solution.py:186
  9.5 1.8 %collective-permute-done.refs_0_ = bf16[2,80,128]{2,1,0:T(8,128)(2,1)S(1)} collective-permute-done((bf16[2,80,128]{2,1,0:T(8,128)(2,1)S(1)}, bf16[2,80,128]{2,1,0:T(8,128)(2,1)S(1)}, u32[]{:S(2)}, u32[]{:S(2)}) %collective-permute-start) | collective-permute-done | bytes 40992 | tf_op jit(solution)/shard_map/ppermute | solution.py:186
  11.4 1.6 %collective-permute-start.2 = (bf16[80,128]{1,0:T(8,128)(2,1)S(1)}, bf16[80,128]{1,0:T(8,128)(2,1)S(1)}, u32[]{:S(2)}, u32[]{:S(2)}) collective-permute-start(bf16[80,128]{1,0:T(8,128)(2,1)S(1)} %get-tuple-element.62), channel_id=1, source_target_pairs={{0,8},{8,16},{16,24},{24,0},{1,9},{9,17},{17,25},{25,1},{2,10},{10... | collective-permute-start | bytes 61448 | tf_op jit(solution)/shard_map/ppermute | solution.py:202
  13.0 2.2 %collective-permute-start.3 = (bf16[80,128]{1,0:T(8,128)(2,1)S(1)}, bf16[80,128]{1,0:T(8,128)(2,1)S(1)}, u32[]{:S(2)}, u32[]{:S(2)}) collective-permute-start(bf16[80,128]{1,0:T(8,128)(2,1)S(1)} %get-tuple-element.63), channel_id=1, source_target_pairs={{0,24},{8,0},{16,8},{24,16},{1,25},{9,1},{17,9},{25,17},{2,26},{10... | collective-permute-start | bytes 61448 | tf_op jit(solution)/shard_map/ppermute | solution.py:201
  15.3 1.8 %collective-permute-done.2.left_ref.refs_1_.refs_3_ = bf16[80,128]{1,0:T(8,128)(2,1)S(1)} collective-permute-done((bf16[80,128]{1,0:T(8,128)(2,1)S(1)}, bf16[80,128]{1,0:T(8,128)(2,1)S(1)}, u32[]{:S(2)}, u32[]{:S(2)}) %collective-permute-start.2) | collective-permute-done | bytes 20512 | tf_op jit(solution)/shard_map/ppermute | solution.py:202
  17.0 1.3 %collective-permute-done.8.refs_0_ = bf16[2080,128]{1,0:T(8,128)(2,1)S(1)} collective-permute-done((bf16[2080,128]{1,0:T(8,128)(2,1)S(1)}, bf16[2080,128]{1,0:T(8,128)(2,1)S(1)}, u32[]{:S(2)}, u32[]{:S(2)}) %collective-permute-start.8) | collective-permute-done | bytes 532512 | tf_op jit(solution)/shard_map/ppermute | solution.py:672
  18.8 1.6 %conv_forward.1 = (bf16[8,80,128]{2,1,0:T(8,128)(2,1)S(1)}, bf16[8,80,128]{2,1,0:T(8,128)(2,1)S(1)}, bf16[8,80,128]{2,1,0:T(8,128)(2,1)S(1)}, bf16[8,80,128]{2,1,0:T(8,128)(2,1)S(1)}) custom-call(bf16[32,80,128]{2,1,0:T(8,128)(2,1)S(1)} %get-tuple-element.56.block_ref.refs_1_, bf16[4,80,128]{2,1,0:T(8,128)(2,1)S(1)} %get-tuple-element.61.halo_ref.refs_2_, ...), custom_call_target="tpu_custom_call" | custom-call | bytes 1474560 | tf_op jit(solution)/shard_map/conv_forward/pallas_call | solution.py:34
  20.5 1.8 %collective-permute-start.5 = (bf16[8,80,128]{2,1,0:T(8,128)(2,1)S(1)}, bf16[8,80,128]{2,1,0:T(8,128)(2,1)S(1)}, u32[]{:S(2)}, u32[]{:S(2)}) collective-permute-start(bf16[8,80,128]{2,1,0:T(8,128)(2,1)S(1)} %get-tuple-element.66), channel_id=1, source_target_pairs={{0,2},{1,3},{2,0},{3,1},{4,6},{5,7},{6,4},{7,5},{8,10},{9,11},{10,... | collective-permute-start | bytes 491528 | tf_op jit(solution)/shard_map/ppermute | solution.py:630
  22.4 1.1 %activation_gradient.1 = (f32[640,1024]{1,0:T(8,128)S(1)}, bf16[384,1024]{1,0:T(8,128)(2,1)S(1)}, bf16[640,640]{1,0:T(8,128)(2,1)S(1)}, bf16[384,640]{1,0:T(8,128)(2,1)S(1)}) custom-call(bf16[1440,128]{1,0:T(8,128)(2,1)S(1)} %get-tuple-element.68.refs_0_, bf16[1440,128]{1,0:T(8,128)(2,1)S(1)} %collective-permute-done.7.refs_1_, ...), custom_call_target="tpu_custom_call" | custom-call | bytes 6520832 | tf_op jit(solution)/shard_map/activation_gradient/pallas_call | solution.py:34
  23.5 4.1 %collective-permute-done.5.refs_2_ = bf16[8,80,128]{2,1,0:T(8,128)(2,1)S(1)} collective-permute-done((bf16[8,80,128]{2,1,0:T(8,128)(2,1)S(1)}, bf16[8,80,128]{2,1,0:T(8,128)(2,1)S(1)}, u32[]{:S(2)}, u32[]{:S(2)}) %collective-permute-start.5) | collective-permute-done | bytes 163872 | tf_op jit(solution)/shard_map/ppermute | solution.py:630
  27.6 2.6 %collective-permute-done.6.refs_3_ = bf16[8,80,128]{2,1,0:T(8,128)(2,1)S(1)} collective-permute-done((bf16[8,80,128]{2,1,0:T(8,128)(2,1)S(1)}, bf16[8,80,128]{2,1,0:T(8,128)(2,1)S(1)}, u32[]{:S(2)}, u32[]{:S(2)}) %collective-permute-start.6) | collective-permute-done | bytes 163872 | tf_op jit(solution)/shard_map/ppermute | solution.py:630
  30.2 3.6 %hidden_gradient.1 = (bf16[640,1024]{1,0:T(8,128)(2,1)S(1)}, f32[2,800,128]{2,1,0:T(8,128)S(1)}, bf16[2,800,128]{2,1,0:T(8,128)(2,1)S(1)}) custom-call(bf16[8,80,128]{2,1,0:T(8,128)(2,1)S(1)} %get-tuple-element.64.refs_0_, bf16[8,80,128]{2,1,0:T(8,128)(2,1)S(1)} %collective-permute-done.4.refs_1_, bf16[8,80,128]{2,1,0:T(8,128)(2,1)S(1)} %collective-permute-done.5.refs_2_, ...), custom_call_target="tpu_custom_call" | custom-call | bytes 7421952 | tf_op jit(solution)/shard_map/hidden_gradient/pallas_call | solution.py:34
  34.1 0.9 %conv_gradient.1 = (bf16[8,80,128]{2,1,0:T(8,128)(2,1)S(1)}, bf16[8,80,128]{2,1,0:T(8,128)(2,1)S(1)}, bf16[8,80,128]{2,1,0:T(8,128)(2,1)S(1)}, bf16[8,80,128]{2,1,0:T(8,128)(2,1)S(1)}) custom-call(bf16[640,1024]{1,0:T(8,128)(2,1)S(1)} %get-tuple-element.74.pre_ref, bf16[384,640]{1,0:T(8,128)(2,1)S(1)} %get-tuple-element.75.t_ref), custom_call_target="tpu_custom_call" | custom-call | bytes 2457600 | tf_op jit(solution)/shard_map/conv_gradient/pallas_call | solution.py:34
  35.3 1.2 %collective-permute-done.10.refs_2_.refs_1_ = bf16[8,80,128]{2,1,0:T(8,128)(2,1)S(1)} collective-permute-done((bf16[8,80,128]{2,1,0:T(8,128)(2,1)S(1)}, bf16[8,80,128]{2,1,0:T(8,128)(2,1)S(1)}, u32[]{:S(2)}, u32[]{:S(2)}) %collective-permute-start.10) | collective-permute-done | bytes 163872 | tf_op jit(solution)/shard_map/ppermute | solution.py:630
  36.6 1.9 %collective-permute-start.14 = (bf16[2,224,128]{2,1,0:T(8,128)(2,1)S(1)}, bf16[2,224,128]{2,1,0:T(8,128)(2,1)S(1)}, u32[]{:S(2)}, u32[]{:S(2)}) collective-permute-start(bf16[2,224,128]{2,1,0:T(8,128)(2,1)S(1)} %get-tuple-element.83), channel_id=1, source_target_pairs={{0,8},{4,12},{8,0},{12,4},{16,24},{20,28},{24,16},{28,20},{1,9},{5... | collective-permute-start | bytes 344072 | tf_op jit(solution)/shard_map/ppermute | solution.py:739
  38.5 3.6 %collective-permute-start.15 = (bf16[2,224,128]{2,1,0:T(8,128)(2,1)S(1)}, bf16[2,224,128]{2,1,0:T(8,128)(2,1)S(1)}, u32[]{:S(2)}, u32[]{:S(2)}) collective-permute-start(bf16[2,224,128]{2,1,0:T(8,128)(2,1)S(1)} %get-tuple-element.84), channel_id=1, source_target_pairs={{0,4},{4,0},{8,12},{12,8},{16,20},{20,16},{24,28},{28,24},{1,5},{5... | collective-permute-start | bytes 344072 | tf_op jit(solution)/shard_map/ppermute | solution.py:739
  43.6 3.4 %collective-permute-done.15.b_ref = bf16[2,224,128]{2,1,0:T(8,128)(2,1)S(1)} collective-permute-done((bf16[2,224,128]{2,1,0:T(8,128)(2,1)S(1)}, bf16[2,224,128]{2,1,0:T(8,128)(2,1)S(1)}, u32[]{:S(2)}, u32[]{:S(2)}) %collective-permute-start.15) | collective-permute-done | bytes 114720 | tf_op jit(solution)/shard_map/ppermute | solution.py:739
  47.0 1.3 %collective-permute-done.16.c_ref = bf16[2,224,128]{2,1,0:T(8,128)(2,1)S(1)} collective-permute-done((bf16[2,224,128]{2,1,0:T(8,128)(2,1)S(1)}, bf16[2,224,128]{2,1,0:T(8,128)(2,1)S(1)}, u32[]{:S(2)}, u32[]{:S(2)}) %collective-permute-start.16) | collective-permute-done | bytes 114720 | tf_op jit(solution)/shard_map/ppermute | solution.py:739
  49.7 0.9 %collective-permute-done.12.refs_3_ = bf16[8,80,128]{2,1,0:T(8,128)(2,1)S(1)} collective-permute-done((bf16[8,80,128]{2,1,0:T(8,128)(2,1)S(1)}, bf16[8,80,128]{2,1,0:T(8,128)(2,1)S(1)}, u32[]{:S(2)}, u32[]{:S(2)}) %collective-permute-start.12) | collective-permute-done | bytes 163872 | tf_op jit(solution)/shard_map/ppermute | solution.py:630
  51.0 1.7 %collective-permute-start.18 = (bf16[2,80,128]{2,1,0:T(8,128)(2,1)S(1)}, bf16[2,80,128]{2,1,0:T(8,128)(2,1)S(1)}, u32[]{:S(2)}, u32[]{:S(2)}) collective-permute-start(bf16[2,80,128]{2,1,0:T(8,128)(2,1)S(1)} %get-tuple-element.89), channel_id=1, source_target_pairs={{0,4},{4,0},{1,5},{5,1},{2,6},{6,2},{3,7},{7,3},{8,12},{12,8},{9,1... | collective-permute-start | bytes 122888 | tf_op jit(solution)/shard_map/ppermute | solution.py:186
  53.4 2.8 %collective-permute-start.22 = (bf16[224,128]{1,0:T(8,128)(2,1)S(1)}, bf16[224,128]{1,0:T(8,128)(2,1)S(1)}, u32[]{:S(2)}, u32[]{:S(2)}) collective-permute-start(bf16[224,128]{1,0:T(8,128)(2,1)S(1)} %add_across.1.refs_5_.mine_ref), channel_id=1, source_target_pairs={{0,16},{8,24},{16,0},{24,8},{1,17},{9,25},{17,1},{25,9},{2,18},{10... | collective-permute-start | bytes 172040 | tf_op jit(solution)/shard_map/ppermute | solution.py:793
  56.2 1.7 %kernel_gradient.1.refs_0_.kernel_ref = bf16[80,128]{1,0:T(8,128)(2,1)S(1)} custom-call(bf16[32,80,128]{2,1,0:T(8,128)(2,1)S(1)} %get-tuple-element.87.refs_0_.block_ref, bf16[32,80,128]{2,1,0:T(8,128)(2,1)S(1)} %get-tuple-element.56.block_ref.refs_1_, bf16[4,80,128]{2,1,0:T(8,128)(2,1)S(1)} %get-tuple-element.61.halo_ref.refs_2_, ...), custom_call_target="tpu_custom_call" | custom-call | bytes 1511424 | tf_op jit(solution)/shard_map/kernel_gradient/pallas_call | solution.py:34
  58.0 1.7 %collective-permute-start.20 = (bf16[80,128]{1,0:T(8,128)(2,1)S(1)}, bf16[80,128]{1,0:T(8,128)(2,1)S(1)}, u32[]{:S(2)}, u32[]{:S(2)}) collective-permute-start(bf16[80,128]{1,0:T(8,128)(2,1)S(1)} %get-tuple-element.94), channel_id=1, source_target_pairs={{0,8},{8,16},{16,24},{24,0},{1,9},{9,17},{17,25},{25,1},{2,10},{10... | collective-permute-start | bytes 61448 | tf_op jit(solution)/shard_map/ppermute | solution.py:202
  59.8 2.2 %collective-permute-start.21 = (bf16[80,128]{1,0:T(8,128)(2,1)S(1)}, bf16[80,128]{1,0:T(8,128)(2,1)S(1)}, u32[]{:S(2)}, u32[]{:S(2)}) collective-permute-start(bf16[80,128]{1,0:T(8,128)(2,1)S(1)} %get-tuple-element.95), channel_id=1, source_target_pairs={{0,24},{8,0},{16,8},{24,16},{1,25},{9,1},{17,9},{25,17},{2,26},{10... | collective-permute-start | bytes 61448 | tf_op jit(solution)/shard_map/ppermute | solution.py:201
  61.9 1.9 %collective-permute-done.20.left_ref = bf16[80,128]{1,0:T(8,128)(2,1)S(1)} collective-permute-done((bf16[80,128]{1,0:T(8,128)(2,1)S(1)}, bf16[80,128]{1,0:T(8,128)(2,1)S(1)}, u32[]{:S(2)}, u32[]{:S(2)}) %collective-permute-start.20) | collective-permute-done | bytes 20512 | tf_op jit(solution)/shard_map/ppermute | solution.py:202
  64.3 3.3 %collective-permute-start.25 = (bf16[304,128]{1,0:T(8,128)(2,1)S(1)}, bf16[304,128]{1,0:T(8,128)(2,1)S(1)}, u32[]{:S(2)}, u32[]{:S(2)}) collective-permute-start(bf16[304,128]{1,0:T(8,128)(2,1)S(1)} %finish_pieces.1.p0), channel_id=1, source_target_pairs={{0,12},{4,8},{8,4},{12,0},{16,28},{20,24},{24,20},{28,16},{1,13},{... | collective-permute-start | bytes 233480 | tf_op jit(solution)/shard_map/ppermute | solution.py:739
  67.6 0.9 %collective-permute-start.23 = (bf16[304,128]{1,0:T(8,128)(2,1)S(1)}, bf16[304,128]{1,0:T(8,128)(2,1)S(1)}, u32[]{:S(2)}, u32[]{:S(2)}) collective-permute-start(bf16[304,128]{1,0:T(8,128)(2,1)S(1)} %finish_pieces.1.p0), channel_id=1, source_target_pairs={{0,8},{4,12},{8,0},{12,4},{16,24},{20,28},{24,16},{28,20},{1,9},{5... | collective-permute-start | bytes 233480 | tf_op jit(solution)/shard_map/ppermute | solution.py:739
  68.4 3.0 %conv_adjoint.1 = bf16[75,32,128]{2,1,0:T(8,128)(2,1)} custom-call(bf16[32,80,128]{2,1,0:T(8,128)(2,1)S(1)} %get-tuple-element.87.refs_0_.block_ref, bf16[4,80,128]{2,1,0:T(8,128)(2,1)S(1)} %get-tuple-element.93.halo_ref, bf16[80,128]{1,0:T(8,128)(2,1)S(1)} %collective-permute-done.20.left_ref, bf16[80,128]{1,0:T(8,128)(2,1)S(1)} %collective-permute-done.21.right_ref, ...), custom_call_target="tpu_custom_call" | custom-call | bytes 2105344 | tf_op jit(solution)/shard_map/conv_adjoint/pallas_call | solution.py:34
  72.4 1.3 %write_parameters.1 = (f32[150,300]{1,0:T(8,128)}, f32[150,300]{1,0:T(8,128)}, f32[1,150]{1,0:T(1,128)}, f32[3,3,75]{2,1,0:T(4,128)}) custom-call(bf16[304,128]{1,0:T(8,128)(2,1)S(1)} %finish_pieces.1.p0, bf16[304,128]{1,0:T(8,128)(2,1)S(1)} %collective-permute-done.23.p1, bf16[304,128]{1,0:T(8,128)(2,1)S(1)} %collective-permute-done.24.p2, ...), custom_call_target="tpu_custom_call" | custom-call | bytes 674596 | tf_op jit(solution)/shard_map/write_parameters/pallas_call | solution.py:34
  (37 shorter events, 7.9 us)
Async XLA Ops:
  3.2 15.1 %collective-permute-start.8 = (bf16[2080,128]{1,0:T(8,128)(2,1)S(1)}, bf16[2080,128]{1,0:T(8,128)(2,1)S(1)}, u32[]{:S(2)}, u32[]{:S(2)}) collective-permute-start(bf16[2080,128]{1,0:T(8,128)(2,1)S(1)} %get-tuple-element.70), channel_id=1, source_target_pairs={{0,2},{1,3},{2,0},{3,1},{4,6},{5,7},{6,4},{7,5},{8,10},{9,11},{10,... | collective-permute-start | bytes 1597448 | tf_op jit(solution)/shard_map/ppermute | solution.py:672
  7.2 4.1 %collective-permute-start = (bf16[2,80,128]{2,1,0:T(8,128)(2,1)S(1)}, bf16[2,80,128]{2,1,0:T(8,128)(2,1)S(1)}, u32[]{:S(2)}, u32[]{:S(2)}) collective-permute-start(bf16[2,80,128]{2,1,0:T(8,128)(2,1)S(1)} %get-tuple-element.57), channel_id=1, source_target_pairs={{0,4},{4,0},{1,5},{5,1},{2,6},{6,2},{3,7},{7,3},{8,12},{12,8},{9,1... | collective-permute-start | bytes 122888 | tf_op jit(solution)/shard_map/ppermute | solution.py:186
  8.8 2.5 %collective-permute-start.1 = (bf16[2,80,128]{2,1,0:T(8,128)(2,1)S(1)}, bf16[2,80,128]{2,1,0:T(8,128)(2,1)S(1)}, u32[]{:S(2)}, u32[]{:S(2)}) collective-permute-start(bf16[2,80,128]{2,1,0:T(8,128)(2,1)S(1)} %get-tuple-element.58), channel_id=1, source_target_pairs={{4,28},{12,20},{20,12},{28,4},{5,29},{13,21},{21,13},{29,5},{6,30}... | collective-permute-start | bytes 122888 | tf_op jit(solution)/shard_map/ppermute | solution.py:193
  11.4 5.6 %collective-permute-start.2 = (bf16[80,128]{1,0:T(8,128)(2,1)S(1)}, bf16[80,128]{1,0:T(8,128)(2,1)S(1)}, u32[]{:S(2)}, u32[]{:S(2)}) collective-permute-start(bf16[80,128]{1,0:T(8,128)(2,1)S(1)} %get-tuple-element.62), channel_id=1, source_target_pairs={{0,8},{8,16},{16,24},{24,0},{1,9},{9,17},{17,25},{25,1},{2,10},{10... | collective-permute-start | bytes 61448 | tf_op jit(solution)/shard_map/ppermute | solution.py:202
  13.0 4.0 %collective-permute-start.3 = (bf16[80,128]{1,0:T(8,128)(2,1)S(1)}, bf16[80,128]{1,0:T(8,128)(2,1)S(1)}, u32[]{:S(2)}, u32[]{:S(2)}) collective-permute-start(bf16[80,128]{1,0:T(8,128)(2,1)S(1)} %get-tuple-element.63), channel_id=1, source_target_pairs={{0,24},{8,0},{16,8},{24,16},{1,25},{9,1},{17,9},{25,17},{2,26},{10... | collective-permute-start | bytes 61448 | tf_op jit(solution)/shard_map/ppermute | solution.py:201
  18.3 4.1 %collective-permute-start.9 = (bf16[2080,128]{1,0:T(8,128)(2,1)S(1)}, bf16[2080,128]{1,0:T(8,128)(2,1)S(1)}, u32[]{:S(2)}, u32[]{:S(2)}) collective-permute-start(bf16[2080,128]{1,0:T(8,128)(2,1)S(1)} %cotan_relay.1.refs_2_), channel_id=1, source_target_pairs={{0,1},{1,0},{2,3},{3,2},{4,5},{5,4},{6,7},{7,6},{8,9},{9,8},{10,11... | collective-permute-start | bytes 1597448 | tf_op jit(solution)/shard_map/ppermute | solution.py:684
  18.3 4.1 %collective-permute-start.7 = (bf16[1440,128]{1,0:T(8,128)(2,1)S(1)}, bf16[1440,128]{1,0:T(8,128)(2,1)S(1)}, u32[]{:S(2)}, u32[]{:S(2)}) collective-permute-start(bf16[1440,128]{1,0:T(8,128)(2,1)S(1)} %get-tuple-element.69), channel_id=1, source_target_pairs={{0,1},{1,0},{2,3},{3,2},{4,5},{5,4},{6,7},{7,6},{8,9},{9,8},{10,11... | collective-permute-start | bytes 1105928 | tf_op jit(solution)/shard_map/ppermute | solution.py:693
  20.5 3.0 %collective-permute-start.4 = (bf16[8,80,128]{2,1,0:T(8,128)(2,1)S(1)}, bf16[8,80,128]{2,1,0:T(8,128)(2,1)S(1)}, u32[]{:S(2)}, u32[]{:S(2)}) collective-permute-start(bf16[8,80,128]{2,1,0:T(8,128)(2,1)S(1)} %get-tuple-element.65), channel_id=1, source_target_pairs={{0,1},{1,0},{2,3},{3,2},{4,5},{5,4},{6,7},{7,6},{8,9},{9,8},{10,11... | collective-permute-start | bytes 491528 | tf_op jit(solution)/shard_map/ppermute | solution.py:630
  20.5 7.1 %collective-permute-start.5 = (bf16[8,80,128]{2,1,0:T(8,128)(2,1)S(1)}, bf16[8,80,128]{2,1,0:T(8,128)(2,1)S(1)}, u32[]{:S(2)}, u32[]{:S(2)}) collective-permute-start(bf16[8,80,128]{2,1,0:T(8,128)(2,1)S(1)} %get-tuple-element.66), channel_id=1, source_target_pairs={{0,2},{1,3},{2,0},{3,1},{4,6},{5,7},{6,4},{7,5},{8,10},{9,11},{10,... | collective-permute-start | bytes 491528 | tf_op jit(solution)/shard_map/ppermute | solution.py:630
  22.3 7.9 %collective-permute-start.6 = (bf16[8,80,128]{2,1,0:T(8,128)(2,1)S(1)}, bf16[8,80,128]{2,1,0:T(8,128)(2,1)S(1)}, u32[]{:S(2)}, u32[]{:S(2)}) collective-permute-start(bf16[8,80,128]{2,1,0:T(8,128)(2,1)S(1)} %get-tuple-element.67), channel_id=1, source_target_pairs={{0,3},{1,2},{2,1},{3,0},{4,7},{5,6},{6,5},{7,4},{8,11},{9,10},{10,... | collective-permute-start | bytes 491528 | tf_op jit(solution)/shard_map/ppermute | solution.py:630
  33.8 2.7 %collective-permute-start.13 = (bf16[2,800,128]{2,1,0:T(8,128)(2,1)S(1)}, bf16[2,800,128]{2,1,0:T(8,128)(2,1)S(1)}, u32[]{:S(2)}, u32[]{:S(2)}) collective-permute-start(bf16[2,800,128]{2,1,0:T(8,128)(2,1)S(1)} %get-tuple-element.81), channel_id=1, source_target_pairs={{0,1},{1,0},{2,3},{3,2},{4,5},{5,4},{6,7},{7,6},{8,9},{9,8},{10,11... | collective-permute-start | bytes 1228808 | tf_op jit(solution)/shard_map/ppermute | solution.py:708
  35.0 1.5 %collective-permute-start.10 = (bf16[8,80,128]{2,1,0:T(8,128)(2,1)S(1)}, bf16[8,80,128]{2,1,0:T(8,128)(2,1)S(1)}, u32[]{:S(2)}, u32[]{:S(2)}) collective-permute-start(bf16[8,80,128]{2,1,0:T(8,128)(2,1)S(1)} %get-tuple-element.77), channel_id=1, source_target_pairs={{0,1},{1,0},{2,3},{3,2},{4,5},{5,4},{6,7},{7,6},{8,9},{9,8},{10,11... | collective-permute-start | bytes 491528 | tf_op jit(solution)/shard_map/ppermute | solution.py:630
  36.6 7.0 %collective-permute-start.14 = (bf16[2,224,128]{2,1,0:T(8,128)(2,1)S(1)}, bf16[2,224,128]{2,1,0:T(8,128)(2,1)S(1)}, u32[]{:S(2)}, u32[]{:S(2)}) collective-permute-start(bf16[2,224,128]{2,1,0:T(8,128)(2,1)S(1)} %get-tuple-element.83), channel_id=1, source_target_pairs={{0,8},{4,12},{8,0},{12,4},{16,24},{20,28},{24,16},{28,20},{1,9},{5... | collective-permute-start | bytes 344072 | tf_op jit(solution)/shard_map/ppermute | solution.py:739
  38.5 8.6 %collective-permute-start.15 = (bf16[2,224,128]{2,1,0:T(8,128)(2,1)S(1)}, bf16[2,224,128]{2,1,0:T(8,128)(2,1)S(1)}, u32[]{:S(2)}, u32[]{:S(2)}) collective-permute-start(bf16[2,224,128]{2,1,0:T(8,128)(2,1)S(1)} %get-tuple-element.84), channel_id=1, source_target_pairs={{0,4},{4,0},{8,12},{12,8},{16,20},{20,16},{24,28},{28,24},{1,5},{5... | collective-permute-start | bytes 344072 | tf_op jit(solution)/shard_map/ppermute | solution.py:739
  42.1 6.2 %collective-permute-start.16 = (bf16[2,224,128]{2,1,0:T(8,128)(2,1)S(1)}, bf16[2,224,128]{2,1,0:T(8,128)(2,1)S(1)}, u32[]{:S(2)}, u32[]{:S(2)}) collective-permute-start(bf16[2,224,128]{2,1,0:T(8,128)(2,1)S(1)} %get-tuple-element.85), channel_id=1, source_target_pairs={{0,12},{4,8},{8,4},{12,0},{16,28},{20,24},{24,20},{28,16},{1,13},{... | collective-permute-start | bytes 344072 | tf_op jit(solution)/shard_map/ppermute | solution.py:739
  42.6 7.1 %collective-permute-start.11 = (bf16[8,80,128]{2,1,0:T(8,128)(2,1)S(1)}, bf16[8,80,128]{2,1,0:T(8,128)(2,1)S(1)}, u32[]{:S(2)}, u32[]{:S(2)}) collective-permute-start(bf16[8,80,128]{2,1,0:T(8,128)(2,1)S(1)} %get-tuple-element.78), channel_id=1, source_target_pairs={{0,2},{1,3},{2,0},{3,1},{4,6},{5,7},{6,4},{7,5},{8,10},{9,11},{10,... | collective-permute-start | bytes 491528 | tf_op jit(solution)/shard_map/ppermute | solution.py:630
  43.0 7.5 %collective-permute-start.12 = (bf16[8,80,128]{2,1,0:T(8,128)(2,1)S(1)}, bf16[8,80,128]{2,1,0:T(8,128)(2,1)S(1)}, u32[]{:S(2)}, u32[]{:S(2)}) collective-permute-start(bf16[8,80,128]{2,1,0:T(8,128)(2,1)S(1)} %get-tuple-element.79), channel_id=1, source_target_pairs={{0,3},{1,2},{2,1},{3,0},{4,7},{5,6},{6,5},{7,4},{8,11},{9,10},{10,... | collective-permute-start | bytes 491528 | tf_op jit(solution)/shard_map/ppermute | solution.py:630
  48.4 5.0 %collective-permute-start.17 = (bf16[224,128]{1,0:T(8,128)(2,1)S(1)}, bf16[224,128]{1,0:T(8,128)(2,1)S(1)}, u32[]{:S(2)}, u32[]{:S(2)}) collective-permute-start(bf16[224,128]{1,0:T(8,128)(2,1)S(1)} %get-tuple-element.86.refs_4_), channel_id=1, source_target_pairs={{0,2},{1,3},{2,0},{3,1},{4,6},{5,7},{6,4},{7,5},{8,10},{9,11},{10,... | collective-permute-start | bytes 172040 | tf_op jit(solution)/shard_map/ppermute | solution.py:760
  51.0 6.9 %collective-permute-start.18 = (bf16[2,80,128]{2,1,0:T(8,128)(2,1)S(1)}, bf16[2,80,128]{2,1,0:T(8,128)(2,1)S(1)}, u32[]{:S(2)}, u32[]{:S(2)}) collective-permute-start(bf16[2,80,128]{2,1,0:T(8,128)(2,1)S(1)} %get-tuple-element.89), channel_id=1, source_target_pairs={{0,4},{4,0},{1,5},{5,1},{2,6},{6,2},{3,7},{7,3},{8,12},{12,8},{9,1... | collective-permute-start | bytes 122888 | tf_op jit(solution)/shard_map/ppermute | solution.py:186
  52.7 5.2 %collective-permute-start.19 = (bf16[2,80,128]{2,1,0:T(8,128)(2,1)S(1)}, bf16[2,80,128]{2,1,0:T(8,128)(2,1)S(1)}, u32[]{:S(2)}, u32[]{:S(2)}) collective-permute-start(bf16[2,80,128]{2,1,0:T(8,128)(2,1)S(1)} %get-tuple-element.90), channel_id=1, source_target_pairs={{4,28},{12,20},{20,12},{28,4},{5,29},{13,21},{21,13},{29,5},{6,30}... | collective-permute-start | bytes 122888 | tf_op jit(solution)/shard_map/ppermute | solution.py:193
  53.4 10.8 %collective-permute-start.22 = (bf16[224,128]{1,0:T(8,128)(2,1)S(1)}, bf16[224,128]{1,0:T(8,128)(2,1)S(1)}, u32[]{:S(2)}, u32[]{:S(2)}) collective-permute-start(bf16[224,128]{1,0:T(8,128)(2,1)S(1)} %add_across.1.refs_5_.mine_ref), channel_id=1, source_target_pairs={{0,16},{8,24},{16,0},{24,8},{1,17},{9,25},{17,1},{25,9},{2,18},{10... | collective-permute-start | bytes 172040 | tf_op jit(solution)/shard_map/ppermute | solution.py:793
  58.0 5.7 %collective-permute-start.20 = (bf16[80,128]{1,0:T(8,128)(2,1)S(1)}, bf16[80,128]{1,0:T(8,128)(2,1)S(1)}, u32[]{:S(2)}, u32[]{:S(2)}) collective-permute-start(bf16[80,128]{1,0:T(8,128)(2,1)S(1)} %get-tuple-element.94), channel_id=1, source_target_pairs={{0,8},{8,16},{16,24},{24,0},{1,9},{9,17},{17,25},{25,1},{2,10},{10... | collective-permute-start | bytes 61448 | tf_op jit(solution)/shard_map/ppermute | solution.py:202
  59.8 4.4 %collective-permute-start.21 = (bf16[80,128]{1,0:T(8,128)(2,1)S(1)}, bf16[80,128]{1,0:T(8,128)(2,1)S(1)}, u32[]{:S(2)}, u32[]{:S(2)}) collective-permute-start(bf16[80,128]{1,0:T(8,128)(2,1)S(1)} %get-tuple-element.95), channel_id=1, source_target_pairs={{0,24},{8,0},{16,8},{24,16},{1,25},{9,1},{17,9},{25,17},{2,26},{10... | collective-permute-start | bytes 61448 | tf_op jit(solution)/shard_map/ppermute | solution.py:201
  64.3 7.1 %collective-permute-start.25 = (bf16[304,128]{1,0:T(8,128)(2,1)S(1)}, bf16[304,128]{1,0:T(8,128)(2,1)S(1)}, u32[]{:S(2)}, u32[]{:S(2)}) collective-permute-start(bf16[304,128]{1,0:T(8,128)(2,1)S(1)} %finish_pieces.1.p0), channel_id=1, source_target_pairs={{0,12},{4,8},{8,4},{12,0},{16,28},{20,24},{24,20},{28,16},{1,13},{... | collective-permute-start | bytes 233480 | tf_op jit(solution)/shard_map/ppermute | solution.py:739
  67.6 4.4 %collective-permute-start.24 = (bf16[304,128]{1,0:T(8,128)(2,1)S(1)}, bf16[304,128]{1,0:T(8,128)(2,1)S(1)}, u32[]{:S(2)}, u32[]{:S(2)}) collective-permute-start(bf16[304,128]{1,0:T(8,128)(2,1)S(1)} %finish_pieces.1.p0), channel_id=1, source_target_pairs={{0,4},{4,0},{8,12},{12,8},{16,20},{20,16},{24,28},{28,24},{1,5},{5... | collective-permute-start | bytes 233480 | tf_op jit(solution)/shard_map/ppermute | solution.py:739
  67.6 4.8 %collective-permute-start.23 = (bf16[304,128]{1,0:T(8,128)(2,1)S(1)}, bf16[304,128]{1,0:T(8,128)(2,1)S(1)}, u32[]{:S(2)}, u32[]{:S(2)}) collective-permute-start(bf16[304,128]{1,0:T(8,128)(2,1)S(1)} %finish_pieces.1.p0), channel_id=1, source_target_pairs={{0,8},{4,12},{8,0},{12,4},{16,24},{20,28},{24,16},{28,20},{1,9},{5... | collective-permute-start | bytes 233480 | tf_op jit(solution)/shard_map/ppermute | solution.py:739

commit v3 on v2

--- a/solution.py
+++ b/solution.py
@@ -10,6 +10,7 @@
 
 DIL = 2
 LANES = 128
+TAP_ROWS = 16
 RIDE = 96
 BF = jnp.bfloat16
 F32 = jnp.float32
@@ -82,18 +83,7 @@
     return jnp.dot(value, flip, preferred_element_type=F32).astype(BF)
 
 
-def emit_strips(read, rows, pad, swap, strips):
-    if swap:
-        strip_ref, fold_ref, left_ref, right_ref = strips
-        at_bottom = lax.axis_index("lat") == 0
-        for t in range(DIL):
-            low, high = read(t), read(rows - DIL + t)
-            strip_ref[t] = jnp.where(at_bottom, high.astype(F32), low.astype(F32)).astype(BF)
-    else:
-        down_ref, up_ref, fold_ref, left_ref, right_ref = strips
-        for t in range(DIL):
-            down_ref[t] = read(t)
-            up_ref[t] = read(rows - DIL + t)
+def emit_strips(read, rows, pad, fold_ref, left_ref, right_ref):
     for t in range(DIL):
         fold_ref[t] = mirrored(read(rows - 1 - t))
     left = jnp.zeros((pad, LANES), F32)
@@ -104,43 +94,36 @@
     right_ref[...] = right.astype(BF)
 
 
-def strip_shapes(pad, swap):
-    one = shape((DIL, pad, LANES), BF)
-    packs = [shape((pad, LANES), BF)] * 2
-    return ([one] if swap else [one, one]) + [one] + packs
-
-
-def prepare_state(swap, state_ref, mask_ref, rows_ref, *rest):
-    strips, scr = rest[:-1], rest[-1]
+def strip_shapes(pad):
+    return [shape((DIL, pad, LANES), BF)] + [shape((pad, LANES), BF)] * 2
+
+
+def outer_shapes(pad, swap):
+    return [shape((DIL, pad, LANES), BF)] * (1 if swap else 2)
+
+
+def emit_outer(low, high, t, swap, outer):
+    if swap:
+        outer[0][t] = jnp.where(lax.axis_index("lat") == 0, high, low).astype(BF)
+    else:
+        outer[0][t] = low.astype(BF)
+        outer[1][t] = high.astype(BF)
+
+
+def prepare_state(state_ref, mask_ref, rows_ref, fold_ref, left_ref, right_ref, scr):
     rows, pad = rows_ref.shape[:2]
     to_rows(state_ref, mask_ref[...].astype(F32), scr, pad)
     for r in range(rows):
         rows_ref[r] = scr[r * pad : (r + 1) * pad, :].astype(BF)
-    emit_strips(lambda r: rows_ref[r], rows, pad, swap, strips)
-
-
-def prepare_cotan(part, *refs):
-    rows_ref, own_ref, core_ref, far_ref, taps_ref, mask_ref, state_ref = refs[9:16]
-    scr, weights_scr, turn_scr, sems = refs[16:20]
-    grad_ref, offset_ref, value_ref = refs[20:23]
-    held = (grad_ref, mask_ref, offset_ref, value_ref, *refs[23:27], state_ref)
-    copies = [pltpu.make_async_copy(refs[k], held[k], sems.at[k]) for k in range(9)]
-    for k in (4, 5, 6, 7, 0, 1, 2, 3, 8):
-        copies[k].start()
-    for k in range(4, 8):
-        copies[k].wait()
-    pack_weights(part, rows_ref.shape[1], *held[4:8], weights_scr, taps_ref, turn_scr)
-    for k in range(0, 4):
-        copies[k].wait()
-    rows, pad, cols = rows_ref.shape
-    me = lax.axis_index("ch")
-    mask = mask_ref[...].astype(F32)
-    to_rows(grad_ref, None, scr, pad)
+    emit_strips(lambda r: rows_ref[r], rows, pad, fold_ref, left_ref, right_ref)
+
+
+def add_swath(scr, stride, rows, start, offset_ref, value_ref, cols):
     offset = offset_ref[...]
     points = offset.shape[1]
     value = value_ref[...]
     total = jnp.zeros((rows, cols), F32)
-    row_hot = iota((rows, points), 0) == offset // cols
+    row_hot = iota((rows, points), 0) + start == offset // cols
     col_hot = (iota((cols, points), 0) == offset % cols).astype(BF)
     for _ in range(3):
         part = value.astype(BF)
@@ -149,22 +132,85 @@
         total = total + lax.dot_general(
             lhs, col_hot, (((1,), (1,)), ((), ())), preferred_element_type=F32
         )
-    total = jnp.where(me == 0, total, 0.0)
-    first = scr[pl.ds(0, rows, stride=pad), :]
-    scr[pl.ds(0, rows, stride=pad), :] = first + total
+    total = jnp.where(lax.axis_index("ch") == 0, total, 0.0)
+    first = scr[pl.ds(0, rows, stride=stride), :]
+    scr[pl.ds(0, rows, stride=stride), :] = first + total
+
+
+def prepare_far(part, swap, count, *refs):
+    outs, (scr, row_scr, weights_scr, turn_scr, sems) = refs[count:-5], refs[-5:]
+    far_ref, tiles_ref, taps_ref, *outer = outs[: -count]
+    held = outs[-count:]
+    copies = [pltpu.make_async_copy(refs[k], held[k], sems.at[k]) for k in range(count)]
+    for k in (4, 5, 6, 7, 0, 1, 2, 3, 8):
+        copies[k].start()
+    for k in range(4, 8):
+        copies[k].wait()
+    grad_ref, mask_ref, offset_ref, value_ref = held[0:4]
+    channels, rows, cols = grad_ref.shape
+    pad = taps_ref.shape[0]
+    pack_weights(part, pad, *held[4:8], weights_scr, taps_ref, turn_scr)
+    hid = weights_scr.shape[0]
+    full = tiles_ref.shape[0]
+    for t in range(full // hid):
+        tiles_ref[t * hid : (t + 1) * hid, :] = weights_scr[:, t * LANES : (t + 1) * LANES]
+    far_ref[0:full, :] = tiles_ref[...]
+    for k in range(0, 4):
+        copies[k].wait()
+    half = rows // 2
+    me = lax.axis_index("ch")
+    start = aligned((1 - me // 2) * half)
+
+    def body(c, carry):
+        scr[pl.ds(c, half, stride=pad), :] = grad_ref[c, pl.ds(start, half), :].astype(F32)
+        return carry
+
+    lax.fori_loop(0, channels, body, 0, unroll=5 if channels % 5 == 0 else 1)
+    for c in range(channels, pad):
+        scr[pl.ds(c, half, stride=pad), :] = jnp.zeros((half, cols), F32)
+    add_swath(scr, pad, half, start, offset_ref, value_ref, cols)
+    mask = mask_ref[pl.ds(start, half), :].astype(F32)
+    count_rows = half // 2
+    for r in range(half):
+        scr[r * pad : (r + 1) * pad, :] = scr[r * pad : (r + 1) * pad, :] * mask[r : r + 1, :]
+    for k in range(2):
+        first = aligned((((me ^ (2 + k)) % 2) * count_rows) * pad)
+        size = count_rows * pad
+        far_ref[full + k * size : full + (k + 1) * size, :] = scr[pl.ds(first, size), :].astype(BF)
+    copies[8].wait()
+    state_ref = held[8]
+    state_mask = mask_ref[...].astype(F32)
+
+    def outer_rows(c, carry):
+        value = state_ref[c].astype(F32) * state_mask
+        row_scr[pl.ds(c, DIL, stride=pad), :] = value[0:DIL, :]
+        row_scr[pl.ds(DIL * pad + c, DIL, stride=pad), :] = value[rows - DIL :, :]
+        return carry
+
+    lax.fori_loop(0, channels, outer_rows, 0, unroll=5 if channels % 5 == 0 else 1)
+    for c in range(channels, pad):
+        row_scr[pl.ds(c, 2 * DIL, stride=pad), :] = jnp.zeros((2 * DIL, cols), F32)
+    for t in range(DIL):
+        low = row_scr[t * pad : (t + 1) * pad, :]
+        high = row_scr[(DIL + t) * pad : (DIL + t + 1) * pad, :]
+        emit_outer(low, high, t, swap, outer)
+
+
+def prepare_near(grad_ref, mask_ref, offset_ref, value_ref, tiles_ref, rows_ref, own_ref, core_ref, scr):
+    rows, pad, cols = rows_ref.shape
+    mask = mask_ref[...].astype(F32)
+    to_rows(grad_ref, None, scr, pad)
+    add_swath(scr, pad, rows, 0, offset_ref, value_ref, cols)
     for r in range(rows):
         rows_ref[r] = (scr[r * pad : (r + 1) * pad, :] * mask[r : r + 1, :]).astype(BF)
-    tiles = weights_scr.shape[1] // LANES
-    hid = weights_scr.shape[0]
-    for to in (own_ref, core_ref, far_ref):
-        for t in range(tiles):
-            to[t * hid : (t + 1) * hid, :] = weights_scr[:, t * LANES : (t + 1) * LANES]
-    count = (own_ref.shape[0] - tiles * hid) // pad
-    for k, (to, slot) in enumerate(((own_ref, 0), (core_ref, 0), (far_ref, 0), (far_ref, 1))):
+    full = tiles_ref.shape[0]
+    count = (own_ref.shape[0] - full) // pad
+    me = lax.axis_index("ch")
+    for k, to in enumerate((own_ref, core_ref)):
+        to[0:full, :] = tiles_ref[...]
         for r in range(count):
-            at = tiles * hid + (slot * count + r) * pad
+            at = full + r * pad
             to[at : at + pad, :] = rows_ref[(me ^ k) * count + r]
-    copies[8].wait()
 
 
 def relay(in_ref, out_ref):
@@ -175,37 +221,7 @@
     return [(i, (i + step) % count) for i in range(count)]
 
 
-def exchange_halo(strips, rows, pad, swap, name, riding=()):
-    n_lat, n_lon = lax.axis_size("lat"), lax.axis_size("lon")
-    top = n_lat - 1
-    fold_pairs = [
-        (lon * n_lat + top, (n_lon - 1 - lon) * n_lat + top) for lon in range(n_lon)
-    ]
-    if swap:
-        strip, fold, left, right = strips
-        moved = [lax.ppermute(strip, "lat", [(0, 1), (1, 0)])]
-    else:
-        down, up, fold, left, right = strips
-        moved = [
-            lax.ppermute(up, "lat", [(i, i + 1) for i in range(n_lat - 1)]),
-            lax.ppermute(down, "lat", [(i + 1, i) for i in range(n_lat - 1)]),
-        ]
-    fold = lax.ppermute(fold, ("lon", "lat"), fold_pairs)
-    kernel = functools.partial(finish_columns, rows, swap, len(riding) > 0)
-    halo, left, right = call(
-        kernel,
-        [shape((2 * DIL, pad, LANES), BF)] + [shape((pad, LANES), BF)] * 2,
-        [*riding, *moved, fold, left, right],
-        name=name,
-    )
-    from_right = lax.ppermute(left, "lon", ring(n_lon, -1))
-    from_left = lax.ppermute(right, "lon", ring(n_lon, 1))
-    return halo, from_left, from_right
-
-
-def finish_columns(rows, swap, riding, *refs):
-    if riding:
-        ride_ref, *refs = refs
+def finish_columns(rows, swap, *refs):
     if swap:
         strip_ref, fold_ref, left_ref, right_ref, halo_ref, left_out, right_out = refs
         low_ref = high_ref = strip_ref
@@ -220,18 +236,119 @@
         halo_ref[DIL + t] = north.astype(BF)
         left, right = pack_columns(south, t, left, right)
         left, right = pack_columns(north, rows + DIL + t, left, right)
-    if riding:
-        ride = pltpu.roll(ride_ref[...].astype(F32), RIDE, 1)
-        left, right = left + ride, right + ride
     left_out[...] = left.astype(BF)
     right_out[...] = right.astype(BF)
+
+
+def odd_lon():
+    return lax.axis_index("lon") % 2 == 1
+
+
+def pack_for_third(rows, riding, *refs):
+    if riding:
+        ride_ref, *refs = refs
+    got_ref, fold_ref, left_ref, right_ref, out_ref = refs
+    low = lax.axis_index("lat") == 0
+    left, right = left_ref[...].astype(F32), right_ref[...].astype(F32)
+    for t in range(DIL):
+        got = got_ref[t].astype(F32)
+        left, right = pack_columns(jnp.where(low, 0.0, got), t, left, right)
+        left, right = pack_columns(jnp.where(low, got, 0.0), rows + DIL + t, left, right)
+        out_ref[t] = fold_ref[t]
+    pack = jnp.where(odd_lon(), right, left)
+    if riding:
+        pack = pack + pltpu.roll(ride_ref[...].astype(F32), RIDE, 1)
+    out_ref[DIL] = pack.astype(BF)
+
+
+def pack_for_first(rows, got_ref, fold_ref, left_ref, right_ref, third_ref, halo_ref, out_ref, side_ref):
+    low = lax.axis_index("lat") == 0
+    odd = odd_lon()
+    left, right = left_ref[...].astype(F32), right_ref[...].astype(F32)
+    side = third_ref[DIL].astype(F32)
+    size = side.shape[1]
+    lane = iota(side.shape, 1)
+    for t in range(DIL):
+        got = got_ref[t].astype(F32)
+        south = jnp.where(low, 0.0, got)
+        north = jnp.where(low, got, third_ref[t].astype(F32))
+        halo_ref[t] = south.astype(BF)
+        halo_ref[DIL + t] = north.astype(BF)
+        left, right = pack_columns(south, t, left, right)
+        left, right = pack_columns(north, rows + DIL + t, left, right)
+        at = 2 * (rows + DIL + t)
+        own = fold_ref[t].astype(F32)
+        own = jnp.where(
+            odd, pltpu.roll(own, at, 1), pltpu.roll(own, (at - (size - DIL)) % size, 1)
+        )
+        here = jnp.logical_and((lane == at) | (lane == at + 1), jnp.logical_not(low))
+        side = jnp.where(here, own, side)
+    out_ref[0] = jnp.where(odd, left, right).astype(BF)
+    for k in range(1, out_ref.shape[0]):
+        out_ref[k] = jnp.zeros(side.shape, BF)
+    side_ref[...] = side.astype(BF)
+
+
+def two_by_four():
+    return lax.axis_size("lat") == 2 and lax.axis_size("lon") == 4
+
+
+def exchange_halo(rows, strips, outer, swap, name, planes=1, riding=(), after=()):
+    n_lat, n_lon = lax.axis_size("lat"), lax.axis_size("lon")
+    fold, left, right = strips
+    pad = left.shape[0]
+    halo_shape, pack = shape((2 * DIL, pad, LANES), BF), shape((pad, LANES), BF)
+    if two_by_four():
+        got = lax.ppermute(outer[0], "lat", [(0, 1), (1, 0)])
+        third_out = call(
+            functools.partial(pack_for_third, rows, len(riding) > 0),
+            [shape((DIL + 1, pad, LANES), BF)],
+            [*riding, got, fold, left, right],
+            (),
+            name + "_third",
+            after=after,
+        )[0]
+        third = lax.ppermute(third_out, "lon", [(lon, lon ^ 3) for lon in range(n_lon)])
+        halo, first, side = call(
+            functools.partial(pack_for_first, rows),
+            [halo_shape, shape((planes, pad, LANES), BF), pack],
+            [got, fold, left, right, third],
+            (),
+            name + "_first",
+        )
+        got = lax.ppermute(first, "lon", [(lon, lon ^ 1) for lon in range(n_lon)])
+        return (halo, got, side), (third_out, third, first)
+    top = n_lat - 1
+    fold_pairs = [(lon * n_lat + top, (n_lon - 1 - lon) * n_lat + top) for lon in range(n_lon)]
+    if swap:
+        moved = [lax.ppermute(outer[0], "lat", [(0, 1), (1, 0)])]
+    else:
+        moved = [
+            lax.ppermute(outer[1], "lat", [(i, i + 1) for i in range(n_lat - 1)]),
+            lax.ppermute(outer[0], "lat", [(i + 1, i) for i in range(n_lat - 1)]),
+        ]
+    fold = lax.ppermute(fold, ("lon", "lat"), fold_pairs)
+    halo, left, right = call(
+        functools.partial(finish_columns, rows, swap),
+        [halo_shape, pack, pack],
+        [*moved, fold, left, right],
+        (),
+        name + "_columns",
+    )
+    from_right = lax.ppermute(left, "lon", ring(n_lon, -1))
+    from_left = lax.ppermute(right, "lon", ring(n_lon, 1))
+    return (halo, from_left, from_right), ()
 
 
 def shifted_rows(block_ref, halo_ref, left_ref, right_ref, group):
     rows = block_ref.shape[0]
     at = pl.ds(aligned(group * 16), 16)
     lane = iota((16, LANES), 1)
-    left, right = left_ref[at, :].astype(F32), right_ref[at, :].astype(F32)
+    left = left_ref[(0, at) if two_by_four() else at].astype(F32)
+    right = right_ref[at, :].astype(F32)
+    if two_by_four():
+        odd = odd_lon()
+        left, right = jnp.where(odd, left, right), jnp.where(odd, right, left)
     for e in range(rows + 2 * DIL):
         if e < DIL:
             row = halo_ref[e, at, :]
@@ -297,7 +414,7 @@
 
 
 def conv_adjoint(
-    block_ref, halo_ref, left_ref, right_ref, tap_ref, cotan_ref, mask_ref, out_ref, scr
+    block_ref, halo_ref, left_ref, right_ref, tap_ref, cotan_ref, mask_ref, out_ref, mark_ref, scr
 ):
     rows, pad = block_ref.shape[:2]
     at_top = lax.axis_index("lat") == lax.axis_size("lat") - 1
@@ -325,15 +442,19 @@
 
     channels = out_ref.shape[0]
     lax.fori_loop(0, channels, write, 0, unroll=5 if channels % 5 == 0 else 1)
-
-
-def collect_grad(swap, q0, q1, q2, q3, rows_ref, *strips):
-    part_rows = q0.shape[0]
+    mark_ref[...] = jnp.zeros(mark_ref.shape, F32)
+
+
+def collect_grad(swap, own, near, far, passed, rows_ref, *rest):
+    part_rows = own.shape[0]
     rows, pad = rows_ref.shape[:2]
     me = lax.axis_index("ch")
-    for k, quarter in enumerate((q0, q1, q2, q3)):
+    for k, quarter in enumerate((own, near, far.at[0], passed.at[1])):
         rows_ref[pl.ds((me ^ k) * part_rows, part_rows)] = quarter[...]
-    emit_strips(lambda r: rows_ref[r], rows, pad, swap, strips)
+    strips, outer = rest[:3], rest[3:]
+    for t in range(DIL):
+        emit_outer(rows_ref[t].astype(F32), rows_ref[rows - DIL + t].astype(F32), t, swap, outer)
+    emit_strips(lambda r: rows_ref[r], rows, pad, *strips)
 
 
 def kernel_gradient(grad_ref, block_ref, halo_ref, left_ref, right_ref, out_ref):
@@ -485,8 +606,9 @@
 
 
 def conv_gradient(pre_ref, t_ref, *rest):
-    outs, scr = rest[:-1], rest[-1]
-    part_rows, pad = outs[0].shape[:2]
+    (own_ref, core_ref, far_ref), scr = rest[:-1], rest[-1]
+    outs = (own_ref, core_ref, far_ref.at[0], far_ref.at[1])
+    part_rows, pad = own_ref.shape[:2]
     me = lax.axis_index("ch")
     step = 256
     for start in range(0, pre_ref.shape[1], step):
@@ -521,22 +643,18 @@
     out_ref[...] = (mine_ref[...] + got_ref[...].astype(F32)).astype(BF)
 
 
-def finish_pieces(mine_ref, line_ref, kernel_ref, left_ref, right_ref, out_ref):
-    piece = mine_ref.shape[0]
+def finish_pieces(mine_ref, line_ref, kernel_ref, third_ref, out_ref, turn_scr):
+    piece, pad = mine_ref.shape[0], kernel_ref.shape[0]
     out_ref[0:piece, :] = (mine_ref[...].astype(F32) + line_ref[...].astype(F32)).astype(BF)
-    even = lax.axis_index("lon") % 2 == 0
-    other = jnp.where(even, left_ref[...].astype(F32), right_ref[...].astype(F32))
-    other = pltpu.roll(other, LANES - RIDE + 16, 1)
-    lane = iota(other.shape, 1)
-    here = kernel_ref[...].astype(F32)
-    out_ref[piece : out_ref.shape[0], :] = jnp.where(
-        lane < 16, here, jnp.where(lane < 32, other, 0.0)
-    ).astype(BF)
+    other = pltpu.roll(third_ref[DIL].astype(F32), LANES - RIDE, 1)
+    turn_scr[...] = jnp.zeros(turn_scr.shape, F32)
+    turn_scr[0:pad, :] = kernel_ref[...].astype(F32) + other
+    out_ref[piece:, :] = jnp.transpose(turn_scr[...])[0:TAP_ROWS, :].astype(BF)
 
 
 def write_parameters(part, pad, scale, hid, p0, p1, p2, p3, *rest):
-    expand_ref, project_ref, bias_ref, taps_ref, all_scr, taps_scr, turn_scr = rest
-    piece = p0.shape[0] - pad
+    expand_ref, project_ref, bias_ref, taps_ref, all_scr, taps_scr = rest
+    piece = p0.shape[0] - TAP_ROWS
     step = piece - 32
     place = 2 * lax.axis_index("lat") + lax.axis_index("lon") % 2
     for k, ref in enumerate((p0, p1, p2, p3)):
@@ -547,25 +665,17 @@
         def _():
             all_scr[4 * step : 4 * step + 32, :] = ref[step:piece, :]
 
-        lat, lon = lax.axis_index("lat") ^ (k >> 1), lax.axis_index("lon") ^ (k & 1)
-        taps = ref[piece : piece + pad, :].astype(F32)
-        taps_scr[pl.ds(aligned((4 * lat + lon) * pad), pad), :] = taps
-        taps_scr[pl.ds(aligned((4 * lat + (lon ^ 3)) * pad), pad), :] = pltpu.roll(
-            taps, LANES - 16, 1
-        )
+        taps_scr[pl.ds(aligned(to * TAP_ROWS), TAP_ROWS), :] = ref[piece:, :].astype(F32)
     unpack(part, pad, scale, hid, all_scr, expand_ref, project_ref, bias_ref)
-    total = taps_scr[0:pad, :]
-    for k in range(1, 8):
-        total = total + taps_scr[k * pad : (k + 1) * pad, :]
-    write_taps(total, scale, taps_ref, turn_scr)
-
-
-def write_taps(total, scale, taps_ref, turn_scr):
-    turn_scr[...] = jnp.zeros(turn_scr.shape, F32)
-    turn_scr[0 : total.shape[0], :] = total * scale
-    turned = jnp.transpose(turn_scr[...])
+    total = taps_scr[0:TAP_ROWS, :]
+    for k in range(1, 4):
+        total = total + taps_scr[k * TAP_ROWS : (k + 1) * TAP_ROWS, :]
+    write_taps(total, scale, taps_ref)
+
+
+def write_taps(total, scale, taps_ref):
     for a in range(3):
-        taps_ref[a] = turned[3 * a : 3 * a + 3, 0 : taps_ref.shape[2]]
+        taps_ref[a] = total[3 * a : 3 * a + 3, 0 : taps_ref.shape[2]] * scale
 
 
 def unpack(part, pad, scale, hid, all_ref, expand_ref, project_ref, bias_ref):
@@ -589,7 +699,9 @@
 
 def unpack_whole(part, pad, scale, hid, all_ref, taps_in, expand_ref, project_ref, bias_ref, taps_ref, turn_scr):
     unpack(part, pad, scale, hid, all_ref, expand_ref, project_ref, bias_ref)
-    write_taps(taps_in[...], scale, taps_ref, turn_scr)
+    turn_scr[...] = jnp.zeros(turn_scr.shape, F32)
+    turn_scr[0:pad, :] = taps_in[...]
+    write_taps(jnp.transpose(turn_scr[...])[0:TAP_ROWS, :], scale, taps_ref)
 
 
 def on_device(
@@ -625,6 +737,7 @@
     flat = pltpu.VMEM((rows * pad, cols), F32)
 
     turn = pltpu.VMEM((LANES, LANES), F32)
+
     def spread_parts(parts):
         return [parts[0]] + [
             lax.ppermute(parts[k], "ch", [(i, i ^ k) for i in range(n_ch)]) for k in (3, 2, 1)
@@ -643,32 +756,41 @@
         depth_kernel,
         ocean_state,
     ]
-    cotan, own, to_core, to_far, taps, land_mask, ocean_state = call(
-        functools.partial(prepare_cotan, part),
+    count = len(prepared)
+    to_far, tiles, taps, *rest = call(
+        functools.partial(prepare_far, part, swap, count),
+        [shape((far_rows, LANES), BF), shape((tile_rows, LANES), BF), shape((pad, LANES), F32)]
+        + outer_shapes(pad, swap)
+        + [shape(a.shape, a.dtype) for a in prepared],
+        prepared,
         [
-            block,
-            shape((near_rows, LANES), BF),
-            shape((near_rows, LANES), BF),
-            shape((far_rows, LANES), BF),
-            shape((pad, LANES), F32),
-            shape(land_mask.shape, land_mask.dtype),
-            shape(ocean_state.shape, ocean_state.dtype),
+            pltpu.VMEM((rows // 2 * pad, cols), F32),
+            pltpu.VMEM((2 * DIL * pad, cols), F32),
+            pltpu.VMEM((hid, wide), BF),
+            turn,
+            pltpu.SemaphoreType.DMA((count,)),
         ],
-        prepared,
-        [flat, pltpu.VMEM((hid, wide), BF), turn, pltpu.SemaphoreType.DMA((9,))]
-        + [pltpu.VMEM(prepared[k].shape, prepared[k].dtype) for k in (0, 2, 3, 4, 5, 6, 7)],
-        "cotan_rows",
+        "far_rows",
         far=True,
     )
+    outer, held = rest[:-count], rest[-count:]
+    land_mask, ocean_state = held[1], held[8]
     masked, *strips = call(
-        functools.partial(prepare_state, swap),
-        [block] + strip_shapes(pad, swap),
+        prepare_state,
+        [block] + strip_shapes(pad),
         [ocean_state, land_mask],
         [flat],
         "state_rows",
-        after=[taps],
-    )
-    around = exchange_halo(strips, rows, pad, swap, "state_columns")
+    )
+    cotan, own, to_core = call(
+        prepare_near,
+        [block, shape((near_rows, LANES), BF), shape((near_rows, LANES), BF)],
+        [*held[0:4], tiles],
+        [flat],
+        "cotan_rows",
+        after=[masked],
+    )
+    around, _ = exchange_halo(rows, strips, outer, swap, "state", after=[to_core])
     from_far = lax.ppermute(to_far, "ch", across)
     conv_parts = call(
         functools.partial(conv_forward, part),
@@ -679,7 +801,7 @@
     )
     all_conv = spread_parts(conv_parts)
     from_far = call(
-        relay, [from_far], [from_far], (), "cotan_relay", aliases={0: 0}, after=around[1:]
+        relay, [from_far], [from_far], (), "cotan_relay", aliases={0: 0}, after=conv_parts[:1]
     )[0]
     passed = lax.ppermute(from_far, "ch", core)
     act_grad, cotan_all, weights_all, weights_turned = call(
@@ -706,15 +828,16 @@
         "hidden_gradient",
     )
     got = lax.ppermute(send, "ch", core)
-    grad_parts = call(
+    grad_own, grad_core, grad_far = call(
         conv_gradient,
-        [quarter] * 4,
+        [quarter, quarter, shape((2, part_rows, pad, cols), BF)],
         [pre_grad, weights_turned],
         [pltpu.VMEM((depth, cells), BF)],
         "conv_gradient",
     )
-    grad_got = spread_parts(grad_parts)
-    staged = n_lat == 2 and n_lon == 4 and tile_rows % 32 == 0
+    grad_near = lax.ppermute(grad_core, "ch", core)
+    grad_far = lax.ppermute(grad_far, "ch", across)
+    staged = two_by_four() and tile_rows % 32 == 0
     if staged:
         step = (tile_rows - 32) // 128 * 32
         piece = step + 32
@@ -725,7 +848,6 @@
             [keep, got],
             (),
             "add_cores",
-            after=grad_got[1:2],
         )
 
         def turn_plane(k):
@@ -745,14 +867,24 @@
             (),
             "add_pieces",
         )
+        grad_far = call(
+            relay, [grad_far], [grad_far], (), "grad_relay", aliases={0: 0}, after=[other]
+        )[0]
     conv_grad, *grad_strips = call(
         functools.partial(collect_grad, swap),
-        [block] + strip_shapes(pad, swap),
-        grad_got,
+        [block] + strip_shapes(pad) + outer_shapes(pad, swap),
+        [grad_own, grad_near, grad_far, lax.ppermute(grad_far, "ch", core)],
         (),
         "grad_rows",
-        after=[other] if staged else [],
-    )
+    )
+    kernel_part = call(
+        kernel_gradient,
+        [shape((pad, LANES), BF)],
+        [conv_grad, masked, *around],
+        (),
+        "kernel_gradient",
+    )[0]
+    grad_around, marks = exchange_halo(rows, grad_strips[:3], grad_strips[3:], swap, "grad", planes=4, riding=[kernel_part])
     if staged:
         mine = call(
             add_across,
@@ -761,22 +893,13 @@
             (),
             "add_across",
         )[0]
-    kernel_part = call(
-        kernel_gradient,
-        [shape((pad, LANES), BF)],
-        [conv_grad, masked, *around],
-        (),
-        "kernel_gradient",
-        after=[mine] if staged else [],
-    )[0]
-    grad_around = exchange_halo(grad_strips, rows, pad, swap, "grad_columns", [kernel_part])
-    state_grad = call(
+    state_grad, mark = call(
         conv_adjoint,
-        [shape((part, rows, cols), BF)],
+        [shape((part, rows, cols), BF), shape((8, LANES), F32)],
         [conv_grad, *grad_around, taps, cotan, land_mask],
         [flat],
         "conv_adjoint",
-    )[0]
+    )
     outs = [
         shape((hidden, channels), F32),
         shape((hidden, channels), F32),
@@ -787,22 +910,24 @@
         far_lon = [(lon, lon ^ 2) for lon in range(n_lon)]
         summed = call(
             finish_pieces,
-            [shape((piece + pad, LANES), BF)],
+            [shape((piece + TAP_ROWS, LANES), BF)],
             [
                 mine,
                 lax.ppermute(mine, "lon", far_lon),
                 kernel_part,
-                *grad_around[1:],
+                marks[1],
             ],
-            (),
+            [turn],
             "finish_pieces",
+            after=marks[2:],
         )[0]
         expand_grad, project_grad, bias_grad, kernel_grad = call(
             functools.partial(write_parameters, part, pad, scale, hid),
             outs,
             [summed, *over_plane([summed] * 3)],
-            [pltpu.VMEM((tile_rows, LANES), BF), pltpu.VMEM((8 * pad, LANES), F32), turn],
+            [pltpu.VMEM((tile_rows, LANES), BF), pltpu.VMEM((4 * TAP_ROWS, LANES), F32)],
             "write_parameters",
+            after=[mark],
         )
     else:
         total = keep + got.astype(F32)

time: 73.9 us -> 71 us (0.961)
  starting transfers between devices: 32.9 us -> 27.6 us
  Pallas kernels: 17.6 us -> 19.1 us
  waiting for transfers between devices: 22.4 us -> 23.3 us
    ppermute x8 -> x9, waiting for transfers between devices: 5.85 us -> 10.9 us  [the longest x2 4.49 us: exchange_halo(): lax.ppermute(third_out, 'lon', [(lon, lon ^ 3) for lon in range(n_lon)])]
    ppermute x6, starting transfers between devices: 10.1 us -> 7.06 us  [over_plane(): lax.ppermute(values[k - 1], ('lon', 'lat'), turn_plane(k))]
    ppermute x6 -> x3, waiting for transfers between devices: 9.58 us -> 6.69 us  [spread_parts(): lax.ppermute(parts[k], 'ch', [(i, i ^ k) for i in range(n_ch)])]
    ppermute x1, starting transfers between devices: 2.79 us -> 0.59 us  [on_device(): lax.ppermute(mine, 'lon', far_lon)]
    pallas_call x17 -> x21, Pallas kernels: 17.6 us -> 19.1 us  [call(): pl.pallas_call(kernel, out_shape=tuple(outs), in_specs=[pl.BlockSpec(memo...]
    ppermute x6 -> x3, starting transfers between devices: 3.27 us -> 1.87 us  [spread_parts(): lax.ppermute(parts[k], 'ch', [(i, i ^ k) for i in range(n_ch)])]
    ppermute x8 -> x9, starting transfers between devices: 12.3 us -> 13.7 us  [the longest x2 7.31 us: exchange_halo(): lax.ppermute(third_out, 'lon', [(lon, lon ^ 3) for lon in range(n_lon)])]
    ppermute x1, waiting for transfers between devices: 1.29 us -> 0.01 us  [on_device(): from_far = lax.ppermute(to_far, 'ch', across)]
  transfers between devices with their start and end apart: 26 -> 24, of which waited for: 14 -> 14; matrix products, arithmetic and copies ran while one was open for 0% -> 0% of each run, Pallas kernels for 13% -> 15%
where the time goes in v3:
time: 71 us; the launch traced here: 70.8 us
  starting transfers between devices  27.6 us (39%)
  waiting for transfers between devices  23.3 us (33%)
  Pallas kernels  19.1 us (27%)
  between operations  0.8 us (1%)
    pallas_call x21, Pallas kernels, call(): pl.pallas_call(kernel, out_shape=tuple(outs), in_specs=[pl.BlockSpec(memo...  19.1 us
    ppermute x2, starting transfers between devices, exchange_halo(): lax.ppermute(third_out, 'lon', [(lon, lon ^ 3) for lon in range(n_lon)])  7.31 us
    ppermute x6, starting transfers between devices, over_plane(): lax.ppermute(values[k - 1], ('lon', 'lat'), turn_plane(k))  7.06 us
    ppermute x3, waiting for transfers between devices, spread_parts(): lax.ppermute(parts[k], 'ch', [(i, i ^ k) for i in range(n_ch)])  6.69 us
    ppermute x6, waiting for transfers between devices, over_plane(): lax.ppermute(values[k - 1], ('lon', 'lat'), turn_plane(k))  5.25 us
    ppermute x2, waiting for transfers between devices, exchange_halo(): lax.ppermute(third_out, 'lon', [(lon, lon ^ 3) for lon in range(n_lon)])  4.49 us
    ppermute x2, waiting for transfers between devices, exchange_halo(): got = lax.ppermute(first, 'lon', [(lon, lon ^ 1) for lon in range(n_lon)])  3.77 us
    ppermute x2, starting transfers between devices, exchange_halo(): got = lax.ppermute(outer[0], 'lat', [(0, 1), (1, 0)])  3.09 us
  transfers between devices with their start and end apart: 24, of which 14 were waited for; matrix products, arithmetic and copies ran while one was open for 0% of the time, Pallas kernels for 15%

profile of v3, /device:TPU:0, one launch (start us, length us, event | category | flops | bytes accessed | tf_op | source)
XLA Modules:
  0.0 70.8 jit_solution(4471534824239244191)
XLA Ops:
  0.6 3.2 %far_rows.1 = (bf16[2080,128]{1,0:T(8,128)(2,1)S(1)}, bf16[800,128]{1,0:T(8,128)(2,1)S(1)}, f32[80,128]{1,0:T(8,128)S(1)}, bf16[2,80,128]{2,1,0:T(8,128)(2,1)S(1...) custom-call(bf16[75,32,128]{2,1,0:T(8,128)(2,1)} %refs_0_.1, ...), custom_call_target="tpu_custom_call" | custom-call | bytes 3684360 | tf_op jit(solution)/shard_map/far_rows/pallas_call | solution.py:35
  3.8 3.0 %collective-permute-start.7 = (bf16[2080,128]{1,0:T(8,128)(2,1)S(1)}, bf16[2080,128]{1,0:T(8,128)(2,1)S(1)}, u32[]{:S(2)}, u32[]{:S(2)}) collective-permute-start(bf16[2080,128]{1,0:T(8,128)(2,1)S(1)} %get-tuple-element.79), channel_id=1, source_target_pairs={{0,2},{1,3},{2,0},{3,1},{4,6},{5,7},{6,4},{7,5},{8,10},{9,11},{10,... | collective-permute-start | bytes 1597448 | tf_op jit(solution)/shard_map/ppermute | solution.py:794
  6.8 1.5 %collective-permute-start = (bf16[2,80,128]{2,1,0:T(8,128)(2,1)S(1)}, bf16[2,80,128]{2,1,0:T(8,128)(2,1)S(1)}, u32[]{:S(2)}, u32[]{:S(2)}) collective-permute-start(bf16[2,80,128]{2,1,0:T(8,128)(2,1)S(1)} %get-tuple-element.61), channel_id=1, source_target_pairs={{0,4},{4,0},{1,5},{5,1},{2,6},{6,2},{3,7},{7,3},{8,12},{12,8},{9,1... | collective-permute-start | bytes 122888 | tf_op jit(solution)/shard_map/ppermute | solution.py:302
  8.3 1.0 %state_rows.1 = (bf16[32,80,128]{2,1,0:T(8,128)(2,1)S(1)}, bf16[2,80,128]{2,1,0:T(8,128)(2,1)S(1)}, bf16[80,128]{1,0:T(8,128)(2,1)S(1)}, bf16[80,128]{1,0:T(8,128)(2,1)S(1)}) custom-call(bf16[75,32,128]{2,1,0:T(8,128)(2,1)S(1)} %get-tuple-element.58.state_ref, s32[32,128]{1,0:T(8,128)S(1)} %get-tuple-element.59.mask_ref.refs_1_), custom_call_target="tpu_custom_call" | custom-call | bytes 1368064 | tf_op jit(solution)/shard_map/state_rows/pallas_call | solution.py:35
  9.3 0.8 %cotan_rows.1 = (bf16[32,80,128]{2,1,0:T(8,128)(2,1)S(1)}, bf16[1440,128]{1,0:T(8,128)(2,1)S(1)}, bf16[1440,128]{1,0:T(8,128)(2,1)S(1)}) custom-call(bf16[75,32,128]{2,1,0:T(8,128)(2,1)S(1)} %get-tuple-element.65.refs_0_, s32[32,128]{1,0:T(8,128)S(1)} %get-tuple-element.59.mask_ref.refs_1_, s32[1,512]{1,0:T(1,128)S(1)} %get-tuple-element.66.refs_2_, ...), custom_call_target="tpu_custom_call" | custom-call | bytes 2887680 | tf_op jit(solution)/shard_map/cotan_rows/pallas_call | solution.py:35
  10.1 0.7 collective-permute-done.refs_0_.got_ref
  10.9 3.7 %collective-permute-start.1 = (bf16[3,80,128]{2,1,0:T(8,128)(2,1)S(1)}, bf16[3,80,128]{2,1,0:T(8,128)(2,1)S(1)}, u32[]{:S(2)}, u32[]{:S(2)}) collective-permute-start(bf16[3,80,128]{2,1,0:T(8,128)(2,1)S(1)} %state_third.1), channel_id=1, source_target_pairs={{0,24},{8,16},{16,8},{24,0},{1,25},{9,17},{17,9},{25,1},{2,26},{10... | collective-permute-start | bytes 184328 | tf_op jit(solution)/shard_map/ppermute | solution.py:311
  14.6 2.4 %collective-permute-done.1.third_ref = bf16[3,80,128]{2,1,0:T(8,128)(2,1)S(1)} collective-permute-done((bf16[3,80,128]{2,1,0:T(8,128)(2,1)S(1)}, bf16[3,80,128]{2,1,0:T(8,128)(2,1)S(1)}, u32[]{:S(2)}, u32[]{:S(2)}) %collective-permute-start.1) | collective-permute-done | bytes 61472 | tf_op jit(solution)/shard_map/ppermute | solution.py:311
  17.2 3.8 %collective-permute-done.2.left_ref = bf16[1,80,128]{2,1,0:T(8,128)(2,1)S(1)} collective-permute-done((bf16[1,80,128]{2,1,0:T(8,128)(2,1)S(1)}, bf16[1,80,128]{2,1,0:T(8,128)(2,1)S(1)}, u32[]{:S(2)}, u32[]{:S(2)}) %collective-permute-start.2) | collective-permute-done | bytes 20512 | tf_op jit(solution)/shard_map/ppermute | solution.py:319
  21.0 1.6 %conv_forward.1 = (bf16[8,80,128]{2,1,0:T(8,128)(2,1)S(1)}, bf16[8,80,128]{2,1,0:T(8,128)(2,1)S(1)}, bf16[8,80,128]{2,1,0:T(8,128)(2,1)S(1)}, bf16[8,80,128]{2,1,0:T(8,128)(2,1)S(1)}) custom-call(bf16[32,80,128]{2,1,0:T(8,128)(2,1)S(1)} %get-tuple-element.60.refs_5_.block_ref, bf16[4,80,128]{2,1,0:T(8,128)(2,1)S(1)} %get-tuple-element.70.halo_ref, ...), custom_call_target="tpu_custom_call" | custom-call | bytes 1474560 | tf_op jit(solution)/shard_map/conv_forward/pallas_call | solution.py:35
  23.7 1.4 %collective-permute-start.5 = (bf16[8,80,128]{2,1,0:T(8,128)(2,1)S(1)}, bf16[8,80,128]{2,1,0:T(8,128)(2,1)S(1)}, u32[]{:S(2)}, u32[]{:S(2)}) collective-permute-start(bf16[8,80,128]{2,1,0:T(8,128)(2,1)S(1)} %get-tuple-element.77), channel_id=1, source_target_pairs={{0,3},{1,2},{2,1},{3,0},{4,7},{5,6},{6,5},{7,4},{8,11},{9,10},{10,... | collective-permute-start | bytes 491528 | tf_op jit(solution)/shard_map/ppermute | solution.py:743
  25.2 1.0 %activation_gradient.1 = (f32[640,1024]{1,0:T(8,128)S(1)}, bf16[384,1024]{1,0:T(8,128)(2,1)S(1)}, bf16[640,640]{1,0:T(8,128)(2,1)S(1)}, bf16[384,640]{1,0:T(8,128)(2,1)S(1)}) custom-call(bf16[1440,128]{1,0:T(8,128)(2,1)S(1)} %get-tuple-element.78.refs_0_, bf16[1440,128]{1,0:T(8,128)(2,1)S(1)} %collective-permute-done.6.refs_1_, ...), custom_call_target="tpu_custom_call" | custom-call | bytes 6520832 | tf_op jit(solution)/shard_map/activation_gradient/pallas_call | solution.py:35
  26.2 4.1 %collective-permute-done.4.refs_2_ = bf16[8,80,128]{2,1,0:T(8,128)(2,1)S(1)} collective-permute-done((bf16[8,80,128]{2,1,0:T(8,128)(2,1)S(1)}, bf16[8,80,128]{2,1,0:T(8,128)(2,1)S(1)}, u32[]{:S(2)}, u32[]{:S(2)}) %collective-permute-start.4) | collective-permute-done | bytes 163872 | tf_op jit(solution)/shard_map/ppermute | solution.py:743
  30.3 2.6 %collective-permute-done.5.refs_3_ = bf16[8,80,128]{2,1,0:T(8,128)(2,1)S(1)} collective-permute-done((bf16[8,80,128]{2,1,0:T(8,128)(2,1)S(1)}, bf16[8,80,128]{2,1,0:T(8,128)(2,1)S(1)}, u32[]{:S(2)}, u32[]{:S(2)}) %collective-permute-start.5) | collective-permute-done | bytes 163872 | tf_op jit(solution)/shard_map/ppermute | solution.py:743
  32.9 3.6 %hidden_gradient.1 = (bf16[640,1024]{1,0:T(8,128)(2,1)S(1)}, f32[2,800,128]{2,1,0:T(8,128)S(1)}, bf16[2,800,128]{2,1,0:T(8,128)(2,1)S(1)}) custom-call(bf16[8,80,128]{2,1,0:T(8,128)(2,1)S(1)} %get-tuple-element.74.refs_1_.refs_0_, bf16[8,80,128]{2,1,0:T(8,128)(2,1)S(1)} %collective-permute-done.3.refs_1_, ...), custom_call_target="tpu_custom_call" | custom-call | bytes 7421952 | tf_op jit(solution)/shard_map/hidden_gradient/pallas_call | solution.py:35
  36.8 0.9 %conv_gradient.1 = (bf16[8,80,128]{2,1,0:T(8,128)(2,1)S(1)}, bf16[8,80,128]{2,1,0:T(8,128)(2,1)S(1)}, bf16[2,8,80,128]{3,2,1,0:T(8,128)(2,1)S(1)}) custom-call(bf16[640,1024]{1,0:T(8,128)(2,1)S(1)} %get-tuple-element.83.pre_ref, bf16[384,640]{1,0:T(8,128)(2,1)S(1)} %get-tuple-element.84.t_ref), custom_call_target="tpu_custom_call" | custom-call | bytes 2457600 | tf_op jit(solution)/shard_map/conv_gradient/pallas_call | solution.py:35
  38.5 1.6 %collective-permute-start.13 = (bf16[2,224,128]{2,1,0:T(8,128)(2,1)S(1)}, bf16[2,224,128]{2,1,0:T(8,128)(2,1)S(1)}, u32[]{:S(2)}, u32[]{:S(2)}) collective-permute-start(bf16[2,224,128]{2,1,0:T(8,128)(2,1)S(1)} %get-tuple-element.92), channel_id=1, source_target_pairs={{0,4},{4,0},{8,12},{12,8},{16,20},{20,16},{24,28},{28,24},{1,5},{5... | collective-permute-start | bytes 344072 | tf_op jit(solution)/shard_map/ppermute | solution.py:861
  40.1 1.9 %collective-permute-start.14 = (bf16[2,224,128]{2,1,0:T(8,128)(2,1)S(1)}, bf16[2,224,128]{2,1,0:T(8,128)(2,1)S(1)}, u32[]{:S(2)}, u32[]{:S(2)}) collective-permute-start(bf16[2,224,128]{2,1,0:T(8,128)(2,1)S(1)} %get-tuple-element.93), channel_id=1, source_target_pairs={{0,12},{4,8},{8,4},{12,0},{16,28},{20,24},{24,20},{28,16},{1,13},{... | collective-permute-start | bytes 344072 | tf_op jit(solution)/shard_map/ppermute | solution.py:861
  41.9 2.5 %collective-permute-done.12.a_ref = bf16[2,224,128]{2,1,0:T(8,128)(2,1)S(1)} collective-permute-done((bf16[2,224,128]{2,1,0:T(8,128)(2,1)S(1)}, bf16[2,224,128]{2,1,0:T(8,128)(2,1)S(1)}, u32[]{:S(2)}, u32[]{:S(2)}) %collective-permute-start.12) | collective-permute-done | bytes 114720 | tf_op jit(solution)/shard_map/ppermute | solution.py:861
  44.4 2.8 %collective-permute-done.14.c_ref = bf16[2,224,128]{2,1,0:T(8,128)(2,1)S(1)} collective-permute-done((bf16[2,224,128]{2,1,0:T(8,128)(2,1)S(1)}, bf16[2,224,128]{2,1,0:T(8,128)(2,1)S(1)}, u32[]{:S(2)}, u32[]{:S(2)}) %collective-permute-start.14) | collective-permute-done | bytes 114720 | tf_op jit(solution)/shard_map/ppermute | solution.py:861
  48.1 1.4 %collective-permute-done.9.near = bf16[8,80,128]{2,1,0:T(8,128)(2,1)S(1)} collective-permute-done((bf16[8,80,128]{2,1,0:T(8,128)(2,1)S(1)}, bf16[8,80,128]{2,1,0:T(8,128)(2,1)S(1)}, u32[]{:S(2)}, u32[]{:S(2)}) %collective-permute-start.9) | collective-permute-done | bytes 163872 | tf_op jit(solution)/shard_map/ppermute | solution.py:838
  50.0 1.6 %collective-permute-start.16 = (bf16[2,80,128]{2,1,0:T(8,128)(2,1)S(1)}, bf16[2,80,128]{2,1,0:T(8,128)(2,1)S(1)}, u32[]{:S(2)}, u32[]{:S(2)}) collective-permute-start(bf16[2,80,128]{2,1,0:T(8,128)(2,1)S(1)} %get-tuple-element.96), channel_id=1, source_target_pairs={{0,4},{4,0},{1,5},{5,1},{2,6},{6,2},{3,7},{7,3},{8,12},{12,8},{9,1... | collective-permute-start | bytes 122888 | tf_op jit(solution)/shard_map/ppermute | solution.py:302
  52.1 1.7 %kernel_gradient.1.refs_0_.refs_2_ = bf16[80,128]{1,0:T(8,128)(2,1)S(1)} custom-call(bf16[32,80,128]{2,1,0:T(8,128)(2,1)S(1)} %get-tuple-element.95.grad_ref.block_ref, bf16[32,80,128]{2,1,0:T(8,128)(2,1)S(1)} %get-tuple-element.60.refs_5_.block_ref, bf16[4,80,128]{2,1,0:T(8,128)(2,1)S(1)} %get-tuple-element.70.halo_ref, ...), custom_call_target="tpu_custom_call" | custom-call | bytes 1454080 | tf_op jit(solution)/shard_map/kernel_gradient/pallas_call | solution.py:35
  54.2 3.7 %collective-permute-start.17 = (bf16[3,80,128]{2,1,0:T(8,128)(2,1)S(1)}, bf16[3,80,128]{2,1,0:T(8,128)(2,1)S(1)}, u32[]{:S(2)}, u32[]{:S(2)}) collective-permute-start(bf16[3,80,128]{2,1,0:T(8,128)(2,1)S(1)} %grad_third.1), channel_id=1, source_target_pairs={{0,24},{8,16},{16,8},{24,0},{1,25},{9,17},{17,9},{25,1},{2,26},{10... | collective-permute-start | bytes 184328 | tf_op jit(solution)/shard_map/ppermute | solution.py:311
  57.9 0.6 collective-permute-start.20
  58.5 2.1 %collective-permute-done.17.third_ref.refs_3_ = bf16[3,80,128]{2,1,0:T(8,128)(2,1)S(1)} collective-permute-done((bf16[3,80,128]{2,1,0:T(8,128)(2,1)S(1)}, bf16[3,80,128]{2,1,0:T(8,128)(2,1)S(1)}, u32[]{:S(2)}, u32[]{:S(2)}) %collective-permute-start.17) | collective-permute-done | bytes 61472 | tf_op jit(solution)/shard_map/ppermute | solution.py:311
  60.6 2.2 %collective-permute-start.18 = (bf16[4,80,128]{2,1,0:T(8,128)(2,1)S(1)}, bf16[4,80,128]{2,1,0:T(8,128)(2,1)S(1)}, u32[]{:S(2)}, u32[]{:S(2)}) collective-permute-start(bf16[4,80,128]{2,1,0:T(8,128)(2,1)S(1)} %get-tuple-element.101.refs_4_), channel_id=1, source_target_pairs={{0,8},{8,0},{16,24},{24,16},{1,9},{9,1},{17,25},{25,17},{2,10},{10... | collective-permute-start | bytes 245768 | tf_op jit(solution)/shard_map/ppermute | solution.py:319
  63.2 0.7 collective-permute-start.23
  63.9 1.0 %collective-permute-start.22 = (bf16[240,128]{1,0:T(8,128)(2,1)S(1)}, bf16[240,128]{1,0:T(8,128)(2,1)S(1)}, u32[]{:S(2)}, u32[]{:S(2)}) collective-permute-start(bf16[240,128]{1,0:T(8,128)(2,1)S(1)} %finish_pieces.1.refs_0_), channel_id=1, source_target_pairs={{0,4},{4,0},{8,12},{12,8},{16,20},{20,16},{24,28},{28,24},{1,5},{5... | collective-permute-start | bytes 184328 | tf_op jit(solution)/shard_map/ppermute | solution.py:861
  64.9 1.9 %collective-permute-start.21 = (bf16[240,128]{1,0:T(8,128)(2,1)S(1)}, bf16[240,128]{1,0:T(8,128)(2,1)S(1)}, u32[]{:S(2)}, u32[]{:S(2)}) collective-permute-start(bf16[240,128]{1,0:T(8,128)(2,1)S(1)} %finish_pieces.1.refs_0_), channel_id=1, source_target_pairs={{0,8},{4,12},{8,0},{12,4},{16,24},{20,28},{24,16},{28,20},{1,9},{5... | collective-permute-start | bytes 184328 | tf_op jit(solution)/shard_map/ppermute | solution.py:861
  66.7 3.0 %conv_adjoint.1 = (bf16[75,32,128]{2,1,0:T(8,128)(2,1)}, f32[8,128]{1,0:T(8,128)S(1)}) custom-call(bf16[32,80,128]{2,1,0:T(8,128)(2,1)S(1)} %get-tuple-element.95.grad_ref.block_ref, bf16[4,80,128]{2,1,0:T(8,128)(2,1)S(1)} %get-tuple-element.100.halo_ref, bf16[4,80,128]{2,1,0:T(8,128)(2,1)S(1)} %collective-permute-done.18.left_ref, ...), custom_call_target="tpu_custom_call" | custom-call | bytes 2170880 | tf_op jit(solution)/shard_map/conv_adjoint/pallas_call | solution.py:35
  69.7 1.1 %write_parameters.1 = (f32[150,300]{1,0:T(8,128)}, f32[150,300]{1,0:T(8,128)}, f32[1,150]{1,0:T(1,128)}, f32[3,3,75]{2,1,0:T(4,128)}) custom-call(bf16[240,128]{1,0:T(8,128)(2,1)S(1)} %finish_pieces.1.refs_0_, bf16[240,128]{1,0:T(8,128)(2,1)S(1)} %collective-permute-done.21.refs_1_, bf16[240,128]{1,0:T(8,128)(2,1)S(1)} %collective-permute-done.22.refs_2_, ...), custom_call_target="tpu_custom_call" | custom-call | bytes 613156 | tf_op jit(solution)/shard_map/write_parameters/pallas_call | solution.py:35
  (37 shorter events, 5.4 us)
Async XLA Ops:
  3.8 18.8 %collective-permute-start.7 = (bf16[2080,128]{1,0:T(8,128)(2,1)S(1)}, bf16[2080,128]{1,0:T(8,128)(2,1)S(1)}, u32[]{:S(2)}, u32[]{:S(2)}) collective-permute-start(bf16[2080,128]{1,0:T(8,128)(2,1)S(1)} %get-tuple-element.79), channel_id=1, source_target_pairs={{0,2},{1,3},{2,0},{3,1},{4,6},{5,7},{6,4},{7,5},{8,10},{9,11},{10,... | collective-permute-start | bytes 1597448 | tf_op jit(solution)/shard_map/ppermute | solution.py:794
  6.8 4.0 %collective-permute-start = (bf16[2,80,128]{2,1,0:T(8,128)(2,1)S(1)}, bf16[2,80,128]{2,1,0:T(8,128)(2,1)S(1)}, u32[]{:S(2)}, u32[]{:S(2)}) collective-permute-start(bf16[2,80,128]{2,1,0:T(8,128)(2,1)S(1)} %get-tuple-element.61), channel_id=1, source_target_pairs={{0,4},{4,0},{1,5},{5,1},{2,6},{6,2},{3,7},{7,3},{8,12},{12,8},{9,1... | collective-permute-start | bytes 122888 | tf_op jit(solution)/shard_map/ppermute | solution.py:302
  10.9 6.1 %collective-permute-start.1 = (bf16[3,80,128]{2,1,0:T(8,128)(2,1)S(1)}, bf16[3,80,128]{2,1,0:T(8,128)(2,1)S(1)}, u32[]{:S(2)}, u32[]{:S(2)}) collective-permute-start(bf16[3,80,128]{2,1,0:T(8,128)(2,1)S(1)} %state_third.1), channel_id=1, source_target_pairs={{0,24},{8,16},{16,8},{24,0},{1,25},{9,17},{17,9},{25,1},{2,26},{10... | collective-permute-start | bytes 184328 | tf_op jit(solution)/shard_map/ppermute | solution.py:311
  17.1 3.8 %collective-permute-start.2 = (bf16[1,80,128]{2,1,0:T(8,128)(2,1)S(1)}, bf16[1,80,128]{2,1,0:T(8,128)(2,1)S(1)}, u32[]{:S(2)}, u32[]{:S(2)}) collective-permute-start(bf16[1,80,128]{2,1,0:T(8,128)(2,1)S(1)} %get-tuple-element.71), channel_id=1, source_target_pairs={{0,8},{8,0},{16,24},{24,16},{1,9},{9,1},{17,25},{25,17},{2,10},{10... | collective-permute-start | bytes 61448 | tf_op jit(solution)/shard_map/ppermute | solution.py:319
  22.6 2.5 %collective-permute-start.8 = (bf16[2080,128]{1,0:T(8,128)(2,1)S(1)}, bf16[2080,128]{1,0:T(8,128)(2,1)S(1)}, u32[]{:S(2)}, u32[]{:S(2)}) collective-permute-start(bf16[2080,128]{1,0:T(8,128)(2,1)S(1)} %cotan_relay.1.refs_2_), channel_id=1, source_target_pairs={{0,1},{1,0},{2,3},{3,2},{4,5},{5,4},{6,7},{7,6},{8,9},{9,8},{10,11... | collective-permute-start | bytes 1597448 | tf_op jit(solution)/shard_map/ppermute | solution.py:806
  22.7 2.4 %collective-permute-start.6 = (bf16[1440,128]{1,0:T(8,128)(2,1)S(1)}, bf16[1440,128]{1,0:T(8,128)(2,1)S(1)}, u32[]{:S(2)}, u32[]{:S(2)}) collective-permute-start(bf16[1440,128]{1,0:T(8,128)(2,1)S(1)} %get-tuple-element.69.refs_4_), channel_id=1, source_target_pairs={{0,1},{1,0},{2,3},{3,2},{4,5},{5,4},{6,7},{7,6},{8,9},{9,8},{10,11... | collective-permute-start | bytes 1105928 | tf_op jit(solution)/shard_map/ppermute | solution.py:815
  23.2 3.0 %collective-permute-start.3 = (bf16[8,80,128]{2,1,0:T(8,128)(2,1)S(1)}, bf16[8,80,128]{2,1,0:T(8,128)(2,1)S(1)}, u32[]{:S(2)}, u32[]{:S(2)}) collective-permute-start(bf16[8,80,128]{2,1,0:T(8,128)(2,1)S(1)} %get-tuple-element.75), channel_id=1, source_target_pairs={{0,1},{1,0},{2,3},{3,2},{4,5},{5,4},{6,7},{7,6},{8,9},{9,8},{10,11... | collective-permute-start | bytes 491528 | tf_op jit(solution)/shard_map/ppermute | solution.py:743
  23.3 7.0 %collective-permute-start.4 = (bf16[8,80,128]{2,1,0:T(8,128)(2,1)S(1)}, bf16[8,80,128]{2,1,0:T(8,128)(2,1)S(1)}, u32[]{:S(2)}, u32[]{:S(2)}) collective-permute-start(bf16[8,80,128]{2,1,0:T(8,128)(2,1)S(1)} %get-tuple-element.76), channel_id=1, source_target_pairs={{0,2},{1,3},{2,0},{3,1},{4,6},{5,7},{6,4},{7,5},{8,10},{9,11},{10,... | collective-permute-start | bytes 491528 | tf_op jit(solution)/shard_map/ppermute | solution.py:743
  23.7 9.2 %collective-permute-start.5 = (bf16[8,80,128]{2,1,0:T(8,128)(2,1)S(1)}, bf16[8,80,128]{2,1,0:T(8,128)(2,1)S(1)}, u32[]{:S(2)}, u32[]{:S(2)}) collective-permute-start(bf16[8,80,128]{2,1,0:T(8,128)(2,1)S(1)} %get-tuple-element.77), channel_id=1, source_target_pairs={{0,3},{1,2},{2,1},{3,0},{4,7},{5,6},{6,5},{7,4},{8,11},{9,10},{10,... | collective-permute-start | bytes 491528 | tf_op jit(solution)/shard_map/ppermute | solution.py:743
  36.5 1.8 %collective-permute-start.11 = (bf16[2,800,128]{2,1,0:T(8,128)(2,1)S(1)}, bf16[2,800,128]{2,1,0:T(8,128)(2,1)S(1)}, u32[]{:S(2)}, u32[]{:S(2)}) collective-permute-start(bf16[2,800,128]{2,1,0:T(8,128)(2,1)S(1)} %get-tuple-element.89), channel_id=1, source_target_pairs={{0,1},{1,0},{2,3},{3,2},{4,5},{5,4},{6,7},{7,6},{8,9},{9,8},{10,11... | collective-permute-start | bytes 1228808 | tf_op jit(solution)/shard_map/ppermute | solution.py:830
  37.7 9.9 %collective-permute-start.10 = (bf16[2,8,80,128]{3,2,1,0:T(8,128)(2,1)S(1)}, bf16[2,8,80,128]{3,2,1,0:T(8,128)(2,1)S(1)}, u32[]{:S(2)}, u32[]{:S(2)}) collective-permute-start(bf16[2,8,80,128]{3,2,1,0:T(8,128)(2,1)S(1)} %get-tuple-element.87), channel_id=1, source_target_pairs={{0,2},{1,3},{2,0},{3,1},{4,6},{5,7},{6,4},{7,5},{8,10},{9,11},{10,... | collective-permute-start | bytes 983048 | tf_op jit(solution)/shard_map/ppermute | solution.py:839
  38.4 6.0 %collective-permute-start.12 = (bf16[2,224,128]{2,1,0:T(8,128)(2,1)S(1)}, bf16[2,224,128]{2,1,0:T(8,128)(2,1)S(1)}, u32[]{:S(2)}, u32[]{:S(2)}) collective-permute-start(bf16[2,224,128]{2,1,0:T(8,128)(2,1)S(1)} %get-tuple-element.91), channel_id=1, source_target_pairs={{0,8},{4,12},{8,0},{12,4},{16,24},{20,28},{24,16},{28,20},{1,9},{5... | collective-permute-start | bytes 344072 | tf_op jit(solution)/shard_map/ppermute | solution.py:861
  38.5 6.0 %collective-permute-start.13 = (bf16[2,224,128]{2,1,0:T(8,128)(2,1)S(1)}, bf16[2,224,128]{2,1,0:T(8,128)(2,1)S(1)}, u32[]{:S(2)}, u32[]{:S(2)}) collective-permute-start(bf16[2,224,128]{2,1,0:T(8,128)(2,1)S(1)} %get-tuple-element.92), channel_id=1, source_target_pairs={{0,4},{4,0},{8,12},{12,8},{16,20},{20,16},{24,28},{28,24},{1,5},{5... | collective-permute-start | bytes 344072 | tf_op jit(solution)/shard_map/ppermute | solution.py:861
  40.1 7.1 %collective-permute-start.14 = (bf16[2,224,128]{2,1,0:T(8,128)(2,1)S(1)}, bf16[2,224,128]{2,1,0:T(8,128)(2,1)S(1)}, u32[]{:S(2)}, u32[]{:S(2)}) collective-permute-start(bf16[2,224,128]{2,1,0:T(8,128)(2,1)S(1)} %get-tuple-element.93), channel_id=1, source_target_pairs={{0,12},{4,8},{8,4},{12,0},{16,28},{20,24},{24,20},{28,16},{1,13},{... | collective-permute-start | bytes 344072 | tf_op jit(solution)/shard_map/ppermute | solution.py:861
  47.6 1.9 %collective-permute-start.15 = (bf16[2,8,80,128]{3,2,1,0:T(8,128)(2,1)S(1)}, bf16[2,8,80,128]{3,2,1,0:T(8,128)(2,1)S(1)}, u32[]{:S(2)}, u32[]{:S(2)}) collective-permute-start(bf16[2,8,80,128]{3,2,1,0:T(8,128)(2,1)S(1)} %grad_relay.1.far), channel_id=1, source_target_pairs={{0,1},{1,0},{2,3},{3,2},{4,5},{5,4},{6,7},{7,6},{8,9},{9,8},{10,11... | collective-permute-start | bytes 983048 | tf_op jit(solution)/shard_map/ppermute | solution.py:876
  47.6 1.9 %collective-permute-start.9 = (bf16[8,80,128]{2,1,0:T(8,128)(2,1)S(1)}, bf16[8,80,128]{2,1,0:T(8,128)(2,1)S(1)}, u32[]{:S(2)}, u32[]{:S(2)}) collective-permute-start(bf16[8,80,128]{2,1,0:T(8,128)(2,1)S(1)} %get-tuple-element.86), channel_id=1, source_target_pairs={{0,1},{1,0},{2,3},{3,2},{4,5},{5,4},{6,7},{7,6},{8,9},{9,8},{10,11... | collective-permute-start | bytes 491528 | tf_op jit(solution)/shard_map/ppermute | solution.py:838
  50.0 4.1 %collective-permute-start.16 = (bf16[2,80,128]{2,1,0:T(8,128)(2,1)S(1)}, bf16[2,80,128]{2,1,0:T(8,128)(2,1)S(1)}, u32[]{:S(2)}, u32[]{:S(2)}) collective-permute-start(bf16[2,80,128]{2,1,0:T(8,128)(2,1)S(1)} %get-tuple-element.96), channel_id=1, source_target_pairs={{0,4},{4,0},{1,5},{5,1},{2,6},{6,2},{3,7},{7,3},{8,12},{12,8},{9,1... | collective-permute-start | bytes 122888 | tf_op jit(solution)/shard_map/ppermute | solution.py:302
  51.6 6.3 %collective-permute-start.19 = (bf16[224,128]{1,0:T(8,128)(2,1)S(1)}, bf16[224,128]{1,0:T(8,128)(2,1)S(1)}, u32[]{:S(2)}, u32[]{:S(2)}) collective-permute-start(bf16[224,128]{1,0:T(8,128)(2,1)S(1)} %get-tuple-element.94.refs_1_), channel_id=1, source_target_pairs={{0,2},{1,3},{2,0},{3,1},{4,6},{5,7},{6,4},{7,5},{8,10},{9,11},{10,... | collective-permute-start | bytes 172040 | tf_op jit(solution)/shard_map/ppermute | solution.py:892
  54.2 6.3 %collective-permute-start.17 = (bf16[3,80,128]{2,1,0:T(8,128)(2,1)S(1)}, bf16[3,80,128]{2,1,0:T(8,128)(2,1)S(1)}, u32[]{:S(2)}, u32[]{:S(2)}) collective-permute-start(bf16[3,80,128]{2,1,0:T(8,128)(2,1)S(1)} %grad_third.1), channel_id=1, source_target_pairs={{0,24},{8,16},{16,8},{24,0},{1,25},{9,17},{17,9},{25,1},{2,26},{10... | collective-permute-start | bytes 184328 | tf_op jit(solution)/shard_map/ppermute | solution.py:311
  57.9 5.2 %collective-permute-start.20 = (bf16[224,128]{1,0:T(8,128)(2,1)S(1)}, bf16[224,128]{1,0:T(8,128)(2,1)S(1)}, u32[]{:S(2)}, u32[]{:S(2)}) collective-permute-start(bf16[224,128]{1,0:T(8,128)(2,1)S(1)} %add_across.1.refs_0_), channel_id=1, source_target_pairs={{0,16},{8,24},{16,0},{24,8},{1,17},{9,25},{17,1},{25,9},{2,18},{10... | collective-permute-start | bytes 172040 | tf_op jit(solution)/shard_map/ppermute | solution.py:916
  60.6 6.1 %collective-permute-start.18 = (bf16[4,80,128]{2,1,0:T(8,128)(2,1)S(1)}, bf16[4,80,128]{2,1,0:T(8,128)(2,1)S(1)}, u32[]{:S(2)}, u32[]{:S(2)}) collective-permute-start(bf16[4,80,128]{2,1,0:T(8,128)(2,1)S(1)} %get-tuple-element.101.refs_4_), channel_id=1, source_target_pairs={{0,8},{8,0},{16,24},{24,16},{1,9},{9,1},{17,25},{25,17},{2,10},{10... | collective-permute-start | bytes 245768 | tf_op jit(solution)/shard_map/ppermute | solution.py:319
  63.2 6.5 %collective-permute-start.23 = (bf16[240,128]{1,0:T(8,128)(2,1)S(1)}, bf16[240,128]{1,0:T(8,128)(2,1)S(1)}, u32[]{:S(2)}, u32[]{:S(2)}) collective-permute-start(bf16[240,128]{1,0:T(8,128)(2,1)S(1)} %finish_pieces.1.refs_0_), channel_id=1, source_target_pairs={{0,12},{4,8},{8,4},{12,0},{16,28},{20,24},{24,20},{28,16},{1,13},{... | collective-permute-start | bytes 184328 | tf_op jit(solution)/shard_map/ppermute | solution.py:861
  63.9 5.8 %collective-permute-start.22 = (bf16[240,128]{1,0:T(8,128)(2,1)S(1)}, bf16[240,128]{1,0:T(8,128)(2,1)S(1)}, u32[]{:S(2)}, u32[]{:S(2)}) collective-permute-start(bf16[240,128]{1,0:T(8,128)(2,1)S(1)} %finish_pieces.1.refs_0_), channel_id=1, source_target_pairs={{0,4},{4,0},{8,12},{12,8},{16,20},{20,16},{24,28},{28,24},{1,5},{5... | collective-permute-start | bytes 184328 | tf_op jit(solution)/shard_map/ppermute | solution.py:861
  64.9 4.9 %collective-permute-start.21 = (bf16[240,128]{1,0:T(8,128)(2,1)S(1)}, bf16[240,128]{1,0:T(8,128)(2,1)S(1)}, u32[]{:S(2)}, u32[]{:S(2)}) collective-permute-start(bf16[240,128]{1,0:T(8,128)(2,1)S(1)} %finish_pieces.1.refs_0_), channel_id=1, source_target_pairs={{0,8},{4,12},{8,0},{12,4},{16,24},{20,28},{24,16},{28,20},{1,9},{5... | collective-permute-start | bytes 184328 | tf_op jit(solution)/shard_map/ppermute | solution.py:861

commit v4 on v3

--- a/solution.py
+++ b/solution.py
@@ -20,7 +20,7 @@
     return jax.ShapeDtypeStruct(dims, kind)
 
 
-def call(kernel, outs, args, scratch=(), name=None, flops=0, aliases=None, far=False, after=()):
+def call(kernel, outs, args, scratch=(), name=None, flops=0, aliases=None, far=False, after=(), writes=0):
     count = len(args)
     if after:
         body, args = kernel, [*args, *after]
@@ -36,7 +36,9 @@
         kernel,
         out_shape=tuple(outs),
         in_specs=[pl.BlockSpec(memory_space=space) for space in spaces],
-        out_specs=tuple(pl.BlockSpec(memory_space=pltpu.VMEM) for _ in outs),
+        out_specs=tuple(
+            pl.BlockSpec(memory_space=pl.ANY if i < writes else pltpu.VMEM) for i in range(len(outs))
+        ),
         scratch_shapes=list(scratch),
         input_output_aliases=aliases or {},
         name=name,
@@ -123,8 +125,8 @@
     points = offset.shape[1]
     value = value_ref[...]
     total = jnp.zeros((rows, cols), F32)
-    row_hot = iota((rows, points), 0) + start == offset // cols
-    col_hot = (iota((cols, points), 0) == offset % cols).astype(BF)
+    row_hot = iota((rows, points), 0) + start == lax.shift_right_logical(offset, LANES.bit_length() - 1)
+    col_hot = (iota((cols, points), 0) == (offset & (LANES - 1))).astype(BF)
     for _ in range(3):
         part = value.astype(BF)
         value = value - part.astype(F32)
@@ -137,26 +139,63 @@
     scr[pl.ds(0, rows, stride=stride), :] = first + total
 
 
-def prepare_far(part, swap, count, *refs):
-    outs, (scr, row_scr, weights_scr, turn_scr, sems) = refs[count:-5], refs[-5:]
-    far_ref, tiles_ref, taps_ref, *outer = outs[: -count]
-    held = outs[-count:]
+def prepare_outer(swap, count, *refs):
+    outs, (row_scr, sems) = refs[count:-2], refs[-2:]
+    outer, held = outs[:-count], outs[-count:]
+    state_ref, mask_ref = held[0:2]
     copies = [pltpu.make_async_copy(refs[k], held[k], sems.at[k]) for k in range(count)]
-    for k in (4, 5, 6, 7, 0, 1, 2, 3, 8):
-        copies[k].start()
-    for k in range(4, 8):
-        copies[k].wait()
-    grad_ref, mask_ref, offset_ref, value_ref = held[0:4]
+    for copy in copies:
+        copy.start()
+    pad = outer[0].shape[1]
+    channels, rows, cols = state_ref.shape
+    half = rows // 2
+    lat = lax.axis_index("lat")
+    for c in range(channels, pad):
+        row_scr[pl.ds(c, 2 * DIL, stride=pad), :] = jnp.zeros((2 * DIL, cols), F32)
+    copies[1].wait()
+    copies[0].wait()
+    if swap:
+        start = aligned((1 - lat) * half)
+        mask = mask_ref[pl.ds(start, half), :].astype(F32)
+
+        def body(c, carry):
+            value = state_ref[c, pl.ds(start, half), :].astype(F32) * mask
+            row_scr[pl.ds(c, DIL, stride=pad), :] = jnp.where(
+                lat == 0, value[half - DIL :, :], value[0:DIL, :]
+            )
+            return carry
+
+    else:
+        mask = mask_ref[...].astype(F32)
+
+        def body(c, carry):
+            value = state_ref[c].astype(F32) * mask
+            row_scr[pl.ds(c, DIL, stride=pad), :] = value[0:DIL, :]
+            row_scr[pl.ds(DIL * pad + c, DIL, stride=pad), :] = value[rows - DIL :, :]
+            return carry
+
+    lax.fori_loop(0, channels, body, 0, unroll=5 if channels % 5 == 0 else 1)
+    for k, to in enumerate(outer):
+        for t in range(DIL):
+            at = (k * DIL + t) * pad
+            to[t] = row_scr[at : at + pad, :].astype(BF)
+    for copy in copies[2:]:
+        copy.wait()
+
+
+def prepare_far(part, *refs):
+    (mask_ref, grad_ref, offset_ref, value_ref), weights = refs[0:4], refs[4:8]
+    far_ref, tiles_ref, taps_ref = refs[8:11]
+    scr, weights_scr, turn_scr, pick_e, pick_p = refs[11:]
     channels, rows, cols = grad_ref.shape
     pad = taps_ref.shape[0]
-    pack_weights(part, pad, *held[4:8], weights_scr, taps_ref, turn_scr)
+    weight_picks(part, pad, weights_scr.shape[1], pick_e.shape[0], pick_e, pick_p)
+    pack_weights(part, pad, *weights, pick_e, pick_p, weights_scr, taps_ref, turn_scr)
     hid = weights_scr.shape[0]
     full = tiles_ref.shape[0]
     for t in range(full // hid):
         tiles_ref[t * hid : (t + 1) * hid, :] = weights_scr[:, t * LANES : (t + 1) * LANES]
     far_ref[0:full, :] = tiles_ref[...]
-    for k in range(0, 4):
-        copies[k].wait()
     half = rows // 2
     me = lax.axis_index("ch")
     start = aligned((1 - me // 2) * half)
@@ -177,26 +216,9 @@
         first = aligned((((me ^ (2 + k)) % 2) * count_rows) * pad)
         size = count_rows * pad
         far_ref[full + k * size : full + (k + 1) * size, :] = scr[pl.ds(first, size), :].astype(BF)
-    copies[8].wait()
-    state_ref = held[8]
-    state_mask = mask_ref[...].astype(F32)
-
-    def outer_rows(c, carry):
-        value = state_ref[c].astype(F32) * state_mask
-        row_scr[pl.ds(c, DIL, stride=pad), :] = value[0:DIL, :]
-        row_scr[pl.ds(DIL * pad + c, DIL, stride=pad), :] = value[rows - DIL :, :]
-        return carry
-
-    lax.fori_loop(0, channels, outer_rows, 0, unroll=5 if channels % 5 == 0 else 1)
-    for c in range(channels, pad):
-        row_scr[pl.ds(c, 2 * DIL, stride=pad), :] = jnp.zeros((2 * DIL, cols), F32)
-    for t in range(DIL):
-        low = row_scr[t * pad : (t + 1) * pad, :]
-        high = row_scr[(DIL + t) * pad : (DIL + t + 1) * pad, :]
-        emit_outer(low, high, t, swap, outer)
-
-
-def prepare_near(grad_ref, mask_ref, offset_ref, value_ref, tiles_ref, rows_ref, own_ref, core_ref, scr):
+
+
+def prepare_near(mask_ref, grad_ref, offset_ref, value_ref, tiles_ref, rows_ref, own_ref, core_ref, scr):
     rows, pad, cols = rows_ref.shape
     mask = mask_ref[...].astype(F32)
     to_rows(grad_ref, None, scr, pad)
@@ -211,6 +233,10 @@
         for r in range(count):
             at = full + r * pad
             to[at : at + pad, :] = rows_ref[(me ^ k) * count + r]
+
+
+def second_half(in_ref, out_ref):
+    out_ref[...] = in_ref[1]
 
 
 def relay(in_ref, out_ref):
@@ -340,23 +366,28 @@
     return (halo, from_left, from_right), ()
 
 
-def shifted_rows(block_ref, halo_ref, left_ref, right_ref, group):
+def padded_row(block_ref, halo_ref, at, e):
     rows = block_ref.shape[0]
-    at = pl.ds(aligned(group * 16), 16)
-    lane = iota((16, LANES), 1)
-    left = left_ref[(0, at) if two_by_four() else at].astype(F32)
+    if e < DIL:
+        return halo_ref[e, at, :]
+    if e < rows + DIL:
+        return block_ref[e - DIL, at, :]
+    return halo_ref[e - rows, at, :]
+
+
+def sides(left_ref, right_ref, at):
+    left = (left_ref[0, at, :] if two_by_four() else left_ref[at, :]).astype(F32)
     right = right_ref[at, :].astype(F32)
     if two_by_four():
         odd = odd_lon()
         left, right = jnp.where(odd, left, right), jnp.where(odd, right, left)
+    return left, right
+
+
+def shifted_rows(rows, read, left, right):
+    lane = iota((16, LANES), 1)
     for e in range(rows + 2 * DIL):
-        if e < DIL:
-            row = halo_ref[e, at, :]
-        elif e < rows + DIL:
-            row = block_ref[e - DIL, at, :]
-        else:
-            row = halo_ref[e - rows, at, :]
-        row = row.astype(F32)
+        row = read(e).astype(F32)
         west = jnp.where(
             lane < DIL, pltpu.roll(left, (-2 * e) % LANES, 1), pltpu.roll(row, DIL, 1)
         )
@@ -368,10 +399,9 @@
         yield e, (west, row, east)
 
 
-def stencil(block_ref, halo_ref, left_ref, right_ref, group, taps, north, emit):
-    rows = block_ref.shape[0]
+def stencil_rows(rows, read, left, right, taps, north, emit):
     sums = {}
-    for e, shifts in shifted_rows(block_ref, halo_ref, left_ref, right_ref, group):
+    for e, shifts in shifted_rows(rows, read, left, right):
         for a in (2, 1, 0):
             r = e - DIL * a
             if not 0 <= r < rows:
@@ -383,6 +413,13 @@
                 emit(r, sums.pop(r))
 
 
+def stencil(block_ref, halo_ref, left_ref, right_ref, group, taps, north, emit):
+    at = pl.ds(aligned(group * 16), 16)
+    left, right = sides(left_ref, right_ref, at)
+    read = functools.partial(padded_row, block_ref, halo_ref, at)
+    stencil_rows(block_ref.shape[0], read, left, right, taps, north, emit)
+
+
 def spread(tap_ref, group):
     values = tap_ref[pl.ds(aligned(group * 16), 16), :]
     return [
@@ -391,65 +428,94 @@
     ]
 
 
-def conv_forward(ones_row, block_ref, halo_ref, left_ref, right_ref, tap_ref, *rest):
-    quarters, scr = rest[:-1], rest[-1]
-    pad = block_ref.shape[1]
+def conv_forward(ones_row, away, block_ref, halo_ref, left_ref, right_ref, tap_ref, *rest):
+    same_ref, others, (row_scr, left_scr, right_scr, scr) = rest[0], rest[1:-4], rest[-4:]
+    rows, pad = block_ref.shape[:2]
+    half = rows // 2
+    me = lax.axis_index("ch")
+    upper = (me // 2 + away) % 2
+    west, east = sides(left_ref, right_ref, slice(None))
+    left_scr[...] = pltpu.roll(west, (LANES - 2 * half * upper) % LANES, 1)
+    right_scr[...] = pltpu.roll(east, (LANES - 2 * half * upper) % LANES, 1)
+    for t in range(DIL):
+        low, high = halo_ref[t].astype(F32), halo_ref[DIL + t].astype(F32)
+        before = block_ref[half - DIL + t].astype(F32)
+        behind = block_ref[half + t].astype(F32)
+        row_scr[t] = jnp.where(upper == 0, low, before).astype(BF)
+        row_scr[half + DIL + t] = jnp.where(upper == 0, behind, high).astype(BF)
+    for r in range(half):
+        row_scr[DIL + r] = block_ref[upper * half + r]
 
     def body(group, carry):
         taps = spread(tap_ref, group)
         is_one = iota((16, LANES), 0) + group * 16 == ones_row
+        at = pl.ds(aligned(group * 16), 16)
 
         def emit(r, value):
             value = jnp.where(is_one, 1.0, value)
-            scr[r, pl.ds(aligned(group * 16), 16), :] = value.astype(BF)
-
-        stencil(block_ref, halo_ref, left_ref, right_ref, group, taps, taps[2], emit)
+            scr[r, at, :] = value.astype(BF)
+
+        left, right = left_scr[at, :], right_scr[at, :]
+        stencil_rows(half, lambda e: row_scr[e, at, :], left, right, taps, taps[2], emit)
         return carry
 
     lax.fori_loop(0, pad // 16, body, 0)
-    me = lax.axis_index("ch")
-    count = quarters[0].shape[0]
-    for k, quarter in enumerate(quarters):
-        quarter[...] = scr[pl.ds((me ^ k) * count, count)]
+    count = half // 2
+    same_ref[...] = scr[pl.ds((me % 2) * count, count)]
+    other = (1 - me % 2) * count
+    size = count // len(others)
+    for k, to in enumerate(others):
+        to[...] = scr[pl.ds(other + k * size, size)]
 
 
 def conv_adjoint(
-    block_ref, halo_ref, left_ref, right_ref, tap_ref, cotan_ref, mask_ref, out_ref, mark_ref, scr
+    block_ref, halo_ref, left_ref, right_ref, tap_ref, cotan_ref, mask_ref, out_ref, mark_ref, scr, done_scr, sems
 ):
     rows, pad = block_ref.shape[:2]
+    channels = out_ref.shape[0]
     at_top = lax.axis_index("lat") == lax.axis_size("lat") - 1
     mask = mask_ref[...].astype(F32)
 
-    def body(group, carry):
+    def copy(group, count):
+        at = pl.ds(group * 16, count)
+        return pltpu.make_async_copy(done_scr.at[at], out_ref.at[at], sems.at[group])
+
+    def body(group, count):
         taps = spread(tap_ref, group)
         back = [[taps[2 - a][2 - b] for b in range(3)] for a in range(3)]
         north = [jnp.where(at_top, taps[2][b], back[2][b]) for b in range(3)]
 
         def emit(r, value):
             cotan = cotan_ref[r, pl.ds(aligned(group * 16), 16), :].astype(F32)
-            scr[pl.ds(pl.multiple_of(r * pad + group * 16, 16), 16), :] = (cotan + value) * mask[
-                r : r + 1, :
-            ]
+            scr[pl.ds(r, 16, stride=rows + 8), :] = (cotan + value) * mask[r : r + 1, :]
 
         stencil(block_ref, halo_ref, left_ref, right_ref, group, back, north, emit)
+        for c in range(count):
+            at = c * (rows + 8)
+            done_scr[group * 16 + c] = scr[at : at + rows, :].astype(BF)
+        copy(group, count).start()
+
+    whole = channels // 16
+
+    def each(group, carry):
+        body(group, 16)
         return carry
 
-    lax.fori_loop(0, pad // 16, body, 0)
-
-    def write(c, carry):
-        out_ref[c] = scr[pl.ds(c, rows, stride=pad), :].astype(BF)
-        return carry
-
-    channels = out_ref.shape[0]
-    lax.fori_loop(0, channels, write, 0, unroll=5 if channels % 5 == 0 else 1)
+    lax.fori_loop(0, whole, each, 0)
+    if channels % 16:
+        body(whole, channels % 16)
     mark_ref[...] = jnp.zeros(mark_ref.shape, F32)
+    for group in range(whole):
+        copy(group, 16).wait()
+    if channels % 16:
+        copy(whole, channels % 16).wait()
 
 
 def collect_grad(swap, own, near, far, passed, rows_ref, *rest):
     part_rows = own.shape[0]
     rows, pad = rows_ref.shape[:2]
     me = lax.axis_index("ch")
-    for k, quarter in enumerate((own, near, far.at[0], passed.at[1])):
+    for k, quarter in enumerate((own, near, far.at[0], passed)):
         rows_ref[pl.ds((me ^ k) * part_rows, part_rows)] = quarter[...]
     strips, outer = rest[:3], rest[3:]
     for t in range(DIL):
@@ -457,13 +523,28 @@
     emit_strips(lambda r: rows_ref[r], rows, pad, *strips)
 
 
-def kernel_gradient(grad_ref, block_ref, halo_ref, left_ref, right_ref, out_ref):
+def shift_columns(block_ref, halo_ref, left_ref, right_ref, west_ref, east_ref):
+    def body(group, carry):
+        at = pl.ds(aligned(group * 16), 16)
+        left, right = sides(left_ref, right_ref, at)
+        read = functools.partial(padded_row, block_ref, halo_ref, at)
+        for e, shifts in shifted_rows(block_ref.shape[0], read, left, right):
+            west_ref[e, at, :] = shifts[0].astype(BF)
+            east_ref[e, at, :] = shifts[2].astype(BF)
+        return carry
+
+    lax.fori_loop(0, block_ref.shape[1] // 16, body, 0)
+
+
+def kernel_gradient(grad_ref, block_ref, halo_ref, west_ref, east_ref, out_ref):
     rows, pad = grad_ref.shape[:2]
 
     def body(group, carry):
         at = pl.ds(aligned(group * 16), 16)
         sums = [[jnp.zeros((16, LANES), F32) for _ in range(3)] for _ in range(3)]
-        for e, shifts in shifted_rows(block_ref, halo_ref, left_ref, right_ref, group):
+        for e in range(rows + 2 * DIL):
+            middle = padded_row(block_ref, halo_ref, at, e)
+            shifts = [part.astype(F32) for part in (west_ref[e, at, :], middle, east_ref[e, at, :])]
             for a in range(3):
                 r = e - DIL * a
                 if 0 <= r < rows:
@@ -498,19 +579,32 @@
     return jnp.where(lane >= LANES, lane - LANES, jnp.where(lane >= low, lane - low + split, -1))
 
 
-def pack_weights(part, pad, expand_ref, bias_ref, project_ref, kernel_ref, out_ref, taps_ref, turn_scr):
+def weight_picks(part, pad, wide, channels, pick_e_ref, pick_p_ref):
+    split = 4 * pad // LANES * LANES
+    lane = iota((channels, wide), 1)
+    row = iota((channels, wide), 0)
+    pick_e_ref[...] = (channel_of(expand_slot(lane, pad), part, pad) == row).astype(BF)
+    slot = jnp.where(lane >= split, project_slot(lane - split, pad, split), -1)
+    pick_p_ref[...] = (channel_of(slot, part, pad) == row).astype(BF)
+
+
+def output_picks(part, pad, pick_e_ref, pick_p_ref):
+    channels, depth = pick_e_ref.shape
+    split = 4 * pad // LANES * LANES
+    lane, row = iota((channels, depth), 1), iota((channels, depth), 0)
+    pick_e_ref[...] = (channel_of(expand_slot(lane, pad), part, pad) == row).astype(BF)
+    pick_p_ref[...] = (channel_of(project_slot(lane, pad, split), part, pad) == row).astype(BF)
+
+
+def pack_weights(
+    part, pad, expand_ref, bias_ref, project_ref, kernel_ref, pick_e_ref, pick_p_ref, out_ref, taps_ref, turn_scr
+):
     hidden, channels = expand_ref.shape
     turn_scr[...] = jnp.zeros(turn_scr.shape, F32)
     for a in range(3):
         turn_scr[3 * a : 3 * a + 3, 0:part] = kernel_ref[a]
     taps_ref[...] = jnp.transpose(turn_scr[...])[0:pad, :]
     wide = out_ref.shape[1]
-    split = 4 * pad // LANES * LANES
-    lane = iota((channels, wide), 1)
-    row = iota((channels, wide), 0)
-    pick_e = (channel_of(expand_slot(lane, pad), part, pad) == row).astype(BF)
-    slot = jnp.where(lane >= split, project_slot(lane - split, pad, split), -1)
-    pick_p = (channel_of(slot, part, pad) == row).astype(BF)
     bias = bias_ref[...]
     parts = jnp.zeros((16, hidden), F32)
     at = iota((16, hidden), 0)
@@ -522,9 +616,9 @@
     pick_b = ((lane == row * pad + part) & (row < 3)).astype(BF)
     turned = (((0,), (0,)), ((), ()))
     packed = (
-        jnp.dot(expand_ref[...], pick_e, preferred_element_type=F32)
+        jnp.dot(expand_ref[...], pick_e_ref[...], preferred_element_type=F32)
         + lax.dot_general(parts.astype(BF), pick_b, turned, preferred_element_type=F32)
-        + jnp.dot(project_ref[...], pick_p, preferred_element_type=F32)
+        + jnp.dot(project_ref[...], pick_p_ref[...], preferred_element_type=F32)
     )
     rows = out_ref.shape[0]
     out_ref[0:hidden, :] = packed.astype(BF)
@@ -534,9 +628,9 @@
 GELU_C = math.sqrt(2.0 / math.pi)
 
 
-def activation_gradient(*refs):
+def activation_gradient(part, *refs):
     parts = refs[0:4]
-    act_ref, y_scr, w_scr, t_scr = refs[4:]
+    act_ref, y_scr, w_scr, t_scr, pick_e_ref, pick_p_ref = refs[4:]
     me = lax.axis_index("ch")
     tiles = w_scr.shape[1] // LANES
     hid = w_scr.shape[0] // 4
@@ -544,6 +638,7 @@
     part_rows = cells // LANES
     pad = (parts[0].shape[0] - tiles * hid) // part_rows
     split = 4 * pad // LANES * LANES
+    output_picks(part, pad, pick_e_ref, pick_p_ref)
     y_scr[0 : depth - 4 * pad, :] = jnp.zeros((depth - 4 * pad, cells), BF)
     for k, ref in enumerate(parts):
         for t in range(tiles):
@@ -569,26 +664,27 @@
 
 
 def hidden_gradient(*refs):
-    xs, (act_ref, y_ref, w_ref) = refs[0:4], refs[4:7]
-    pre_ref, keep_ref, send_ref, x_scr, value_scr = refs[7:]
+    xs, (act_ref, y_ref, w_ref) = refs[0:5], refs[5:8]
+    pre_ref, keep_ref, send_ref, x_scr, value_scr = refs[8:]
     part_rows, pad = xs[0].shape[:2]
     hid = w_ref.shape[0] // 4
     split = 4 * pad // LANES * LANES
     depth, cells = x_scr.shape
     me = lax.axis_index("ch")
     x_scr[4 * pad : depth, :] = jnp.zeros((depth - 4 * pad, cells), BF)
-    for k in range(4):
-        for r in range(part_rows):
-            x_scr[pl.ds(aligned((me ^ k) * pad), pad), r * LANES : (r + 1) * LANES] = xs[k][r]
+    for k, ref, first in ((0, 0, 0), (1, 1, 0), (1, 2, part_rows // 2), (2, 3, 0), (3, 4, 0)):
+        for r in range(xs[ref].shape[0]):
+            cols = slice((first + r) * LANES, (first + r + 1) * LANES)
+            x_scr[pl.ds(aligned((me ^ k) * pad), pad), cols] = xs[ref][r]
     step = 256
     for start in range(0, cells, step):
         cols = slice(start, start + step)
         hidden = jnp.dot(w_ref[:, 0:depth], x_scr[:, cols], preferred_element_type=F32)
         square = hidden * hidden
-        tanh = jnp.tanh(GELU_C * hidden * (1.0 + 0.044715 * square))
-        half = 0.5 * (1.0 + tanh)
-        slope = half + (0.5 * GELU_C) * hidden * (1.0 - tanh * tanh) * (
-            1.0 + (3 * 0.044715) * square
+        tanh = jnp.tanh(hidden * (GELU_C + (0.044715 * GELU_C) * square))
+        half = 0.5 + 0.5 * tanh
+        slope = half + hidden * (0.5 * GELU_C + (1.5 * 0.044715 * GELU_C) * square) * (
+            1.0 - tanh * tanh
         )
         value_scr[:, cols] = (hidden * half).astype(BF)
         pre_ref[:, cols] = (act_ref[:, cols] * slope).astype(BF)
@@ -599,32 +695,39 @@
     tiles = [expand[:, t * LANES : (t + 1) * LANES] for t in range(shared)]
     tiles.append(expand[:, split : split + LANES] + project[:, 0:LANES])
     tiles += [project[:, t * LANES : (t + 1) * LANES] for t in range(1, shared + 1)]
+    used = len(tiles) * hid
+    for ref in (keep_ref, send_ref):
+        for k in range(2):
+            ref[k, used:, :] = jnp.zeros((ref.shape[1] - used, LANES), ref.dtype)
     for k in range(4):
         to = send_ref if k % 2 else keep_ref
         for t, tile in enumerate(tiles):
             to[k // 2, t * hid : (t + 1) * hid, :] = tile[k * hid : (k + 1) * hid].astype(to.dtype)
 
 
-def conv_gradient(pre_ref, t_ref, *rest):
-    (own_ref, core_ref, far_ref), scr = rest[:-1], rest[-1]
-    outs = (own_ref, core_ref, far_ref.at[0], far_ref.at[1])
-    part_rows, pad = own_ref.shape[:2]
+def conv_gradient(away, pre_ref, t_ref, *rest):
+    outs, scr = rest[:-1], rest[-1]
+    if away:
+        outs = (rest[0].at[0], rest[0].at[1])
+    part_rows, pad = outs[0].shape[:2]
     me = lax.axis_index("ch")
+    first = ((me // 2 + away) % 2) * 2 * pad
+    weights = t_ref[pl.ds(aligned(first), 2 * pad), :]
     step = 256
     for start in range(0, pre_ref.shape[1], step):
         cols = slice(start, start + step)
-        scr[:, cols] = jnp.dot(t_ref[...], pre_ref[:, cols], preferred_element_type=F32).astype(BF)
+        scr[:, cols] = jnp.dot(weights, pre_ref[:, cols], preferred_element_type=F32).astype(BF)
     for k, to in enumerate(outs):
+        at = pl.ds(aligned(((me + k) % 2) * pad), pad)
         for r in range(part_rows):
-            to[r] = scr[pl.ds(aligned((me ^ k) * pad), pad), r * LANES : (r + 1) * LANES]
+            to[r] = scr[at, r * LANES : (r + 1) * LANES]
 
 
 def add_cores(keep_ref, got_ref, own_ref, *sends):
     piece = own_ref.shape[1]
-    step = piece - 32
     place = 2 * lax.axis_index("lat") + lax.axis_index("lon") % 2
     for k in range(4):
-        at = pl.ds(pl.multiple_of((place ^ k) * step, 32), piece)
+        at = pl.ds(aligned((place ^ k) * piece), piece)
         for group in range(2):
             total = keep_ref[group, at, :] + got_ref[group, at, :].astype(F32)
             to = sends[k - 1] if k else own_ref
@@ -652,21 +755,15 @@
     out_ref[piece:, :] = jnp.transpose(turn_scr[...])[0:TAP_ROWS, :].astype(BF)
 
 
-def write_parameters(part, pad, scale, hid, p0, p1, p2, p3, *rest):
+def write_parameters(part, pad, scale, hid, p0, p1, p2, p3, pick_e, pick_p, *rest):
     expand_ref, project_ref, bias_ref, taps_ref, all_scr, taps_scr = rest
     piece = p0.shape[0] - TAP_ROWS
-    step = piece - 32
     place = 2 * lax.axis_index("lat") + lax.axis_index("lon") % 2
     for k, ref in enumerate((p0, p1, p2, p3)):
         to = place ^ k
-        all_scr[pl.ds(pl.multiple_of(to * step, 32), step), :] = ref[0:step, :]
-
-        @pl.when(to == 3)
-        def _():
-            all_scr[4 * step : 4 * step + 32, :] = ref[step:piece, :]
-
+        all_scr[pl.ds(aligned(to * piece), piece), :] = ref[0:piece, :]
         taps_scr[pl.ds(aligned(to * TAP_ROWS), TAP_ROWS), :] = ref[piece:, :].astype(F32)
-    unpack(part, pad, scale, hid, all_scr, expand_ref, project_ref, bias_ref)
+    unpack(part, pad, scale, hid, all_scr, pick_e, pick_p, expand_ref, project_ref, bias_ref)
     total = taps_scr[0:TAP_ROWS, :]
     for k in range(1, 4):
         total = total + taps_scr[k * TAP_ROWS : (k + 1) * TAP_ROWS, :]
@@ -678,27 +775,25 @@
         taps_ref[a] = total[3 * a : 3 * a + 3, 0 : taps_ref.shape[2]] * scale
 
 
-def unpack(part, pad, scale, hid, all_ref, expand_ref, project_ref, bias_ref):
-    hidden, channels = expand_ref.shape
+def unpack(part, pad, scale, hid, all_ref, pick_e, pick_p, expand_ref, project_ref, bias_ref):
+    hidden = expand_ref.shape[0]
     split = 4 * pad // LANES * LANES
     shared = split // LANES
     tiles = [all_ref[t * hid : (t + 1) * hid, :] for t in range(2 * shared + 1)]
     depth = (shared + 1) * LANES
     expand = jnp.concatenate(tiles[: shared + 1], axis=1)
     project = jnp.concatenate(tiles[shared:], axis=1)
-    lane, row = iota((channels, depth), 1), iota((channels, depth), 0)
-    pick_e = (channel_of(expand_slot(lane, pad), part, pad) == row).astype(BF)
-    pick_p = (channel_of(project_slot(lane, pad, split), part, pad) == row).astype(BF)
     pick_b = (iota((16, depth), 1) == part).astype(BF)
     last = (((1,), (1,)), ((), ()))
     dot = functools.partial(lax.dot_general, dimension_numbers=last, preferred_element_type=F32)
-    expand_ref[...] = dot(expand, pick_e)[0:hidden, :] * scale
+    expand_ref[...] = dot(expand, pick_e[...])[0:hidden, :] * scale
     bias_ref[...] = dot(pick_b, expand)[0:1, 0:hidden] * scale
-    project_ref[...] = dot(project, pick_p)[0:hidden, :] * scale
-
-
-def unpack_whole(part, pad, scale, hid, all_ref, taps_in, expand_ref, project_ref, bias_ref, taps_ref, turn_scr):
-    unpack(part, pad, scale, hid, all_ref, expand_ref, project_ref, bias_ref)
+    project_ref[...] = dot(project, pick_p[...])[0:hidden, :] * scale
+
+
+def unpack_whole(part, pad, scale, hid, all_ref, taps_in, pick_e, pick_p, *rest):
+    expand_ref, project_ref, bias_ref, taps_ref, turn_scr = rest
+    unpack(part, pad, scale, hid, all_ref, pick_e, pick_p, expand_ref, project_ref, bias_ref)
     turn_scr[...] = jnp.zeros(turn_scr.shape, F32)
     turn_scr[0:pad, :] = taps_in[...]
     write_taps(jnp.transpose(turn_scr[...])[0:TAP_ROWS, :], scale, taps_ref)
@@ -738,110 +833,141 @@
 
     turn = pltpu.VMEM((LANES, LANES), F32)
 
-    def spread_parts(parts):
-        return [parts[0]] + [
-            lax.ppermute(parts[k], "ch", [(i, i ^ k) for i in range(n_ch)]) for k in (3, 2, 1)
-        ][::-1]
-
     tile_rows = wide // LANES * hid
+    sum_rows = (tile_rows + 63) // 64 * 64
     near_rows, far_rows = tile_rows + part_rows * pad, tile_rows + 2 * part_rows * pad
-    prepared = [
+    fetched = [
+        ocean_state,
+        land_mask,
         out_grad,
-        land_mask,
         swath_offset.reshape(1, -1),
         swath_value.reshape(1, -1),
         expand_weight.T,
         expand_bias.reshape(1, hidden),
         project_weight,
         depth_kernel,
-        ocean_state,
     ]
-    count = len(prepared)
-    to_far, tiles, taps, *rest = call(
-        functools.partial(prepare_far, part, swap, count),
-        [shape((far_rows, LANES), BF), shape((tile_rows, LANES), BF), shape((pad, LANES), F32)]
-        + outer_shapes(pad, swap)
-        + [shape(a.shape, a.dtype) for a in prepared],
-        prepared,
+    count = len(fetched)
+    outs = call(
+        functools.partial(prepare_outer, swap, count),
+        outer_shapes(pad, swap) + [shape(a.shape, a.dtype) for a in fetched],
+        fetched,
+        [pltpu.VMEM((2 * DIL * pad, cols), F32), pltpu.SemaphoreType.DMA((count,))],
+        "outer_rows",
+        far=True,
+    )
+    outer, (ocean_state, land_mask, *held) = outs[:-count], outs[-count:]
+    to_far, tiles, taps = call(
+        functools.partial(prepare_far, part),
+        [shape((far_rows, LANES), BF), shape((tile_rows, LANES), BF), shape((pad, LANES), F32)],
+        [land_mask, *held],
         [
             pltpu.VMEM((rows // 2 * pad, cols), F32),
-            pltpu.VMEM((2 * DIL * pad, cols), F32),
             pltpu.VMEM((hid, wide), BF),
             turn,
-            pltpu.SemaphoreType.DMA((count,)),
+            pltpu.VMEM((channels, wide), BF),
+            pltpu.VMEM((channels, wide), BF),
         ],
         "far_rows",
-        far=True,
-    )
-    outer, held = rest[:-count], rest[-count:]
-    land_mask, ocean_state = held[1], held[8]
+    )
     masked, *strips = call(
         prepare_state,
         [block] + strip_shapes(pad),
         [ocean_state, land_mask],
         [flat],
         "state_rows",
+        after=[taps],
     )
     cotan, own, to_core = call(
         prepare_near,
         [block, shape((near_rows, LANES), BF), shape((near_rows, LANES), BF)],
-        [*held[0:4], tiles],
+        [land_mask, *held[0:3], tiles],
         [flat],
         "cotan_rows",
-        after=[masked],
     )
     around, _ = exchange_halo(rows, strips, outer, swap, "state", after=[to_core])
     from_far = lax.ppermute(to_far, "ch", across)
-    conv_parts = call(
-        functools.partial(conv_forward, part),
-        [quarter] * 4,
-        [masked, *around, taps],
-        [pltpu.VMEM((rows, pad, cols), BF)],
-        "conv_forward",
-    )
-    all_conv = spread_parts(conv_parts)
+    ones = functools.partial(conv_forward, part)
+    conv_operands = [masked, *around, taps]
+    conv_scratch = [
+        pltpu.VMEM((rows // 2 + 2 * DIL, pad, cols), BF),
+        pltpu.VMEM((pad, LANES), F32),
+        pltpu.VMEM((pad, LANES), F32),
+        pltpu.VMEM((rows // 2, pad, cols), BF),
+    ]
+    conv_far = call(
+        functools.partial(ones, 1), [quarter] * 2, conv_operands, conv_scratch, "conv_away"
+    )
+    eighth = shape((part_rows // 2, pad, cols), BF)
+    conv_own, *conv_core = call(
+        functools.partial(ones, 0),
+        [quarter, eighth, eighth],
+        conv_operands,
+        conv_scratch,
+        "conv_here",
+        after=conv_far[:1],
+    )
+    both = [(i, i ^ 3) for i in range(n_ch)]
+    all_conv = [
+        conv_own,
+        *[lax.ppermute(piece, "ch", core) for piece in conv_core],
+        lax.ppermute(conv_far[0], "ch", across),
+        lax.ppermute(conv_far[1], "ch", both),
+    ]
     from_far = call(
-        relay, [from_far], [from_far], (), "cotan_relay", aliases={0: 0}, after=conv_parts[:1]
+        relay, [from_far], [from_far], (), "cotan_relay", aliases={0: 0}, after=around[1:2]
     )[0]
     passed = lax.ppermute(from_far, "ch", core)
-    act_grad, cotan_all, weights_all, weights_turned = call(
-        activation_gradient,
+    padded = shape((rows + 2 * DIL, pad, cols), BF)
+    shifted = call(shift_columns, [padded, padded], [masked, *around], (), "shift_columns")
+    act_grad, cotan_all, weights_all, weights_turned, *picks = call(
+        functools.partial(activation_gradient, part),
         [
             shape((n_ch * hid, cells), F32),
             shape((depth, cells), BF),
             shape((n_ch * hid, wide), BF),
             shape((depth, n_ch * hid), BF),
+            shape((channels, depth), BF),
+            shape((channels, depth), BF),
         ],
         [own, lax.ppermute(to_core, "ch", core), from_far, passed],
         (),
         "activation_gradient",
+        after=shifted[:1],
     )
     pre_grad, keep, send = call(
         hidden_gradient,
         [
             shape((n_ch * hid, cells), BF),
-            shape((2, tile_rows, LANES), F32),
-            shape((2, tile_rows, LANES), BF),
+            shape((2, sum_rows, LANES), F32),
+            shape((2, sum_rows, LANES), BF),
         ],
         [*all_conv, act_grad, cotan_all, weights_all],
         [pltpu.VMEM((depth, cells), BF), pltpu.VMEM((n_ch * hid, cells), BF)],
         "hidden_gradient",
     )
     got = lax.ppermute(send, "ch", core)
-    grad_own, grad_core, grad_far = call(
-        conv_gradient,
-        [quarter, quarter, shape((2, part_rows, pad, cols), BF)],
+    grad_scratch = [pltpu.VMEM((2 * pad, cells), BF)]
+    grad_far = call(
+        functools.partial(conv_gradient, 1),
+        [shape((2, part_rows, pad, cols), BF)],
         [pre_grad, weights_turned],
-        [pltpu.VMEM((depth, cells), BF)],
-        "conv_gradient",
+        grad_scratch,
+        "gradient_away",
+    )[0]
+    grad_own, grad_core = call(
+        functools.partial(conv_gradient, 0),
+        [quarter] * 2,
+        [pre_grad, weights_turned],
+        grad_scratch,
+        "gradient_here",
+        after=[grad_far],
     )
     grad_near = lax.ppermute(grad_core, "ch", core)
     grad_far = lax.ppermute(grad_far, "ch", across)
-    staged = two_by_four() and tile_rows % 32 == 0
+    staged = two_by_four()
     if staged:
-        step = (tile_rows - 32) // 128 * 32
-        piece = step + 32
-        assert 3 * step + piece == tile_rows
+        piece = sum_rows // 4
         mine, *sends = call(
             add_cores,
             [shape((2, piece, LANES), F32)] + [shape((2, piece, LANES), BF)] * 3,
@@ -866,21 +992,22 @@
             [mine, *over_plane(sends)],
             (),
             "add_pieces",
+            after=[grad_near],
         )
-        grad_far = call(
-            relay, [grad_far], [grad_far], (), "grad_relay", aliases={0: 0}, after=[other]
-        )[0]
+    passed = call(
+        second_half, [quarter], [grad_far], (), "grad_half", after=[other] if staged else []
+    )[0]
     conv_grad, *grad_strips = call(
         functools.partial(collect_grad, swap),
         [block] + strip_shapes(pad) + outer_shapes(pad, swap),
-        [grad_own, grad_near, grad_far, lax.ppermute(grad_far, "ch", core)],
+        [grad_own, grad_near, grad_far, lax.ppermute(passed, "ch", core)],
         (),
         "grad_rows",
     )
     kernel_part = call(
         kernel_gradient,
         [shape((pad, LANES), BF)],
-        [conv_grad, masked, *around],
+        [conv_grad, masked, around[0], *shifted],
         (),
         "kernel_gradient",
     )[0]
@@ -897,8 +1024,13 @@
         conv_adjoint,
         [shape((part, rows, cols), BF), shape((8, LANES), F32)],
         [conv_grad, *grad_around, taps, cotan, land_mask],
-        [flat],
+        [
+            pltpu.VMEM((16 * (rows + 8), cols), F32),
+            pltpu.VMEM((part, rows, cols), BF),
+            pltpu.SemaphoreType.DMA((-(-part // 16),)),
+        ],
         "conv_adjoint",
+        writes=1,
     )
     outs = [
         shape((hidden, channels), F32),
@@ -924,8 +1056,8 @@
         expand_grad, project_grad, bias_grad, kernel_grad = call(
             functools.partial(write_parameters, part, pad, scale, hid),
             outs,
-            [summed, *over_plane([summed] * 3)],
-            [pltpu.VMEM((tile_rows, LANES), BF), pltpu.VMEM((4 * TAP_ROWS, LANES), F32)],
+            [summed, *over_plane([summed] * 3), *picks],
+            [pltpu.VMEM((sum_rows, LANES), BF), pltpu.VMEM((4 * TAP_ROWS, LANES), F32)],
             "write_parameters",
             after=[mark],
         )
@@ -936,7 +1068,7 @@
         expand_grad, project_grad, bias_grad, kernel_grad = call(
             functools.partial(unpack_whole, part, pad, scale, hid),
             outs,
-            [total.astype(BF), kernel_sum],
+            [total.astype(BF), kernel_sum, *picks],
             [turn],
             "write_parameters",
         )

time: 71 us -> 68.9 us (0.970)
  waiting for transfers between devices: 23.3 us -> 21 us
    ppermute x1, waiting for transfers between devices: 1.35 us -> 0.01 us  [on_device(): grad_near = lax.ppermute(grad_core, 'ch', core)]
    ppermute x4 -> x5, waiting for transfers between devices: 6.69 us -> 5.49 us  [the longest x1 3.76 us: on_device(): lax.ppermute(conv_far[0], 'ch', across)]
    pallas_call x21 -> x25, Pallas kernels: 19.1 us -> 19.7 us  [call(): pl.pallas_call(kernel, out_shape=tuple(outs), in_specs=[pl.BlockSpec(memo...]
    ppermute x4 -> x5, starting transfers between devices: 1.88 us -> 2.4 us  [the longest x1 1.62 us: on_device(): lax.ppermute(conv_far[0], 'ch', across)]
  transfers between devices with their start and end apart: 24 -> 25, of which waited for: 14 -> 14; matrix products, arithmetic and copies ran while one was open for 0% -> 0% of each run, Pallas kernels for 15% -> 17%
where the time goes in v4:
time: 68.9 us; the launch traced here: 68.7 us
  starting transfers between devices  27.2 us (39%)
  waiting for transfers between devices  21 us (30%)
  Pallas kernels  19.7 us (29%)
  between operations  0.87 us (1%)
    pallas_call x25, Pallas kernels, call(): pl.pallas_call(kernel, out_shape=tuple(outs), in_specs=[pl.BlockSpec(memo...  19.7 us
    ppermute x2, starting transfers between devices, exchange_halo(): lax.ppermute(third_out, 'lon', [(lon, lon ^ 3) for lon in range(n_lon)])  7.34 us
    ppermute x6, starting transfers between devices, over_plane(): lax.ppermute(values[k - 1], ('lon', 'lat'), turn_plane(k))  7.07 us
    ppermute x6, waiting for transfers between devices, over_plane(): lax.ppermute(values[k - 1], ('lon', 'lat'), turn_plane(k))  4.99 us
    ppermute x2, waiting for transfers between devices, exchange_halo(): lax.ppermute(third_out, 'lon', [(lon, lon ^ 3) for lon in range(n_lon)])  4.42 us
    ppermute x2, waiting for transfers between devices, exchange_halo(): got = lax.ppermute(first, 'lon', [(lon, lon ^ 1) for lon in range(n_lon)])  3.77 us
    ppermute x1, waiting for transfers between devices, on_device(): lax.ppermute(conv_far[0], 'ch', across)  3.76 us
    ppermute x2, starting transfers between devices, exchange_halo(): got = lax.ppermute(outer[0], 'lat', [(0, 1), (1, 0)])  3.11 us
  transfers between devices with their start and end apart: 25, of which 14 were waited for; matrix products, arithmetic and copies ran while one was open for 0% of the time, Pallas kernels for 17%

profile of v4, /device:TPU:0, one launch (start us, length us, event | category | flops | bytes accessed | tf_op | source)
XLA Modules:
  0.0 68.7 jit_solution(12938759546717147154)
XLA Ops:
  0.6 1.5 %outer_rows.1 = (bf16[2,80,128]{2,1,0:T(8,128)(2,1)S(1)}, bf16[75,32,128]{2,1,0:T(8,128)(2,1)S(1)}, s32[32,128]{1,0:T(8,128)S(1)}, bf16[75,32,128]{2,1,0:T(8,128...) custom-call(bf16[75,32,128]{2,1,0:T(8,128)(2,1)} %refs_0_.1, ...), custom_call_target="tpu_custom_call" | custom-call | bytes 2906120 | tf_op jit(solution)/shard_map/outer_rows/pallas_call | solution.py:35
  2.1 1.3 %far_rows.1 = (bf16[2080,128]{1,0:T(8,128)(2,1)S(1)}, bf16[800,128]{1,0:T(8,128)(2,1)S(1)}, f32[80,128]{1,0:T(8,128)S(1)}) custom-call(s32[32,128]{1,0:T(8,128)S(1)} %get-tuple-element.67.refs_0_.refs_1_.mask_ref, bf16[75,32,128]{2,1,0:T(8,128)(2,1)S(1)} %get-tuple-element.68.refs_1_.grad_ref, s32[1,512]{1,0:T(1,128)S(1)} %get-tuple-element.69.refs_2_.offset_ref, ...), custom_call_target="tpu_custom_call" | custom-call | bytes 1596420 | tf_op jit(solution)/shard_map/far_rows/pallas_call | solution.py:35
  3.4 3.0 %collective-permute-start.8 = (bf16[2080,128]{1,0:T(8,128)(2,1)S(1)}, bf16[2080,128]{1,0:T(8,128)(2,1)S(1)}, u32[]{:S(2)}, u32[]{:S(2)}) collective-permute-start(bf16[2080,128]{1,0:T(8,128)(2,1)S(1)} %get-tuple-element.92), channel_id=1, source_target_pairs={{0,2},{1,3},{2,0},{3,1},{4,6},{5,7},{6,4},{7,5},{8,10},{9,11},{10,... | collective-permute-start | bytes 1597448 | tf_op jit(solution)/shard_map/ppermute | solution.py:889
  6.4 1.5 %collective-permute-start = (bf16[2,80,128]{2,1,0:T(8,128)(2,1)S(1)}, bf16[2,80,128]{2,1,0:T(8,128)(2,1)S(1)}, u32[]{:S(2)}, u32[]{:S(2)}) collective-permute-start(bf16[2,80,128]{2,1,0:T(8,128)(2,1)S(1)} %get-tuple-element.77), channel_id=1, source_target_pairs={{0,4},{4,0},{1,5},{5,1},{2,6},{6,2},{3,7},{7,3},{8,12},{12,8},{9,1... | collective-permute-start | bytes 122888 | tf_op jit(solution)/shard_map/ppermute | solution.py:328
  7.9 0.8 %cotan_rows.1 = (bf16[32,80,128]{2,1,0:T(8,128)(2,1)S(1)}, bf16[1440,128]{1,0:T(8,128)(2,1)S(1)}, bf16[1440,128]{1,0:T(8,128)(2,1)S(1)}) custom-call(s32[32,128]{1,0:T(8,128)S(1)} %get-tuple-element.67.refs_0_.refs_1_.mask_ref, bf16[75,32,128]{2,1,0:T(8,128)(2,1)S(1)} %get-tuple-element.68.refs_1_.grad_ref, ...), custom_call_target="tpu_custom_call" | custom-call | bytes 2232320 | tf_op jit(solution)/shard_map/cotan_rows/pallas_call | solution.py:35
  8.7 1.0 %state_rows.1 = (bf16[32,80,128]{2,1,0:T(8,128)(2,1)S(1)}, bf16[2,80,128]{2,1,0:T(8,128)(2,1)S(1)}, bf16[80,128]{1,0:T(8,128)(2,1)S(1)}, bf16[80,128]{1,0:T(8,128)(2,1)S(1)}) custom-call(bf16[75,32,128]{2,1,0:T(8,128)(2,1)S(1)} %get-tuple-element.66.refs_0_, s32[32,128]{1,0:T(8,128)S(1)} %get-tuple-element.67.refs_0_.refs_1_.mask_ref, ...), custom_call_target="tpu_custom_call" | custom-call | bytes 1409024 | tf_op jit(solution)/shard_map/state_rows/pallas_call | solution.py:35
  10.5 3.7 %collective-permute-start.1 = (bf16[3,80,128]{2,1,0:T(8,128)(2,1)S(1)}, bf16[3,80,128]{2,1,0:T(8,128)(2,1)S(1)}, u32[]{:S(2)}, u32[]{:S(2)}) collective-permute-start(bf16[3,80,128]{2,1,0:T(8,128)(2,1)S(1)} %state_third.1), channel_id=1, source_target_pairs={{0,24},{8,16},{16,8},{24,0},{1,25},{9,17},{17,9},{25,1},{2,26},{10... | collective-permute-start | bytes 184328 | tf_op jit(solution)/shard_map/ppermute | solution.py:337
  14.2 2.4 %collective-permute-done.1.third_ref = bf16[3,80,128]{2,1,0:T(8,128)(2,1)S(1)} collective-permute-done((bf16[3,80,128]{2,1,0:T(8,128)(2,1)S(1)}, bf16[3,80,128]{2,1,0:T(8,128)(2,1)S(1)}, u32[]{:S(2)}, u32[]{:S(2)}) %collective-permute-start.1) | collective-permute-done | bytes 61472 | tf_op jit(solution)/shard_map/ppermute | solution.py:337
  16.8 3.8 %collective-permute-done.2.left_ref.refs_2_.refs_1_ = bf16[1,80,128]{2,1,0:T(8,128)(2,1)S(1)} collective-permute-done((bf16[1,80,128]{2,1,0:T(8,128)(2,1)S(1)}, bf16[1,80,128]{2,1,0:T(8,128)(2,1)S(1)}, u32[]{:S(2)}, u32[]{:S(2)}) %collective-permute-start.2) | collective-permute-done | bytes 20512 | tf_op jit(solution)/shard_map/ppermute | solution.py:345
  21.1 1.3 %conv_away.1 = (bf16[8,80,128]{2,1,0:T(8,128)(2,1)S(1)}, bf16[8,80,128]{2,1,0:T(8,128)(2,1)S(1)}) custom-call(bf16[32,80,128]{2,1,0:T(8,128)(2,1)S(1)} %get-tuple-element.76.block_ref.refs_0_, bf16[4,80,128]{2,1,0:T(8,128)(2,1)S(1)} %get-tuple-element.83.halo_ref.refs_1_, bf16[1,80,128]{2,1,0:T(8,128)(2,1)S(1)} %collective-permute-done.2.left_ref.refs_2_.refs_1_, ...), custom_call_target="tpu_custom_call" | custom-call | bytes 1146880 | tf_op jit(solution)/shard_map/conv_away/pallas_call | solution.py:35
  22.5 1.6 %collective-permute-start.5 = (bf16[8,80,128]{2,1,0:T(8,128)(2,1)S(1)}, bf16[8,80,128]{2,1,0:T(8,128)(2,1)S(1)}, u32[]{:S(2)}, u32[]{:S(2)}) collective-permute-start(bf16[8,80,128]{2,1,0:T(8,128)(2,1)S(1)} %get-tuple-element.86.refs_5_), channel_id=1, source_target_pairs={{0,2},{1,3},{2,0},{3,1},{4,6},{5,7},{6,4},{7,5},{8,10},{9,11},{10,... | collective-permute-start | bytes 491528 | tf_op jit(solution)/shard_map/ppermute | solution.py:914
  24.1 1.3 %conv_here.1 = (bf16[8,80,128]{2,1,0:T(8,128)(2,1)S(1)}, bf16[4,80,128]{2,1,0:T(8,128)(2,1)S(1)}, bf16[4,80,128]{2,1,0:T(8,128)(2,1)S(1)}) custom-call(bf16[32,80,128]{2,1,0:T(8,128)(2,1)S(1)} %get-tuple-element.76.block_ref.refs_0_, bf16[4,80,128]{2,1,0:T(8,128)(2,1)S(1)} %get-tuple-element.83.halo_ref.refs_1_, ...), custom_call_target="tpu_custom_call" | custom-call | bytes 1310720 | tf_op jit(solution)/shard_map/conv_here/pallas_call | solution.py:35
  26.0 1.2 %shift_columns.1 = (bf16[36,80,128]{2,1,0:T(8,128)(2,1)S(1)}, bf16[36,80,128]{2,1,0:T(8,128)(2,1)S(1)}) custom-call(bf16[32,80,128]{2,1,0:T(8,128)(2,1)S(1)} %get-tuple-element.76.block_ref.refs_0_, bf16[4,80,128]{2,1,0:T(8,128)(2,1)S(1)} %get-tuple-element.83.halo_ref.refs_1_, bf16[1,80,128]{2,1,0:T(8,128)(2,1)S(1)} %collective-permute-done.2.left_ref.refs_2_.refs_1_, ...), custom_call_target="tpu_custom_call" | custom-call | bytes 2252800 | tf_op jit(solution)/shard_map/shift_columns/pallas_call | solution.py:35
  27.2 1.1 %activation_gradient.1 = (f32[640,1024]{1,0:T(8,128)S(1)}, bf16[384,1024]{1,0:T(8,128)(2,1)S(1)}, bf16[640,640]{1,0:T(8,128)(2,1)S(1)}, bf16[384,640]{1,0:T(8,12...) custom-call(bf16[1440,128]{1,0:T(8,128)(2,1)S(1)} %get-tuple-element.91.refs_0_, ...), custom_call_target="tpu_custom_call" | custom-call | bytes 7718912 | tf_op jit(solution)/shard_map/activation_gradient/pallas_call | solution.py:35
  28.7 3.8 %collective-permute-done.5.refs_3_ = bf16[8,80,128]{2,1,0:T(8,128)(2,1)S(1)} collective-permute-done((bf16[8,80,128]{2,1,0:T(8,128)(2,1)S(1)}, bf16[8,80,128]{2,1,0:T(8,128)(2,1)S(1)}, u32[]{:S(2)}, u32[]{:S(2)}) %collective-permute-start.5) | collective-permute-done | bytes 163872 | tf_op jit(solution)/shard_map/ppermute | solution.py:914
  32.5 3.4 %hidden_gradient.1 = (bf16[640,1024]{1,0:T(8,128)(2,1)S(1)}, f32[2,832,128]{2,1,0:T(8,128)S(1)}, bf16[2,832,128]{2,1,0:T(8,128)(2,1)S(1)}) custom-call(bf16[8,80,128]{2,1,0:T(8,128)(2,1)S(1)} %get-tuple-element.87.refs_0_, bf16[4,80,128]{2,1,0:T(8,128)(2,1)S(1)} %collective-permute-done.3.refs_1_, bf16[4,80,128]{2,1,0:T(8,128)(2,1)S(1)} %collective-permute-done.4.refs_2_, ...), custom_call_target="tpu_custom_call" | custom-call | bytes 7471104 | tf_op jit(solution)/shard_map/hidden_gradient/pallas_call | solution.py:35
  37.8 0.8 %collective-permute-start.13 = (bf16[2,208,128]{2,1,0:T(8,128)(2,1)S(1)}, bf16[2,208,128]{2,1,0:T(8,128)(2,1)S(1)}, u32[]{:S(2)}, u32[]{:S(2)}) collective-permute-start(bf16[2,208,128]{2,1,0:T(8,128)(2,1)S(1)} %get-tuple-element.104), channel_id=1, source_target_pairs={{0,8},{4,12},{8,0},{12,4},{16,24},{20,28},{24,16},{28,20},{1,9},{5... | collective-permute-start | bytes 319496 | tf_op jit(solution)/shard_map/ppermute | solution.py:987
  38.6 1.5 %collective-permute-start.14 = (bf16[2,208,128]{2,1,0:T(8,128)(2,1)S(1)}, bf16[2,208,128]{2,1,0:T(8,128)(2,1)S(1)}, u32[]{:S(2)}, u32[]{:S(2)}) collective-permute-start(bf16[2,208,128]{2,1,0:T(8,128)(2,1)S(1)} %get-tuple-element.105), channel_id=1, source_target_pairs={{0,4},{4,0},{8,12},{12,8},{16,20},{20,16},{24,28},{28,24},{1,5},{5... | collective-permute-start | bytes 319496 | tf_op jit(solution)/shard_map/ppermute | solution.py:987
  40.1 1.2 %collective-permute-start.15 = (bf16[2,208,128]{2,1,0:T(8,128)(2,1)S(1)}, bf16[2,208,128]{2,1,0:T(8,128)(2,1)S(1)}, u32[]{:S(2)}, u32[]{:S(2)}) collective-permute-start(bf16[2,208,128]{2,1,0:T(8,128)(2,1)S(1)} %get-tuple-element.106), channel_id=1, source_target_pairs={{0,12},{4,8},{8,4},{12,0},{16,28},{20,24},{24,20},{28,16},{1,13},{... | collective-permute-start | bytes 319496 | tf_op jit(solution)/shard_map/ppermute | solution.py:987
  41.4 2.2 %collective-permute-done.13.refs_1_ = bf16[2,208,128]{2,1,0:T(8,128)(2,1)S(1)} collective-permute-done((bf16[2,208,128]{2,1,0:T(8,128)(2,1)S(1)}, bf16[2,208,128]{2,1,0:T(8,128)(2,1)S(1)}, u32[]{:S(2)}, u32[]{:S(2)}) %collective-permute-start.13) | collective-permute-done | bytes 106528 | tf_op jit(solution)/shard_map/ppermute | solution.py:987
  43.5 1.3 %collective-permute-done.14.refs_2_ = bf16[2,208,128]{2,1,0:T(8,128)(2,1)S(1)} collective-permute-done((bf16[2,208,128]{2,1,0:T(8,128)(2,1)S(1)}, bf16[2,208,128]{2,1,0:T(8,128)(2,1)S(1)}, u32[]{:S(2)}, u32[]{:S(2)}) %collective-permute-start.14) | collective-permute-done | bytes 106528 | tf_op jit(solution)/shard_map/ppermute | solution.py:987
  44.9 1.5 %collective-permute-done.15.refs_3_ = bf16[2,208,128]{2,1,0:T(8,128)(2,1)S(1)} collective-permute-done((bf16[2,208,128]{2,1,0:T(8,128)(2,1)S(1)}, bf16[2,208,128]{2,1,0:T(8,128)(2,1)S(1)}, u32[]{:S(2)}, u32[]{:S(2)}) %collective-permute-start.15) | collective-permute-done | bytes 106528 | tf_op jit(solution)/shard_map/ppermute | solution.py:987
  46.7 1.4 %collective-permute-done.16.passed = bf16[8,80,128]{2,1,0:T(8,128)(2,1)S(1)} collective-permute-done((bf16[8,80,128]{2,1,0:T(8,128)(2,1)S(1)}, bf16[8,80,128]{2,1,0:T(8,128)(2,1)S(1)}, u32[]{:S(2)}, u32[]{:S(2)}) %collective-permute-start.16) | collective-permute-done | bytes 163872 | tf_op jit(solution)/shard_map/ppermute | solution.py:1003
  48.5 1.6 %collective-permute-start.17 = (bf16[2,80,128]{2,1,0:T(8,128)(2,1)S(1)}, bf16[2,80,128]{2,1,0:T(8,128)(2,1)S(1)}, u32[]{:S(2)}, u32[]{:S(2)}) collective-permute-start(bf16[2,80,128]{2,1,0:T(8,128)(2,1)S(1)} %get-tuple-element.109), channel_id=1, source_target_pairs={{0,4},{4,0},{1,5},{5,1},{2,6},{6,2},{3,7},{7,3},{8,12},{12,8},{9,1... | collective-permute-start | bytes 122888 | tf_op jit(solution)/shard_map/ppermute | solution.py:328
  50.7 1.2 %kernel_gradient.1.refs_0_.refs_2_ = bf16[80,128]{1,0:T(8,128)(2,1)S(1)} custom-call(bf16[32,80,128]{2,1,0:T(8,128)(2,1)S(1)} %get-tuple-element.108.grad_ref.block_ref, bf16[32,80,128]{2,1,0:T(8,128)(2,1)S(1)} %get-tuple-element.76.block_ref.refs_0_, bf16[4,80,128]{2,1,0:T(8,128)(2,1)S(1)} %get-tuple-element.83.halo_ref.refs_1_, ...), custom_call_target="tpu_custom_call" | custom-call | bytes 2887680 | tf_op jit(solution)/shard_map/kernel_gradient/pallas_call | solution.py:35
  52.7 3.7 %collective-permute-start.18 = (bf16[3,80,128]{2,1,0:T(8,128)(2,1)S(1)}, bf16[3,80,128]{2,1,0:T(8,128)(2,1)S(1)}, u32[]{:S(2)}, u32[]{:S(2)}) collective-permute-start(bf16[3,80,128]{2,1,0:T(8,128)(2,1)S(1)} %grad_third.1), channel_id=1, source_target_pairs={{0,24},{8,16},{16,8},{24,0},{1,25},{9,17},{17,9},{25,1},{2,26},{10... | collective-permute-start | bytes 184328 | tf_op jit(solution)/shard_map/ppermute | solution.py:337
  57.1 2.0 %collective-permute-done.18.third_ref.refs_3_ = bf16[3,80,128]{2,1,0:T(8,128)(2,1)S(1)} collective-permute-done((bf16[3,80,128]{2,1,0:T(8,128)(2,1)S(1)}, bf16[3,80,128]{2,1,0:T(8,128)(2,1)S(1)}, u32[]{:S(2)}, u32[]{:S(2)}) %collective-permute-start.18) | collective-permute-done | bytes 61472 | tf_op jit(solution)/shard_map/ppermute | solution.py:337
  59.3 1.6 %collective-permute-start.19 = (bf16[4,80,128]{2,1,0:T(8,128)(2,1)S(1)}, bf16[4,80,128]{2,1,0:T(8,128)(2,1)S(1)}, u32[]{:S(2)}, u32[]{:S(2)}) collective-permute-start(bf16[4,80,128]{2,1,0:T(8,128)(2,1)S(1)} %get-tuple-element.115.refs_4_), channel_id=1, source_target_pairs={{0,8},{8,0},{16,24},{24,16},{1,9},{9,1},{17,25},{25,17},{2,10},{10... | collective-permute-start | bytes 245768 | tf_op jit(solution)/shard_map/ppermute | solution.py:345
  62.5 0.8 %collective-permute-start.23 = (bf16[224,128]{1,0:T(8,128)(2,1)S(1)}, bf16[224,128]{1,0:T(8,128)(2,1)S(1)}, u32[]{:S(2)}, u32[]{:S(2)}) collective-permute-start(bf16[224,128]{1,0:T(8,128)(2,1)S(1)} %finish_pieces.1.refs_0_), channel_id=1, source_target_pairs={{0,4},{4,0},{8,12},{12,8},{16,20},{20,16},{24,28},{28,24},{1,5},{5... | collective-permute-start | bytes 172040 | tf_op jit(solution)/shard_map/ppermute | solution.py:987
  63.3 1.9 %collective-permute-start.22 = (bf16[224,128]{1,0:T(8,128)(2,1)S(1)}, bf16[224,128]{1,0:T(8,128)(2,1)S(1)}, u32[]{:S(2)}, u32[]{:S(2)}) collective-permute-start(bf16[224,128]{1,0:T(8,128)(2,1)S(1)} %finish_pieces.1.refs_0_), channel_id=1, source_target_pairs={{0,8},{4,12},{8,0},{12,4},{16,24},{20,28},{24,16},{28,20},{1,9},{5... | collective-permute-start | bytes 172040 | tf_op jit(solution)/shard_map/ppermute | solution.py:987
  65.2 2.4 %conv_adjoint.1 = (bf16[75,32,128]{2,1,0:T(8,128)(2,1)}, f32[8,128]{1,0:T(8,128)S(1)}) custom-call(bf16[32,80,128]{2,1,0:T(8,128)(2,1)S(1)} %get-tuple-element.108.grad_ref.block_ref, bf16[4,80,128]{2,1,0:T(8,128)(2,1)S(1)} %get-tuple-element.114.halo_ref, bf16[4,80,128]{2,1,0:T(8,128)(2,1)S(1)} %collective-permute-done.19.left_ref, ...), custom_call_target="tpu_custom_call" | custom-call | bytes 2170880 | tf_op jit(solution)/shard_map/conv_adjoint/pallas_call | solution.py:35
  67.6 1.1 %write_parameters.1 = (f32[150,300]{1,0:T(8,128)}, f32[150,300]{1,0:T(8,128)}, f32[1,150]{1,0:T(1,128)}, f32[3,3,75]{2,1,0:T(4,128)}) custom-call(bf16[224,128]{1,0:T(8,128)(2,1)S(1)} %finish_pieces.1.refs_0_, bf16[224,128]{1,0:T(8,128)(2,1)S(1)} %collective-permute-done.22.refs_1_, bf16[224,128]{1,0:T(8,128)(2,1)S(1)} %collective-permute-done.23.refs_2_, ...), custom_call_target="tpu_custom_call" | custom-call | bytes 1057572 | tf_op jit(solution)/shard_map/write_parameters/pallas_call | solution.py:35
  (43 shorter events, 9.1 us)
Async XLA Ops:
  3.4 17.2 %collective-permute-start.8 = (bf16[2080,128]{1,0:T(8,128)(2,1)S(1)}, bf16[2080,128]{1,0:T(8,128)(2,1)S(1)}, u32[]{:S(2)}, u32[]{:S(2)}) collective-permute-start(bf16[2080,128]{1,0:T(8,128)(2,1)S(1)} %get-tuple-element.92), channel_id=1, source_target_pairs={{0,2},{1,3},{2,0},{3,1},{4,6},{5,7},{6,4},{7,5},{8,10},{9,11},{10,... | collective-permute-start | bytes 1597448 | tf_op jit(solution)/shard_map/ppermute | solution.py:889
  6.4 4.0 %collective-permute-start = (bf16[2,80,128]{2,1,0:T(8,128)(2,1)S(1)}, bf16[2,80,128]{2,1,0:T(8,128)(2,1)S(1)}, u32[]{:S(2)}, u32[]{:S(2)}) collective-permute-start(bf16[2,80,128]{2,1,0:T(8,128)(2,1)S(1)} %get-tuple-element.77), channel_id=1, source_target_pairs={{0,4},{4,0},{1,5},{5,1},{2,6},{6,2},{3,7},{7,3},{8,12},{12,8},{9,1... | collective-permute-start | bytes 122888 | tf_op jit(solution)/shard_map/ppermute | solution.py:328
  10.5 6.1 %collective-permute-start.1 = (bf16[3,80,128]{2,1,0:T(8,128)(2,1)S(1)}, bf16[3,80,128]{2,1,0:T(8,128)(2,1)S(1)}, u32[]{:S(2)}, u32[]{:S(2)}) collective-permute-start(bf16[3,80,128]{2,1,0:T(8,128)(2,1)S(1)} %state_third.1), channel_id=1, source_target_pairs={{0,24},{8,16},{16,8},{24,0},{1,25},{9,17},{17,9},{25,1},{2,26},{10... | collective-permute-start | bytes 184328 | tf_op jit(solution)/shard_map/ppermute | solution.py:337
  16.7 3.8 %collective-permute-start.2 = (bf16[1,80,128]{2,1,0:T(8,128)(2,1)S(1)}, bf16[1,80,128]{2,1,0:T(8,128)(2,1)S(1)}, u32[]{:S(2)}, u32[]{:S(2)}) collective-permute-start(bf16[1,80,128]{2,1,0:T(8,128)(2,1)S(1)} %get-tuple-element.84), channel_id=1, source_target_pairs={{0,8},{8,0},{16,24},{24,16},{1,9},{9,1},{17,25},{25,17},{2,10},{10... | collective-permute-start | bytes 61448 | tf_op jit(solution)/shard_map/ppermute | solution.py:345
  20.6 6.6 %collective-permute-start.9 = (bf16[2080,128]{1,0:T(8,128)(2,1)S(1)}, bf16[2080,128]{1,0:T(8,128)(2,1)S(1)}, u32[]{:S(2)}, u32[]{:S(2)}) collective-permute-start(bf16[2080,128]{1,0:T(8,128)(2,1)S(1)} %cotan_relay.1.refs_2_), channel_id=1, source_target_pairs={{0,1},{1,0},{2,3},{3,2},{4,5},{5,4},{6,7},{7,6},{8,9},{9,8},{10,11... | collective-permute-start | bytes 1597448 | tf_op jit(solution)/shard_map/ppermute | solution.py:920
  20.6 5.1 %collective-permute-start.7 = (bf16[1440,128]{1,0:T(8,128)(2,1)S(1)}, bf16[1440,128]{1,0:T(8,128)(2,1)S(1)}, u32[]{:S(2)}, u32[]{:S(2)}) collective-permute-start(bf16[1440,128]{1,0:T(8,128)(2,1)S(1)} %get-tuple-element.82.refs_4_), channel_id=1, source_target_pairs={{0,1},{1,0},{2,3},{3,2},{4,5},{5,4},{6,7},{7,6},{8,9},{9,8},{10,11... | collective-permute-start | bytes 1105928 | tf_op jit(solution)/shard_map/ppermute | solution.py:933
  22.4 6.3 %collective-permute-start.6 = (bf16[8,80,128]{2,1,0:T(8,128)(2,1)S(1)}, bf16[8,80,128]{2,1,0:T(8,128)(2,1)S(1)}, u32[]{:S(2)}, u32[]{:S(2)}) collective-permute-start(bf16[8,80,128]{2,1,0:T(8,128)(2,1)S(1)} %get-tuple-element.90), channel_id=1, source_target_pairs={{0,3},{1,2},{2,1},{3,0},{4,7},{5,6},{6,5},{7,4},{8,11},{9,10},{10,... | collective-permute-start | bytes 491528 | tf_op jit(solution)/shard_map/ppermute | solution.py:915
  22.5 9.9 %collective-permute-start.5 = (bf16[8,80,128]{2,1,0:T(8,128)(2,1)S(1)}, bf16[8,80,128]{2,1,0:T(8,128)(2,1)S(1)}, u32[]{:S(2)}, u32[]{:S(2)}) collective-permute-start(bf16[8,80,128]{2,1,0:T(8,128)(2,1)S(1)} %get-tuple-element.86.refs_5_), channel_id=1, source_target_pairs={{0,2},{1,3},{2,0},{3,1},{4,6},{5,7},{6,4},{7,5},{8,10},{9,11},{10,... | collective-permute-start | bytes 491528 | tf_op jit(solution)/shard_map/ppermute | solution.py:914
  25.4 2.9 %collective-permute-start.3 = (bf16[4,80,128]{2,1,0:T(8,128)(2,1)S(1)}, bf16[4,80,128]{2,1,0:T(8,128)(2,1)S(1)}, u32[]{:S(2)}, u32[]{:S(2)}) collective-permute-start(bf16[4,80,128]{2,1,0:T(8,128)(2,1)S(1)} %get-tuple-element.88), channel_id=1, source_target_pairs={{0,1},{1,0},{2,3},{3,2},{4,5},{5,4},{6,7},{7,6},{8,9},{9,8},{10,11... | collective-permute-start | bytes 245768 | tf_op jit(solution)/shard_map/ppermute | solution.py:913
  25.6 2.7 %collective-permute-start.4 = (bf16[4,80,128]{2,1,0:T(8,128)(2,1)S(1)}, bf16[4,80,128]{2,1,0:T(8,128)(2,1)S(1)}, u32[]{:S(2)}, u32[]{:S(2)}) collective-permute-start(bf16[4,80,128]{2,1,0:T(8,128)(2,1)S(1)} %get-tuple-element.89), channel_id=1, source_target_pairs={{0,1},{1,0},{2,3},{3,2},{4,5},{5,4},{6,7},{7,6},{8,9},{9,8},{10,11... | collective-permute-start | bytes 245768 | tf_op jit(solution)/shard_map/ppermute | solution.py:913
  35.9 1.8 %collective-permute-start.12 = (bf16[2,832,128]{2,1,0:T(8,128)(2,1)S(1)}, bf16[2,832,128]{2,1,0:T(8,128)(2,1)S(1)}, u32[]{:S(2)}, u32[]{:S(2)}) collective-permute-start(bf16[2,832,128]{2,1,0:T(8,128)(2,1)S(1)} %get-tuple-element.102), channel_id=1, source_target_pairs={{0,1},{1,0},{2,3},{3,2},{4,5},{5,4},{6,7},{7,6},{8,9},{9,8},{10,11... | collective-permute-start | bytes 1277960 | tf_op jit(solution)/shard_map/ppermute | solution.py:949
  36.4 10.2 %collective-permute-start.11 = (bf16[2,8,80,128]{3,2,1,0:T(8,128)(2,1)S(1)}, bf16[2,8,80,128]{3,2,1,0:T(8,128)(2,1)S(1)}, u32[]{:S(2)}, u32[]{:S(2)}) collective-permute-start(bf16[2,8,80,128]{3,2,1,0:T(8,128)(2,1)S(1)} %gradient_away.1.refs_2_), channel_id=1, source_target_pairs={{0,2},{1,3},{2,0},{3,1},{4,6},{5,7},{6,4},{7,5},{8,10},{9,11},{10,... | collective-permute-start | bytes 983048 | tf_op jit(solution)/shard_map/ppermute | solution.py:967
  37.4 4.0 %collective-permute-start.10 = (bf16[8,80,128]{2,1,0:T(8,128)(2,1)S(1)}, bf16[8,80,128]{2,1,0:T(8,128)(2,1)S(1)}, u32[]{:S(2)}, u32[]{:S(2)}) collective-permute-start(bf16[8,80,128]{2,1,0:T(8,128)(2,1)S(1)} %get-tuple-element.100), channel_id=1, source_target_pairs={{0,1},{1,0},{2,3},{3,2},{4,5},{5,4},{6,7},{7,6},{8,9},{9,8},{10,11... | collective-permute-start | bytes 491528 | tf_op jit(solution)/shard_map/ppermute | solution.py:966
  37.8 5.7 %collective-permute-start.13 = (bf16[2,208,128]{2,1,0:T(8,128)(2,1)S(1)}, bf16[2,208,128]{2,1,0:T(8,128)(2,1)S(1)}, u32[]{:S(2)}, u32[]{:S(2)}) collective-permute-start(bf16[2,208,128]{2,1,0:T(8,128)(2,1)S(1)} %get-tuple-element.104), channel_id=1, source_target_pairs={{0,8},{4,12},{8,0},{12,4},{16,24},{20,28},{24,16},{28,20},{1,9},{5... | collective-permute-start | bytes 319496 | tf_op jit(solution)/shard_map/ppermute | solution.py:987
  38.6 6.2 %collective-permute-start.14 = (bf16[2,208,128]{2,1,0:T(8,128)(2,1)S(1)}, bf16[2,208,128]{2,1,0:T(8,128)(2,1)S(1)}, u32[]{:S(2)}, u32[]{:S(2)}) collective-permute-start(bf16[2,208,128]{2,1,0:T(8,128)(2,1)S(1)} %get-tuple-element.105), channel_id=1, source_target_pairs={{0,4},{4,0},{8,12},{12,8},{16,20},{20,16},{24,28},{28,24},{1,5},{5... | collective-permute-start | bytes 319496 | tf_op jit(solution)/shard_map/ppermute | solution.py:987
  40.1 6.2 %collective-permute-start.15 = (bf16[2,208,128]{2,1,0:T(8,128)(2,1)S(1)}, bf16[2,208,128]{2,1,0:T(8,128)(2,1)S(1)}, u32[]{:S(2)}, u32[]{:S(2)}) collective-permute-start(bf16[2,208,128]{2,1,0:T(8,128)(2,1)S(1)} %get-tuple-element.106), channel_id=1, source_target_pairs={{0,12},{4,8},{8,4},{12,0},{16,28},{20,24},{24,20},{28,16},{1,13},{... | collective-permute-start | bytes 319496 | tf_op jit(solution)/shard_map/ppermute | solution.py:987
  46.6 1.5 %collective-permute-start.16 = (bf16[8,80,128]{2,1,0:T(8,128)(2,1)S(1)}, bf16[8,80,128]{2,1,0:T(8,128)(2,1)S(1)}, u32[]{:S(2)}, u32[]{:S(2)}) collective-permute-start(bf16[8,80,128]{2,1,0:T(8,128)(2,1)S(1)} %grad_half.1), channel_id=1, source_target_pairs={{0,1},{1,0},{2,3},{3,2},{4,5},{5,4},{6,7},{7,6},{8,9},{9,8},{10,11... | collective-permute-start | bytes 491528 | tf_op jit(solution)/shard_map/ppermute | solution.py:1003
  48.5 4.1 %collective-permute-start.17 = (bf16[2,80,128]{2,1,0:T(8,128)(2,1)S(1)}, bf16[2,80,128]{2,1,0:T(8,128)(2,1)S(1)}, u32[]{:S(2)}, u32[]{:S(2)}) collective-permute-start(bf16[2,80,128]{2,1,0:T(8,128)(2,1)S(1)} %get-tuple-element.109), channel_id=1, source_target_pairs={{0,4},{4,0},{1,5},{5,1},{2,6},{6,2},{3,7},{7,3},{8,12},{12,8},{9,1... | collective-permute-start | bytes 122888 | tf_op jit(solution)/shard_map/ppermute | solution.py:328
  50.1 6.3 %collective-permute-start.20 = (bf16[208,128]{1,0:T(8,128)(2,1)S(1)}, bf16[208,128]{1,0:T(8,128)(2,1)S(1)}, u32[]{:S(2)}, u32[]{:S(2)}) collective-permute-start(bf16[208,128]{1,0:T(8,128)(2,1)S(1)} %get-tuple-element.107.refs_1_), channel_id=1, source_target_pairs={{0,2},{1,3},{2,0},{3,1},{4,6},{5,7},{6,4},{7,5},{8,10},{9,11},{10,... | collective-permute-start | bytes 159752 | tf_op jit(solution)/shard_map/ppermute | solution.py:1019
  52.7 6.4 %collective-permute-start.18 = (bf16[3,80,128]{2,1,0:T(8,128)(2,1)S(1)}, bf16[3,80,128]{2,1,0:T(8,128)(2,1)S(1)}, u32[]{:S(2)}, u32[]{:S(2)}) collective-permute-start(bf16[3,80,128]{2,1,0:T(8,128)(2,1)S(1)} %grad_third.1), channel_id=1, source_target_pairs={{0,24},{8,16},{16,8},{24,0},{1,25},{9,17},{17,9},{25,1},{2,26},{10... | collective-permute-start | bytes 184328 | tf_op jit(solution)/shard_map/ppermute | solution.py:337
  56.4 5.1 %collective-permute-start.21 = (bf16[208,128]{1,0:T(8,128)(2,1)S(1)}, bf16[208,128]{1,0:T(8,128)(2,1)S(1)}, u32[]{:S(2)}, u32[]{:S(2)}) collective-permute-start(bf16[208,128]{1,0:T(8,128)(2,1)S(1)} %add_across.1.refs_0_), channel_id=1, source_target_pairs={{0,16},{8,24},{16,0},{24,8},{1,17},{9,25},{17,1},{25,9},{2,18},{10... | collective-permute-start | bytes 159752 | tf_op jit(solution)/shard_map/ppermute | solution.py:1048
  59.3 5.9 %collective-permute-start.19 = (bf16[4,80,128]{2,1,0:T(8,128)(2,1)S(1)}, bf16[4,80,128]{2,1,0:T(8,128)(2,1)S(1)}, u32[]{:S(2)}, u32[]{:S(2)}) collective-permute-start(bf16[4,80,128]{2,1,0:T(8,128)(2,1)S(1)} %get-tuple-element.115.refs_4_), channel_id=1, source_target_pairs={{0,8},{8,0},{16,24},{24,16},{1,9},{9,1},{17,25},{25,17},{2,10},{10... | collective-permute-start | bytes 245768 | tf_op jit(solution)/shard_map/ppermute | solution.py:345
  61.7 5.9 %collective-permute-start.24 = (bf16[224,128]{1,0:T(8,128)(2,1)S(1)}, bf16[224,128]{1,0:T(8,128)(2,1)S(1)}, u32[]{:S(2)}, u32[]{:S(2)}) collective-permute-start(bf16[224,128]{1,0:T(8,128)(2,1)S(1)} %finish_pieces.1.refs_0_), channel_id=1, source_target_pairs={{0,12},{4,8},{8,4},{12,0},{16,28},{20,24},{24,20},{28,16},{1,13},{... | collective-permute-start | bytes 172040 | tf_op jit(solution)/shard_map/ppermute | solution.py:987
  62.5 5.1 %collective-permute-start.23 = (bf16[224,128]{1,0:T(8,128)(2,1)S(1)}, bf16[224,128]{1,0:T(8,128)(2,1)S(1)}, u32[]{:S(2)}, u32[]{:S(2)}) collective-permute-start(bf16[224,128]{1,0:T(8,128)(2,1)S(1)} %finish_pieces.1.refs_0_), channel_id=1, source_target_pairs={{0,4},{4,0},{8,12},{12,8},{16,20},{20,16},{24,28},{28,24},{1,5},{5... | collective-permute-start | bytes 172040 | tf_op jit(solution)/shard_map/ppermute | solution.py:987
  63.3 4.3 %collective-permute-start.22 = (bf16[224,128]{1,0:T(8,128)(2,1)S(1)}, bf16[224,128]{1,0:T(8,128)(2,1)S(1)}, u32[]{:S(2)}, u32[]{:S(2)}) collective-permute-start(bf16[224,128]{1,0:T(8,128)(2,1)S(1)} %finish_pieces.1.refs_0_), channel_id=1, source_target_pairs={{0,8},{4,12},{8,0},{12,4},{16,24},{20,28},{24,16},{28,20},{1,9},{5... | collective-permute-start | bytes 172040 | tf_op jit(solution)/shard_map/ppermute | solution.py:987

commit v5 on v4

--- a/solution.py
+++ b/solution.py
@@ -429,7 +429,7 @@
 
 
 def conv_forward(ones_row, away, block_ref, halo_ref, left_ref, right_ref, tap_ref, *rest):
-    same_ref, others, (row_scr, left_scr, right_scr, scr) = rest[0], rest[1:-4], rest[-4:]
+    outs, (row_scr, left_scr, right_scr, scr) = rest[:-4], rest[-4:]
     rows, pad = block_ref.shape[:2]
     half = rows // 2
     me = lax.axis_index("ch")
@@ -461,11 +461,10 @@
 
     lax.fori_loop(0, pad // 16, body, 0)
     count = half // 2
-    same_ref[...] = scr[pl.ds((me % 2) * count, count)]
-    other = (1 - me % 2) * count
-    size = count // len(others)
-    for k, to in enumerate(others):
-        to[...] = scr[pl.ds(other + k * size, size)]
+    size = outs[0].shape[0]
+    for k, to in enumerate(outs):
+        first = ((me + k % 2) % 2) * count
+        to[...] = scr[pl.ds(first + k // 2 * size, size)]
 
 
 def conv_adjoint(
@@ -663,34 +662,40 @@
         )
 
 
-def hidden_gradient(*refs):
-    xs, (act_ref, y_ref, w_ref) = refs[0:5], refs[5:8]
-    pre_ref, keep_ref, send_ref, x_scr, value_scr = refs[8:]
+def hidden_gradient(half, *refs):
+    xs, (act_ref, y_ref, w_ref), refs = refs[0:4], refs[4:7], refs[7:]
+    sums = ()
+    if half:
+        sums, refs = refs[0:2], refs[2:]
+    pre_ref, keep_ref, send_ref, x_scr, value_scr = refs
     part_rows, pad = xs[0].shape[:2]
     hid = w_ref.shape[0] // 4
     split = 4 * pad // LANES * LANES
     depth, cells = x_scr.shape
+    offset = half * cells
     me = lax.axis_index("ch")
     x_scr[4 * pad : depth, :] = jnp.zeros((depth - 4 * pad, cells), BF)
-    for k, ref, first in ((0, 0, 0), (1, 1, 0), (1, 2, part_rows // 2), (2, 3, 0), (3, 4, 0)):
-        for r in range(xs[ref].shape[0]):
-            cols = slice((first + r) * LANES, (first + r + 1) * LANES)
-            x_scr[pl.ds(aligned((me ^ k) * pad), pad), cols] = xs[ref][r]
+    for k in range(4):
+        for r in range(part_rows):
+            cols = slice(r * LANES, (r + 1) * LANES)
+            x_scr[pl.ds(aligned((me ^ k) * pad), pad), cols] = xs[k][r]
     step = 256
     for start in range(0, cells, step):
         cols = slice(start, start + step)
         hidden = jnp.dot(w_ref[:, 0:depth], x_scr[:, cols], preferred_element_type=F32)
         square = hidden * hidden
         tanh = jnp.tanh(hidden * (GELU_C + (0.044715 * GELU_C) * square))
-        half = 0.5 + 0.5 * tanh
-        slope = half + hidden * (0.5 * GELU_C + (1.5 * 0.044715 * GELU_C) * square) * (
+        each = 0.5 + 0.5 * tanh
+        slope = each + hidden * (0.5 * GELU_C + (1.5 * 0.044715 * GELU_C) * square) * (
             1.0 - tanh * tanh
         )
-        value_scr[:, cols] = (hidden * half).astype(BF)
-        pre_ref[:, cols] = (act_ref[:, cols] * slope).astype(BF)
+        value_scr[:, cols] = (hidden * each).astype(BF)
+        pre_ref[:, cols] = (act_ref[:, offset + start : offset + start + step] * slope).astype(BF)
     over_cells = (((1,), (1,)), ((), ()))
     expand = lax.dot_general(pre_ref[...], x_scr[...], over_cells, preferred_element_type=F32)
-    project = lax.dot_general(value_scr[...], y_ref[...], over_cells, preferred_element_type=F32)
+    project = lax.dot_general(
+        value_scr[...], y_ref[:, offset : offset + cells], over_cells, preferred_element_type=F32
+    )
     shared = split // LANES
     tiles = [expand[:, t * LANES : (t + 1) * LANES] for t in range(shared)]
     tiles.append(expand[:, split : split + LANES] + project[:, 0:LANES])
@@ -702,10 +707,14 @@
     for k in range(4):
         to = send_ref if k % 2 else keep_ref
         for t, tile in enumerate(tiles):
-            to[k // 2, t * hid : (t + 1) * hid, :] = tile[k * hid : (k + 1) * hid].astype(to.dtype)
-
-
-def conv_gradient(away, pre_ref, t_ref, *rest):
+            at = (k // 2, slice(t * hid, (t + 1) * hid), slice(None))
+            value = tile[k * hid : (k + 1) * hid]
+            if half:
+                value = value + sums[k % 2][at]
+            to[at] = value.astype(to.dtype)
+
+
+def conv_gradient(away, first_ref, second_ref, t_ref, *rest):
     outs, scr = rest[:-1], rest[-1]
     if away:
         outs = (rest[0].at[0], rest[0].at[1])
@@ -714,9 +723,10 @@
     first = ((me // 2 + away) % 2) * 2 * pad
     weights = t_ref[pl.ds(aligned(first), 2 * pad), :]
     step = 256
-    for start in range(0, pre_ref.shape[1], step):
-        cols = slice(start, start + step)
-        scr[:, cols] = jnp.dot(weights, pre_ref[:, cols], preferred_element_type=F32).astype(BF)
+    half = first_ref.shape[1]
+    for start in range(0, 2 * half, step):
+        pre = (first_ref if start < half else second_ref)[:, start % half : start % half + step]
+        scr[:, start : start + step] = jnp.dot(weights, pre, preferred_element_type=F32).astype(BF)
     for k, to in enumerate(outs):
         at = pl.ds(aligned(((me + k) % 2) * pad), pad)
         for r in range(part_rows):
@@ -895,31 +905,32 @@
         pltpu.VMEM((pad, LANES), F32),
         pltpu.VMEM((rows // 2, pad, cols), BF),
     ]
+    eighth = shape((part_rows // 2, pad, cols), BF)
     conv_far = call(
-        functools.partial(ones, 1), [quarter] * 2, conv_operands, conv_scratch, "conv_away"
-    )
-    eighth = shape((part_rows // 2, pad, cols), BF)
-    conv_own, *conv_core = call(
-        functools.partial(ones, 0),
-        [quarter, eighth, eighth],
-        conv_operands,
-        conv_scratch,
-        "conv_here",
-        after=conv_far[:1],
-    )
-    both = [(i, i ^ 3) for i in range(n_ch)]
-    all_conv = [
-        conv_own,
-        *[lax.ppermute(piece, "ch", core) for piece in conv_core],
-        lax.ppermute(conv_far[0], "ch", across),
-        lax.ppermute(conv_far[1], "ch", both),
-    ]
+        functools.partial(ones, 1), [eighth] * 4, conv_operands, conv_scratch, "conv_away"
+    )
     from_far = call(
         relay, [from_far], [from_far], (), "cotan_relay", aliases={0: 0}, after=around[1:2]
     )[0]
     passed = lax.ppermute(from_far, "ch", core)
-    padded = shape((rows + 2 * DIL, pad, cols), BF)
-    shifted = call(shift_columns, [padded, padded], [masked, *around], (), "shift_columns")
+    conv_near = call(
+        functools.partial(ones, 0),
+        [eighth] * 4,
+        conv_operands,
+        conv_scratch,
+        "conv_here",
+        after=[conv_far[0], passed],
+    )
+    both = [(i, i ^ 3) for i in range(n_ch)]
+    halves = [
+        [
+            conv_near[2 * h],
+            lax.ppermute(conv_near[2 * h + 1], "ch", core),
+            lax.ppermute(conv_far[2 * h], "ch", across),
+            lax.ppermute(conv_far[2 * h + 1], "ch", both),
+        ]
+        for h in range(2)
+    ]
     act_grad, cotan_all, weights_all, weights_turned, *picks = call(
         functools.partial(activation_gradient, part),
         [
@@ -933,32 +944,35 @@
         [own, lax.ppermute(to_core, "ch", core), from_far, passed],
         (),
         "activation_gradient",
-        after=shifted[:1],
-    )
-    pre_grad, keep, send = call(
-        hidden_gradient,
-        [
-            shape((n_ch * hid, cells), BF),
-            shape((2, sum_rows, LANES), F32),
-            shape((2, sum_rows, LANES), BF),
-        ],
-        [*all_conv, act_grad, cotan_all, weights_all],
-        [pltpu.VMEM((depth, cells), BF), pltpu.VMEM((n_ch * hid, cells), BF)],
-        "hidden_gradient",
-    )
+    )
+    pre_grad, sums = [], ()
+    for h in range(2):
+        pre, *sums = call(
+            functools.partial(hidden_gradient, h),
+            [
+                shape((n_ch * hid, cells // 2), BF),
+                shape((2, sum_rows, LANES), F32),
+                shape((2, sum_rows, LANES), BF if h else F32),
+            ],
+            [*halves[h], act_grad, cotan_all, weights_all, *sums],
+            [pltpu.VMEM((depth, cells // 2), BF), pltpu.VMEM((n_ch * hid, cells // 2), BF)],
+            "hidden_first" if h == 0 else "hidden_second",
+        )
+        pre_grad.append(pre)
+    keep, send = sums
     got = lax.ppermute(send, "ch", core)
     grad_scratch = [pltpu.VMEM((2 * pad, cells), BF)]
     grad_far = call(
         functools.partial(conv_gradient, 1),
         [shape((2, part_rows, pad, cols), BF)],
-        [pre_grad, weights_turned],
+        [*pre_grad, weights_turned],
         grad_scratch,
         "gradient_away",
     )[0]
     grad_own, grad_core = call(
         functools.partial(conv_gradient, 0),
         [quarter] * 2,
-        [pre_grad, weights_turned],
+        [*pre_grad, weights_turned],
         grad_scratch,
         "gradient_here",
         after=[grad_far],
@@ -966,6 +980,9 @@
     grad_near = lax.ppermute(grad_core, "ch", core)
     grad_far = lax.ppermute(grad_far, "ch", across)
     staged = two_by_four()
+    padded = shape((rows + 2 * DIL, pad, cols), BF)
+    if not staged:
+        shifted = call(shift_columns, [padded, padded], [masked, *around], (), "shift_columns")
     if staged:
         piece = sum_rows // 4
         mine, *sends = call(
@@ -976,6 +993,10 @@
             "add_cores",
         )
 
+        shifted = call(
+            shift_columns, [padded, padded], [masked, *around], (), "shift_columns", after=sends[:1]
+        )
+
         def turn_plane(k):
             pairs = []
             for lon in range(n_lon):
@@ -992,7 +1013,7 @@
             [mine, *over_plane(sends)],
             (),
             "add_pieces",
-            after=[grad_near],
+            after=[grad_near, shifted[0]],
         )
     passed = call(
         second_half, [quarter], [grad_far], (), "grad_half", after=[other] if staged else []

time: 68.9 us -> 67.4 us (0.978)
  waiting for transfers between devices: 21 us -> 19 us
    ppermute x4 -> x6, waiting for transfers between devices: 4.11 us -> 2.25 us  [the longest x2 1.96 us: on_device(): lax.ppermute(conv_far[2 * h + 1], 'ch', both)]
    ppermute x1, waiting for transfers between devices: 0.63 us -> 1.7 us  [on_device(): lax.ppermute(mine, 'lon', far_lon)]
    ppermute x2, starting transfers between devices: 1.71 us -> 0.71 us  [exchange_halo(): got = lax.ppermute(first, 'lon', [(lon, lon ^ 1) for lon in range(n_lon)])]
    ppermute x1, starting transfers between devices: 0.54 us -> 1.53 us  [on_device(): lax.ppermute(other, 'ch', across)]
    ppermute x4 -> x6, starting transfers between devices: 2.33 us -> 3.26 us  [the longest x2 2.03 us: on_device(): lax.ppermute(conv_far[2 * h], 'ch', across)]
    ppermute x6, waiting for transfers between devices: 4.99 us -> 4.09 us  [over_plane(): lax.ppermute(values[k - 1], ('lon', 'lat'), turn_plane(k))]
    ppermute x2, waiting for transfers between devices: 1.4 us -> 0.68 us  [exchange_halo(): got = lax.ppermute(outer[0], 'lat', [(0, 1), (1, 0)])]
    pallas_call x25 -> x26, Pallas kernels: 19.7 us -> 19.9 us  [call(): pl.pallas_call(kernel, out_shape=tuple(outs), in_specs=[pl.BlockSpec(memo...]
  transfers between devices with their start and end apart: 25 -> 27, of which waited for: 14 -> 14; matrix products, arithmetic and copies ran while one was open for 0% -> 0% of each run, Pallas kernels for 17% -> 20%
where the time goes in v5:
time: 67.4 us; the launch traced here: 67.3 us
  starting transfers between devices  27.6 us (41%)
  Pallas kernels  19.9 us (30%)
  waiting for transfers between devices  19 us (28%)
  between operations  0.87 us (1%)
    pallas_call x26, Pallas kernels, call(): pl.pallas_call(kernel, out_shape=tuple(outs), in_specs=[pl.BlockSpec(memo...  19.9 us
    ppermute x2, starting transfers between devices, exchange_halo(): lax.ppermute(third_out, 'lon', [(lon, lon ^ 3) for lon in range(n_lon)])  7.35 us
    ppermute x6, starting transfers between devices, over_plane(): lax.ppermute(values[k - 1], ('lon', 'lat'), turn_plane(k))  7.09 us
    ppermute x2, waiting for transfers between devices, exchange_halo(): lax.ppermute(third_out, 'lon', [(lon, lon ^ 3) for lon in range(n_lon)])  5.02 us
    ppermute x6, waiting for transfers between devices, over_plane(): lax.ppermute(values[k - 1], ('lon', 'lat'), turn_plane(k))  4.09 us
    ppermute x2, waiting for transfers between devices, exchange_halo(): got = lax.ppermute(first, 'lon', [(lon, lon ^ 1) for lon in range(n_lon)])  3.77 us
    ppermute x2, starting transfers between devices, exchange_halo(): got = lax.ppermute(outer[0], 'lat', [(0, 1), (1, 0)])  3.16 us
    ppermute x1, starting transfers between devices, on_device(): from_far = lax.ppermute(to_far, 'ch', across)  3 us
  transfers between devices with their start and end apart: 27, of which 14 were waited for; matrix products, arithmetic and copies ran while one was open for 0% of the time, Pallas kernels for 20%

profile of v5, /device:TPU:0, one launch (start us, length us, event | category | flops | bytes accessed | tf_op | source)
XLA Modules:
  0.0 67.3 jit_solution(3421866962420850255)
XLA Ops:
  0.6 1.5 %outer_rows.1 = (bf16[2,80,128]{2,1,0:T(8,128)(2,1)S(1)}, bf16[75,32,128]{2,1,0:T(8,128)(2,1)S(1)}, s32[32,128]{1,0:T(8,128)S(1)}, bf16[75,32,128]{2,1,0:T(8,128...) custom-call(bf16[75,32,128]{2,1,0:T(8,128)(2,1)} %refs_0_.1, ...), custom_call_target="tpu_custom_call" | custom-call | bytes 2906120 | tf_op jit(solution)/shard_map/outer_rows/pallas_call | solution.py:35
  2.1 1.3 %far_rows.1 = (bf16[2080,128]{1,0:T(8,128)(2,1)S(1)}, bf16[800,128]{1,0:T(8,128)(2,1)S(1)}, f32[80,128]{1,0:T(8,128)S(1)}) custom-call(s32[32,128]{1,0:T(8,128)S(1)} %get-tuple-element.73.refs_0_.refs_1_.mask_ref, bf16[75,32,128]{2,1,0:T(8,128)(2,1)S(1)} %get-tuple-element.74.refs_1_.grad_ref, s32[1,512]{1,0:T(1,128)S(1)} %get-tuple-element.75.refs_2_.offset_ref, ...), custom_call_target="tpu_custom_call" | custom-call | bytes 1596420 | tf_op jit(solution)/shard_map/far_rows/pallas_call | solution.py:35
  3.4 3.0 %collective-permute-start.3 = (bf16[2080,128]{1,0:T(8,128)(2,1)S(1)}, bf16[2080,128]{1,0:T(8,128)(2,1)S(1)}, u32[]{:S(2)}, u32[]{:S(2)}) collective-permute-start(bf16[2080,128]{1,0:T(8,128)(2,1)S(1)} %get-tuple-element.93), channel_id=1, source_target_pairs={{0,2},{1,3},{2,0},{3,1},{4,6},{5,7},{6,4},{7,5},{8,10},{9,11},{10,... | collective-permute-start | bytes 1597448 | tf_op jit(solution)/shard_map/ppermute | solution.py:899
  6.4 1.5 %collective-permute-start = (bf16[2,80,128]{2,1,0:T(8,128)(2,1)S(1)}, bf16[2,80,128]{2,1,0:T(8,128)(2,1)S(1)}, u32[]{:S(2)}, u32[]{:S(2)}) collective-permute-start(bf16[2,80,128]{2,1,0:T(8,128)(2,1)S(1)} %get-tuple-element.83), channel_id=1, source_target_pairs={{0,4},{4,0},{1,5},{5,1},{2,6},{6,2},{3,7},{7,3},{8,12},{12,8},{9,1... | collective-permute-start | bytes 122888 | tf_op jit(solution)/shard_map/ppermute | solution.py:328
  8.7 1.0 %state_rows.1 = (bf16[32,80,128]{2,1,0:T(8,128)(2,1)S(1)}, bf16[2,80,128]{2,1,0:T(8,128)(2,1)S(1)}, bf16[80,128]{1,0:T(8,128)(2,1)S(1)}, bf16[80,128]{1,0:T(8,128)(2,1)S(1)}) custom-call(bf16[75,32,128]{2,1,0:T(8,128)(2,1)S(1)} %get-tuple-element.72.refs_0_, s32[32,128]{1,0:T(8,128)S(1)} %get-tuple-element.73.refs_0_.refs_1_.mask_ref, ...), custom_call_target="tpu_custom_call" | custom-call | bytes 1409024 | tf_op jit(solution)/shard_map/state_rows/pallas_call | solution.py:35
  10.5 3.7 %collective-permute-start.1 = (bf16[3,80,128]{2,1,0:T(8,128)(2,1)S(1)}, bf16[3,80,128]{2,1,0:T(8,128)(2,1)S(1)}, u32[]{:S(2)}, u32[]{:S(2)}) collective-permute-start(bf16[3,80,128]{2,1,0:T(8,128)(2,1)S(1)} %state_third.1), channel_id=1, source_target_pairs={{0,24},{8,16},{16,8},{24,0},{1,25},{9,17},{17,9},{25,1},{2,26},{10... | collective-permute-start | bytes 184328 | tf_op jit(solution)/shard_map/ppermute | solution.py:337
  14.2 2.4 %collective-permute-done.1.third_ref = bf16[3,80,128]{2,1,0:T(8,128)(2,1)S(1)} collective-permute-done((bf16[3,80,128]{2,1,0:T(8,128)(2,1)S(1)}, bf16[3,80,128]{2,1,0:T(8,128)(2,1)S(1)}, u32[]{:S(2)}, u32[]{:S(2)}) %collective-permute-start.1) | collective-permute-done | bytes 61472 | tf_op jit(solution)/shard_map/ppermute | solution.py:337
  16.8 3.8 %collective-permute-done.2.left_ref.refs_1_.refs_2_ = bf16[1,80,128]{2,1,0:T(8,128)(2,1)S(1)} collective-permute-done((bf16[1,80,128]{2,1,0:T(8,128)(2,1)S(1)}, bf16[1,80,128]{2,1,0:T(8,128)(2,1)S(1)}, u32[]{:S(2)}, u32[]{:S(2)}) %collective-permute-start.2) | collective-permute-done | bytes 20512 | tf_op jit(solution)/shard_map/ppermute | solution.py:345
  21.1 1.3 %conv_away.1 = (bf16[4,80,128]{2,1,0:T(8,128)(2,1)S(1)}, bf16[4,80,128]{2,1,0:T(8,128)(2,1)S(1)}, bf16[4,80,128]{2,1,0:T(8,128)(2,1)S(1)}, bf16[4,80,128]{2,1,0:T(8,128)(2,1)S(1)}) custom-call(bf16[32,80,128]{2,1,0:T(8,128)(2,1)S(1)} %get-tuple-element.82.block_ref.refs_0_, bf16[4,80,128]{2,1,0:T(8,128)(2,1)S(1)} %get-tuple-element.89.halo_ref.refs_1_, ...), custom_call_target="tpu_custom_call" | custom-call | bytes 1146880 | tf_op jit(solution)/shard_map/conv_away/pallas_call | solution.py:35
  22.5 1.6 %collective-permute-start.6 = (bf16[4,80,128]{2,1,0:T(8,128)(2,1)S(1)}, bf16[4,80,128]{2,1,0:T(8,128)(2,1)S(1)}, u32[]{:S(2)}, u32[]{:S(2)}) collective-permute-start(bf16[4,80,128]{2,1,0:T(8,128)(2,1)S(1)} %get-tuple-element.92.refs_5_), channel_id=1, source_target_pairs={{0,2},{1,3},{2,0},{3,1},{4,6},{5,7},{6,4},{7,5},{8,10},{9,11},{10,... | collective-permute-start | bytes 245768 | tf_op jit(solution)/shard_map/ppermute | solution.py:929
  24.1 1.3 %conv_here.1 = (bf16[4,80,128]{2,1,0:T(8,128)(2,1)S(1)}, bf16[4,80,128]{2,1,0:T(8,128)(2,1)S(1)}, bf16[4,80,128]{2,1,0:T(8,128)(2,1)S(1)}, bf16[4,80,128]{2,1,0:T(8,128)(2,1)S(1)}) custom-call(bf16[32,80,128]{2,1,0:T(8,128)(2,1)S(1)} %get-tuple-element.82.block_ref.refs_0_, bf16[4,80,128]{2,1,0:T(8,128)(2,1)S(1)} %get-tuple-element.89.halo_ref.refs_1_, ...), custom_call_target="tpu_custom_call" | custom-call | bytes 1761280 | tf_op jit(solution)/shard_map/conv_here/pallas_call | solution.py:35
  26.1 0.9 %collective-permute-done.7.refs_3_ = bf16[4,80,128]{2,1,0:T(8,128)(2,1)S(1)} collective-permute-done((bf16[4,80,128]{2,1,0:T(8,128)(2,1)S(1)}, bf16[4,80,128]{2,1,0:T(8,128)(2,1)S(1)}, u32[]{:S(2)}, u32[]{:S(2)}) %collective-permute-start.7) | collective-permute-done | bytes 81952 | tf_op jit(solution)/shard_map/ppermute | solution.py:930
  27.8 1.2 %activation_gradient.1 = (f32[640,1024]{1,0:T(8,128)S(1)}, bf16[384,1024]{1,0:T(8,128)(2,1)S(1)}, bf16[640,640]{1,0:T(8,128)(2,1)S(1)}, bf16[384,640]{1,0:T(8,12...) custom-call(bf16[1440,128]{1,0:T(8,128)(2,1)S(1)} %get-tuple-element.97.refs_0_, ...), custom_call_target="tpu_custom_call" | custom-call | bytes 6981632 | tf_op jit(solution)/shard_map/activation_gradient/pallas_call | solution.py:35
  29.2 1.8 %hidden_first.1 = (bf16[640,512]{1,0:T(8,128)(2,1)S(1)}, f32[2,832,128]{2,1,0:T(8,128)S(1)}, f32[2,832,128]{2,1,0:T(8,128)S(1)}) custom-call(bf16[4,80,128]{2,1,0:T(8,128)(2,1)S(1)} %get-tuple-element.94.refs_0_, bf16[4,80,128]{2,1,0:T(8,128)(2,1)S(1)} %collective-permute-done.5.refs_1_, bf16[4,80,128]{2,1,0:T(8,128)(2,1)S(1)} %collective-permute-done.6.refs_2_, ...), custom_call_target="tpu_custom_call" | custom-call | bytes 6914048 | tf_op jit(solution)/shard_map/hidden_first/pallas_call | solution.py:35
  31.0 1.1 %collective-permute-done.11.refs_3_ = bf16[4,80,128]{2,1,0:T(8,128)(2,1)S(1)} collective-permute-done((bf16[4,80,128]{2,1,0:T(8,128)(2,1)S(1)}, bf16[4,80,128]{2,1,0:T(8,128)(2,1)S(1)}, u32[]{:S(2)}, u32[]{:S(2)}) %collective-permute-start.11) | collective-permute-done | bytes 81952 | tf_op jit(solution)/shard_map/ppermute | solution.py:930
  32.1 1.8 %hidden_second.1 = (bf16[640,512]{1,0:T(8,128)(2,1)S(1)}, f32[2,832,128]{2,1,0:T(8,128)S(1)}, bf16[2,832,128]{2,1,0:T(8,128)(2,1)S(1)}) custom-call(bf16[4,80,128]{2,1,0:T(8,128)(2,1)S(1)} %get-tuple-element.102.refs_0_, bf16[4,80,128]{2,1,0:T(8,128)(2,1)S(1)} %collective-permute-done.9.refs_1_, bf16[4,80,128]{2,1,0:T(8,128)(2,1)S(1)} %collective-permute-done.10.refs_2_, ...), custom_call_target="tpu_custom_call" | custom-call | bytes 8192000 | tf_op jit(solution)/shard_map/hidden_second/pallas_call | solution.py:35
  35.8 1.6 %collective-permute-start.16 = (bf16[2,208,128]{2,1,0:T(8,128)(2,1)S(1)}, bf16[2,208,128]{2,1,0:T(8,128)(2,1)S(1)}, u32[]{:S(2)}, u32[]{:S(2)}) collective-permute-start(bf16[2,208,128]{2,1,0:T(8,128)(2,1)S(1)} %get-tuple-element.116), channel_id=1, source_target_pairs={{0,4},{4,0},{8,12},{12,8},{16,20},{20,16},{24,28},{28,24},{1,5},{5... | collective-permute-start | bytes 319496 | tf_op jit(solution)/shard_map/ppermute | solution.py:1008
  38.1 1.3 %collective-permute-start.15 = (bf16[2,208,128]{2,1,0:T(8,128)(2,1)S(1)}, bf16[2,208,128]{2,1,0:T(8,128)(2,1)S(1)}, u32[]{:S(2)}, u32[]{:S(2)}) collective-permute-start(bf16[2,208,128]{2,1,0:T(8,128)(2,1)S(1)} %get-tuple-element.115.refs_4_), channel_id=1, source_target_pairs={{0,8},{4,12},{8,0},{12,4},{16,24},{20,28},{24,16},{28,20},{1,9},{5... | collective-permute-start | bytes 319496 | tf_op jit(solution)/shard_map/ppermute | solution.py:1008
  39.4 1.2 %shift_columns.1 = (bf16[36,80,128]{2,1,0:T(8,128)(2,1)S(1)}, bf16[36,80,128]{2,1,0:T(8,128)(2,1)S(1)}) custom-call(bf16[32,80,128]{2,1,0:T(8,128)(2,1)S(1)} %get-tuple-element.82.block_ref.refs_0_, bf16[4,80,128]{2,1,0:T(8,128)(2,1)S(1)} %get-tuple-element.89.halo_ref.refs_1_, bf16[1,80,128]{2,1,0:T(8,128)(2,1)S(1)} %collective-permute-done.2.left_ref.refs_1_.refs_2_, ...), custom_call_target="tpu_custom_call" | custom-call | bytes 2359296 | tf_op jit(solution)/shard_map/shift_columns/pallas_call | solution.py:35
  40.6 2.0 %collective-permute-done.16.refs_2_ = bf16[2,208,128]{2,1,0:T(8,128)(2,1)S(1)} collective-permute-done((bf16[2,208,128]{2,1,0:T(8,128)(2,1)S(1)}, bf16[2,208,128]{2,1,0:T(8,128)(2,1)S(1)}, u32[]{:S(2)}, u32[]{:S(2)}) %collective-permute-start.16) | collective-permute-done | bytes 106528 | tf_op jit(solution)/shard_map/ppermute | solution.py:1008
  42.6 1.6 %collective-permute-done.17.refs_3_ = bf16[2,208,128]{2,1,0:T(8,128)(2,1)S(1)} collective-permute-done((bf16[2,208,128]{2,1,0:T(8,128)(2,1)S(1)}, bf16[2,208,128]{2,1,0:T(8,128)(2,1)S(1)}, u32[]{:S(2)}, u32[]{:S(2)}) %collective-permute-start.17) | collective-permute-done | bytes 106528 | tf_op jit(solution)/shard_map/ppermute | solution.py:1008
  44.8 1.4 %collective-permute-done.18.passed = bf16[8,80,128]{2,1,0:T(8,128)(2,1)S(1)} collective-permute-done((bf16[8,80,128]{2,1,0:T(8,128)(2,1)S(1)}, bf16[8,80,128]{2,1,0:T(8,128)(2,1)S(1)}, u32[]{:S(2)}, u32[]{:S(2)}) %collective-permute-start.18) | collective-permute-done | bytes 163872 | tf_op jit(solution)/shard_map/ppermute | solution.py:1024
  46.7 1.6 %collective-permute-start.19 = (bf16[2,80,128]{2,1,0:T(8,128)(2,1)S(1)}, bf16[2,80,128]{2,1,0:T(8,128)(2,1)S(1)}, u32[]{:S(2)}, u32[]{:S(2)}) collective-permute-start(bf16[2,80,128]{2,1,0:T(8,128)(2,1)S(1)} %get-tuple-element.121), channel_id=1, source_target_pairs={{0,4},{4,0},{1,5},{5,1},{2,6},{6,2},{3,7},{7,3},{8,12},{12,8},{9,1... | collective-permute-start | bytes 122888 | tf_op jit(solution)/shard_map/ppermute | solution.py:328
  48.4 1.5 %collective-permute-start.22 = (bf16[208,128]{1,0:T(8,128)(2,1)S(1)}, bf16[208,128]{1,0:T(8,128)(2,1)S(1)}, u32[]{:S(2)}, u32[]{:S(2)}) collective-permute-start(bf16[208,128]{1,0:T(8,128)(2,1)S(1)} %get-tuple-element.119.refs_1_), channel_id=1, source_target_pairs={{0,2},{1,3},{2,0},{3,1},{4,6},{5,7},{6,4},{7,5},{8,10},{9,11},{10,... | collective-permute-start | bytes 159752 | tf_op jit(solution)/shard_map/ppermute | solution.py:1040
  49.9 1.2 %kernel_gradient.1.refs_0_.refs_2_ = bf16[80,128]{1,0:T(8,128)(2,1)S(1)} custom-call(bf16[32,80,128]{2,1,0:T(8,128)(2,1)S(1)} %get-tuple-element.120.grad_ref.block_ref, bf16[32,80,128]{2,1,0:T(8,128)(2,1)S(1)} %get-tuple-element.82.block_ref.refs_0_, bf16[4,80,128]{2,1,0:T(8,128)(2,1)S(1)} %get-tuple-element.89.halo_ref.refs_1_, ...), custom_call_target="tpu_custom_call" | custom-call | bytes 2887680 | tf_op jit(solution)/shard_map/kernel_gradient/pallas_call | solution.py:35
  51.2 3.7 %collective-permute-start.20 = (bf16[3,80,128]{2,1,0:T(8,128)(2,1)S(1)}, bf16[3,80,128]{2,1,0:T(8,128)(2,1)S(1)}, u32[]{:S(2)}, u32[]{:S(2)}) collective-permute-start(bf16[3,80,128]{2,1,0:T(8,128)(2,1)S(1)} %grad_third.1), channel_id=1, source_target_pairs={{0,24},{8,16},{16,8},{24,0},{1,25},{9,17},{17,9},{25,1},{2,26},{10... | collective-permute-start | bytes 184328 | tf_op jit(solution)/shard_map/ppermute | solution.py:337
  55.0 2.6 %collective-permute-done.20.third_ref.refs_3_ = bf16[3,80,128]{2,1,0:T(8,128)(2,1)S(1)} collective-permute-done((bf16[3,80,128]{2,1,0:T(8,128)(2,1)S(1)}, bf16[3,80,128]{2,1,0:T(8,128)(2,1)S(1)}, u32[]{:S(2)}, u32[]{:S(2)}) %collective-permute-start.20) | collective-permute-done | bytes 61472 | tf_op jit(solution)/shard_map/ppermute | solution.py:337
  58.4 1.7 %collective-permute-done.23.refs_1_ = bf16[208,128]{1,0:T(8,128)(2,1)S(1)} collective-permute-done((bf16[208,128]{1,0:T(8,128)(2,1)S(1)}, bf16[208,128]{1,0:T(8,128)(2,1)S(1)}, u32[]{:S(2)}, u32[]{:S(2)}) %collective-permute-start.23) | collective-permute-done | bytes 53280 | tf_op jit(solution)/shard_map/ppermute | solution.py:1069
  60.4 1.1 %collective-permute-start.25 = (bf16[224,128]{1,0:T(8,128)(2,1)S(1)}, bf16[224,128]{1,0:T(8,128)(2,1)S(1)}, u32[]{:S(2)}, u32[]{:S(2)}) collective-permute-start(bf16[224,128]{1,0:T(8,128)(2,1)S(1)} %finish_pieces.1.refs_0_), channel_id=1, source_target_pairs={{0,4},{4,0},{8,12},{12,8},{16,20},{20,16},{24,28},{28,24},{1,5},{5... | collective-permute-start | bytes 172040 | tf_op jit(solution)/shard_map/ppermute | solution.py:1008
  61.5 2.2 %collective-permute-start.24 = (bf16[224,128]{1,0:T(8,128)(2,1)S(1)}, bf16[224,128]{1,0:T(8,128)(2,1)S(1)}, u32[]{:S(2)}, u32[]{:S(2)}) collective-permute-start(bf16[224,128]{1,0:T(8,128)(2,1)S(1)} %finish_pieces.1.refs_0_), channel_id=1, source_target_pairs={{0,8},{4,12},{8,0},{12,4},{16,24},{20,28},{24,16},{28,20},{1,9},{5... | collective-permute-start | bytes 172040 | tf_op jit(solution)/shard_map/ppermute | solution.py:1008
  63.8 2.4 %conv_adjoint.1 = (bf16[75,32,128]{2,1,0:T(8,128)(2,1)}, f32[8,128]{1,0:T(8,128)S(1)}) custom-call(bf16[32,80,128]{2,1,0:T(8,128)(2,1)S(1)} %get-tuple-element.120.grad_ref.block_ref, bf16[4,80,128]{2,1,0:T(8,128)(2,1)S(1)} %get-tuple-element.126.halo_ref, bf16[4,80,128]{2,1,0:T(8,128)(2,1)S(1)} %collective-permute-done.21.left_ref, ...), custom_call_target="tpu_custom_call" | custom-call | bytes 2170880 | tf_op jit(solution)/shard_map/conv_adjoint/pallas_call | solution.py:35
  66.2 1.1 %write_parameters.1 = (f32[150,300]{1,0:T(8,128)}, f32[150,300]{1,0:T(8,128)}, f32[1,150]{1,0:T(1,128)}, f32[3,3,75]{2,1,0:T(4,128)}) custom-call(bf16[224,128]{1,0:T(8,128)(2,1)S(1)} %finish_pieces.1.refs_0_, bf16[224,128]{1,0:T(8,128)(2,1)S(1)} %collective-permute-done.24.refs_1_, bf16[224,128]{1,0:T(8,128)(2,1)S(1)} %collective-permute-done.25.refs_2_, ...), custom_call_target="tpu_custom_call" | custom-call | bytes 1057572 | tf_op jit(solution)/shard_map/write_parameters/pallas_call | solution.py:35
  (48 shorter events, 9.2 us)
Async XLA Ops:
  3.4 17.2 %collective-permute-start.3 = (bf16[2080,128]{1,0:T(8,128)(2,1)S(1)}, bf16[2080,128]{1,0:T(8,128)(2,1)S(1)}, u32[]{:S(2)}, u32[]{:S(2)}) collective-permute-start(bf16[2080,128]{1,0:T(8,128)(2,1)S(1)} %get-tuple-element.93), channel_id=1, source_target_pairs={{0,2},{1,3},{2,0},{3,1},{4,6},{5,7},{6,4},{7,5},{8,10},{9,11},{10,... | collective-permute-start | bytes 1597448 | tf_op jit(solution)/shard_map/ppermute | solution.py:899
  6.4 4.0 %collective-permute-start = (bf16[2,80,128]{2,1,0:T(8,128)(2,1)S(1)}, bf16[2,80,128]{2,1,0:T(8,128)(2,1)S(1)}, u32[]{:S(2)}, u32[]{:S(2)}) collective-permute-start(bf16[2,80,128]{2,1,0:T(8,128)(2,1)S(1)} %get-tuple-element.83), channel_id=1, source_target_pairs={{0,4},{4,0},{1,5},{5,1},{2,6},{6,2},{3,7},{7,3},{8,12},{12,8},{9,1... | collective-permute-start | bytes 122888 | tf_op jit(solution)/shard_map/ppermute | solution.py:328
  10.5 6.1 %collective-permute-start.1 = (bf16[3,80,128]{2,1,0:T(8,128)(2,1)S(1)}, bf16[3,80,128]{2,1,0:T(8,128)(2,1)S(1)}, u32[]{:S(2)}, u32[]{:S(2)}) collective-permute-start(bf16[3,80,128]{2,1,0:T(8,128)(2,1)S(1)} %state_third.1), channel_id=1, source_target_pairs={{0,24},{8,16},{16,8},{24,0},{1,25},{9,17},{17,9},{25,1},{2,26},{10... | collective-permute-start | bytes 184328 | tf_op jit(solution)/shard_map/ppermute | solution.py:337
  16.7 3.8 %collective-permute-start.2 = (bf16[1,80,128]{2,1,0:T(8,128)(2,1)S(1)}, bf16[1,80,128]{2,1,0:T(8,128)(2,1)S(1)}, u32[]{:S(2)}, u32[]{:S(2)}) collective-permute-start(bf16[1,80,128]{2,1,0:T(8,128)(2,1)S(1)} %get-tuple-element.90), channel_id=1, source_target_pairs={{0,8},{8,0},{16,24},{24,16},{1,9},{9,1},{17,25},{25,17},{2,10},{10... | collective-permute-start | bytes 61448 | tf_op jit(solution)/shard_map/ppermute | solution.py:345
  20.6 3.6 %collective-permute-start.4 = (bf16[2080,128]{1,0:T(8,128)(2,1)S(1)}, bf16[2080,128]{1,0:T(8,128)(2,1)S(1)}, u32[]{:S(2)}, u32[]{:S(2)}) collective-permute-start(bf16[2080,128]{1,0:T(8,128)(2,1)S(1)} %cotan_relay.1.refs_2_), channel_id=1, source_target_pairs={{0,1},{1,0},{2,3},{3,2},{4,5},{5,4},{6,7},{7,6},{8,9},{9,8},{10,11... | collective-permute-start | bytes 1597448 | tf_op jit(solution)/shard_map/ppermute | solution.py:915
  20.6 6.8 %collective-permute-start.8 = (bf16[1440,128]{1,0:T(8,128)(2,1)S(1)}, bf16[1440,128]{1,0:T(8,128)(2,1)S(1)}, u32[]{:S(2)}, u32[]{:S(2)}) collective-permute-start(bf16[1440,128]{1,0:T(8,128)(2,1)S(1)} %get-tuple-element.88.refs_4_), channel_id=1, source_target_pairs={{0,1},{1,0},{2,3},{3,2},{4,5},{5,4},{6,7},{7,6},{8,9},{9,8},{10,11... | collective-permute-start | bytes 1105928 | tf_op jit(solution)/shard_map/ppermute | solution.py:944
  22.4 4.6 %collective-permute-start.7 = (bf16[4,80,128]{2,1,0:T(8,128)(2,1)S(1)}, bf16[4,80,128]{2,1,0:T(8,128)(2,1)S(1)}, u32[]{:S(2)}, u32[]{:S(2)}) collective-permute-start(bf16[4,80,128]{2,1,0:T(8,128)(2,1)S(1)} %get-tuple-element.96), channel_id=1, source_target_pairs={{0,3},{1,2},{2,1},{3,0},{4,7},{5,6},{6,5},{7,4},{8,11},{9,10},{10,... | collective-permute-start | bytes 245768 | tf_op jit(solution)/shard_map/ppermute | solution.py:930
  22.5 6.7 %collective-permute-start.6 = (bf16[4,80,128]{2,1,0:T(8,128)(2,1)S(1)}, bf16[4,80,128]{2,1,0:T(8,128)(2,1)S(1)}, u32[]{:S(2)}, u32[]{:S(2)}) collective-permute-start(bf16[4,80,128]{2,1,0:T(8,128)(2,1)S(1)} %get-tuple-element.92.refs_5_), channel_id=1, source_target_pairs={{0,2},{1,3},{2,0},{3,1},{4,6},{5,7},{6,4},{7,5},{8,10},{9,11},{10,... | collective-permute-start | bytes 245768 | tf_op jit(solution)/shard_map/ppermute | solution.py:929
  25.4 3.8 %collective-permute-start.5 = (bf16[4,80,128]{2,1,0:T(8,128)(2,1)S(1)}, bf16[4,80,128]{2,1,0:T(8,128)(2,1)S(1)}, u32[]{:S(2)}, u32[]{:S(2)}) collective-permute-start(bf16[4,80,128]{2,1,0:T(8,128)(2,1)S(1)} %get-tuple-element.95), channel_id=1, source_target_pairs={{0,1},{1,0},{2,3},{3,2},{4,5},{5,4},{6,7},{7,6},{8,9},{9,8},{10,11... | collective-permute-start | bytes 245768 | tf_op jit(solution)/shard_map/ppermute | solution.py:928
  25.7 5.4 %collective-permute-start.10 = (bf16[4,80,128]{2,1,0:T(8,128)(2,1)S(1)}, bf16[4,80,128]{2,1,0:T(8,128)(2,1)S(1)}, u32[]{:S(2)}, u32[]{:S(2)}) collective-permute-start(bf16[4,80,128]{2,1,0:T(8,128)(2,1)S(1)} %get-tuple-element.104), channel_id=1, source_target_pairs={{0,2},{1,3},{2,0},{3,1},{4,6},{5,7},{6,4},{7,5},{8,10},{9,11},{10,... | collective-permute-start | bytes 245768 | tf_op jit(solution)/shard_map/ppermute | solution.py:929
  26.9 5.2 %collective-permute-start.11 = (bf16[4,80,128]{2,1,0:T(8,128)(2,1)S(1)}, bf16[4,80,128]{2,1,0:T(8,128)(2,1)S(1)}, u32[]{:S(2)}, u32[]{:S(2)}) collective-permute-start(bf16[4,80,128]{2,1,0:T(8,128)(2,1)S(1)} %get-tuple-element.105), channel_id=1, source_target_pairs={{0,3},{1,2},{2,1},{3,0},{4,7},{5,6},{6,5},{7,4},{8,11},{9,10},{10,... | collective-permute-start | bytes 245768 | tf_op jit(solution)/shard_map/ppermute | solution.py:930
  27.4 4.8 %collective-permute-start.9 = (bf16[4,80,128]{2,1,0:T(8,128)(2,1)S(1)}, bf16[4,80,128]{2,1,0:T(8,128)(2,1)S(1)}, u32[]{:S(2)}, u32[]{:S(2)}) collective-permute-start(bf16[4,80,128]{2,1,0:T(8,128)(2,1)S(1)} %get-tuple-element.103), channel_id=1, source_target_pairs={{0,1},{1,0},{2,3},{3,2},{4,5},{5,4},{6,7},{7,6},{8,9},{9,8},{10,11... | collective-permute-start | bytes 245768 | tf_op jit(solution)/shard_map/ppermute | solution.py:928
  33.9 1.8 %collective-permute-start.14 = (bf16[2,832,128]{2,1,0:T(8,128)(2,1)S(1)}, bf16[2,832,128]{2,1,0:T(8,128)(2,1)S(1)}, u32[]{:S(2)}, u32[]{:S(2)}) collective-permute-start(bf16[2,832,128]{2,1,0:T(8,128)(2,1)S(1)} %get-tuple-element.113), channel_id=1, source_target_pairs={{0,1},{1,0},{2,3},{3,2},{4,5},{5,4},{6,7},{7,6},{8,9},{9,8},{10,11... | collective-permute-start | bytes 1277960 | tf_op jit(solution)/shard_map/ppermute | solution.py:963
  34.6 10.1 %collective-permute-start.13 = (bf16[2,8,80,128]{3,2,1,0:T(8,128)(2,1)S(1)}, bf16[2,8,80,128]{3,2,1,0:T(8,128)(2,1)S(1)}, u32[]{:S(2)}, u32[]{:S(2)}) collective-permute-start(bf16[2,8,80,128]{3,2,1,0:T(8,128)(2,1)S(1)} %gradient_away.1.refs_3_), channel_id=1, source_target_pairs={{0,2},{1,3},{2,0},{3,1},{4,6},{5,7},{6,4},{7,5},{8,10},{9,11},{10,... | collective-permute-start | bytes 983048 | tf_op jit(solution)/shard_map/ppermute | solution.py:981
  35.5 5.0 %collective-permute-start.12 = (bf16[8,80,128]{2,1,0:T(8,128)(2,1)S(1)}, bf16[8,80,128]{2,1,0:T(8,128)(2,1)S(1)}, u32[]{:S(2)}, u32[]{:S(2)}) collective-permute-start(bf16[8,80,128]{2,1,0:T(8,128)(2,1)S(1)} %get-tuple-element.111), channel_id=1, source_target_pairs={{0,1},{1,0},{2,3},{3,2},{4,5},{5,4},{6,7},{7,6},{8,9},{9,8},{10,11... | collective-permute-start | bytes 491528 | tf_op jit(solution)/shard_map/ppermute | solution.py:980
  35.8 6.8 %collective-permute-start.16 = (bf16[2,208,128]{2,1,0:T(8,128)(2,1)S(1)}, bf16[2,208,128]{2,1,0:T(8,128)(2,1)S(1)}, u32[]{:S(2)}, u32[]{:S(2)}) collective-permute-start(bf16[2,208,128]{2,1,0:T(8,128)(2,1)S(1)} %get-tuple-element.116), channel_id=1, source_target_pairs={{0,4},{4,0},{8,12},{12,8},{16,20},{20,16},{24,28},{28,24},{1,5},{5... | collective-permute-start | bytes 319496 | tf_op jit(solution)/shard_map/ppermute | solution.py:1008
  37.5 6.7 %collective-permute-start.17 = (bf16[2,208,128]{2,1,0:T(8,128)(2,1)S(1)}, bf16[2,208,128]{2,1,0:T(8,128)(2,1)S(1)}, u32[]{:S(2)}, u32[]{:S(2)}) collective-permute-start(bf16[2,208,128]{2,1,0:T(8,128)(2,1)S(1)} %get-tuple-element.117), channel_id=1, source_target_pairs={{0,12},{4,8},{8,4},{12,0},{16,28},{20,24},{24,20},{28,16},{1,13},{... | collective-permute-start | bytes 319496 | tf_op jit(solution)/shard_map/ppermute | solution.py:1008
  38.1 6.6 %collective-permute-start.15 = (bf16[2,208,128]{2,1,0:T(8,128)(2,1)S(1)}, bf16[2,208,128]{2,1,0:T(8,128)(2,1)S(1)}, u32[]{:S(2)}, u32[]{:S(2)}) collective-permute-start(bf16[2,208,128]{2,1,0:T(8,128)(2,1)S(1)} %get-tuple-element.115.refs_4_), channel_id=1, source_target_pairs={{0,8},{4,12},{8,0},{12,4},{16,24},{20,28},{24,16},{28,20},{1,9},{5... | collective-permute-start | bytes 319496 | tf_op jit(solution)/shard_map/ppermute | solution.py:1008
  44.8 1.5 %collective-permute-start.18 = (bf16[8,80,128]{2,1,0:T(8,128)(2,1)S(1)}, bf16[8,80,128]{2,1,0:T(8,128)(2,1)S(1)}, u32[]{:S(2)}, u32[]{:S(2)}) collective-permute-start(bf16[8,80,128]{2,1,0:T(8,128)(2,1)S(1)} %grad_half.1), channel_id=1, source_target_pairs={{0,1},{1,0},{2,3},{3,2},{4,5},{5,4},{6,7},{7,6},{8,9},{9,8},{10,11... | collective-permute-start | bytes 491528 | tf_op jit(solution)/shard_map/ppermute | solution.py:1024
  46.7 4.4 %collective-permute-start.19 = (bf16[2,80,128]{2,1,0:T(8,128)(2,1)S(1)}, bf16[2,80,128]{2,1,0:T(8,128)(2,1)S(1)}, u32[]{:S(2)}, u32[]{:S(2)}) collective-permute-start(bf16[2,80,128]{2,1,0:T(8,128)(2,1)S(1)} %get-tuple-element.121), channel_id=1, source_target_pairs={{0,4},{4,0},{1,5},{5,1},{2,6},{6,2},{3,7},{7,3},{8,12},{12,8},{9,1... | collective-permute-start | bytes 122888 | tf_op jit(solution)/shard_map/ppermute | solution.py:328
  48.4 6.6 %collective-permute-start.22 = (bf16[208,128]{1,0:T(8,128)(2,1)S(1)}, bf16[208,128]{1,0:T(8,128)(2,1)S(1)}, u32[]{:S(2)}, u32[]{:S(2)}) collective-permute-start(bf16[208,128]{1,0:T(8,128)(2,1)S(1)} %get-tuple-element.119.refs_1_), channel_id=1, source_target_pairs={{0,2},{1,3},{2,0},{3,1},{4,6},{5,7},{6,4},{7,5},{8,10},{9,11},{10,... | collective-permute-start | bytes 159752 | tf_op jit(solution)/shard_map/ppermute | solution.py:1040
  51.2 6.4 %collective-permute-start.20 = (bf16[3,80,128]{2,1,0:T(8,128)(2,1)S(1)}, bf16[3,80,128]{2,1,0:T(8,128)(2,1)S(1)}, u32[]{:S(2)}, u32[]{:S(2)}) collective-permute-start(bf16[3,80,128]{2,1,0:T(8,128)(2,1)S(1)} %grad_third.1), channel_id=1, source_target_pairs={{0,24},{8,16},{16,8},{24,0},{1,25},{9,17},{17,9},{25,1},{2,26},{10... | collective-permute-start | bytes 184328 | tf_op jit(solution)/shard_map/ppermute | solution.py:337
  54.9 5.2 %collective-permute-start.23 = (bf16[208,128]{1,0:T(8,128)(2,1)S(1)}, bf16[208,128]{1,0:T(8,128)(2,1)S(1)}, u32[]{:S(2)}, u32[]{:S(2)}) collective-permute-start(bf16[208,128]{1,0:T(8,128)(2,1)S(1)} %add_across.1.refs_0_), channel_id=1, source_target_pairs={{0,16},{8,24},{16,0},{24,8},{1,17},{9,25},{17,1},{25,9},{2,18},{10... | collective-permute-start | bytes 159752 | tf_op jit(solution)/shard_map/ppermute | solution.py:1069
  57.8 6.0 %collective-permute-start.21 = (bf16[4,80,128]{2,1,0:T(8,128)(2,1)S(1)}, bf16[4,80,128]{2,1,0:T(8,128)(2,1)S(1)}, u32[]{:S(2)}, u32[]{:S(2)}) collective-permute-start(bf16[4,80,128]{2,1,0:T(8,128)(2,1)S(1)} %get-tuple-element.127.refs_4_), channel_id=1, source_target_pairs={{0,8},{8,0},{16,24},{24,16},{1,9},{9,1},{17,25},{25,17},{2,10},{10... | collective-permute-start | bytes 245768 | tf_op jit(solution)/shard_map/ppermute | solution.py:345
  60.2 5.9 %collective-permute-start.26 = (bf16[224,128]{1,0:T(8,128)(2,1)S(1)}, bf16[224,128]{1,0:T(8,128)(2,1)S(1)}, u32[]{:S(2)}, u32[]{:S(2)}) collective-permute-start(bf16[224,128]{1,0:T(8,128)(2,1)S(1)} %finish_pieces.1.refs_0_), channel_id=1, source_target_pairs={{0,12},{4,8},{8,4},{12,0},{16,28},{20,24},{24,20},{28,16},{1,13},{... | collective-permute-start | bytes 172040 | tf_op jit(solution)/shard_map/ppermute | solution.py:1008
  60.4 5.8 %collective-permute-start.25 = (bf16[224,128]{1,0:T(8,128)(2,1)S(1)}, bf16[224,128]{1,0:T(8,128)(2,1)S(1)}, u32[]{:S(2)}, u32[]{:S(2)}) collective-permute-start(bf16[224,128]{1,0:T(8,128)(2,1)S(1)} %finish_pieces.1.refs_0_), channel_id=1, source_target_pairs={{0,4},{4,0},{8,12},{12,8},{16,20},{20,16},{24,28},{28,24},{1,5},{5... | collective-permute-start | bytes 172040 | tf_op jit(solution)/shard_map/ppermute | solution.py:1008
  61.5 4.6 %collective-permute-start.24 = (bf16[224,128]{1,0:T(8,128)(2,1)S(1)}, bf16[224,128]{1,0:T(8,128)(2,1)S(1)}, u32[]{:S(2)}, u32[]{:S(2)}) collective-permute-start(bf16[224,128]{1,0:T(8,128)(2,1)S(1)} %finish_pieces.1.refs_0_), channel_id=1, source_target_pairs={{0,8},{4,12},{8,0},{12,4},{16,24},{20,28},{24,16},{28,20},{1,9},{5... | collective-permute-start | bytes 172040 | tf_op jit(solution)/shard_map/ppermute | solution.py:1008

commit v6 on v5

--- a/solution.py
+++ b/solution.py
@@ -120,12 +120,13 @@
     emit_strips(lambda r: rows_ref[r], rows, pad, fold_ref, left_ref, right_ref)
 
 
-def add_swath(scr, stride, rows, start, offset_ref, value_ref, cols):
+def swath_rows(rows, start, offset_ref, value_ref, cols):
     offset = offset_ref[...]
     points = offset.shape[1]
     value = value_ref[...]
     total = jnp.zeros((rows, cols), F32)
-    row_hot = iota((rows, points), 0) + start == lax.shift_right_logical(offset, LANES.bit_length() - 1)
+    row = lax.shift_right_logical(offset, LANES.bit_length() - 1)
+    row_hot = iota((rows, points), 0) + start == row
     col_hot = (iota((cols, points), 0) == (offset & (LANES - 1))).astype(BF)
     for _ in range(3):
         part = value.astype(BF)
@@ -134,9 +135,12 @@
         total = total + lax.dot_general(
             lhs, col_hot, (((1,), (1,)), ((), ())), preferred_element_type=F32
         )
-    total = jnp.where(lax.axis_index("ch") == 0, total, 0.0)
-    first = scr[pl.ds(0, rows, stride=stride), :]
-    scr[pl.ds(0, rows, stride=stride), :] = first + total
+    return total
+
+
+def with_first(tile, row):
+    lifted = jnp.broadcast_to(row, tile.shape)
+    return jnp.where(iota(tile.shape, 0) == 0, tile.astype(F32) + lifted, tile.astype(F32))
 
 
 def prepare_outer(swap, count, *refs):
@@ -184,9 +188,9 @@
 
 
 def prepare_far(part, *refs):
-    (mask_ref, grad_ref, offset_ref, value_ref), weights = refs[0:4], refs[4:8]
-    far_ref, tiles_ref, taps_ref = refs[8:11]
-    scr, weights_scr, turn_scr, pick_e, pick_p = refs[11:]
+    (mask_ref, grad_ref), weights = refs[0:2], refs[2:6]
+    far_ref, tiles_ref, taps_ref = refs[6:9]
+    scr, weights_scr, turn_scr, pick_e, pick_p = refs[9:]
     channels, rows, cols = grad_ref.shape
     pad = taps_ref.shape[0]
     weight_picks(part, pad, weights_scr.shape[1], pick_e.shape[0], pick_e, pick_p)
@@ -207,7 +211,6 @@
     lax.fori_loop(0, channels, body, 0, unroll=5 if channels % 5 == 0 else 1)
     for c in range(channels, pad):
         scr[pl.ds(c, half, stride=pad), :] = jnp.zeros((half, cols), F32)
-    add_swath(scr, pad, half, start, offset_ref, value_ref, cols)
     mask = mask_ref[pl.ds(start, half), :].astype(F32)
     count_rows = half // 2
     for r in range(half):
@@ -222,7 +225,6 @@
     rows, pad, cols = rows_ref.shape
     mask = mask_ref[...].astype(F32)
     to_rows(grad_ref, None, scr, pad)
-    add_swath(scr, pad, rows, 0, offset_ref, value_ref, cols)
     for r in range(rows):
         rows_ref[r] = (scr[r * pad : (r + 1) * pad, :] * mask[r : r + 1, :]).astype(BF)
     full = tiles_ref.shape[0]
@@ -233,6 +235,10 @@
         for r in range(count):
             at = full + r * pad
             to[at : at + pad, :] = rows_ref[(me ^ k) * count + r]
+    swath = swath_rows(rows, 0, offset_ref, value_ref, cols) * mask
+    swath = jnp.where(me == 0, swath, 0.0)
+    for r in range(rows):
+        rows_ref[r, 0:16, :] = with_first(rows_ref[r, 0:16, :], swath[r : r + 1, :]).astype(BF)
 
 
 def second_half(in_ref, out_ref):
@@ -628,8 +634,8 @@
 
 
 def activation_gradient(part, *refs):
-    parts = refs[0:4]
-    act_ref, y_scr, w_scr, t_scr, pick_e_ref, pick_p_ref = refs[4:]
+    parts, (mask_ref, offset_ref, value_ref) = refs[0:4], refs[4:7]
+    act_ref, y_scr, w_scr, t_scr, pick_e_ref, pick_p_ref = refs[7:]
     me = lax.axis_index("ch")
     tiles = w_scr.shape[1] // LANES
     hid = w_scr.shape[0] // 4
@@ -653,6 +659,12 @@
                 to = jnp.where(slot < split, slot + LANES, slot - split + depth - 4 * pad)
                 at = start + r * pad + 16 * u
                 y_scr[pl.ds(aligned(to), 16), cols] = ref[at : at + 16, :]
+    rows = pl.ds(pl.multiple_of(me * part_rows, part_rows), part_rows)
+    swath = swath_rows(part_rows, me * part_rows, offset_ref, value_ref, LANES)
+    swath = swath * mask_ref[rows, :].astype(F32)
+    for r in range(part_rows):
+        at = (slice(LANES, LANES + 16), slice(r * LANES, (r + 1) * LANES))
+        y_scr[at] = with_first(y_scr[at], swath[r : r + 1, :]).astype(BF)
     t_scr[...] = jnp.transpose(w_scr[:, 0:depth])
     step = 256
     for start in range(0, cells, step):
@@ -870,7 +882,7 @@
     to_far, tiles, taps = call(
         functools.partial(prepare_far, part),
         [shape((far_rows, LANES), BF), shape((tile_rows, LANES), BF), shape((pad, LANES), F32)],
-        [land_mask, *held],
+        [land_mask, held[0], *held[3:]],
         [
             pltpu.VMEM((rows // 2 * pad, cols), F32),
             pltpu.VMEM((hid, wide), BF),
@@ -941,7 +953,7 @@
             shape((channels, depth), BF),
             shape((channels, depth), BF),
         ],
-        [own, lax.ppermute(to_core, "ch", core), from_far, passed],
+        [own, lax.ppermute(to_core, "ch", core), from_far, passed, land_mask, *held[1:3]],
         (),
         "activation_gradient",
     )

time: 67.4 us -> 67.1 us (level)
  transfers between devices with their start and end apart: 27 -> 27, of which waited for: 14 -> 12; matrix products, arithmetic and copies ran while one was open for 0% -> 0% of each run, Pallas kernels for 20% -> 21%
where the time goes in v6:
time: 67.1 us; the launch traced here: 67 us
  starting transfers between devices  27 us (40%)
  Pallas kernels  19.8 us (30%)
  waiting for transfers between devices  19.3 us (29%)
  between operations  0.9 us (1%)
    pallas_call x26, Pallas kernels, call(): pl.pallas_call(kernel, out_shape=tuple(outs), in_specs=[pl.BlockSpec(memo...  19.8 us
    ppermute x2, starting transfers between devices, exchange_halo(): lax.ppermute(third_out, 'lon', [(lon, lon ^ 3) for lon in range(n_lon)])  7.36 us
    ppermute x6, starting transfers between devices, over_plane(): lax.ppermute(values[k - 1], ('lon', 'lat'), turn_plane(k))  7.07 us
    ppermute x2, waiting for transfers between devices, exchange_halo(): lax.ppermute(third_out, 'lon', [(lon, lon ^ 3) for lon in range(n_lon)])  5 us
    ppermute x6, waiting for transfers between devices, over_plane(): lax.ppermute(values[k - 1], ('lon', 'lat'), turn_plane(k))  4.16 us
    ppermute x2, waiting for transfers between devices, exchange_halo(): got = lax.ppermute(first, 'lon', [(lon, lon ^ 1) for lon in range(n_lon)])  3.77 us
    ppermute x2, starting transfers between devices, exchange_halo(): got = lax.ppermute(outer[0], 'lat', [(0, 1), (1, 0)])  3.15 us
    ppermute x1, starting transfers between devices, on_device(): from_far = lax.ppermute(to_far, 'ch', across)  3 us
  transfers between devices with their start and end apart: 27, of which 12 were waited for; matrix products, arithmetic and copies ran while one was open for 0% of the time, Pallas kernels for 21%

profile of v6, /device:TPU:0, one launch (start us, length us, event | category | flops | bytes accessed | tf_op | source)
XLA Modules:
  0.0 67.0 jit_solution(11934463137122588552)
XLA Ops:
  0.6 1.5 %outer_rows.1 = (bf16[2,80,128]{2,1,0:T(8,128)(2,1)S(1)}, bf16[75,32,128]{2,1,0:T(8,128)(2,1)S(1)}, s32[32,128]{1,0:T(8,128)S(1)}, bf16[75,32,128]{2,1,0:T(8,128...) custom-call(bf16[75,32,128]{2,1,0:T(8,128)(2,1)} %refs_0_.1, ...), custom_call_target="tpu_custom_call" | custom-call | bytes 2906120 | tf_op jit(solution)/shard_map/outer_rows/pallas_call | solution.py:35
  2.1 0.9 %far_rows.1 = (bf16[2080,128]{1,0:T(8,128)(2,1)S(1)}, bf16[800,128]{1,0:T(8,128)(2,1)S(1)}, f32[80,128]{1,0:T(8,128)S(1)}) custom-call(s32[32,128]{1,0:T(8,128)S(1)} %get-tuple-element.73.refs_0_.refs_1_.mask_ref.refs_4_, bf16[75,32,128]{2,1,0:T(8,128)(2,1)S(1)} %get-tuple-element.74.refs_1_.grad_ref, bf16[150,300]{1,0:T(8,128)(2,1)S(1)} %get-tuple-element.75.refs_2_, ...), custom_call_target="tpu_custom_call" | custom-call | bytes 1592324 | tf_op jit(solution)/shard_map/far_rows/pallas_call | solution.py:35
  3.0 3.0 %collective-permute-start.3 = (bf16[2080,128]{1,0:T(8,128)(2,1)S(1)}, bf16[2080,128]{1,0:T(8,128)(2,1)S(1)}, u32[]{:S(2)}, u32[]{:S(2)}) collective-permute-start(bf16[2080,128]{1,0:T(8,128)(2,1)S(1)} %get-tuple-element.93), channel_id=1, source_target_pairs={{0,2},{1,3},{2,0},{3,1},{4,6},{5,7},{6,4},{7,5},{8,10},{9,11},{10,... | collective-permute-start | bytes 1597448 | tf_op jit(solution)/shard_map/ppermute | solution.py:911
  6.0 1.5 %collective-permute-start = (bf16[2,80,128]{2,1,0:T(8,128)(2,1)S(1)}, bf16[2,80,128]{2,1,0:T(8,128)(2,1)S(1)}, u32[]{:S(2)}, u32[]{:S(2)}) collective-permute-start(bf16[2,80,128]{2,1,0:T(8,128)(2,1)S(1)} %get-tuple-element.81), channel_id=1, source_target_pairs={{0,4},{4,0},{1,5},{5,1},{2,6},{6,2},{3,7},{7,3},{8,12},{12,8},{9,1... | collective-permute-start | bytes 122888 | tf_op jit(solution)/shard_map/ppermute | solution.py:334
  7.6 1.0 %state_rows.1 = (bf16[32,80,128]{2,1,0:T(8,128)(2,1)S(1)}, bf16[2,80,128]{2,1,0:T(8,128)(2,1)S(1)}, bf16[80,128]{1,0:T(8,128)(2,1)S(1)}, bf16[80,128]{1,0:T(8,128)(2,1)S(1)}) custom-call(bf16[75,32,128]{2,1,0:T(8,128)(2,1)S(1)} %get-tuple-element.72.refs_0_, s32[32,128]{1,0:T(8,128)S(1)} %get-tuple-element.73.refs_0_.refs_1_.mask_ref.refs_4_, ...), custom_call_target="tpu_custom_call" | custom-call | bytes 1409024 | tf_op jit(solution)/shard_map/state_rows/pallas_call | solution.py:35
  10.2 3.7 %collective-permute-start.1 = (bf16[3,80,128]{2,1,0:T(8,128)(2,1)S(1)}, bf16[3,80,128]{2,1,0:T(8,128)(2,1)S(1)}, u32[]{:S(2)}, u32[]{:S(2)}) collective-permute-start(bf16[3,80,128]{2,1,0:T(8,128)(2,1)S(1)} %state_third.1), channel_id=1, source_target_pairs={{0,24},{8,16},{16,8},{24,0},{1,25},{9,17},{17,9},{25,1},{2,26},{10... | collective-permute-start | bytes 184328 | tf_op jit(solution)/shard_map/ppermute | solution.py:343
  13.8 2.4 %collective-permute-done.1.third_ref = bf16[3,80,128]{2,1,0:T(8,128)(2,1)S(1)} collective-permute-done((bf16[3,80,128]{2,1,0:T(8,128)(2,1)S(1)}, bf16[3,80,128]{2,1,0:T(8,128)(2,1)S(1)}, u32[]{:S(2)}, u32[]{:S(2)}) %collective-permute-start.1) | collective-permute-done | bytes 61472 | tf_op jit(solution)/shard_map/ppermute | solution.py:343
  16.5 3.8 %collective-permute-done.2.left_ref.refs_1_.refs_2_ = bf16[1,80,128]{2,1,0:T(8,128)(2,1)S(1)} collective-permute-done((bf16[1,80,128]{2,1,0:T(8,128)(2,1)S(1)}, bf16[1,80,128]{2,1,0:T(8,128)(2,1)S(1)}, u32[]{:S(2)}, u32[]{:S(2)}) %collective-permute-start.2) | collective-permute-done | bytes 20512 | tf_op jit(solution)/shard_map/ppermute | solution.py:351
  20.8 1.3 %conv_away.1 = (bf16[4,80,128]{2,1,0:T(8,128)(2,1)S(1)}, bf16[4,80,128]{2,1,0:T(8,128)(2,1)S(1)}, bf16[4,80,128]{2,1,0:T(8,128)(2,1)S(1)}, bf16[4,80,128]{2,1,0:T(8,128)(2,1)S(1)}) custom-call(bf16[32,80,128]{2,1,0:T(8,128)(2,1)S(1)} %get-tuple-element.80.block_ref.refs_0_, bf16[4,80,128]{2,1,0:T(8,128)(2,1)S(1)} %get-tuple-element.89.halo_ref.refs_1_, ...), custom_call_target="tpu_custom_call" | custom-call | bytes 1146880 | tf_op jit(solution)/shard_map/conv_away/pallas_call | solution.py:35
  22.2 1.6 %collective-permute-start.6 = (bf16[4,80,128]{2,1,0:T(8,128)(2,1)S(1)}, bf16[4,80,128]{2,1,0:T(8,128)(2,1)S(1)}, u32[]{:S(2)}, u32[]{:S(2)}) collective-permute-start(bf16[4,80,128]{2,1,0:T(8,128)(2,1)S(1)} %get-tuple-element.92.refs_5_), channel_id=1, source_target_pairs={{0,2},{1,3},{2,0},{3,1},{4,6},{5,7},{6,4},{7,5},{8,10},{9,11},{10,... | collective-permute-start | bytes 245768 | tf_op jit(solution)/shard_map/ppermute | solution.py:941
  23.8 1.3 %conv_here.1 = (bf16[4,80,128]{2,1,0:T(8,128)(2,1)S(1)}, bf16[4,80,128]{2,1,0:T(8,128)(2,1)S(1)}, bf16[4,80,128]{2,1,0:T(8,128)(2,1)S(1)}, bf16[4,80,128]{2,1,0:T(8,128)(2,1)S(1)}) custom-call(bf16[32,80,128]{2,1,0:T(8,128)(2,1)S(1)} %get-tuple-element.80.block_ref.refs_0_, bf16[4,80,128]{2,1,0:T(8,128)(2,1)S(1)} %get-tuple-element.89.halo_ref.refs_1_, ...), custom_call_target="tpu_custom_call" | custom-call | bytes 1761280 | tf_op jit(solution)/shard_map/conv_here/pallas_call | solution.py:35
  25.7 0.9 %collective-permute-done.7.refs_3_ = bf16[4,80,128]{2,1,0:T(8,128)(2,1)S(1)} collective-permute-done((bf16[4,80,128]{2,1,0:T(8,128)(2,1)S(1)}, bf16[4,80,128]{2,1,0:T(8,128)(2,1)S(1)}, u32[]{:S(2)}, u32[]{:S(2)}) %collective-permute-start.7) | collective-permute-done | bytes 81952 | tf_op jit(solution)/shard_map/ppermute | solution.py:942
  27.5 1.4 %activation_gradient.1 = (f32[640,1024]{1,0:T(8,128)S(1)}, bf16[384,1024]{1,0:T(8,128)(2,1)S(1)}, bf16[640,640]{1,0:T(8,128)(2,1)S(1)}, bf16[384,640]{1,0:T(8,12...) custom-call(bf16[1440,128]{1,0:T(8,128)(2,1)S(1)} %get-tuple-element.97.refs_0_, ...), custom_call_target="tpu_custom_call" | custom-call | bytes 7002112 | tf_op jit(solution)/shard_map/activation_gradient/pallas_call | solution.py:35
  28.9 1.8 %hidden_first.1 = (bf16[640,512]{1,0:T(8,128)(2,1)S(1)}, f32[2,832,128]{2,1,0:T(8,128)S(1)}, f32[2,832,128]{2,1,0:T(8,128)S(1)}) custom-call(bf16[4,80,128]{2,1,0:T(8,128)(2,1)S(1)} %get-tuple-element.94.refs_0_, bf16[4,80,128]{2,1,0:T(8,128)(2,1)S(1)} %collective-permute-done.5.refs_1_, bf16[4,80,128]{2,1,0:T(8,128)(2,1)S(1)} %collective-permute-done.6.refs_2_, ...), custom_call_target="tpu_custom_call" | custom-call | bytes 6914048 | tf_op jit(solution)/shard_map/hidden_first/pallas_call | solution.py:35
  30.7 1.0 %collective-permute-done.11.refs_3_ = bf16[4,80,128]{2,1,0:T(8,128)(2,1)S(1)} collective-permute-done((bf16[4,80,128]{2,1,0:T(8,128)(2,1)S(1)}, bf16[4,80,128]{2,1,0:T(8,128)(2,1)S(1)}, u32[]{:S(2)}, u32[]{:S(2)}) %collective-permute-start.11) | collective-permute-done | bytes 81952 | tf_op jit(solution)/shard_map/ppermute | solution.py:942
  31.8 1.8 %hidden_second.1 = (bf16[640,512]{1,0:T(8,128)(2,1)S(1)}, f32[2,832,128]{2,1,0:T(8,128)S(1)}, bf16[2,832,128]{2,1,0:T(8,128)(2,1)S(1)}) custom-call(bf16[4,80,128]{2,1,0:T(8,128)(2,1)S(1)} %get-tuple-element.102.refs_0_, bf16[4,80,128]{2,1,0:T(8,128)(2,1)S(1)} %collective-permute-done.9.refs_1_, bf16[4,80,128]{2,1,0:T(8,128)(2,1)S(1)} %collective-permute-done.10.refs_2_, ...), custom_call_target="tpu_custom_call" | custom-call | bytes 8192000 | tf_op jit(solution)/shard_map/hidden_second/pallas_call | solution.py:35
  35.5 1.6 %collective-permute-start.16 = (bf16[2,208,128]{2,1,0:T(8,128)(2,1)S(1)}, bf16[2,208,128]{2,1,0:T(8,128)(2,1)S(1)}, u32[]{:S(2)}, u32[]{:S(2)}) collective-permute-start(bf16[2,208,128]{2,1,0:T(8,128)(2,1)S(1)} %get-tuple-element.116), channel_id=1, source_target_pairs={{0,4},{4,0},{8,12},{12,8},{16,20},{20,16},{24,28},{28,24},{1,5},{5... | collective-permute-start | bytes 319496 | tf_op jit(solution)/shard_map/ppermute | solution.py:1020
  37.7 1.3 %collective-permute-start.15 = (bf16[2,208,128]{2,1,0:T(8,128)(2,1)S(1)}, bf16[2,208,128]{2,1,0:T(8,128)(2,1)S(1)}, u32[]{:S(2)}, u32[]{:S(2)}) collective-permute-start(bf16[2,208,128]{2,1,0:T(8,128)(2,1)S(1)} %get-tuple-element.115.refs_4_), channel_id=1, source_target_pairs={{0,8},{4,12},{8,0},{12,4},{16,24},{20,28},{24,16},{28,20},{1,9},{5... | collective-permute-start | bytes 319496 | tf_op jit(solution)/shard_map/ppermute | solution.py:1020
  39.0 1.2 %shift_columns.1 = (bf16[36,80,128]{2,1,0:T(8,128)(2,1)S(1)}, bf16[36,80,128]{2,1,0:T(8,128)(2,1)S(1)}) custom-call(bf16[32,80,128]{2,1,0:T(8,128)(2,1)S(1)} %get-tuple-element.80.block_ref.refs_0_, bf16[4,80,128]{2,1,0:T(8,128)(2,1)S(1)} %get-tuple-element.89.halo_ref.refs_1_, bf16[1,80,128]{2,1,0:T(8,128)(2,1)S(1)} %collective-permute-done.2.left_ref.refs_1_.refs_2_, ...), custom_call_target="tpu_custom_call" | custom-call | bytes 2359296 | tf_op jit(solution)/shard_map/shift_columns/pallas_call | solution.py:35
  40.2 2.0 %collective-permute-done.16.refs_2_ = bf16[2,208,128]{2,1,0:T(8,128)(2,1)S(1)} collective-permute-done((bf16[2,208,128]{2,1,0:T(8,128)(2,1)S(1)}, bf16[2,208,128]{2,1,0:T(8,128)(2,1)S(1)}, u32[]{:S(2)}, u32[]{:S(2)}) %collective-permute-start.16) | collective-permute-done | bytes 106528 | tf_op jit(solution)/shard_map/ppermute | solution.py:1020
  42.3 1.6 %collective-permute-done.17.refs_3_ = bf16[2,208,128]{2,1,0:T(8,128)(2,1)S(1)} collective-permute-done((bf16[2,208,128]{2,1,0:T(8,128)(2,1)S(1)}, bf16[2,208,128]{2,1,0:T(8,128)(2,1)S(1)}, u32[]{:S(2)}, u32[]{:S(2)}) %collective-permute-start.17) | collective-permute-done | bytes 106528 | tf_op jit(solution)/shard_map/ppermute | solution.py:1020
  44.5 1.4 %collective-permute-done.18.passed = bf16[8,80,128]{2,1,0:T(8,128)(2,1)S(1)} collective-permute-done((bf16[8,80,128]{2,1,0:T(8,128)(2,1)S(1)}, bf16[8,80,128]{2,1,0:T(8,128)(2,1)S(1)}, u32[]{:S(2)}, u32[]{:S(2)}) %collective-permute-start.18) | collective-permute-done | bytes 163872 | tf_op jit(solution)/shard_map/ppermute | solution.py:1036
  46.4 1.6 %collective-permute-start.19 = (bf16[2,80,128]{2,1,0:T(8,128)(2,1)S(1)}, bf16[2,80,128]{2,1,0:T(8,128)(2,1)S(1)}, u32[]{:S(2)}, u32[]{:S(2)}) collective-permute-start(bf16[2,80,128]{2,1,0:T(8,128)(2,1)S(1)} %get-tuple-element.121), channel_id=1, source_target_pairs={{0,4},{4,0},{1,5},{5,1},{2,6},{6,2},{3,7},{7,3},{8,12},{12,8},{9,1... | collective-permute-start | bytes 122888 | tf_op jit(solution)/shard_map/ppermute | solution.py:334
  48.0 1.5 %collective-permute-start.22 = (bf16[208,128]{1,0:T(8,128)(2,1)S(1)}, bf16[208,128]{1,0:T(8,128)(2,1)S(1)}, u32[]{:S(2)}, u32[]{:S(2)}) collective-permute-start(bf16[208,128]{1,0:T(8,128)(2,1)S(1)} %get-tuple-element.119.refs_1_), channel_id=1, source_target_pairs={{0,2},{1,3},{2,0},{3,1},{4,6},{5,7},{6,4},{7,5},{8,10},{9,11},{10,... | collective-permute-start | bytes 159752 | tf_op jit(solution)/shard_map/ppermute | solution.py:1052
  49.5 1.2 %kernel_gradient.1.refs_0_.refs_2_ = bf16[80,128]{1,0:T(8,128)(2,1)S(1)} custom-call(bf16[32,80,128]{2,1,0:T(8,128)(2,1)S(1)} %get-tuple-element.120.grad_ref.block_ref, bf16[32,80,128]{2,1,0:T(8,128)(2,1)S(1)} %get-tuple-element.80.block_ref.refs_0_, bf16[4,80,128]{2,1,0:T(8,128)(2,1)S(1)} %get-tuple-element.89.halo_ref.refs_1_, ...), custom_call_target="tpu_custom_call" | custom-call | bytes 2887680 | tf_op jit(solution)/shard_map/kernel_gradient/pallas_call | solution.py:35
  50.9 3.7 %collective-permute-start.20 = (bf16[3,80,128]{2,1,0:T(8,128)(2,1)S(1)}, bf16[3,80,128]{2,1,0:T(8,128)(2,1)S(1)}, u32[]{:S(2)}, u32[]{:S(2)}) collective-permute-start(bf16[3,80,128]{2,1,0:T(8,128)(2,1)S(1)} %grad_third.1), channel_id=1, source_target_pairs={{0,24},{8,16},{16,8},{24,0},{1,25},{9,17},{17,9},{25,1},{2,26},{10... | collective-permute-start | bytes 184328 | tf_op jit(solution)/shard_map/ppermute | solution.py:343
  54.7 2.6 %collective-permute-done.20.third_ref.refs_3_ = bf16[3,80,128]{2,1,0:T(8,128)(2,1)S(1)} collective-permute-done((bf16[3,80,128]{2,1,0:T(8,128)(2,1)S(1)}, bf16[3,80,128]{2,1,0:T(8,128)(2,1)S(1)}, u32[]{:S(2)}, u32[]{:S(2)}) %collective-permute-start.20) | collective-permute-done | bytes 61472 | tf_op jit(solution)/shard_map/ppermute | solution.py:343
  57.5 2.3 %collective-permute-done.23.refs_1_ = bf16[208,128]{1,0:T(8,128)(2,1)S(1)} collective-permute-done((bf16[208,128]{1,0:T(8,128)(2,1)S(1)}, bf16[208,128]{1,0:T(8,128)(2,1)S(1)}, u32[]{:S(2)}, u32[]{:S(2)}) %collective-permute-start.23) | collective-permute-done | bytes 53280 | tf_op jit(solution)/shard_map/ppermute | solution.py:1081
  60.1 1.1 %collective-permute-start.25 = (bf16[224,128]{1,0:T(8,128)(2,1)S(1)}, bf16[224,128]{1,0:T(8,128)(2,1)S(1)}, u32[]{:S(2)}, u32[]{:S(2)}) collective-permute-start(bf16[224,128]{1,0:T(8,128)(2,1)S(1)} %finish_pieces.1.refs_0_), channel_id=1, source_target_pairs={{0,4},{4,0},{8,12},{12,8},{16,20},{20,16},{24,28},{28,24},{1,5},{5... | collective-permute-start | bytes 172040 | tf_op jit(solution)/shard_map/ppermute | solution.py:1020
  61.2 2.2 %collective-permute-start.24 = (bf16[224,128]{1,0:T(8,128)(2,1)S(1)}, bf16[224,128]{1,0:T(8,128)(2,1)S(1)}, u32[]{:S(2)}, u32[]{:S(2)}) collective-permute-start(bf16[224,128]{1,0:T(8,128)(2,1)S(1)} %finish_pieces.1.refs_0_), channel_id=1, source_target_pairs={{0,8},{4,12},{8,0},{12,4},{16,24},{20,28},{24,16},{28,20},{1,9},{5... | collective-permute-start | bytes 172040 | tf_op jit(solution)/shard_map/ppermute | solution.py:1020
  63.4 2.4 %conv_adjoint.1 = (bf16[75,32,128]{2,1,0:T(8,128)(2,1)}, f32[8,128]{1,0:T(8,128)S(1)}) custom-call(bf16[32,80,128]{2,1,0:T(8,128)(2,1)S(1)} %get-tuple-element.120.grad_ref.block_ref, bf16[4,80,128]{2,1,0:T(8,128)(2,1)S(1)} %get-tuple-element.126.halo_ref, bf16[4,80,128]{2,1,0:T(8,128)(2,1)S(1)} %collective-permute-done.21.left_ref, ...), custom_call_target="tpu_custom_call" | custom-call | bytes 2170880 | tf_op jit(solution)/shard_map/conv_adjoint/pallas_call | solution.py:35
  65.9 1.1 %write_parameters.1 = (f32[150,300]{1,0:T(8,128)}, f32[150,300]{1,0:T(8,128)}, f32[1,150]{1,0:T(1,128)}, f32[3,3,75]{2,1,0:T(4,128)}) custom-call(bf16[224,128]{1,0:T(8,128)(2,1)S(1)} %finish_pieces.1.refs_0_, bf16[224,128]{1,0:T(8,128)(2,1)S(1)} %collective-permute-done.24.refs_1_, bf16[224,128]{1,0:T(8,128)(2,1)S(1)} %collective-permute-done.25.refs_2_, ...), custom_call_target="tpu_custom_call" | custom-call | bytes 1057572 | tf_op jit(solution)/shard_map/write_parameters/pallas_call | solution.py:35
  (48 shorter events, 8.4 us)
Async XLA Ops:
  3.0 17.2 %collective-permute-start.3 = (bf16[2080,128]{1,0:T(8,128)(2,1)S(1)}, bf16[2080,128]{1,0:T(8,128)(2,1)S(1)}, u32[]{:S(2)}, u32[]{:S(2)}) collective-permute-start(bf16[2080,128]{1,0:T(8,128)(2,1)S(1)} %get-tuple-element.93), channel_id=1, source_target_pairs={{0,2},{1,3},{2,0},{3,1},{4,6},{5,7},{6,4},{7,5},{8,10},{9,11},{10,... | collective-permute-start | bytes 1597448 | tf_op jit(solution)/shard_map/ppermute | solution.py:911
  6.0 4.0 %collective-permute-start = (bf16[2,80,128]{2,1,0:T(8,128)(2,1)S(1)}, bf16[2,80,128]{2,1,0:T(8,128)(2,1)S(1)}, u32[]{:S(2)}, u32[]{:S(2)}) collective-permute-start(bf16[2,80,128]{2,1,0:T(8,128)(2,1)S(1)} %get-tuple-element.81), channel_id=1, source_target_pairs={{0,4},{4,0},{1,5},{5,1},{2,6},{6,2},{3,7},{7,3},{8,12},{12,8},{9,1... | collective-permute-start | bytes 122888 | tf_op jit(solution)/shard_map/ppermute | solution.py:334
  10.2 6.1 %collective-permute-start.1 = (bf16[3,80,128]{2,1,0:T(8,128)(2,1)S(1)}, bf16[3,80,128]{2,1,0:T(8,128)(2,1)S(1)}, u32[]{:S(2)}, u32[]{:S(2)}) collective-permute-start(bf16[3,80,128]{2,1,0:T(8,128)(2,1)S(1)} %state_third.1), channel_id=1, source_target_pairs={{0,24},{8,16},{16,8},{24,0},{1,25},{9,17},{17,9},{25,1},{2,26},{10... | collective-permute-start | bytes 184328 | tf_op jit(solution)/shard_map/ppermute | solution.py:343
  16.4 3.8 %collective-permute-start.2 = (bf16[1,80,128]{2,1,0:T(8,128)(2,1)S(1)}, bf16[1,80,128]{2,1,0:T(8,128)(2,1)S(1)}, u32[]{:S(2)}, u32[]{:S(2)}) collective-permute-start(bf16[1,80,128]{2,1,0:T(8,128)(2,1)S(1)} %get-tuple-element.90), channel_id=1, source_target_pairs={{0,8},{8,0},{16,24},{24,16},{1,9},{9,1},{17,25},{25,17},{2,10},{10... | collective-permute-start | bytes 61448 | tf_op jit(solution)/shard_map/ppermute | solution.py:351
  20.2 3.6 %collective-permute-start.4 = (bf16[2080,128]{1,0:T(8,128)(2,1)S(1)}, bf16[2080,128]{1,0:T(8,128)(2,1)S(1)}, u32[]{:S(2)}, u32[]{:S(2)}) collective-permute-start(bf16[2080,128]{1,0:T(8,128)(2,1)S(1)} %cotan_relay.1.refs_2_), channel_id=1, source_target_pairs={{0,1},{1,0},{2,3},{3,2},{4,5},{5,4},{6,7},{7,6},{8,9},{9,8},{10,11... | collective-permute-start | bytes 1597448 | tf_op jit(solution)/shard_map/ppermute | solution.py:927
  20.2 6.8 %collective-permute-start.8 = (bf16[1440,128]{1,0:T(8,128)(2,1)S(1)}, bf16[1440,128]{1,0:T(8,128)(2,1)S(1)}, u32[]{:S(2)}, u32[]{:S(2)}) collective-permute-start(bf16[1440,128]{1,0:T(8,128)(2,1)S(1)} %get-tuple-element.88.refs_4_), channel_id=1, source_target_pairs={{0,1},{1,0},{2,3},{3,2},{4,5},{5,4},{6,7},{7,6},{8,9},{9,8},{10,11... | collective-permute-start | bytes 1105928 | tf_op jit(solution)/shard_map/ppermute | solution.py:956
  22.0 4.6 %collective-permute-start.7 = (bf16[4,80,128]{2,1,0:T(8,128)(2,1)S(1)}, bf16[4,80,128]{2,1,0:T(8,128)(2,1)S(1)}, u32[]{:S(2)}, u32[]{:S(2)}) collective-permute-start(bf16[4,80,128]{2,1,0:T(8,128)(2,1)S(1)} %get-tuple-element.96), channel_id=1, source_target_pairs={{0,3},{1,2},{2,1},{3,0},{4,7},{5,6},{6,5},{7,4},{8,11},{9,10},{10,... | collective-permute-start | bytes 245768 | tf_op jit(solution)/shard_map/ppermute | solution.py:942
  22.2 6.7 %collective-permute-start.6 = (bf16[4,80,128]{2,1,0:T(8,128)(2,1)S(1)}, bf16[4,80,128]{2,1,0:T(8,128)(2,1)S(1)}, u32[]{:S(2)}, u32[]{:S(2)}) collective-permute-start(bf16[4,80,128]{2,1,0:T(8,128)(2,1)S(1)} %get-tuple-element.92.refs_5_), channel_id=1, source_target_pairs={{0,2},{1,3},{2,0},{3,1},{4,6},{5,7},{6,4},{7,5},{8,10},{9,11},{10,... | collective-permute-start | bytes 245768 | tf_op jit(solution)/shard_map/ppermute | solution.py:941
  25.1 3.8 %collective-permute-start.5 = (bf16[4,80,128]{2,1,0:T(8,128)(2,1)S(1)}, bf16[4,80,128]{2,1,0:T(8,128)(2,1)S(1)}, u32[]{:S(2)}, u32[]{:S(2)}) collective-permute-start(bf16[4,80,128]{2,1,0:T(8,128)(2,1)S(1)} %get-tuple-element.95), channel_id=1, source_target_pairs={{0,1},{1,0},{2,3},{3,2},{4,5},{5,4},{6,7},{7,6},{8,9},{9,8},{10,11... | collective-permute-start | bytes 245768 | tf_op jit(solution)/shard_map/ppermute | solution.py:940
  25.3 5.4 %collective-permute-start.10 = (bf16[4,80,128]{2,1,0:T(8,128)(2,1)S(1)}, bf16[4,80,128]{2,1,0:T(8,128)(2,1)S(1)}, u32[]{:S(2)}, u32[]{:S(2)}) collective-permute-start(bf16[4,80,128]{2,1,0:T(8,128)(2,1)S(1)} %get-tuple-element.104), channel_id=1, source_target_pairs={{0,2},{1,3},{2,0},{3,1},{4,6},{5,7},{6,4},{7,5},{8,10},{9,11},{10,... | collective-permute-start | bytes 245768 | tf_op jit(solution)/shard_map/ppermute | solution.py:941
  26.6 5.2 %collective-permute-start.11 = (bf16[4,80,128]{2,1,0:T(8,128)(2,1)S(1)}, bf16[4,80,128]{2,1,0:T(8,128)(2,1)S(1)}, u32[]{:S(2)}, u32[]{:S(2)}) collective-permute-start(bf16[4,80,128]{2,1,0:T(8,128)(2,1)S(1)} %get-tuple-element.105), channel_id=1, source_target_pairs={{0,3},{1,2},{2,1},{3,0},{4,7},{5,6},{6,5},{7,4},{8,11},{9,10},{10,... | collective-permute-start | bytes 245768 | tf_op jit(solution)/shard_map/ppermute | solution.py:942
  27.0 4.8 %collective-permute-start.9 = (bf16[4,80,128]{2,1,0:T(8,128)(2,1)S(1)}, bf16[4,80,128]{2,1,0:T(8,128)(2,1)S(1)}, u32[]{:S(2)}, u32[]{:S(2)}) collective-permute-start(bf16[4,80,128]{2,1,0:T(8,128)(2,1)S(1)} %get-tuple-element.103), channel_id=1, source_target_pairs={{0,1},{1,0},{2,3},{3,2},{4,5},{5,4},{6,7},{7,6},{8,9},{9,8},{10,11... | collective-permute-start | bytes 245768 | tf_op jit(solution)/shard_map/ppermute | solution.py:940
  33.6 1.8 %collective-permute-start.14 = (bf16[2,832,128]{2,1,0:T(8,128)(2,1)S(1)}, bf16[2,832,128]{2,1,0:T(8,128)(2,1)S(1)}, u32[]{:S(2)}, u32[]{:S(2)}) collective-permute-start(bf16[2,832,128]{2,1,0:T(8,128)(2,1)S(1)} %get-tuple-element.113), channel_id=1, source_target_pairs={{0,1},{1,0},{2,3},{3,2},{4,5},{5,4},{6,7},{7,6},{8,9},{9,8},{10,11... | collective-permute-start | bytes 1277960 | tf_op jit(solution)/shard_map/ppermute | solution.py:975
  34.3 10.2 %collective-permute-start.13 = (bf16[2,8,80,128]{3,2,1,0:T(8,128)(2,1)S(1)}, bf16[2,8,80,128]{3,2,1,0:T(8,128)(2,1)S(1)}, u32[]{:S(2)}, u32[]{:S(2)}) collective-permute-start(bf16[2,8,80,128]{3,2,1,0:T(8,128)(2,1)S(1)} %gradient_away.1.refs_3_), channel_id=1, source_target_pairs={{0,2},{1,3},{2,0},{3,1},{4,6},{5,7},{6,4},{7,5},{8,10},{9,11},{10,... | collective-permute-start | bytes 983048 | tf_op jit(solution)/shard_map/ppermute | solution.py:993
  35.2 5.0 %collective-permute-start.12 = (bf16[8,80,128]{2,1,0:T(8,128)(2,1)S(1)}, bf16[8,80,128]{2,1,0:T(8,128)(2,1)S(1)}, u32[]{:S(2)}, u32[]{:S(2)}) collective-permute-start(bf16[8,80,128]{2,1,0:T(8,128)(2,1)S(1)} %get-tuple-element.111), channel_id=1, source_target_pairs={{0,1},{1,0},{2,3},{3,2},{4,5},{5,4},{6,7},{7,6},{8,9},{9,8},{10,11... | collective-permute-start | bytes 491528 | tf_op jit(solution)/shard_map/ppermute | solution.py:992
  35.5 6.8 %collective-permute-start.16 = (bf16[2,208,128]{2,1,0:T(8,128)(2,1)S(1)}, bf16[2,208,128]{2,1,0:T(8,128)(2,1)S(1)}, u32[]{:S(2)}, u32[]{:S(2)}) collective-permute-start(bf16[2,208,128]{2,1,0:T(8,128)(2,1)S(1)} %get-tuple-element.116), channel_id=1, source_target_pairs={{0,4},{4,0},{8,12},{12,8},{16,20},{20,16},{24,28},{28,24},{1,5},{5... | collective-permute-start | bytes 319496 | tf_op jit(solution)/shard_map/ppermute | solution.py:1020
  37.1 6.7 %collective-permute-start.17 = (bf16[2,208,128]{2,1,0:T(8,128)(2,1)S(1)}, bf16[2,208,128]{2,1,0:T(8,128)(2,1)S(1)}, u32[]{:S(2)}, u32[]{:S(2)}) collective-permute-start(bf16[2,208,128]{2,1,0:T(8,128)(2,1)S(1)} %get-tuple-element.117), channel_id=1, source_target_pairs={{0,12},{4,8},{8,4},{12,0},{16,28},{20,24},{24,20},{28,16},{1,13},{... | collective-permute-start | bytes 319496 | tf_op jit(solution)/shard_map/ppermute | solution.py:1020
  37.7 6.6 %collective-permute-start.15 = (bf16[2,208,128]{2,1,0:T(8,128)(2,1)S(1)}, bf16[2,208,128]{2,1,0:T(8,128)(2,1)S(1)}, u32[]{:S(2)}, u32[]{:S(2)}) collective-permute-start(bf16[2,208,128]{2,1,0:T(8,128)(2,1)S(1)} %get-tuple-element.115.refs_4_), channel_id=1, source_target_pairs={{0,8},{4,12},{8,0},{12,4},{16,24},{20,28},{24,16},{28,20},{1,9},{5... | collective-permute-start | bytes 319496 | tf_op jit(solution)/shard_map/ppermute | solution.py:1020
  44.5 1.5 %collective-permute-start.18 = (bf16[8,80,128]{2,1,0:T(8,128)(2,1)S(1)}, bf16[8,80,128]{2,1,0:T(8,128)(2,1)S(1)}, u32[]{:S(2)}, u32[]{:S(2)}) collective-permute-start(bf16[8,80,128]{2,1,0:T(8,128)(2,1)S(1)} %grad_half.1), channel_id=1, source_target_pairs={{0,1},{1,0},{2,3},{3,2},{4,5},{5,4},{6,7},{7,6},{8,9},{9,8},{10,11... | collective-permute-start | bytes 491528 | tf_op jit(solution)/shard_map/ppermute | solution.py:1036
  46.4 4.4 %collective-permute-start.19 = (bf16[2,80,128]{2,1,0:T(8,128)(2,1)S(1)}, bf16[2,80,128]{2,1,0:T(8,128)(2,1)S(1)}, u32[]{:S(2)}, u32[]{:S(2)}) collective-permute-start(bf16[2,80,128]{2,1,0:T(8,128)(2,1)S(1)} %get-tuple-element.121), channel_id=1, source_target_pairs={{0,4},{4,0},{1,5},{5,1},{2,6},{6,2},{3,7},{7,3},{8,12},{12,8},{9,1... | collective-permute-start | bytes 122888 | tf_op jit(solution)/shard_map/ppermute | solution.py:334
  48.0 6.6 %collective-permute-start.22 = (bf16[208,128]{1,0:T(8,128)(2,1)S(1)}, bf16[208,128]{1,0:T(8,128)(2,1)S(1)}, u32[]{:S(2)}, u32[]{:S(2)}) collective-permute-start(bf16[208,128]{1,0:T(8,128)(2,1)S(1)} %get-tuple-element.119.refs_1_), channel_id=1, source_target_pairs={{0,2},{1,3},{2,0},{3,1},{4,6},{5,7},{6,4},{7,5},{8,10},{9,11},{10,... | collective-permute-start | bytes 159752 | tf_op jit(solution)/shard_map/ppermute | solution.py:1052
  50.9 6.4 %collective-permute-start.20 = (bf16[3,80,128]{2,1,0:T(8,128)(2,1)S(1)}, bf16[3,80,128]{2,1,0:T(8,128)(2,1)S(1)}, u32[]{:S(2)}, u32[]{:S(2)}) collective-permute-start(bf16[3,80,128]{2,1,0:T(8,128)(2,1)S(1)} %grad_third.1), channel_id=1, source_target_pairs={{0,24},{8,16},{16,8},{24,0},{1,25},{9,17},{17,9},{25,1},{2,26},{10... | collective-permute-start | bytes 184328 | tf_op jit(solution)/shard_map/ppermute | solution.py:343
  54.6 5.2 %collective-permute-start.23 = (bf16[208,128]{1,0:T(8,128)(2,1)S(1)}, bf16[208,128]{1,0:T(8,128)(2,1)S(1)}, u32[]{:S(2)}, u32[]{:S(2)}) collective-permute-start(bf16[208,128]{1,0:T(8,128)(2,1)S(1)} %add_across.1.refs_0_), channel_id=1, source_target_pairs={{0,16},{8,24},{16,0},{24,8},{1,17},{9,25},{17,1},{25,9},{2,18},{10... | collective-permute-start | bytes 159752 | tf_op jit(solution)/shard_map/ppermute | solution.py:1081
  57.4 6.0 %collective-permute-start.21 = (bf16[4,80,128]{2,1,0:T(8,128)(2,1)S(1)}, bf16[4,80,128]{2,1,0:T(8,128)(2,1)S(1)}, u32[]{:S(2)}, u32[]{:S(2)}) collective-permute-start(bf16[4,80,128]{2,1,0:T(8,128)(2,1)S(1)} %get-tuple-element.127.refs_4_), channel_id=1, source_target_pairs={{0,8},{8,0},{16,24},{24,16},{1,9},{9,1},{17,25},{25,17},{2,10},{10... | collective-permute-start | bytes 245768 | tf_op jit(solution)/shard_map/ppermute | solution.py:351
  59.9 5.9 %collective-permute-start.26 = (bf16[224,128]{1,0:T(8,128)(2,1)S(1)}, bf16[224,128]{1,0:T(8,128)(2,1)S(1)}, u32[]{:S(2)}, u32[]{:S(2)}) collective-permute-start(bf16[224,128]{1,0:T(8,128)(2,1)S(1)} %finish_pieces.1.refs_0_), channel_id=1, source_target_pairs={{0,12},{4,8},{8,4},{12,0},{16,28},{20,24},{24,20},{28,16},{1,13},{... | collective-permute-start | bytes 172040 | tf_op jit(solution)/shard_map/ppermute | solution.py:1020
  60.1 5.8 %collective-permute-start.25 = (bf16[224,128]{1,0:T(8,128)(2,1)S(1)}, bf16[224,128]{1,0:T(8,128)(2,1)S(1)}, u32[]{:S(2)}, u32[]{:S(2)}) collective-permute-start(bf16[224,128]{1,0:T(8,128)(2,1)S(1)} %finish_pieces.1.refs_0_), channel_id=1, source_target_pairs={{0,4},{4,0},{8,12},{12,8},{16,20},{20,16},{24,28},{28,24},{1,5},{5... | collective-permute-start | bytes 172040 | tf_op jit(solution)/shard_map/ppermute | solution.py:1020
  61.2 4.7 %collective-permute-start.24 = (bf16[224,128]{1,0:T(8,128)(2,1)S(1)}, bf16[224,128]{1,0:T(8,128)(2,1)S(1)}, u32[]{:S(2)}, u32[]{:S(2)}) collective-permute-start(bf16[224,128]{1,0:T(8,128)(2,1)S(1)} %finish_pieces.1.refs_0_), channel_id=1, source_target_pairs={{0,8},{4,12},{8,0},{12,4},{16,24},{20,28},{24,16},{28,20},{1,9},{5... | collective-permute-start | bytes 172040 | tf_op jit(solution)/shard_map/ppermute | solution.py:1020

commit v7 on v6

--- a/solution.py
+++ b/solution.py
@@ -851,7 +851,7 @@
     across = [(i, i ^ 2) for i in range(n_ch)]
     block = shape((rows, pad, cols), BF)
     quarter = shape((part_rows, pad, cols), BF)
-    flat = pltpu.VMEM((rows * pad, cols), F32)
+    flat = pltpu.VMEM(((rows + 1) * pad, cols), F32)
 
     turn = pltpu.VMEM((LANES, LANES), F32)
 
@@ -874,7 +874,7 @@
         functools.partial(prepare_outer, swap, count),
         outer_shapes(pad, swap) + [shape(a.shape, a.dtype) for a in fetched],
         fetched,
-        [pltpu.VMEM((2 * DIL * pad, cols), F32), pltpu.SemaphoreType.DMA((count,))],
+        [pltpu.VMEM(((2 * DIL + 1) * pad, cols), F32), pltpu.SemaphoreType.DMA((count,))],
         "outer_rows",
         far=True,
     )
@@ -884,7 +884,7 @@
         [shape((far_rows, LANES), BF), shape((tile_rows, LANES), BF), shape((pad, LANES), F32)],
         [land_mask, held[0], *held[3:]],
         [
-            pltpu.VMEM((rows // 2 * pad, cols), F32),
+            pltpu.VMEM(((rows // 2 + 1) * pad, cols), F32),
             pltpu.VMEM((hid, wide), BF),
             turn,
             pltpu.VMEM((channels, wide), BF),
@@ -1058,7 +1058,7 @@
         [shape((part, rows, cols), BF), shape((8, LANES), F32)],
         [conv_grad, *grad_around, taps, cotan, land_mask],
         [
-            pltpu.VMEM((16 * (rows + 8), cols), F32),
+            pltpu.VMEM((17 * (rows + 8), cols), F32),
             pltpu.VMEM((part, rows, cols), BF),
             pltpu.SemaphoreType.DMA((-(-part // 16),)),
         ],

time: 67.1 us -> 67.1 us (level)
  no operation moved by 1% of the time
where the time goes in v7:
time: 67.1 us; the launch traced here: 67 us
  starting transfers between devices  27.5 us (41%)
  Pallas kernels  19.8 us (30%)
  waiting for transfers between devices  18.7 us (28%)
  between operations  0.9 us (1%)
    pallas_call x26, Pallas kernels, call(): pl.pallas_call(kernel, out_shape=tuple(outs), in_specs=[pl.BlockSpec(memo...  19.8 us
    ppermute x2, starting transfers between devices, exchange_halo(): lax.ppermute(third_out, 'lon', [(lon, lon ^ 3) for lon in range(n_lon)])  7.35 us
    ppermute x6, starting transfers between devices, over_plane(): lax.ppermute(values[k - 1], ('lon', 'lat'), turn_plane(k))  7.07 us
    ppermute x2, waiting for transfers between devices, exchange_halo(): lax.ppermute(third_out, 'lon', [(lon, lon ^ 3) for lon in range(n_lon)])  5.02 us
    ppermute x6, waiting for transfers between devices, over_plane(): lax.ppermute(values[k - 1], ('lon', 'lat'), turn_plane(k))  4.15 us
    ppermute x2, waiting for transfers between devices, exchange_halo(): got = lax.ppermute(first, 'lon', [(lon, lon ^ 1) for lon in range(n_lon)])  3.77 us
    ppermute x2, starting transfers between devices, exchange_halo(): got = lax.ppermute(outer[0], 'lat', [(0, 1), (1, 0)])  3.15 us
    ppermute x1, starting transfers between devices, on_device(): from_far = lax.ppermute(to_far, 'ch', across)  3 us
  transfers between devices with their start and end apart: 27, of which 12 were waited for; matrix products, arithmetic and copies ran while one was open for 0% of the time, Pallas kernels for 21%

profile of v7, /device:TPU:0, one launch (start us, length us, event | category | flops | bytes accessed | tf_op | source)
XLA Modules:
  0.0 67.0 jit_solution(306900611075508150)
XLA Ops:
  0.6 1.5 %outer_rows.1 = (bf16[2,80,128]{2,1,0:T(8,128)(2,1)S(1)}, bf16[75,32,128]{2,1,0:T(8,128)(2,1)S(1)}, s32[32,128]{1,0:T(8,128)S(1)}, bf16[75,32,128]{2,1,0:T(8,128...) custom-call(bf16[75,32,128]{2,1,0:T(8,128)(2,1)} %refs_0_.1, ...), custom_call_target="tpu_custom_call" | custom-call | bytes 2906120 | tf_op jit(solution)/shard_map/outer_rows/pallas_call | solution.py:35
  2.1 0.9 %far_rows.1 = (bf16[2080,128]{1,0:T(8,128)(2,1)S(1)}, bf16[800,128]{1,0:T(8,128)(2,1)S(1)}, f32[80,128]{1,0:T(8,128)S(1)}) custom-call(s32[32,128]{1,0:T(8,128)S(1)} %get-tuple-element.73.refs_0_.refs_1_.mask_ref.refs_4_, bf16[75,32,128]{2,1,0:T(8,128)(2,1)S(1)} %get-tuple-element.74.refs_1_.grad_ref, bf16[150,300]{1,0:T(8,128)(2,1)S(1)} %get-tuple-element.75.refs_2_, ...), custom_call_target="tpu_custom_call" | custom-call | bytes 1592324 | tf_op jit(solution)/shard_map/far_rows/pallas_call | solution.py:35
  3.0 3.0 %collective-permute-start.3 = (bf16[2080,128]{1,0:T(8,128)(2,1)S(1)}, bf16[2080,128]{1,0:T(8,128)(2,1)S(1)}, u32[]{:S(2)}, u32[]{:S(2)}) collective-permute-start(bf16[2080,128]{1,0:T(8,128)(2,1)S(1)} %get-tuple-element.93), channel_id=1, source_target_pairs={{0,2},{1,3},{2,0},{3,1},{4,6},{5,7},{6,4},{7,5},{8,10},{9,11},{10,... | collective-permute-start | bytes 1597448 | tf_op jit(solution)/shard_map/ppermute | solution.py:911
  6.0 1.5 %collective-permute-start = (bf16[2,80,128]{2,1,0:T(8,128)(2,1)S(1)}, bf16[2,80,128]{2,1,0:T(8,128)(2,1)S(1)}, u32[]{:S(2)}, u32[]{:S(2)}) collective-permute-start(bf16[2,80,128]{2,1,0:T(8,128)(2,1)S(1)} %get-tuple-element.81), channel_id=1, source_target_pairs={{0,4},{4,0},{1,5},{5,1},{2,6},{6,2},{3,7},{7,3},{8,12},{12,8},{9,1... | collective-permute-start | bytes 122888 | tf_op jit(solution)/shard_map/ppermute | solution.py:334
  7.6 1.0 %state_rows.1 = (bf16[32,80,128]{2,1,0:T(8,128)(2,1)S(1)}, bf16[2,80,128]{2,1,0:T(8,128)(2,1)S(1)}, bf16[80,128]{1,0:T(8,128)(2,1)S(1)}, bf16[80,128]{1,0:T(8,128)(2,1)S(1)}) custom-call(bf16[75,32,128]{2,1,0:T(8,128)(2,1)S(1)} %get-tuple-element.72.refs_0_, s32[32,128]{1,0:T(8,128)S(1)} %get-tuple-element.73.refs_0_.refs_1_.mask_ref.refs_4_, ...), custom_call_target="tpu_custom_call" | custom-call | bytes 1409024 | tf_op jit(solution)/shard_map/state_rows/pallas_call | solution.py:35
  10.2 3.7 %collective-permute-start.1 = (bf16[3,80,128]{2,1,0:T(8,128)(2,1)S(1)}, bf16[3,80,128]{2,1,0:T(8,128)(2,1)S(1)}, u32[]{:S(2)}, u32[]{:S(2)}) collective-permute-start(bf16[3,80,128]{2,1,0:T(8,128)(2,1)S(1)} %state_third.1), channel_id=1, source_target_pairs={{0,24},{8,16},{16,8},{24,0},{1,25},{9,17},{17,9},{25,1},{2,26},{10... | collective-permute-start | bytes 184328 | tf_op jit(solution)/shard_map/ppermute | solution.py:343
  13.8 2.4 %collective-permute-done.1.third_ref = bf16[3,80,128]{2,1,0:T(8,128)(2,1)S(1)} collective-permute-done((bf16[3,80,128]{2,1,0:T(8,128)(2,1)S(1)}, bf16[3,80,128]{2,1,0:T(8,128)(2,1)S(1)}, u32[]{:S(2)}, u32[]{:S(2)}) %collective-permute-start.1) | collective-permute-done | bytes 61472 | tf_op jit(solution)/shard_map/ppermute | solution.py:343
  16.5 3.8 %collective-permute-done.2.left_ref.refs_1_.refs_2_ = bf16[1,80,128]{2,1,0:T(8,128)(2,1)S(1)} collective-permute-done((bf16[1,80,128]{2,1,0:T(8,128)(2,1)S(1)}, bf16[1,80,128]{2,1,0:T(8,128)(2,1)S(1)}, u32[]{:S(2)}, u32[]{:S(2)}) %collective-permute-start.2) | collective-permute-done | bytes 20512 | tf_op jit(solution)/shard_map/ppermute | solution.py:351
  20.8 1.3 %conv_away.1 = (bf16[4,80,128]{2,1,0:T(8,128)(2,1)S(1)}, bf16[4,80,128]{2,1,0:T(8,128)(2,1)S(1)}, bf16[4,80,128]{2,1,0:T(8,128)(2,1)S(1)}, bf16[4,80,128]{2,1,0:T(8,128)(2,1)S(1)}) custom-call(bf16[32,80,128]{2,1,0:T(8,128)(2,1)S(1)} %get-tuple-element.80.block_ref.refs_0_, bf16[4,80,128]{2,1,0:T(8,128)(2,1)S(1)} %get-tuple-element.89.halo_ref.refs_1_, ...), custom_call_target="tpu_custom_call" | custom-call | bytes 1146880 | tf_op jit(solution)/shard_map/conv_away/pallas_call | solution.py:35
  22.2 1.6 %collective-permute-start.6 = (bf16[4,80,128]{2,1,0:T(8,128)(2,1)S(1)}, bf16[4,80,128]{2,1,0:T(8,128)(2,1)S(1)}, u32[]{:S(2)}, u32[]{:S(2)}) collective-permute-start(bf16[4,80,128]{2,1,0:T(8,128)(2,1)S(1)} %get-tuple-element.92.refs_5_), channel_id=1, source_target_pairs={{0,2},{1,3},{2,0},{3,1},{4,6},{5,7},{6,4},{7,5},{8,10},{9,11},{10,... | collective-permute-start | bytes 245768 | tf_op jit(solution)/shard_map/ppermute | solution.py:941
  23.8 1.3 %conv_here.1 = (bf16[4,80,128]{2,1,0:T(8,128)(2,1)S(1)}, bf16[4,80,128]{2,1,0:T(8,128)(2,1)S(1)}, bf16[4,80,128]{2,1,0:T(8,128)(2,1)S(1)}, bf16[4,80,128]{2,1,0:T(8,128)(2,1)S(1)}) custom-call(bf16[32,80,128]{2,1,0:T(8,128)(2,1)S(1)} %get-tuple-element.80.block_ref.refs_0_, bf16[4,80,128]{2,1,0:T(8,128)(2,1)S(1)} %get-tuple-element.89.halo_ref.refs_1_, ...), custom_call_target="tpu_custom_call" | custom-call | bytes 1761280 | tf_op jit(solution)/shard_map/conv_here/pallas_call | solution.py:35
  25.7 0.9 %collective-permute-done.7.refs_3_ = bf16[4,80,128]{2,1,0:T(8,128)(2,1)S(1)} collective-permute-done((bf16[4,80,128]{2,1,0:T(8,128)(2,1)S(1)}, bf16[4,80,128]{2,1,0:T(8,128)(2,1)S(1)}, u32[]{:S(2)}, u32[]{:S(2)}) %collective-permute-start.7) | collective-permute-done | bytes 81952 | tf_op jit(solution)/shard_map/ppermute | solution.py:942
  27.5 1.4 %activation_gradient.1 = (f32[640,1024]{1,0:T(8,128)S(1)}, bf16[384,1024]{1,0:T(8,128)(2,1)S(1)}, bf16[640,640]{1,0:T(8,128)(2,1)S(1)}, bf16[384,640]{1,0:T(8,12...) custom-call(bf16[1440,128]{1,0:T(8,128)(2,1)S(1)} %get-tuple-element.97.refs_0_, ...), custom_call_target="tpu_custom_call" | custom-call | bytes 7002112 | tf_op jit(solution)/shard_map/activation_gradient/pallas_call | solution.py:35
  28.9 1.8 %hidden_first.1 = (bf16[640,512]{1,0:T(8,128)(2,1)S(1)}, f32[2,832,128]{2,1,0:T(8,128)S(1)}, f32[2,832,128]{2,1,0:T(8,128)S(1)}) custom-call(bf16[4,80,128]{2,1,0:T(8,128)(2,1)S(1)} %get-tuple-element.94.refs_0_, bf16[4,80,128]{2,1,0:T(8,128)(2,1)S(1)} %collective-permute-done.5.refs_1_, bf16[4,80,128]{2,1,0:T(8,128)(2,1)S(1)} %collective-permute-done.6.refs_2_, ...), custom_call_target="tpu_custom_call" | custom-call | bytes 6914048 | tf_op jit(solution)/shard_map/hidden_first/pallas_call | solution.py:35
  30.7 1.0 %collective-permute-done.11.refs_3_ = bf16[4,80,128]{2,1,0:T(8,128)(2,1)S(1)} collective-permute-done((bf16[4,80,128]{2,1,0:T(8,128)(2,1)S(1)}, bf16[4,80,128]{2,1,0:T(8,128)(2,1)S(1)}, u32[]{:S(2)}, u32[]{:S(2)}) %collective-permute-start.11) | collective-permute-done | bytes 81952 | tf_op jit(solution)/shard_map/ppermute | solution.py:942
  31.8 1.8 %hidden_second.1 = (bf16[640,512]{1,0:T(8,128)(2,1)S(1)}, f32[2,832,128]{2,1,0:T(8,128)S(1)}, bf16[2,832,128]{2,1,0:T(8,128)(2,1)S(1)}) custom-call(bf16[4,80,128]{2,1,0:T(8,128)(2,1)S(1)} %get-tuple-element.102.refs_0_, bf16[4,80,128]{2,1,0:T(8,128)(2,1)S(1)} %collective-permute-done.9.refs_1_, bf16[4,80,128]{2,1,0:T(8,128)(2,1)S(1)} %collective-permute-done.10.refs_2_, ...), custom_call_target="tpu_custom_call" | custom-call | bytes 8192000 | tf_op jit(solution)/shard_map/hidden_second/pallas_call | solution.py:35
  35.5 1.6 %collective-permute-start.16 = (bf16[2,208,128]{2,1,0:T(8,128)(2,1)S(1)}, bf16[2,208,128]{2,1,0:T(8,128)(2,1)S(1)}, u32[]{:S(2)}, u32[]{:S(2)}) collective-permute-start(bf16[2,208,128]{2,1,0:T(8,128)(2,1)S(1)} %get-tuple-element.116), channel_id=1, source_target_pairs={{0,4},{4,0},{8,12},{12,8},{16,20},{20,16},{24,28},{28,24},{1,5},{5... | collective-permute-start | bytes 319496 | tf_op jit(solution)/shard_map/ppermute | solution.py:1020
  37.7 1.3 %collective-permute-start.15 = (bf16[2,208,128]{2,1,0:T(8,128)(2,1)S(1)}, bf16[2,208,128]{2,1,0:T(8,128)(2,1)S(1)}, u32[]{:S(2)}, u32[]{:S(2)}) collective-permute-start(bf16[2,208,128]{2,1,0:T(8,128)(2,1)S(1)} %get-tuple-element.115.refs_4_), channel_id=1, source_target_pairs={{0,8},{4,12},{8,0},{12,4},{16,24},{20,28},{24,16},{28,20},{1,9},{5... | collective-permute-start | bytes 319496 | tf_op jit(solution)/shard_map/ppermute | solution.py:1020
  39.0 1.2 %shift_columns.1 = (bf16[36,80,128]{2,1,0:T(8,128)(2,1)S(1)}, bf16[36,80,128]{2,1,0:T(8,128)(2,1)S(1)}) custom-call(bf16[32,80,128]{2,1,0:T(8,128)(2,1)S(1)} %get-tuple-element.80.block_ref.refs_0_, bf16[4,80,128]{2,1,0:T(8,128)(2,1)S(1)} %get-tuple-element.89.halo_ref.refs_1_, bf16[1,80,128]{2,1,0:T(8,128)(2,1)S(1)} %collective-permute-done.2.left_ref.refs_1_.refs_2_, ...), custom_call_target="tpu_custom_call" | custom-call | bytes 2359296 | tf_op jit(solution)/shard_map/shift_columns/pallas_call | solution.py:35
  40.2 2.0 %collective-permute-done.16.refs_2_ = bf16[2,208,128]{2,1,0:T(8,128)(2,1)S(1)} collective-permute-done((bf16[2,208,128]{2,1,0:T(8,128)(2,1)S(1)}, bf16[2,208,128]{2,1,0:T(8,128)(2,1)S(1)}, u32[]{:S(2)}, u32[]{:S(2)}) %collective-permute-start.16) | collective-permute-done | bytes 106528 | tf_op jit(solution)/shard_map/ppermute | solution.py:1020
  42.3 1.6 %collective-permute-done.17.refs_3_ = bf16[2,208,128]{2,1,0:T(8,128)(2,1)S(1)} collective-permute-done((bf16[2,208,128]{2,1,0:T(8,128)(2,1)S(1)}, bf16[2,208,128]{2,1,0:T(8,128)(2,1)S(1)}, u32[]{:S(2)}, u32[]{:S(2)}) %collective-permute-start.17) | collective-permute-done | bytes 106528 | tf_op jit(solution)/shard_map/ppermute | solution.py:1020
  44.5 1.4 %collective-permute-done.18.passed = bf16[8,80,128]{2,1,0:T(8,128)(2,1)S(1)} collective-permute-done((bf16[8,80,128]{2,1,0:T(8,128)(2,1)S(1)}, bf16[8,80,128]{2,1,0:T(8,128)(2,1)S(1)}, u32[]{:S(2)}, u32[]{:S(2)}) %collective-permute-start.18) | collective-permute-done | bytes 163872 | tf_op jit(solution)/shard_map/ppermute | solution.py:1036
  46.4 1.6 %collective-permute-start.19 = (bf16[2,80,128]{2,1,0:T(8,128)(2,1)S(1)}, bf16[2,80,128]{2,1,0:T(8,128)(2,1)S(1)}, u32[]{:S(2)}, u32[]{:S(2)}) collective-permute-start(bf16[2,80,128]{2,1,0:T(8,128)(2,1)S(1)} %get-tuple-element.121), channel_id=1, source_target_pairs={{0,4},{4,0},{1,5},{5,1},{2,6},{6,2},{3,7},{7,3},{8,12},{12,8},{9,1... | collective-permute-start | bytes 122888 | tf_op jit(solution)/shard_map/ppermute | solution.py:334
  48.0 1.5 %collective-permute-start.22 = (bf16[208,128]{1,0:T(8,128)(2,1)S(1)}, bf16[208,128]{1,0:T(8,128)(2,1)S(1)}, u32[]{:S(2)}, u32[]{:S(2)}) collective-permute-start(bf16[208,128]{1,0:T(8,128)(2,1)S(1)} %get-tuple-element.119.refs_1_), channel_id=1, source_target_pairs={{0,2},{1,3},{2,0},{3,1},{4,6},{5,7},{6,4},{7,5},{8,10},{9,11},{10,... | collective-permute-start | bytes 159752 | tf_op jit(solution)/shard_map/ppermute | solution.py:1052
  49.5 1.2 %kernel_gradient.1.refs_0_.refs_2_ = bf16[80,128]{1,0:T(8,128)(2,1)S(1)} custom-call(bf16[32,80,128]{2,1,0:T(8,128)(2,1)S(1)} %get-tuple-element.120.grad_ref.block_ref, bf16[32,80,128]{2,1,0:T(8,128)(2,1)S(1)} %get-tuple-element.80.block_ref.refs_0_, bf16[4,80,128]{2,1,0:T(8,128)(2,1)S(1)} %get-tuple-element.89.halo_ref.refs_1_, ...), custom_call_target="tpu_custom_call" | custom-call | bytes 2887680 | tf_op jit(solution)/shard_map/kernel_gradient/pallas_call | solution.py:35
  50.9 3.7 %collective-permute-start.20 = (bf16[3,80,128]{2,1,0:T(8,128)(2,1)S(1)}, bf16[3,80,128]{2,1,0:T(8,128)(2,1)S(1)}, u32[]{:S(2)}, u32[]{:S(2)}) collective-permute-start(bf16[3,80,128]{2,1,0:T(8,128)(2,1)S(1)} %grad_third.1), channel_id=1, source_target_pairs={{0,24},{8,16},{16,8},{24,0},{1,25},{9,17},{17,9},{25,1},{2,26},{10... | collective-permute-start | bytes 184328 | tf_op jit(solution)/shard_map/ppermute | solution.py:343
  54.7 2.6 %collective-permute-done.20.third_ref.refs_3_ = bf16[3,80,128]{2,1,0:T(8,128)(2,1)S(1)} collective-permute-done((bf16[3,80,128]{2,1,0:T(8,128)(2,1)S(1)}, bf16[3,80,128]{2,1,0:T(8,128)(2,1)S(1)}, u32[]{:S(2)}, u32[]{:S(2)}) %collective-permute-start.20) | collective-permute-done | bytes 61472 | tf_op jit(solution)/shard_map/ppermute | solution.py:343
  58.1 1.7 %collective-permute-done.23.refs_1_ = bf16[208,128]{1,0:T(8,128)(2,1)S(1)} collective-permute-done((bf16[208,128]{1,0:T(8,128)(2,1)S(1)}, bf16[208,128]{1,0:T(8,128)(2,1)S(1)}, u32[]{:S(2)}, u32[]{:S(2)}) %collective-permute-start.23) | collective-permute-done | bytes 53280 | tf_op jit(solution)/shard_map/ppermute | solution.py:1081
  60.1 1.1 %collective-permute-start.25 = (bf16[224,128]{1,0:T(8,128)(2,1)S(1)}, bf16[224,128]{1,0:T(8,128)(2,1)S(1)}, u32[]{:S(2)}, u32[]{:S(2)}) collective-permute-start(bf16[224,128]{1,0:T(8,128)(2,1)S(1)} %finish_pieces.1.refs_0_), channel_id=1, source_target_pairs={{0,4},{4,0},{8,12},{12,8},{16,20},{20,16},{24,28},{28,24},{1,5},{5... | collective-permute-start | bytes 172040 | tf_op jit(solution)/shard_map/ppermute | solution.py:1020
  61.2 2.2 %collective-permute-start.24 = (bf16[224,128]{1,0:T(8,128)(2,1)S(1)}, bf16[224,128]{1,0:T(8,128)(2,1)S(1)}, u32[]{:S(2)}, u32[]{:S(2)}) collective-permute-start(bf16[224,128]{1,0:T(8,128)(2,1)S(1)} %finish_pieces.1.refs_0_), channel_id=1, source_target_pairs={{0,8},{4,12},{8,0},{12,4},{16,24},{20,28},{24,16},{28,20},{1,9},{5... | collective-permute-start | bytes 172040 | tf_op jit(solution)/shard_map/ppermute | solution.py:1020
  63.4 2.4 %conv_adjoint.1 = (bf16[75,32,128]{2,1,0:T(8,128)(2,1)}, f32[8,128]{1,0:T(8,128)S(1)}) custom-call(bf16[32,80,128]{2,1,0:T(8,128)(2,1)S(1)} %get-tuple-element.120.grad_ref.block_ref, bf16[4,80,128]{2,1,0:T(8,128)(2,1)S(1)} %get-tuple-element.126.halo_ref, bf16[4,80,128]{2,1,0:T(8,128)(2,1)S(1)} %collective-permute-done.21.left_ref, ...), custom_call_target="tpu_custom_call" | custom-call | bytes 2170880 | tf_op jit(solution)/shard_map/conv_adjoint/pallas_call | solution.py:35
  65.8 1.1 %write_parameters.1 = (f32[150,300]{1,0:T(8,128)}, f32[150,300]{1,0:T(8,128)}, f32[1,150]{1,0:T(1,128)}, f32[3,3,75]{2,1,0:T(4,128)}) custom-call(bf16[224,128]{1,0:T(8,128)(2,1)S(1)} %finish_pieces.1.refs_0_, bf16[224,128]{1,0:T(8,128)(2,1)S(1)} %collective-permute-done.24.refs_1_, bf16[224,128]{1,0:T(8,128)(2,1)S(1)} %collective-permute-done.25.refs_2_, ...), custom_call_target="tpu_custom_call" | custom-call | bytes 1057572 | tf_op jit(solution)/shard_map/write_parameters/pallas_call | solution.py:35
  (48 shorter events, 9.0 us)
Async XLA Ops:
  3.0 17.2 %collective-permute-start.3 = (bf16[2080,128]{1,0:T(8,128)(2,1)S(1)}, bf16[2080,128]{1,0:T(8,128)(2,1)S(1)}, u32[]{:S(2)}, u32[]{:S(2)}) collective-permute-start(bf16[2080,128]{1,0:T(8,128)(2,1)S(1)} %get-tuple-element.93), channel_id=1, source_target_pairs={{0,2},{1,3},{2,0},{3,1},{4,6},{5,7},{6,4},{7,5},{8,10},{9,11},{10,... | collective-permute-start | bytes 1597448 | tf_op jit(solution)/shard_map/ppermute | solution.py:911
  6.0 4.0 %collective-permute-start = (bf16[2,80,128]{2,1,0:T(8,128)(2,1)S(1)}, bf16[2,80,128]{2,1,0:T(8,128)(2,1)S(1)}, u32[]{:S(2)}, u32[]{:S(2)}) collective-permute-start(bf16[2,80,128]{2,1,0:T(8,128)(2,1)S(1)} %get-tuple-element.81), channel_id=1, source_target_pairs={{0,4},{4,0},{1,5},{5,1},{2,6},{6,2},{3,7},{7,3},{8,12},{12,8},{9,1... | collective-permute-start | bytes 122888 | tf_op jit(solution)/shard_map/ppermute | solution.py:334
  10.2 6.1 %collective-permute-start.1 = (bf16[3,80,128]{2,1,0:T(8,128)(2,1)S(1)}, bf16[3,80,128]{2,1,0:T(8,128)(2,1)S(1)}, u32[]{:S(2)}, u32[]{:S(2)}) collective-permute-start(bf16[3,80,128]{2,1,0:T(8,128)(2,1)S(1)} %state_third.1), channel_id=1, source_target_pairs={{0,24},{8,16},{16,8},{24,0},{1,25},{9,17},{17,9},{25,1},{2,26},{10... | collective-permute-start | bytes 184328 | tf_op jit(solution)/shard_map/ppermute | solution.py:343
  16.4 3.8 %collective-permute-start.2 = (bf16[1,80,128]{2,1,0:T(8,128)(2,1)S(1)}, bf16[1,80,128]{2,1,0:T(8,128)(2,1)S(1)}, u32[]{:S(2)}, u32[]{:S(2)}) collective-permute-start(bf16[1,80,128]{2,1,0:T(8,128)(2,1)S(1)} %get-tuple-element.90), channel_id=1, source_target_pairs={{0,8},{8,0},{16,24},{24,16},{1,9},{9,1},{17,25},{25,17},{2,10},{10... | collective-permute-start | bytes 61448 | tf_op jit(solution)/shard_map/ppermute | solution.py:351
  20.2 3.6 %collective-permute-start.4 = (bf16[2080,128]{1,0:T(8,128)(2,1)S(1)}, bf16[2080,128]{1,0:T(8,128)(2,1)S(1)}, u32[]{:S(2)}, u32[]{:S(2)}) collective-permute-start(bf16[2080,128]{1,0:T(8,128)(2,1)S(1)} %cotan_relay.1.refs_2_), channel_id=1, source_target_pairs={{0,1},{1,0},{2,3},{3,2},{4,5},{5,4},{6,7},{7,6},{8,9},{9,8},{10,11... | collective-permute-start | bytes 1597448 | tf_op jit(solution)/shard_map/ppermute | solution.py:927
  20.2 6.8 %collective-permute-start.8 = (bf16[1440,128]{1,0:T(8,128)(2,1)S(1)}, bf16[1440,128]{1,0:T(8,128)(2,1)S(1)}, u32[]{:S(2)}, u32[]{:S(2)}) collective-permute-start(bf16[1440,128]{1,0:T(8,128)(2,1)S(1)} %get-tuple-element.88.refs_4_), channel_id=1, source_target_pairs={{0,1},{1,0},{2,3},{3,2},{4,5},{5,4},{6,7},{7,6},{8,9},{9,8},{10,11... | collective-permute-start | bytes 1105928 | tf_op jit(solution)/shard_map/ppermute | solution.py:956
  22.0 4.6 %collective-permute-start.7 = (bf16[4,80,128]{2,1,0:T(8,128)(2,1)S(1)}, bf16[4,80,128]{2,1,0:T(8,128)(2,1)S(1)}, u32[]{:S(2)}, u32[]{:S(2)}) collective-permute-start(bf16[4,80,128]{2,1,0:T(8,128)(2,1)S(1)} %get-tuple-element.96), channel_id=1, source_target_pairs={{0,3},{1,2},{2,1},{3,0},{4,7},{5,6},{6,5},{7,4},{8,11},{9,10},{10,... | collective-permute-start | bytes 245768 | tf_op jit(solution)/shard_map/ppermute | solution.py:942
  22.2 6.7 %collective-permute-start.6 = (bf16[4,80,128]{2,1,0:T(8,128)(2,1)S(1)}, bf16[4,80,128]{2,1,0:T(8,128)(2,1)S(1)}, u32[]{:S(2)}, u32[]{:S(2)}) collective-permute-start(bf16[4,80,128]{2,1,0:T(8,128)(2,1)S(1)} %get-tuple-element.92.refs_5_), channel_id=1, source_target_pairs={{0,2},{1,3},{2,0},{3,1},{4,6},{5,7},{6,4},{7,5},{8,10},{9,11},{10,... | collective-permute-start | bytes 245768 | tf_op jit(solution)/shard_map/ppermute | solution.py:941
  25.1 3.8 %collective-permute-start.5 = (bf16[4,80,128]{2,1,0:T(8,128)(2,1)S(1)}, bf16[4,80,128]{2,1,0:T(8,128)(2,1)S(1)}, u32[]{:S(2)}, u32[]{:S(2)}) collective-permute-start(bf16[4,80,128]{2,1,0:T(8,128)(2,1)S(1)} %get-tuple-element.95), channel_id=1, source_target_pairs={{0,1},{1,0},{2,3},{3,2},{4,5},{5,4},{6,7},{7,6},{8,9},{9,8},{10,11... | collective-permute-start | bytes 245768 | tf_op jit(solution)/shard_map/ppermute | solution.py:940
  25.3 5.4 %collective-permute-start.10 = (bf16[4,80,128]{2,1,0:T(8,128)(2,1)S(1)}, bf16[4,80,128]{2,1,0:T(8,128)(2,1)S(1)}, u32[]{:S(2)}, u32[]{:S(2)}) collective-permute-start(bf16[4,80,128]{2,1,0:T(8,128)(2,1)S(1)} %get-tuple-element.104), channel_id=1, source_target_pairs={{0,2},{1,3},{2,0},{3,1},{4,6},{5,7},{6,4},{7,5},{8,10},{9,11},{10,... | collective-permute-start | bytes 245768 | tf_op jit(solution)/shard_map/ppermute | solution.py:941
  26.6 5.2 %collective-permute-start.11 = (bf16[4,80,128]{2,1,0:T(8,128)(2,1)S(1)}, bf16[4,80,128]{2,1,0:T(8,128)(2,1)S(1)}, u32[]{:S(2)}, u32[]{:S(2)}) collective-permute-start(bf16[4,80,128]{2,1,0:T(8,128)(2,1)S(1)} %get-tuple-element.105), channel_id=1, source_target_pairs={{0,3},{1,2},{2,1},{3,0},{4,7},{5,6},{6,5},{7,4},{8,11},{9,10},{10,... | collective-permute-start | bytes 245768 | tf_op jit(solution)/shard_map/ppermute | solution.py:942
  27.0 4.8 %collective-permute-start.9 = (bf16[4,80,128]{2,1,0:T(8,128)(2,1)S(1)}, bf16[4,80,128]{2,1,0:T(8,128)(2,1)S(1)}, u32[]{:S(2)}, u32[]{:S(2)}) collective-permute-start(bf16[4,80,128]{2,1,0:T(8,128)(2,1)S(1)} %get-tuple-element.103), channel_id=1, source_target_pairs={{0,1},{1,0},{2,3},{3,2},{4,5},{5,4},{6,7},{7,6},{8,9},{9,8},{10,11... | collective-permute-start | bytes 245768 | tf_op jit(solution)/shard_map/ppermute | solution.py:940
  33.6 1.8 %collective-permute-start.14 = (bf16[2,832,128]{2,1,0:T(8,128)(2,1)S(1)}, bf16[2,832,128]{2,1,0:T(8,128)(2,1)S(1)}, u32[]{:S(2)}, u32[]{:S(2)}) collective-permute-start(bf16[2,832,128]{2,1,0:T(8,128)(2,1)S(1)} %get-tuple-element.113), channel_id=1, source_target_pairs={{0,1},{1,0},{2,3},{3,2},{4,5},{5,4},{6,7},{7,6},{8,9},{9,8},{10,11... | collective-permute-start | bytes 1277960 | tf_op jit(solution)/shard_map/ppermute | solution.py:975
  34.3 10.2 %collective-permute-start.13 = (bf16[2,8,80,128]{3,2,1,0:T(8,128)(2,1)S(1)}, bf16[2,8,80,128]{3,2,1,0:T(8,128)(2,1)S(1)}, u32[]{:S(2)}, u32[]{:S(2)}) collective-permute-start(bf16[2,8,80,128]{3,2,1,0:T(8,128)(2,1)S(1)} %gradient_away.1.refs_3_), channel_id=1, source_target_pairs={{0,2},{1,3},{2,0},{3,1},{4,6},{5,7},{6,4},{7,5},{8,10},{9,11},{10,... | collective-permute-start | bytes 983048 | tf_op jit(solution)/shard_map/ppermute | solution.py:993
  35.2 5.0 %collective-permute-start.12 = (bf16[8,80,128]{2,1,0:T(8,128)(2,1)S(1)}, bf16[8,80,128]{2,1,0:T(8,128)(2,1)S(1)}, u32[]{:S(2)}, u32[]{:S(2)}) collective-permute-start(bf16[8,80,128]{2,1,0:T(8,128)(2,1)S(1)} %get-tuple-element.111), channel_id=1, source_target_pairs={{0,1},{1,0},{2,3},{3,2},{4,5},{5,4},{6,7},{7,6},{8,9},{9,8},{10,11... | collective-permute-start | bytes 491528 | tf_op jit(solution)/shard_map/ppermute | solution.py:992
  35.5 6.8 %collective-permute-start.16 = (bf16[2,208,128]{2,1,0:T(8,128)(2,1)S(1)}, bf16[2,208,128]{2,1,0:T(8,128)(2,1)S(1)}, u32[]{:S(2)}, u32[]{:S(2)}) collective-permute-start(bf16[2,208,128]{2,1,0:T(8,128)(2,1)S(1)} %get-tuple-element.116), channel_id=1, source_target_pairs={{0,4},{4,0},{8,12},{12,8},{16,20},{20,16},{24,28},{28,24},{1,5},{5... | collective-permute-start | bytes 319496 | tf_op jit(solution)/shard_map/ppermute | solution.py:1020
  37.1 6.7 %collective-permute-start.17 = (bf16[2,208,128]{2,1,0:T(8,128)(2,1)S(1)}, bf16[2,208,128]{2,1,0:T(8,128)(2,1)S(1)}, u32[]{:S(2)}, u32[]{:S(2)}) collective-permute-start(bf16[2,208,128]{2,1,0:T(8,128)(2,1)S(1)} %get-tuple-element.117), channel_id=1, source_target_pairs={{0,12},{4,8},{8,4},{12,0},{16,28},{20,24},{24,20},{28,16},{1,13},{... | collective-permute-start | bytes 319496 | tf_op jit(solution)/shard_map/ppermute | solution.py:1020
  37.7 6.6 %collective-permute-start.15 = (bf16[2,208,128]{2,1,0:T(8,128)(2,1)S(1)}, bf16[2,208,128]{2,1,0:T(8,128)(2,1)S(1)}, u32[]{:S(2)}, u32[]{:S(2)}) collective-permute-start(bf16[2,208,128]{2,1,0:T(8,128)(2,1)S(1)} %get-tuple-element.115.refs_4_), channel_id=1, source_target_pairs={{0,8},{4,12},{8,0},{12,4},{16,24},{20,28},{24,16},{28,20},{1,9},{5... | collective-permute-start | bytes 319496 | tf_op jit(solution)/shard_map/ppermute | solution.py:1020
  44.5 1.5 %collective-permute-start.18 = (bf16[8,80,128]{2,1,0:T(8,128)(2,1)S(1)}, bf16[8,80,128]{2,1,0:T(8,128)(2,1)S(1)}, u32[]{:S(2)}, u32[]{:S(2)}) collective-permute-start(bf16[8,80,128]{2,1,0:T(8,128)(2,1)S(1)} %grad_half.1), channel_id=1, source_target_pairs={{0,1},{1,0},{2,3},{3,2},{4,5},{5,4},{6,7},{7,6},{8,9},{9,8},{10,11... | collective-permute-start | bytes 491528 | tf_op jit(solution)/shard_map/ppermute | solution.py:1036
  46.4 4.4 %collective-permute-start.19 = (bf16[2,80,128]{2,1,0:T(8,128)(2,1)S(1)}, bf16[2,80,128]{2,1,0:T(8,128)(2,1)S(1)}, u32[]{:S(2)}, u32[]{:S(2)}) collective-permute-start(bf16[2,80,128]{2,1,0:T(8,128)(2,1)S(1)} %get-tuple-element.121), channel_id=1, source_target_pairs={{0,4},{4,0},{1,5},{5,1},{2,6},{6,2},{3,7},{7,3},{8,12},{12,8},{9,1... | collective-permute-start | bytes 122888 | tf_op jit(solution)/shard_map/ppermute | solution.py:334
  48.0 6.5 %collective-permute-start.22 = (bf16[208,128]{1,0:T(8,128)(2,1)S(1)}, bf16[208,128]{1,0:T(8,128)(2,1)S(1)}, u32[]{:S(2)}, u32[]{:S(2)}) collective-permute-start(bf16[208,128]{1,0:T(8,128)(2,1)S(1)} %get-tuple-element.119.refs_1_), channel_id=1, source_target_pairs={{0,2},{1,3},{2,0},{3,1},{4,6},{5,7},{6,4},{7,5},{8,10},{9,11},{10,... | collective-permute-start | bytes 159752 | tf_op jit(solution)/shard_map/ppermute | solution.py:1052
  50.9 6.4 %collective-permute-start.20 = (bf16[3,80,128]{2,1,0:T(8,128)(2,1)S(1)}, bf16[3,80,128]{2,1,0:T(8,128)(2,1)S(1)}, u32[]{:S(2)}, u32[]{:S(2)}) collective-permute-start(bf16[3,80,128]{2,1,0:T(8,128)(2,1)S(1)} %grad_third.1), channel_id=1, source_target_pairs={{0,24},{8,16},{16,8},{24,0},{1,25},{9,17},{17,9},{25,1},{2,26},{10... | collective-permute-start | bytes 184328 | tf_op jit(solution)/shard_map/ppermute | solution.py:343
  54.6 5.2 %collective-permute-start.23 = (bf16[208,128]{1,0:T(8,128)(2,1)S(1)}, bf16[208,128]{1,0:T(8,128)(2,1)S(1)}, u32[]{:S(2)}, u32[]{:S(2)}) collective-permute-start(bf16[208,128]{1,0:T(8,128)(2,1)S(1)} %add_across.1.refs_0_), channel_id=1, source_target_pairs={{0,16},{8,24},{16,0},{24,8},{1,17},{9,25},{17,1},{25,9},{2,18},{10... | collective-permute-start | bytes 159752 | tf_op jit(solution)/shard_map/ppermute | solution.py:1081
  57.4 6.0 %collective-permute-start.21 = (bf16[4,80,128]{2,1,0:T(8,128)(2,1)S(1)}, bf16[4,80,128]{2,1,0:T(8,128)(2,1)S(1)}, u32[]{:S(2)}, u32[]{:S(2)}) collective-permute-start(bf16[4,80,128]{2,1,0:T(8,128)(2,1)S(1)} %get-tuple-element.127.refs_4_), channel_id=1, source_target_pairs={{0,8},{8,0},{16,24},{24,16},{1,9},{9,1},{17,25},{25,17},{2,10},{10... | collective-permute-start | bytes 245768 | tf_op jit(solution)/shard_map/ppermute | solution.py:351
  59.9 5.9 %collective-permute-start.26 = (bf16[224,128]{1,0:T(8,128)(2,1)S(1)}, bf16[224,128]{1,0:T(8,128)(2,1)S(1)}, u32[]{:S(2)}, u32[]{:S(2)}) collective-permute-start(bf16[224,128]{1,0:T(8,128)(2,1)S(1)} %finish_pieces.1.refs_0_), channel_id=1, source_target_pairs={{0,12},{4,8},{8,4},{12,0},{16,28},{20,24},{24,20},{28,16},{1,13},{... | collective-permute-start | bytes 172040 | tf_op jit(solution)/shard_map/ppermute | solution.py:1020
  60.1 5.8 %collective-permute-start.25 = (bf16[224,128]{1,0:T(8,128)(2,1)S(1)}, bf16[224,128]{1,0:T(8,128)(2,1)S(1)}, u32[]{:S(2)}, u32[]{:S(2)}) collective-permute-start(bf16[224,128]{1,0:T(8,128)(2,1)S(1)} %finish_pieces.1.refs_0_), channel_id=1, source_target_pairs={{0,4},{4,0},{8,12},{12,8},{16,20},{20,16},{24,28},{28,24},{1,5},{5... | collective-permute-start | bytes 172040 | tf_op jit(solution)/shard_map/ppermute | solution.py:1020
  61.2 4.6 %collective-permute-start.24 = (bf16[224,128]{1,0:T(8,128)(2,1)S(1)}, bf16[224,128]{1,0:T(8,128)(2,1)S(1)}, u32[]{:S(2)}, u32[]{:S(2)}) collective-permute-start(bf16[224,128]{1,0:T(8,128)(2,1)S(1)} %finish_pieces.1.refs_0_), channel_id=1, source_target_pairs={{0,8},{4,12},{8,0},{12,4},{16,24},{20,28},{24,16},{28,20},{1,9},{5... | collective-permute-start | bytes 172040 | tf_op jit(solution)/shard_map/ppermute | solution.py:1020

commit v8 on v7

--- a/solution.py
+++ b/solution.py
@@ -761,11 +761,15 @@
         total = own_ref[group] + (
             a_ref[group].astype(F32) + b_ref[group].astype(F32) + c_ref[group].astype(F32)
         )
-        to[...] = total.astype(to.dtype)
+        piece = total.shape[0]
+        to[0:piece, :] = total.astype(to.dtype)
+        if to.shape[0] > piece:
+            to[piece:, :] = jnp.zeros((to.shape[0] - piece, LANES), to.dtype)
 
 
 def add_across(mine_ref, got_ref, out_ref):
-    out_ref[...] = (mine_ref[...] + got_ref[...].astype(F32)).astype(BF)
+    piece = mine_ref.shape[0]
+    out_ref[...] = (mine_ref[...] + got_ref[0:piece, :].astype(F32)).astype(BF)
 
 
 def finish_pieces(mine_ref, line_ref, kernel_ref, third_ref, out_ref, turn_scr):
@@ -1021,7 +1025,7 @@
 
         mine, other = call(
             add_pieces,
-            [shape((piece, LANES), F32), shape((piece, LANES), BF)],
+            [shape((piece, LANES), F32), shape((piece + 112, LANES), BF)],
             [mine, *over_plane(sends)],
             (),
             "add_pieces",

time: 67.1 us -> 67 us (level)
    ppermute x1, waiting for transfers between devices: 1.38 us -> 0.01 us  [on_device(): lax.ppermute(passed, 'ch', core)]
    ppermute x2, waiting for transfers between devices: 0.65 us -> 1.93 us  [exchange_halo(): got = lax.ppermute(outer[0], 'lat', [(0, 1), (1, 0)])]
    ppermute x1, waiting for transfers between devices: 1.7 us -> 2.48 us  [on_device(): lax.ppermute(mine, 'lon', far_lon)]
  transfers between devices with their start and end apart: 27 -> 27, of which waited for: 12 -> 12; matrix products, arithmetic and copies ran while one was open for 0% -> 0% of each run, Pallas kernels for 21% -> 22%
where the time goes in v8:
time: 67 us; the launch traced here: 66.8 us
  starting transfers between devices  27 us (40%)
  Pallas kernels  19.8 us (30%)
  waiting for transfers between devices  19.1 us (29%)
  between operations  0.89 us (1%)
    pallas_call x26, Pallas kernels, call(): pl.pallas_call(kernel, out_shape=tuple(outs), in_specs=[pl.BlockSpec(memo...  19.8 us
    ppermute x2, starting transfers between devices, exchange_halo(): lax.ppermute(third_out, 'lon', [(lon, lon ^ 3) for lon in range(n_lon)])  7.34 us
    ppermute x6, starting transfers between devices, over_plane(): lax.ppermute(values[k - 1], ('lon', 'lat'), turn_plane(k))  7.07 us
    ppermute x2, waiting for transfers between devices, exchange_halo(): lax.ppermute(third_out, 'lon', [(lon, lon ^ 3) for lon in range(n_lon)])  4.74 us
    ppermute x6, waiting for transfers between devices, over_plane(): lax.ppermute(values[k - 1], ('lon', 'lat'), turn_plane(k))  4.15 us
    ppermute x2, waiting for transfers between devices, exchange_halo(): got = lax.ppermute(first, 'lon', [(lon, lon ^ 1) for lon in range(n_lon)])  3.77 us
    ppermute x2, starting transfers between devices, exchange_halo(): got = lax.ppermute(outer[0], 'lat', [(0, 1), (1, 0)])  3.08 us
    ppermute x1, starting transfers between devices, on_device(): from_far = lax.ppermute(to_far, 'ch', across)  3 us
  transfers between devices with their start and end apart: 27, of which 12 were waited for; matrix products, arithmetic and copies ran while one was open for 0% of the time, Pallas kernels for 22%

profile of v8, /device:TPU:0, one launch (start us, length us, event | category | flops | bytes accessed | tf_op | source)
XLA Modules:
  0.0 66.8 jit_solution(6188149515586634554)
XLA Ops:
  0.6 1.5 %outer_rows.1 = (bf16[2,80,128]{2,1,0:T(8,128)(2,1)S(1)}, bf16[75,32,128]{2,1,0:T(8,128)(2,1)S(1)}, s32[32,128]{1,0:T(8,128)S(1)}, bf16[75,32,128]{2,1,0:T(8,128...) custom-call(bf16[75,32,128]{2,1,0:T(8,128)(2,1)} %refs_0_.1, ...), custom_call_target="tpu_custom_call" | custom-call | bytes 2906120 | tf_op jit(solution)/shard_map/outer_rows/pallas_call | solution.py:35
  2.1 0.9 %far_rows.1 = (bf16[2080,128]{1,0:T(8,128)(2,1)S(1)}, bf16[800,128]{1,0:T(8,128)(2,1)S(1)}, f32[80,128]{1,0:T(8,128)S(1)}) custom-call(s32[32,128]{1,0:T(8,128)S(1)} %get-tuple-element.73.refs_0_.refs_1_.mask_ref.refs_4_, bf16[75,32,128]{2,1,0:T(8,128)(2,1)S(1)} %get-tuple-element.74.refs_1_.grad_ref, bf16[150,300]{1,0:T(8,128)(2,1)S(1)} %get-tuple-element.75.refs_2_, ...), custom_call_target="tpu_custom_call" | custom-call | bytes 1592324 | tf_op jit(solution)/shard_map/far_rows/pallas_call | solution.py:35
  3.0 3.0 %collective-permute-start.3 = (bf16[2080,128]{1,0:T(8,128)(2,1)S(1)}, bf16[2080,128]{1,0:T(8,128)(2,1)S(1)}, u32[]{:S(2)}, u32[]{:S(2)}) collective-permute-start(bf16[2080,128]{1,0:T(8,128)(2,1)S(1)} %get-tuple-element.93), channel_id=1, source_target_pairs={{0,2},{1,3},{2,0},{3,1},{4,6},{5,7},{6,4},{7,5},{8,10},{9,11},{10,... | collective-permute-start | bytes 1597448 | tf_op jit(solution)/shard_map/ppermute | solution.py:915
  6.0 1.5 %collective-permute-start = (bf16[2,80,128]{2,1,0:T(8,128)(2,1)S(1)}, bf16[2,80,128]{2,1,0:T(8,128)(2,1)S(1)}, u32[]{:S(2)}, u32[]{:S(2)}) collective-permute-start(bf16[2,80,128]{2,1,0:T(8,128)(2,1)S(1)} %get-tuple-element.81), channel_id=1, source_target_pairs={{0,4},{4,0},{1,5},{5,1},{2,6},{6,2},{3,7},{7,3},{8,12},{12,8},{9,1... | collective-permute-start | bytes 122888 | tf_op jit(solution)/shard_map/ppermute | solution.py:334
  7.6 1.0 %state_rows.1 = (bf16[32,80,128]{2,1,0:T(8,128)(2,1)S(1)}, bf16[2,80,128]{2,1,0:T(8,128)(2,1)S(1)}, bf16[80,128]{1,0:T(8,128)(2,1)S(1)}, bf16[80,128]{1,0:T(8,128)(2,1)S(1)}) custom-call(bf16[75,32,128]{2,1,0:T(8,128)(2,1)S(1)} %get-tuple-element.72.refs_0_, s32[32,128]{1,0:T(8,128)S(1)} %get-tuple-element.73.refs_0_.refs_1_.mask_ref.refs_4_, ...), custom_call_target="tpu_custom_call" | custom-call | bytes 1409024 | tf_op jit(solution)/shard_map/state_rows/pallas_call | solution.py:35
  10.2 3.7 %collective-permute-start.1 = (bf16[3,80,128]{2,1,0:T(8,128)(2,1)S(1)}, bf16[3,80,128]{2,1,0:T(8,128)(2,1)S(1)}, u32[]{:S(2)}, u32[]{:S(2)}) collective-permute-start(bf16[3,80,128]{2,1,0:T(8,128)(2,1)S(1)} %state_third.1), channel_id=1, source_target_pairs={{0,24},{8,16},{16,8},{24,0},{1,25},{9,17},{17,9},{25,1},{2,26},{10... | collective-permute-start | bytes 184328 | tf_op jit(solution)/shard_map/ppermute | solution.py:343
  13.8 2.4 %collective-permute-done.1.third_ref = bf16[3,80,128]{2,1,0:T(8,128)(2,1)S(1)} collective-permute-done((bf16[3,80,128]{2,1,0:T(8,128)(2,1)S(1)}, bf16[3,80,128]{2,1,0:T(8,128)(2,1)S(1)}, u32[]{:S(2)}, u32[]{:S(2)}) %collective-permute-start.1) | collective-permute-done | bytes 61472 | tf_op jit(solution)/shard_map/ppermute | solution.py:343
  16.5 3.8 %collective-permute-done.2.left_ref.refs_1_.refs_2_ = bf16[1,80,128]{2,1,0:T(8,128)(2,1)S(1)} collective-permute-done((bf16[1,80,128]{2,1,0:T(8,128)(2,1)S(1)}, bf16[1,80,128]{2,1,0:T(8,128)(2,1)S(1)}, u32[]{:S(2)}, u32[]{:S(2)}) %collective-permute-start.2) | collective-permute-done | bytes 20512 | tf_op jit(solution)/shard_map/ppermute | solution.py:351
  20.8 1.3 %conv_away.1 = (bf16[4,80,128]{2,1,0:T(8,128)(2,1)S(1)}, bf16[4,80,128]{2,1,0:T(8,128)(2,1)S(1)}, bf16[4,80,128]{2,1,0:T(8,128)(2,1)S(1)}, bf16[4,80,128]{2,1,0:T(8,128)(2,1)S(1)}) custom-call(bf16[32,80,128]{2,1,0:T(8,128)(2,1)S(1)} %get-tuple-element.80.block_ref.refs_0_, bf16[4,80,128]{2,1,0:T(8,128)(2,1)S(1)} %get-tuple-element.89.halo_ref.refs_1_, ...), custom_call_target="tpu_custom_call" | custom-call | bytes 1146880 | tf_op jit(solution)/shard_map/conv_away/pallas_call | solution.py:35
  22.2 1.6 %collective-permute-start.6 = (bf16[4,80,128]{2,1,0:T(8,128)(2,1)S(1)}, bf16[4,80,128]{2,1,0:T(8,128)(2,1)S(1)}, u32[]{:S(2)}, u32[]{:S(2)}) collective-permute-start(bf16[4,80,128]{2,1,0:T(8,128)(2,1)S(1)} %get-tuple-element.92.refs_5_), channel_id=1, source_target_pairs={{0,2},{1,3},{2,0},{3,1},{4,6},{5,7},{6,4},{7,5},{8,10},{9,11},{10,... | collective-permute-start | bytes 245768 | tf_op jit(solution)/shard_map/ppermute | solution.py:945
  23.8 1.3 %conv_here.1 = (bf16[4,80,128]{2,1,0:T(8,128)(2,1)S(1)}, bf16[4,80,128]{2,1,0:T(8,128)(2,1)S(1)}, bf16[4,80,128]{2,1,0:T(8,128)(2,1)S(1)}, bf16[4,80,128]{2,1,0:T(8,128)(2,1)S(1)}) custom-call(bf16[32,80,128]{2,1,0:T(8,128)(2,1)S(1)} %get-tuple-element.80.block_ref.refs_0_, bf16[4,80,128]{2,1,0:T(8,128)(2,1)S(1)} %get-tuple-element.89.halo_ref.refs_1_, ...), custom_call_target="tpu_custom_call" | custom-call | bytes 1761280 | tf_op jit(solution)/shard_map/conv_here/pallas_call | solution.py:35
  25.7 0.9 %collective-permute-done.7.refs_3_ = bf16[4,80,128]{2,1,0:T(8,128)(2,1)S(1)} collective-permute-done((bf16[4,80,128]{2,1,0:T(8,128)(2,1)S(1)}, bf16[4,80,128]{2,1,0:T(8,128)(2,1)S(1)}, u32[]{:S(2)}, u32[]{:S(2)}) %collective-permute-start.7) | collective-permute-done | bytes 81952 | tf_op jit(solution)/shard_map/ppermute | solution.py:946
  27.5 1.4 %activation_gradient.1 = (f32[640,1024]{1,0:T(8,128)S(1)}, bf16[384,1024]{1,0:T(8,128)(2,1)S(1)}, bf16[640,640]{1,0:T(8,128)(2,1)S(1)}, bf16[384,640]{1,0:T(8,12...) custom-call(bf16[1440,128]{1,0:T(8,128)(2,1)S(1)} %get-tuple-element.97.refs_0_, ...), custom_call_target="tpu_custom_call" | custom-call | bytes 7002112 | tf_op jit(solution)/shard_map/activation_gradient/pallas_call | solution.py:35
  28.9 1.8 %hidden_first.1 = (bf16[640,512]{1,0:T(8,128)(2,1)S(1)}, f32[2,832,128]{2,1,0:T(8,128)S(1)}, f32[2,832,128]{2,1,0:T(8,128)S(1)}) custom-call(bf16[4,80,128]{2,1,0:T(8,128)(2,1)S(1)} %get-tuple-element.94.refs_0_, bf16[4,80,128]{2,1,0:T(8,128)(2,1)S(1)} %collective-permute-done.5.refs_1_, bf16[4,80,128]{2,1,0:T(8,128)(2,1)S(1)} %collective-permute-done.6.refs_2_, ...), custom_call_target="tpu_custom_call" | custom-call | bytes 6914048 | tf_op jit(solution)/shard_map/hidden_first/pallas_call | solution.py:35
  30.7 1.0 %collective-permute-done.11.refs_3_ = bf16[4,80,128]{2,1,0:T(8,128)(2,1)S(1)} collective-permute-done((bf16[4,80,128]{2,1,0:T(8,128)(2,1)S(1)}, bf16[4,80,128]{2,1,0:T(8,128)(2,1)S(1)}, u32[]{:S(2)}, u32[]{:S(2)}) %collective-permute-start.11) | collective-permute-done | bytes 81952 | tf_op jit(solution)/shard_map/ppermute | solution.py:946
  31.8 1.8 %hidden_second.1 = (bf16[640,512]{1,0:T(8,128)(2,1)S(1)}, f32[2,832,128]{2,1,0:T(8,128)S(1)}, bf16[2,832,128]{2,1,0:T(8,128)(2,1)S(1)}) custom-call(bf16[4,80,128]{2,1,0:T(8,128)(2,1)S(1)} %get-tuple-element.102.refs_0_, bf16[4,80,128]{2,1,0:T(8,128)(2,1)S(1)} %collective-permute-done.9.refs_1_, bf16[4,80,128]{2,1,0:T(8,128)(2,1)S(1)} %collective-permute-done.10.refs_2_, ...), custom_call_target="tpu_custom_call" | custom-call | bytes 8192000 | tf_op jit(solution)/shard_map/hidden_second/pallas_call | solution.py:35
  35.5 1.6 %collective-permute-start.16 = (bf16[2,208,128]{2,1,0:T(8,128)(2,1)S(1)}, bf16[2,208,128]{2,1,0:T(8,128)(2,1)S(1)}, u32[]{:S(2)}, u32[]{:S(2)}) collective-permute-start(bf16[2,208,128]{2,1,0:T(8,128)(2,1)S(1)} %get-tuple-element.116), channel_id=1, source_target_pairs={{0,4},{4,0},{8,12},{12,8},{16,20},{20,16},{24,28},{28,24},{1,5},{5... | collective-permute-start | bytes 319496 | tf_op jit(solution)/shard_map/ppermute | solution.py:1024
  37.7 1.3 %collective-permute-start.15 = (bf16[2,208,128]{2,1,0:T(8,128)(2,1)S(1)}, bf16[2,208,128]{2,1,0:T(8,128)(2,1)S(1)}, u32[]{:S(2)}, u32[]{:S(2)}) collective-permute-start(bf16[2,208,128]{2,1,0:T(8,128)(2,1)S(1)} %get-tuple-element.115.refs_4_), channel_id=1, source_target_pairs={{0,8},{4,12},{8,0},{12,4},{16,24},{20,28},{24,16},{28,20},{1,9},{5... | collective-permute-start | bytes 319496 | tf_op jit(solution)/shard_map/ppermute | solution.py:1024
  39.0 1.2 %shift_columns.1 = (bf16[36,80,128]{2,1,0:T(8,128)(2,1)S(1)}, bf16[36,80,128]{2,1,0:T(8,128)(2,1)S(1)}) custom-call(bf16[32,80,128]{2,1,0:T(8,128)(2,1)S(1)} %get-tuple-element.80.block_ref.refs_0_, bf16[4,80,128]{2,1,0:T(8,128)(2,1)S(1)} %get-tuple-element.89.halo_ref.refs_1_, bf16[1,80,128]{2,1,0:T(8,128)(2,1)S(1)} %collective-permute-done.2.left_ref.refs_1_.refs_2_, ...), custom_call_target="tpu_custom_call" | custom-call | bytes 2359296 | tf_op jit(solution)/shard_map/shift_columns/pallas_call | solution.py:35
  40.2 2.0 %collective-permute-done.16.refs_2_ = bf16[2,208,128]{2,1,0:T(8,128)(2,1)S(1)} collective-permute-done((bf16[2,208,128]{2,1,0:T(8,128)(2,1)S(1)}, bf16[2,208,128]{2,1,0:T(8,128)(2,1)S(1)}, u32[]{:S(2)}, u32[]{:S(2)}) %collective-permute-start.16) | collective-permute-done | bytes 106528 | tf_op jit(solution)/shard_map/ppermute | solution.py:1024
  42.3 1.6 %collective-permute-done.17.refs_3_ = bf16[2,208,128]{2,1,0:T(8,128)(2,1)S(1)} collective-permute-done((bf16[2,208,128]{2,1,0:T(8,128)(2,1)S(1)}, bf16[2,208,128]{2,1,0:T(8,128)(2,1)S(1)}, u32[]{:S(2)}, u32[]{:S(2)}) %collective-permute-start.17) | collective-permute-done | bytes 106528 | tf_op jit(solution)/shard_map/ppermute | solution.py:1024
  44.5 1.6 %collective-permute-start.22 = (bf16[320,128]{1,0:T(8,128)(2,1)S(1)}, bf16[320,128]{1,0:T(8,128)(2,1)S(1)}, u32[]{:S(2)}, u32[]{:S(2)}) collective-permute-start(bf16[320,128]{1,0:T(8,128)(2,1)S(1)} %get-tuple-element.119.refs_1_), channel_id=1, source_target_pairs={{0,2},{1,3},{2,0},{3,1},{4,6},{5,7},{6,4},{7,5},{8,10},{9,11},{10,... | collective-permute-start | bytes 245768 | tf_op jit(solution)/shard_map/ppermute | solution.py:1056
  46.7 1.6 %collective-permute-start.19 = (bf16[2,80,128]{2,1,0:T(8,128)(2,1)S(1)}, bf16[2,80,128]{2,1,0:T(8,128)(2,1)S(1)}, u32[]{:S(2)}, u32[]{:S(2)}) collective-permute-start(bf16[2,80,128]{2,1,0:T(8,128)(2,1)S(1)} %get-tuple-element.121), channel_id=1, source_target_pairs={{0,4},{4,0},{1,5},{5,1},{2,6},{6,2},{3,7},{7,3},{8,12},{12,8},{9,1... | collective-permute-start | bytes 122888 | tf_op jit(solution)/shard_map/ppermute | solution.py:334
  48.2 1.2 %kernel_gradient.1.refs_0_.refs_2_ = bf16[80,128]{1,0:T(8,128)(2,1)S(1)} custom-call(bf16[32,80,128]{2,1,0:T(8,128)(2,1)S(1)} %get-tuple-element.120.grad_ref.block_ref, bf16[32,80,128]{2,1,0:T(8,128)(2,1)S(1)} %get-tuple-element.80.block_ref.refs_0_, bf16[4,80,128]{2,1,0:T(8,128)(2,1)S(1)} %get-tuple-element.89.halo_ref.refs_1_, ...), custom_call_target="tpu_custom_call" | custom-call | bytes 2887680 | tf_op jit(solution)/shard_map/kernel_gradient/pallas_call | solution.py:35
  49.5 1.3 %collective-permute-done.19.refs_1_.got_ref = bf16[2,80,128]{2,1,0:T(8,128)(2,1)S(1)} collective-permute-done((bf16[2,80,128]{2,1,0:T(8,128)(2,1)S(1)}, bf16[2,80,128]{2,1,0:T(8,128)(2,1)S(1)}, u32[]{:S(2)}, u32[]{:S(2)}) %collective-permute-start.19) | collective-permute-done | bytes 40992 | tf_op jit(solution)/shard_map/ppermute | solution.py:334
  50.9 3.7 %collective-permute-start.20 = (bf16[3,80,128]{2,1,0:T(8,128)(2,1)S(1)}, bf16[3,80,128]{2,1,0:T(8,128)(2,1)S(1)}, u32[]{:S(2)}, u32[]{:S(2)}) collective-permute-start(bf16[3,80,128]{2,1,0:T(8,128)(2,1)S(1)} %grad_third.1), channel_id=1, source_target_pairs={{0,24},{8,16},{16,8},{24,0},{1,25},{9,17},{17,9},{25,1},{2,26},{10... | collective-permute-start | bytes 184328 | tf_op jit(solution)/shard_map/ppermute | solution.py:343
  54.6 2.3 %collective-permute-done.20.third_ref.refs_3_ = bf16[3,80,128]{2,1,0:T(8,128)(2,1)S(1)} collective-permute-done((bf16[3,80,128]{2,1,0:T(8,128)(2,1)S(1)}, bf16[3,80,128]{2,1,0:T(8,128)(2,1)S(1)}, u32[]{:S(2)}, u32[]{:S(2)}) %collective-permute-start.20) | collective-permute-done | bytes 61472 | tf_op jit(solution)/shard_map/ppermute | solution.py:343
  57.2 2.5 %collective-permute-done.23.refs_1_ = bf16[208,128]{1,0:T(8,128)(2,1)S(1)} collective-permute-done((bf16[208,128]{1,0:T(8,128)(2,1)S(1)}, bf16[208,128]{1,0:T(8,128)(2,1)S(1)}, u32[]{:S(2)}, u32[]{:S(2)}) %collective-permute-start.23) | collective-permute-done | bytes 53280 | tf_op jit(solution)/shard_map/ppermute | solution.py:1085
  60.3 1.1 %collective-permute-start.25 = (bf16[224,128]{1,0:T(8,128)(2,1)S(1)}, bf16[224,128]{1,0:T(8,128)(2,1)S(1)}, u32[]{:S(2)}, u32[]{:S(2)}) collective-permute-start(bf16[224,128]{1,0:T(8,128)(2,1)S(1)} %finish_pieces.1.refs_0_), channel_id=1, source_target_pairs={{0,4},{4,0},{8,12},{12,8},{16,20},{20,16},{24,28},{28,24},{1,5},{5... | collective-permute-start | bytes 172040 | tf_op jit(solution)/shard_map/ppermute | solution.py:1024
  61.4 1.9 %collective-permute-start.24 = (bf16[224,128]{1,0:T(8,128)(2,1)S(1)}, bf16[224,128]{1,0:T(8,128)(2,1)S(1)}, u32[]{:S(2)}, u32[]{:S(2)}) collective-permute-start(bf16[224,128]{1,0:T(8,128)(2,1)S(1)} %finish_pieces.1.refs_0_), channel_id=1, source_target_pairs={{0,8},{4,12},{8,0},{12,4},{16,24},{20,28},{24,16},{28,20},{1,9},{5... | collective-permute-start | bytes 172040 | tf_op jit(solution)/shard_map/ppermute | solution.py:1024
  63.3 2.4 %conv_adjoint.1 = (bf16[75,32,128]{2,1,0:T(8,128)(2,1)}, f32[8,128]{1,0:T(8,128)S(1)}) custom-call(bf16[32,80,128]{2,1,0:T(8,128)(2,1)S(1)} %get-tuple-element.120.grad_ref.block_ref, bf16[4,80,128]{2,1,0:T(8,128)(2,1)S(1)} %get-tuple-element.126.halo_ref, bf16[4,80,128]{2,1,0:T(8,128)(2,1)S(1)} %collective-permute-done.21.left_ref, ...), custom_call_target="tpu_custom_call" | custom-call | bytes 2170880 | tf_op jit(solution)/shard_map/conv_adjoint/pallas_call | solution.py:35
  65.7 1.1 %write_parameters.1 = (f32[150,300]{1,0:T(8,128)}, f32[150,300]{1,0:T(8,128)}, f32[1,150]{1,0:T(1,128)}, f32[3,3,75]{2,1,0:T(4,128)}) custom-call(bf16[224,128]{1,0:T(8,128)(2,1)S(1)} %finish_pieces.1.refs_0_, bf16[224,128]{1,0:T(8,128)(2,1)S(1)} %collective-permute-done.24.refs_1_, bf16[224,128]{1,0:T(8,128)(2,1)S(1)} %collective-permute-done.25.refs_2_, ...), custom_call_target="tpu_custom_call" | custom-call | bytes 1057572 | tf_op jit(solution)/shard_map/write_parameters/pallas_call | solution.py:35
  (48 shorter events, 8.7 us)
Async XLA Ops:
  3.0 17.2 %collective-permute-start.3 = (bf16[2080,128]{1,0:T(8,128)(2,1)S(1)}, bf16[2080,128]{1,0:T(8,128)(2,1)S(1)}, u32[]{:S(2)}, u32[]{:S(2)}) collective-permute-start(bf16[2080,128]{1,0:T(8,128)(2,1)S(1)} %get-tuple-element.93), channel_id=1, source_target_pairs={{0,2},{1,3},{2,0},{3,1},{4,6},{5,7},{6,4},{7,5},{8,10},{9,11},{10,... | collective-permute-start | bytes 1597448 | tf_op jit(solution)/shard_map/ppermute | solution.py:915
  6.0 4.0 %collective-permute-start = (bf16[2,80,128]{2,1,0:T(8,128)(2,1)S(1)}, bf16[2,80,128]{2,1,0:T(8,128)(2,1)S(1)}, u32[]{:S(2)}, u32[]{:S(2)}) collective-permute-start(bf16[2,80,128]{2,1,0:T(8,128)(2,1)S(1)} %get-tuple-element.81), channel_id=1, source_target_pairs={{0,4},{4,0},{1,5},{5,1},{2,6},{6,2},{3,7},{7,3},{8,12},{12,8},{9,1... | collective-permute-start | bytes 122888 | tf_op jit(solution)/shard_map/ppermute | solution.py:334
  10.2 6.1 %collective-permute-start.1 = (bf16[3,80,128]{2,1,0:T(8,128)(2,1)S(1)}, bf16[3,80,128]{2,1,0:T(8,128)(2,1)S(1)}, u32[]{:S(2)}, u32[]{:S(2)}) collective-permute-start(bf16[3,80,128]{2,1,0:T(8,128)(2,1)S(1)} %state_third.1), channel_id=1, source_target_pairs={{0,24},{8,16},{16,8},{24,0},{1,25},{9,17},{17,9},{25,1},{2,26},{10... | collective-permute-start | bytes 184328 | tf_op jit(solution)/shard_map/ppermute | solution.py:343
  16.4 3.8 %collective-permute-start.2 = (bf16[1,80,128]{2,1,0:T(8,128)(2,1)S(1)}, bf16[1,80,128]{2,1,0:T(8,128)(2,1)S(1)}, u32[]{:S(2)}, u32[]{:S(2)}) collective-permute-start(bf16[1,80,128]{2,1,0:T(8,128)(2,1)S(1)} %get-tuple-element.90), channel_id=1, source_target_pairs={{0,8},{8,0},{16,24},{24,16},{1,9},{9,1},{17,25},{25,17},{2,10},{10... | collective-permute-start | bytes 61448 | tf_op jit(solution)/shard_map/ppermute | solution.py:351
  20.2 3.6 %collective-permute-start.4 = (bf16[2080,128]{1,0:T(8,128)(2,1)S(1)}, bf16[2080,128]{1,0:T(8,128)(2,1)S(1)}, u32[]{:S(2)}, u32[]{:S(2)}) collective-permute-start(bf16[2080,128]{1,0:T(8,128)(2,1)S(1)} %cotan_relay.1.refs_2_), channel_id=1, source_target_pairs={{0,1},{1,0},{2,3},{3,2},{4,5},{5,4},{6,7},{7,6},{8,9},{9,8},{10,11... | collective-permute-start | bytes 1597448 | tf_op jit(solution)/shard_map/ppermute | solution.py:931
  20.2 6.8 %collective-permute-start.8 = (bf16[1440,128]{1,0:T(8,128)(2,1)S(1)}, bf16[1440,128]{1,0:T(8,128)(2,1)S(1)}, u32[]{:S(2)}, u32[]{:S(2)}) collective-permute-start(bf16[1440,128]{1,0:T(8,128)(2,1)S(1)} %get-tuple-element.88.refs_4_), channel_id=1, source_target_pairs={{0,1},{1,0},{2,3},{3,2},{4,5},{5,4},{6,7},{7,6},{8,9},{9,8},{10,11... | collective-permute-start | bytes 1105928 | tf_op jit(solution)/shard_map/ppermute | solution.py:960
  22.0 4.6 %collective-permute-start.7 = (bf16[4,80,128]{2,1,0:T(8,128)(2,1)S(1)}, bf16[4,80,128]{2,1,0:T(8,128)(2,1)S(1)}, u32[]{:S(2)}, u32[]{:S(2)}) collective-permute-start(bf16[4,80,128]{2,1,0:T(8,128)(2,1)S(1)} %get-tuple-element.96), channel_id=1, source_target_pairs={{0,3},{1,2},{2,1},{3,0},{4,7},{5,6},{6,5},{7,4},{8,11},{9,10},{10,... | collective-permute-start | bytes 245768 | tf_op jit(solution)/shard_map/ppermute | solution.py:946
  22.2 6.7 %collective-permute-start.6 = (bf16[4,80,128]{2,1,0:T(8,128)(2,1)S(1)}, bf16[4,80,128]{2,1,0:T(8,128)(2,1)S(1)}, u32[]{:S(2)}, u32[]{:S(2)}) collective-permute-start(bf16[4,80,128]{2,1,0:T(8,128)(2,1)S(1)} %get-tuple-element.92.refs_5_), channel_id=1, source_target_pairs={{0,2},{1,3},{2,0},{3,1},{4,6},{5,7},{6,4},{7,5},{8,10},{9,11},{10,... | collective-permute-start | bytes 245768 | tf_op jit(solution)/shard_map/ppermute | solution.py:945
  25.1 3.8 %collective-permute-start.5 = (bf16[4,80,128]{2,1,0:T(8,128)(2,1)S(1)}, bf16[4,80,128]{2,1,0:T(8,128)(2,1)S(1)}, u32[]{:S(2)}, u32[]{:S(2)}) collective-permute-start(bf16[4,80,128]{2,1,0:T(8,128)(2,1)S(1)} %get-tuple-element.95), channel_id=1, source_target_pairs={{0,1},{1,0},{2,3},{3,2},{4,5},{5,4},{6,7},{7,6},{8,9},{9,8},{10,11... | collective-permute-start | bytes 245768 | tf_op jit(solution)/shard_map/ppermute | solution.py:944
  25.3 5.4 %collective-permute-start.10 = (bf16[4,80,128]{2,1,0:T(8,128)(2,1)S(1)}, bf16[4,80,128]{2,1,0:T(8,128)(2,1)S(1)}, u32[]{:S(2)}, u32[]{:S(2)}) collective-permute-start(bf16[4,80,128]{2,1,0:T(8,128)(2,1)S(1)} %get-tuple-element.104), channel_id=1, source_target_pairs={{0,2},{1,3},{2,0},{3,1},{4,6},{5,7},{6,4},{7,5},{8,10},{9,11},{10,... | collective-permute-start | bytes 245768 | tf_op jit(solution)/shard_map/ppermute | solution.py:945
  26.6 5.2 %collective-permute-start.11 = (bf16[4,80,128]{2,1,0:T(8,128)(2,1)S(1)}, bf16[4,80,128]{2,1,0:T(8,128)(2,1)S(1)}, u32[]{:S(2)}, u32[]{:S(2)}) collective-permute-start(bf16[4,80,128]{2,1,0:T(8,128)(2,1)S(1)} %get-tuple-element.105), channel_id=1, source_target_pairs={{0,3},{1,2},{2,1},{3,0},{4,7},{5,6},{6,5},{7,4},{8,11},{9,10},{10,... | collective-permute-start | bytes 245768 | tf_op jit(solution)/shard_map/ppermute | solution.py:946
  27.0 4.8 %collective-permute-start.9 = (bf16[4,80,128]{2,1,0:T(8,128)(2,1)S(1)}, bf16[4,80,128]{2,1,0:T(8,128)(2,1)S(1)}, u32[]{:S(2)}, u32[]{:S(2)}) collective-permute-start(bf16[4,80,128]{2,1,0:T(8,128)(2,1)S(1)} %get-tuple-element.103), channel_id=1, source_target_pairs={{0,1},{1,0},{2,3},{3,2},{4,5},{5,4},{6,7},{7,6},{8,9},{9,8},{10,11... | collective-permute-start | bytes 245768 | tf_op jit(solution)/shard_map/ppermute | solution.py:944
  33.6 1.8 %collective-permute-start.14 = (bf16[2,832,128]{2,1,0:T(8,128)(2,1)S(1)}, bf16[2,832,128]{2,1,0:T(8,128)(2,1)S(1)}, u32[]{:S(2)}, u32[]{:S(2)}) collective-permute-start(bf16[2,832,128]{2,1,0:T(8,128)(2,1)S(1)} %get-tuple-element.113), channel_id=1, source_target_pairs={{0,1},{1,0},{2,3},{3,2},{4,5},{5,4},{6,7},{7,6},{8,9},{9,8},{10,11... | collective-permute-start | bytes 1277960 | tf_op jit(solution)/shard_map/ppermute | solution.py:979
  34.3 10.2 %collective-permute-start.13 = (bf16[2,8,80,128]{3,2,1,0:T(8,128)(2,1)S(1)}, bf16[2,8,80,128]{3,2,1,0:T(8,128)(2,1)S(1)}, u32[]{:S(2)}, u32[]{:S(2)}) collective-permute-start(bf16[2,8,80,128]{3,2,1,0:T(8,128)(2,1)S(1)} %gradient_away.1.refs_3_), channel_id=1, source_target_pairs={{0,2},{1,3},{2,0},{3,1},{4,6},{5,7},{6,4},{7,5},{8,10},{9,11},{10,... | collective-permute-start | bytes 983048 | tf_op jit(solution)/shard_map/ppermute | solution.py:997
  35.2 5.0 %collective-permute-start.12 = (bf16[8,80,128]{2,1,0:T(8,128)(2,1)S(1)}, bf16[8,80,128]{2,1,0:T(8,128)(2,1)S(1)}, u32[]{:S(2)}, u32[]{:S(2)}) collective-permute-start(bf16[8,80,128]{2,1,0:T(8,128)(2,1)S(1)} %get-tuple-element.111), channel_id=1, source_target_pairs={{0,1},{1,0},{2,3},{3,2},{4,5},{5,4},{6,7},{7,6},{8,9},{9,8},{10,11... | collective-permute-start | bytes 491528 | tf_op jit(solution)/shard_map/ppermute | solution.py:996
  35.5 6.8 %collective-permute-start.16 = (bf16[2,208,128]{2,1,0:T(8,128)(2,1)S(1)}, bf16[2,208,128]{2,1,0:T(8,128)(2,1)S(1)}, u32[]{:S(2)}, u32[]{:S(2)}) collective-permute-start(bf16[2,208,128]{2,1,0:T(8,128)(2,1)S(1)} %get-tuple-element.116), channel_id=1, source_target_pairs={{0,4},{4,0},{8,12},{12,8},{16,20},{20,16},{24,28},{28,24},{1,5},{5... | collective-permute-start | bytes 319496 | tf_op jit(solution)/shard_map/ppermute | solution.py:1024
  37.1 6.7 %collective-permute-start.17 = (bf16[2,208,128]{2,1,0:T(8,128)(2,1)S(1)}, bf16[2,208,128]{2,1,0:T(8,128)(2,1)S(1)}, u32[]{:S(2)}, u32[]{:S(2)}) collective-permute-start(bf16[2,208,128]{2,1,0:T(8,128)(2,1)S(1)} %get-tuple-element.117), channel_id=1, source_target_pairs={{0,12},{4,8},{8,4},{12,0},{16,28},{20,24},{24,20},{28,16},{1,13},{... | collective-permute-start | bytes 319496 | tf_op jit(solution)/shard_map/ppermute | solution.py:1024
  37.7 6.6 %collective-permute-start.15 = (bf16[2,208,128]{2,1,0:T(8,128)(2,1)S(1)}, bf16[2,208,128]{2,1,0:T(8,128)(2,1)S(1)}, u32[]{:S(2)}, u32[]{:S(2)}) collective-permute-start(bf16[2,208,128]{2,1,0:T(8,128)(2,1)S(1)} %get-tuple-element.115.refs_4_), channel_id=1, source_target_pairs={{0,8},{4,12},{8,0},{12,4},{16,24},{20,28},{24,16},{28,20},{1,9},{5... | collective-permute-start | bytes 319496 | tf_op jit(solution)/shard_map/ppermute | solution.py:1024
  44.5 1.7 %collective-permute-start.18 = (bf16[8,80,128]{2,1,0:T(8,128)(2,1)S(1)}, bf16[8,80,128]{2,1,0:T(8,128)(2,1)S(1)}, u32[]{:S(2)}, u32[]{:S(2)}) collective-permute-start(bf16[8,80,128]{2,1,0:T(8,128)(2,1)S(1)} %grad_half.1), channel_id=1, source_target_pairs={{0,1},{1,0},{2,3},{3,2},{4,5},{5,4},{6,7},{7,6},{8,9},{9,8},{10,11... | collective-permute-start | bytes 491528 | tf_op jit(solution)/shard_map/ppermute | solution.py:1040
  44.5 10.0 %collective-permute-start.22 = (bf16[320,128]{1,0:T(8,128)(2,1)S(1)}, bf16[320,128]{1,0:T(8,128)(2,1)S(1)}, u32[]{:S(2)}, u32[]{:S(2)}) collective-permute-start(bf16[320,128]{1,0:T(8,128)(2,1)S(1)} %get-tuple-element.119.refs_1_), channel_id=1, source_target_pairs={{0,2},{1,3},{2,0},{3,1},{4,6},{5,7},{6,4},{7,5},{8,10},{9,11},{10,... | collective-permute-start | bytes 245768 | tf_op jit(solution)/shard_map/ppermute | solution.py:1056
  46.7 4.1 %collective-permute-start.19 = (bf16[2,80,128]{2,1,0:T(8,128)(2,1)S(1)}, bf16[2,80,128]{2,1,0:T(8,128)(2,1)S(1)}, u32[]{:S(2)}, u32[]{:S(2)}) collective-permute-start(bf16[2,80,128]{2,1,0:T(8,128)(2,1)S(1)} %get-tuple-element.121), channel_id=1, source_target_pairs={{0,4},{4,0},{1,5},{5,1},{2,6},{6,2},{3,7},{7,3},{8,12},{12,8},{9,1... | collective-permute-start | bytes 122888 | tf_op jit(solution)/shard_map/ppermute | solution.py:334
  50.9 6.1 %collective-permute-start.20 = (bf16[3,80,128]{2,1,0:T(8,128)(2,1)S(1)}, bf16[3,80,128]{2,1,0:T(8,128)(2,1)S(1)}, u32[]{:S(2)}, u32[]{:S(2)}) collective-permute-start(bf16[3,80,128]{2,1,0:T(8,128)(2,1)S(1)} %grad_third.1), channel_id=1, source_target_pairs={{0,24},{8,16},{16,8},{24,0},{1,25},{9,17},{17,9},{25,1},{2,26},{10... | collective-permute-start | bytes 184328 | tf_op jit(solution)/shard_map/ppermute | solution.py:343
  54.5 5.1 %collective-permute-start.23 = (bf16[208,128]{1,0:T(8,128)(2,1)S(1)}, bf16[208,128]{1,0:T(8,128)(2,1)S(1)}, u32[]{:S(2)}, u32[]{:S(2)}) collective-permute-start(bf16[208,128]{1,0:T(8,128)(2,1)S(1)} %add_across.1.refs_0_), channel_id=1, source_target_pairs={{0,16},{8,24},{16,0},{24,8},{1,17},{9,25},{17,1},{25,9},{2,18},{10... | collective-permute-start | bytes 159752 | tf_op jit(solution)/shard_map/ppermute | solution.py:1085
  57.1 6.2 %collective-permute-start.21 = (bf16[4,80,128]{2,1,0:T(8,128)(2,1)S(1)}, bf16[4,80,128]{2,1,0:T(8,128)(2,1)S(1)}, u32[]{:S(2)}, u32[]{:S(2)}) collective-permute-start(bf16[4,80,128]{2,1,0:T(8,128)(2,1)S(1)} %get-tuple-element.127.refs_4_), channel_id=1, source_target_pairs={{0,8},{8,0},{16,24},{24,16},{1,9},{9,1},{17,25},{25,17},{2,10},{10... | collective-permute-start | bytes 245768 | tf_op jit(solution)/shard_map/ppermute | solution.py:351
  59.8 5.9 %collective-permute-start.26 = (bf16[224,128]{1,0:T(8,128)(2,1)S(1)}, bf16[224,128]{1,0:T(8,128)(2,1)S(1)}, u32[]{:S(2)}, u32[]{:S(2)}) collective-permute-start(bf16[224,128]{1,0:T(8,128)(2,1)S(1)} %finish_pieces.1.refs_0_), channel_id=1, source_target_pairs={{0,12},{4,8},{8,4},{12,0},{16,28},{20,24},{24,20},{28,16},{1,13},{... | collective-permute-start | bytes 172040 | tf_op jit(solution)/shard_map/ppermute | solution.py:1024
  60.3 5.4 %collective-permute-start.25 = (bf16[224,128]{1,0:T(8,128)(2,1)S(1)}, bf16[224,128]{1,0:T(8,128)(2,1)S(1)}, u32[]{:S(2)}, u32[]{:S(2)}) collective-permute-start(bf16[224,128]{1,0:T(8,128)(2,1)S(1)} %finish_pieces.1.refs_0_), channel_id=1, source_target_pairs={{0,4},{4,0},{8,12},{12,8},{16,20},{20,16},{24,28},{28,24},{1,5},{5... | collective-permute-start | bytes 172040 | tf_op jit(solution)/shard_map/ppermute | solution.py:1024
  61.4 4.3 %collective-permute-start.24 = (bf16[224,128]{1,0:T(8,128)(2,1)S(1)}, bf16[224,128]{1,0:T(8,128)(2,1)S(1)}, u32[]{:S(2)}, u32[]{:S(2)}) collective-permute-start(bf16[224,128]{1,0:T(8,128)(2,1)S(1)} %finish_pieces.1.refs_0_), channel_id=1, source_target_pairs={{0,8},{4,12},{8,0},{12,4},{16,24},{20,28},{24,16},{28,20},{1,9},{5... | collective-permute-start | bytes 172040 | tf_op jit(solution)/shard_map/ppermute | solution.py:1024

commit v9 on v8

--- a/solution.py
+++ b/solution.py
@@ -143,9 +143,9 @@
     return jnp.where(iota(tile.shape, 0) == 0, tile.astype(F32) + lifted, tile.astype(F32))
 
 
-def prepare_outer(swap, count, *refs):
+def prepare_outer(part, swap, count, *refs):
     outs, (row_scr, sems) = refs[count:-2], refs[-2:]
-    outer, held = outs[:-count], outs[-count:]
+    (*outer, pick_e, pick_p), held = outs[:-count], outs[-count:]
     state_ref, mask_ref = held[0:2]
     copies = [pltpu.make_async_copy(refs[k], held[k], sems.at[k]) for k in range(count)]
     for copy in copies:
@@ -156,6 +156,7 @@
     lat = lax.axis_index("lat")
     for c in range(channels, pad):
         row_scr[pl.ds(c, 2 * DIL, stride=pad), :] = jnp.zeros((2 * DIL, cols), F32)
+    weight_picks(part, pad, pick_e.shape[1], pick_e.shape[0], pick_e, pick_p)
     copies[1].wait()
     copies[0].wait()
     if swap:
@@ -188,12 +189,11 @@
 
 
 def prepare_far(part, *refs):
-    (mask_ref, grad_ref), weights = refs[0:2], refs[2:6]
-    far_ref, tiles_ref, taps_ref = refs[6:9]
-    scr, weights_scr, turn_scr, pick_e, pick_p = refs[9:]
+    (mask_ref, grad_ref), weights, (pick_e, pick_p) = refs[0:2], refs[2:6], refs[6:8]
+    far_ref, tiles_ref, taps_ref = refs[8:11]
+    scr, weights_scr, turn_scr = refs[11:]
     channels, rows, cols = grad_ref.shape
     pad = taps_ref.shape[0]
-    weight_picks(part, pad, weights_scr.shape[1], pick_e.shape[0], pick_e, pick_p)
     pack_weights(part, pad, *weights, pick_e, pick_p, weights_scr, taps_ref, turn_scr)
     hid = weights_scr.shape[0]
     full = tiles_ref.shape[0]
@@ -875,24 +875,24 @@
     ]
     count = len(fetched)
     outs = call(
-        functools.partial(prepare_outer, swap, count),
-        outer_shapes(pad, swap) + [shape(a.shape, a.dtype) for a in fetched],
+        functools.partial(prepare_outer, part, swap, count),
+        outer_shapes(pad, swap)
+        + [shape((channels, wide), BF)] * 2
+        + [shape(a.shape, a.dtype) for a in fetched],
         fetched,
         [pltpu.VMEM(((2 * DIL + 1) * pad, cols), F32), pltpu.SemaphoreType.DMA((count,))],
         "outer_rows",
         far=True,
     )
-    outer, (ocean_state, land_mask, *held) = outs[:-count], outs[-count:]
+    (*outer, pick_e, pick_p), (ocean_state, land_mask, *held) = outs[:-count], outs[-count:]
     to_far, tiles, taps = call(
         functools.partial(prepare_far, part),
         [shape((far_rows, LANES), BF), shape((tile_rows, LANES), BF), shape((pad, LANES), F32)],
-        [land_mask, held[0], *held[3:]],
+        [land_mask, held[0], *held[3:], pick_e, pick_p],
         [
             pltpu.VMEM(((rows // 2 + 1) * pad, cols), F32),
             pltpu.VMEM((hid, wide), BF),
             turn,
-            pltpu.VMEM((channels, wide), BF),
-            pltpu.VMEM((channels, wide), BF),
         ],
         "far_rows",
     )

time: 67 us -> 67 us (level)
  no operation moved by 1% of the time
where the time goes in v9:
time: 67 us; the launch traced here: 66.8 us
  starting transfers between devices  27 us (40%)
  Pallas kernels  19.8 us (30%)
  waiting for transfers between devices  19.1 us (29%)
  between operations  0.89 us (1%)
    pallas_call x26, Pallas kernels, call(): pl.pallas_call(kernel, out_shape=tuple(outs), in_specs=[pl.BlockSpec(memo...  19.8 us
    ppermute x2, starting transfers between devices, exchange_halo(): lax.ppermute(third_out, 'lon', [(lon, lon ^ 3) for lon in range(n_lon)])  7.34 us
    ppermute x6, starting transfers between devices, over_plane(): lax.ppermute(values[k - 1], ('lon', 'lat'), turn_plane(k))  7.07 us
    ppermute x2, waiting for transfers between devices, exchange_halo(): lax.ppermute(third_out, 'lon', [(lon, lon ^ 3) for lon in range(n_lon)])  4.74 us
    ppermute x6, waiting for transfers between devices, over_plane(): lax.ppermute(values[k - 1], ('lon', 'lat'), turn_plane(k))  4.15 us
    ppermute x2, waiting for transfers between devices, exchange_halo(): got = lax.ppermute(first, 'lon', [(lon, lon ^ 1) for lon in range(n_lon)])  3.77 us
    ppermute x2, starting transfers between devices, exchange_halo(): got = lax.ppermute(outer[0], 'lat', [(0, 1), (1, 0)])  3.09 us
    ppermute x1, starting transfers between devices, on_device(): from_far = lax.ppermute(to_far, 'ch', across)  3 us
  transfers between devices with their start and end apart: 27, of which 12 were waited for; matrix products, arithmetic and copies ran while one was open for 0% of the time, Pallas kernels for 22%

profile of v9, /device:TPU:0, one launch (start us, length us, event | category | flops | bytes accessed | tf_op | source)
XLA Modules:
  0.0 66.8 jit_solution(10181305620653911202)
XLA Ops:
  0.6 1.5 %outer_rows.1 = (bf16[2,80,128]{2,1,0:T(8,128)(2,1)S(1)}, bf16[300,640]{1,0:T(8,128)(2,1)S(1)}, bf16[300,640]{1,0:T(8,128)(2,1)S(1)}, bf16[75,32,128]{2,1,0:T(8,...) custom-call(bf16[75,32,128]{2,1,0:T(8,128)(2,1)} %refs_0_.1, ...), custom_call_target="tpu_custom_call" | custom-call | bytes 3674120 | tf_op jit(solution)/shard_map/outer_rows/pallas_call | solution.py:35
  2.1 0.9 %far_rows.1 = (bf16[2080,128]{1,0:T(8,128)(2,1)S(1)}, bf16[800,128]{1,0:T(8,128)(2,1)S(1)}, f32[80,128]{1,0:T(8,128)S(1)}) custom-call(s32[32,128]{1,0:T(8,128)S(1)} %get-tuple-element.75.refs_0_.refs_1_.mask_ref.refs_4_, bf16[75,32,128]{2,1,0:T(8,128)(2,1)S(1)} %get-tuple-element.76.refs_1_.grad_ref, bf16[150,300]{1,0:T(8,128)(2,1)S(1)} %get-tuple-element.77.refs_2_, ...), custom_call_target="tpu_custom_call" | custom-call | bytes 2360324 | tf_op jit(solution)/shard_map/far_rows/pallas_call | solution.py:35
  3.0 3.0 %collective-permute-start.3 = (bf16[2080,128]{1,0:T(8,128)(2,1)S(1)}, bf16[2080,128]{1,0:T(8,128)(2,1)S(1)}, u32[]{:S(2)}, u32[]{:S(2)}) collective-permute-start(bf16[2080,128]{1,0:T(8,128)(2,1)S(1)} %get-tuple-element.97), channel_id=1, source_target_pairs={{0,2},{1,3},{2,0},{3,1},{4,6},{5,7},{6,4},{7,5},{8,10},{9,11},{10,... | collective-permute-start | bytes 1597448 | tf_op jit(solution)/shard_map/ppermute | solution.py:915
  6.0 1.5 %collective-permute-start = (bf16[2,80,128]{2,1,0:T(8,128)(2,1)S(1)}, bf16[2,80,128]{2,1,0:T(8,128)(2,1)S(1)}, u32[]{:S(2)}, u32[]{:S(2)}) collective-permute-start(bf16[2,80,128]{2,1,0:T(8,128)(2,1)S(1)} %get-tuple-element.85), channel_id=1, source_target_pairs={{0,4},{4,0},{1,5},{5,1},{2,6},{6,2},{3,7},{7,3},{8,12},{12,8},{9,1... | collective-permute-start | bytes 122888 | tf_op jit(solution)/shard_map/ppermute | solution.py:334
  7.6 1.0 %state_rows.1 = (bf16[32,80,128]{2,1,0:T(8,128)(2,1)S(1)}, bf16[2,80,128]{2,1,0:T(8,128)(2,1)S(1)}, bf16[80,128]{1,0:T(8,128)(2,1)S(1)}, bf16[80,128]{1,0:T(8,128)(2,1)S(1)}) custom-call(bf16[75,32,128]{2,1,0:T(8,128)(2,1)S(1)} %get-tuple-element.74.refs_0_, s32[32,128]{1,0:T(8,128)S(1)} %get-tuple-element.75.refs_0_.refs_1_.mask_ref.refs_4_, ...), custom_call_target="tpu_custom_call" | custom-call | bytes 1409024 | tf_op jit(solution)/shard_map/state_rows/pallas_call | solution.py:35
  10.2 3.7 %collective-permute-start.1 = (bf16[3,80,128]{2,1,0:T(8,128)(2,1)S(1)}, bf16[3,80,128]{2,1,0:T(8,128)(2,1)S(1)}, u32[]{:S(2)}, u32[]{:S(2)}) collective-permute-start(bf16[3,80,128]{2,1,0:T(8,128)(2,1)S(1)} %state_third.1), channel_id=1, source_target_pairs={{0,24},{8,16},{16,8},{24,0},{1,25},{9,17},{17,9},{25,1},{2,26},{10... | collective-permute-start | bytes 184328 | tf_op jit(solution)/shard_map/ppermute | solution.py:343
  13.8 2.4 %collective-permute-done.1.third_ref = bf16[3,80,128]{2,1,0:T(8,128)(2,1)S(1)} collective-permute-done((bf16[3,80,128]{2,1,0:T(8,128)(2,1)S(1)}, bf16[3,80,128]{2,1,0:T(8,128)(2,1)S(1)}, u32[]{:S(2)}, u32[]{:S(2)}) %collective-permute-start.1) | collective-permute-done | bytes 61472 | tf_op jit(solution)/shard_map/ppermute | solution.py:343
  16.5 3.8 %collective-permute-done.2.left_ref.refs_1_.refs_2_ = bf16[1,80,128]{2,1,0:T(8,128)(2,1)S(1)} collective-permute-done((bf16[1,80,128]{2,1,0:T(8,128)(2,1)S(1)}, bf16[1,80,128]{2,1,0:T(8,128)(2,1)S(1)}, u32[]{:S(2)}, u32[]{:S(2)}) %collective-permute-start.2) | collective-permute-done | bytes 20512 | tf_op jit(solution)/shard_map/ppermute | solution.py:351
  20.7 1.3 %conv_away.1 = (bf16[4,80,128]{2,1,0:T(8,128)(2,1)S(1)}, bf16[4,80,128]{2,1,0:T(8,128)(2,1)S(1)}, bf16[4,80,128]{2,1,0:T(8,128)(2,1)S(1)}, bf16[4,80,128]{2,1,0:T(8,128)(2,1)S(1)}) custom-call(bf16[32,80,128]{2,1,0:T(8,128)(2,1)S(1)} %get-tuple-element.84.block_ref.refs_0_, bf16[4,80,128]{2,1,0:T(8,128)(2,1)S(1)} %get-tuple-element.93.halo_ref.refs_1_, ...), custom_call_target="tpu_custom_call" | custom-call | bytes 1146880 | tf_op jit(solution)/shard_map/conv_away/pallas_call | solution.py:35
  22.2 1.6 %collective-permute-start.6 = (bf16[4,80,128]{2,1,0:T(8,128)(2,1)S(1)}, bf16[4,80,128]{2,1,0:T(8,128)(2,1)S(1)}, u32[]{:S(2)}, u32[]{:S(2)}) collective-permute-start(bf16[4,80,128]{2,1,0:T(8,128)(2,1)S(1)} %get-tuple-element.96.refs_5_), channel_id=1, source_target_pairs={{0,2},{1,3},{2,0},{3,1},{4,6},{5,7},{6,4},{7,5},{8,10},{9,11},{10,... | collective-permute-start | bytes 245768 | tf_op jit(solution)/shard_map/ppermute | solution.py:945
  23.8 1.3 %conv_here.1 = (bf16[4,80,128]{2,1,0:T(8,128)(2,1)S(1)}, bf16[4,80,128]{2,1,0:T(8,128)(2,1)S(1)}, bf16[4,80,128]{2,1,0:T(8,128)(2,1)S(1)}, bf16[4,80,128]{2,1,0:T(8,128)(2,1)S(1)}) custom-call(bf16[32,80,128]{2,1,0:T(8,128)(2,1)S(1)} %get-tuple-element.84.block_ref.refs_0_, bf16[4,80,128]{2,1,0:T(8,128)(2,1)S(1)} %get-tuple-element.93.halo_ref.refs_1_, ...), custom_call_target="tpu_custom_call" | custom-call | bytes 1761280 | tf_op jit(solution)/shard_map/conv_here/pallas_call | solution.py:35
  25.7 0.9 %collective-permute-done.7.refs_3_ = bf16[4,80,128]{2,1,0:T(8,128)(2,1)S(1)} collective-permute-done((bf16[4,80,128]{2,1,0:T(8,128)(2,1)S(1)}, bf16[4,80,128]{2,1,0:T(8,128)(2,1)S(1)}, u32[]{:S(2)}, u32[]{:S(2)}) %collective-permute-start.7) | collective-permute-done | bytes 81952 | tf_op jit(solution)/shard_map/ppermute | solution.py:946
  27.4 1.4 %activation_gradient.1 = (f32[640,1024]{1,0:T(8,128)S(1)}, bf16[384,1024]{1,0:T(8,128)(2,1)S(1)}, bf16[640,640]{1,0:T(8,128)(2,1)S(1)}, bf16[384,640]{1,0:T(8,12...) custom-call(bf16[1440,128]{1,0:T(8,128)(2,1)S(1)} %get-tuple-element.101.refs_0_, ...), custom_call_target="tpu_custom_call" | custom-call | bytes 7002112 | tf_op jit(solution)/shard_map/activation_gradient/pallas_call | solution.py:35
  28.9 1.8 %hidden_first.1 = (bf16[640,512]{1,0:T(8,128)(2,1)S(1)}, f32[2,832,128]{2,1,0:T(8,128)S(1)}, f32[2,832,128]{2,1,0:T(8,128)S(1)}) custom-call(bf16[4,80,128]{2,1,0:T(8,128)(2,1)S(1)} %get-tuple-element.98.refs_0_, bf16[4,80,128]{2,1,0:T(8,128)(2,1)S(1)} %collective-permute-done.5.refs_1_, bf16[4,80,128]{2,1,0:T(8,128)(2,1)S(1)} %collective-permute-done.6.refs_2_, ...), custom_call_target="tpu_custom_call" | custom-call | bytes 6914048 | tf_op jit(solution)/shard_map/hidden_first/pallas_call | solution.py:35
  30.7 1.0 %collective-permute-done.11.refs_3_ = bf16[4,80,128]{2,1,0:T(8,128)(2,1)S(1)} collective-permute-done((bf16[4,80,128]{2,1,0:T(8,128)(2,1)S(1)}, bf16[4,80,128]{2,1,0:T(8,128)(2,1)S(1)}, u32[]{:S(2)}, u32[]{:S(2)}) %collective-permute-start.11) | collective-permute-done | bytes 81952 | tf_op jit(solution)/shard_map/ppermute | solution.py:946
  31.8 1.8 %hidden_second.1 = (bf16[640,512]{1,0:T(8,128)(2,1)S(1)}, f32[2,832,128]{2,1,0:T(8,128)S(1)}, bf16[2,832,128]{2,1,0:T(8,128)(2,1)S(1)}) custom-call(bf16[4,80,128]{2,1,0:T(8,128)(2,1)S(1)} %get-tuple-element.106.refs_0_, bf16[4,80,128]{2,1,0:T(8,128)(2,1)S(1)} %collective-permute-done.9.refs_1_, bf16[4,80,128]{2,1,0:T(8,128)(2,1)S(1)} %collective-permute-done.10.refs_2_, ...), custom_call_target="tpu_custom_call" | custom-call | bytes 8192000 | tf_op jit(solution)/shard_map/hidden_second/pallas_call | solution.py:35
  35.5 1.6 %collective-permute-start.16 = (bf16[2,208,128]{2,1,0:T(8,128)(2,1)S(1)}, bf16[2,208,128]{2,1,0:T(8,128)(2,1)S(1)}, u32[]{:S(2)}, u32[]{:S(2)}) collective-permute-start(bf16[2,208,128]{2,1,0:T(8,128)(2,1)S(1)} %get-tuple-element.120), channel_id=1, source_target_pairs={{0,4},{4,0},{8,12},{12,8},{16,20},{20,16},{24,28},{28,24},{1,5},{5... | collective-permute-start | bytes 319496 | tf_op jit(solution)/shard_map/ppermute | solution.py:1024
  37.7 1.3 %collective-permute-start.15 = (bf16[2,208,128]{2,1,0:T(8,128)(2,1)S(1)}, bf16[2,208,128]{2,1,0:T(8,128)(2,1)S(1)}, u32[]{:S(2)}, u32[]{:S(2)}) collective-permute-start(bf16[2,208,128]{2,1,0:T(8,128)(2,1)S(1)} %get-tuple-element.119.refs_4_), channel_id=1, source_target_pairs={{0,8},{4,12},{8,0},{12,4},{16,24},{20,28},{24,16},{28,20},{1,9},{5... | collective-permute-start | bytes 319496 | tf_op jit(solution)/shard_map/ppermute | solution.py:1024
  39.0 1.2 %shift_columns.1 = (bf16[36,80,128]{2,1,0:T(8,128)(2,1)S(1)}, bf16[36,80,128]{2,1,0:T(8,128)(2,1)S(1)}) custom-call(bf16[32,80,128]{2,1,0:T(8,128)(2,1)S(1)} %get-tuple-element.84.block_ref.refs_0_, bf16[4,80,128]{2,1,0:T(8,128)(2,1)S(1)} %get-tuple-element.93.halo_ref.refs_1_, bf16[1,80,128]{2,1,0:T(8,128)(2,1)S(1)} %collective-permute-done.2.left_ref.refs_1_.refs_2_, ...), custom_call_target="tpu_custom_call" | custom-call | bytes 2359296 | tf_op jit(solution)/shard_map/shift_columns/pallas_call | solution.py:35
  40.2 2.0 %collective-permute-done.16.refs_2_ = bf16[2,208,128]{2,1,0:T(8,128)(2,1)S(1)} collective-permute-done((bf16[2,208,128]{2,1,0:T(8,128)(2,1)S(1)}, bf16[2,208,128]{2,1,0:T(8,128)(2,1)S(1)}, u32[]{:S(2)}, u32[]{:S(2)}) %collective-permute-start.16) | collective-permute-done | bytes 106528 | tf_op jit(solution)/shard_map/ppermute | solution.py:1024
  42.3 1.6 %collective-permute-done.17.refs_3_ = bf16[2,208,128]{2,1,0:T(8,128)(2,1)S(1)} collective-permute-done((bf16[2,208,128]{2,1,0:T(8,128)(2,1)S(1)}, bf16[2,208,128]{2,1,0:T(8,128)(2,1)S(1)}, u32[]{:S(2)}, u32[]{:S(2)}) %collective-permute-start.17) | collective-permute-done | bytes 106528 | tf_op jit(solution)/shard_map/ppermute | solution.py:1024
  44.5 1.6 %collective-permute-start.22 = (bf16[320,128]{1,0:T(8,128)(2,1)S(1)}, bf16[320,128]{1,0:T(8,128)(2,1)S(1)}, u32[]{:S(2)}, u32[]{:S(2)}) collective-permute-start(bf16[320,128]{1,0:T(8,128)(2,1)S(1)} %get-tuple-element.123.refs_1_), channel_id=1, source_target_pairs={{0,2},{1,3},{2,0},{3,1},{4,6},{5,7},{6,4},{7,5},{8,10},{9,11},{10,... | collective-permute-start | bytes 245768 | tf_op jit(solution)/shard_map/ppermute | solution.py:1056
  46.6 1.6 %collective-permute-start.19 = (bf16[2,80,128]{2,1,0:T(8,128)(2,1)S(1)}, bf16[2,80,128]{2,1,0:T(8,128)(2,1)S(1)}, u32[]{:S(2)}, u32[]{:S(2)}) collective-permute-start(bf16[2,80,128]{2,1,0:T(8,128)(2,1)S(1)} %get-tuple-element.125), channel_id=1, source_target_pairs={{0,4},{4,0},{1,5},{5,1},{2,6},{6,2},{3,7},{7,3},{8,12},{12,8},{9,1... | collective-permute-start | bytes 122888 | tf_op jit(solution)/shard_map/ppermute | solution.py:334
  48.2 1.2 %kernel_gradient.1.refs_0_.refs_2_ = bf16[80,128]{1,0:T(8,128)(2,1)S(1)} custom-call(bf16[32,80,128]{2,1,0:T(8,128)(2,1)S(1)} %get-tuple-element.124.grad_ref.block_ref, bf16[32,80,128]{2,1,0:T(8,128)(2,1)S(1)} %get-tuple-element.84.block_ref.refs_0_, bf16[4,80,128]{2,1,0:T(8,128)(2,1)S(1)} %get-tuple-element.93.halo_ref.refs_1_, ...), custom_call_target="tpu_custom_call" | custom-call | bytes 2887680 | tf_op jit(solution)/shard_map/kernel_gradient/pallas_call | solution.py:35
  49.4 1.3 %collective-permute-done.19.refs_1_.got_ref = bf16[2,80,128]{2,1,0:T(8,128)(2,1)S(1)} collective-permute-done((bf16[2,80,128]{2,1,0:T(8,128)(2,1)S(1)}, bf16[2,80,128]{2,1,0:T(8,128)(2,1)S(1)}, u32[]{:S(2)}, u32[]{:S(2)}) %collective-permute-start.19) | collective-permute-done | bytes 40992 | tf_op jit(solution)/shard_map/ppermute | solution.py:334
  50.8 3.7 %collective-permute-start.20 = (bf16[3,80,128]{2,1,0:T(8,128)(2,1)S(1)}, bf16[3,80,128]{2,1,0:T(8,128)(2,1)S(1)}, u32[]{:S(2)}, u32[]{:S(2)}) collective-permute-start(bf16[3,80,128]{2,1,0:T(8,128)(2,1)S(1)} %grad_third.1), channel_id=1, source_target_pairs={{0,24},{8,16},{16,8},{24,0},{1,25},{9,17},{17,9},{25,1},{2,26},{10... | collective-permute-start | bytes 184328 | tf_op jit(solution)/shard_map/ppermute | solution.py:343
  54.6 2.3 %collective-permute-done.20.third_ref.refs_3_ = bf16[3,80,128]{2,1,0:T(8,128)(2,1)S(1)} collective-permute-done((bf16[3,80,128]{2,1,0:T(8,128)(2,1)S(1)}, bf16[3,80,128]{2,1,0:T(8,128)(2,1)S(1)}, u32[]{:S(2)}, u32[]{:S(2)}) %collective-permute-start.20) | collective-permute-done | bytes 61472 | tf_op jit(solution)/shard_map/ppermute | solution.py:343
  57.2 2.5 %collective-permute-done.23.refs_1_ = bf16[208,128]{1,0:T(8,128)(2,1)S(1)} collective-permute-done((bf16[208,128]{1,0:T(8,128)(2,1)S(1)}, bf16[208,128]{1,0:T(8,128)(2,1)S(1)}, u32[]{:S(2)}, u32[]{:S(2)}) %collective-permute-start.23) | collective-permute-done | bytes 53280 | tf_op jit(solution)/shard_map/ppermute | solution.py:1085
  60.3 1.1 %collective-permute-start.25 = (bf16[224,128]{1,0:T(8,128)(2,1)S(1)}, bf16[224,128]{1,0:T(8,128)(2,1)S(1)}, u32[]{:S(2)}, u32[]{:S(2)}) collective-permute-start(bf16[224,128]{1,0:T(8,128)(2,1)S(1)} %finish_pieces.1.refs_0_), channel_id=1, source_target_pairs={{0,4},{4,0},{8,12},{12,8},{16,20},{20,16},{24,28},{28,24},{1,5},{5... | collective-permute-start | bytes 172040 | tf_op jit(solution)/shard_map/ppermute | solution.py:1024
  61.4 1.9 %collective-permute-start.24 = (bf16[224,128]{1,0:T(8,128)(2,1)S(1)}, bf16[224,128]{1,0:T(8,128)(2,1)S(1)}, u32[]{:S(2)}, u32[]{:S(2)}) collective-permute-start(bf16[224,128]{1,0:T(8,128)(2,1)S(1)} %finish_pieces.1.refs_0_), channel_id=1, source_target_pairs={{0,8},{4,12},{8,0},{12,4},{16,24},{20,28},{24,16},{28,20},{1,9},{5... | collective-permute-start | bytes 172040 | tf_op jit(solution)/shard_map/ppermute | solution.py:1024
  63.3 2.4 %conv_adjoint.1 = (bf16[75,32,128]{2,1,0:T(8,128)(2,1)}, f32[8,128]{1,0:T(8,128)S(1)}) custom-call(bf16[32,80,128]{2,1,0:T(8,128)(2,1)S(1)} %get-tuple-element.124.grad_ref.block_ref, bf16[4,80,128]{2,1,0:T(8,128)(2,1)S(1)} %get-tuple-element.130.halo_ref, bf16[4,80,128]{2,1,0:T(8,128)(2,1)S(1)} %collective-permute-done.21.left_ref, ...), custom_call_target="tpu_custom_call" | custom-call | bytes 2170880 | tf_op jit(solution)/shard_map/conv_adjoint/pallas_call | solution.py:35
  65.7 1.1 %write_parameters.1 = (f32[150,300]{1,0:T(8,128)}, f32[150,300]{1,0:T(8,128)}, f32[1,150]{1,0:T(1,128)}, f32[3,3,75]{2,1,0:T(4,128)}) custom-call(bf16[224,128]{1,0:T(8,128)(2,1)S(1)} %finish_pieces.1.refs_0_, bf16[224,128]{1,0:T(8,128)(2,1)S(1)} %collective-permute-done.24.refs_1_, bf16[224,128]{1,0:T(8,128)(2,1)S(1)} %collective-permute-done.25.refs_2_, ...), custom_call_target="tpu_custom_call" | custom-call | bytes 1057572 | tf_op jit(solution)/shard_map/write_parameters/pallas_call | solution.py:35
  (48 shorter events, 8.7 us)
Async XLA Ops:
  3.0 17.2 %collective-permute-start.3 = (bf16[2080,128]{1,0:T(8,128)(2,1)S(1)}, bf16[2080,128]{1,0:T(8,128)(2,1)S(1)}, u32[]{:S(2)}, u32[]{:S(2)}) collective-permute-start(bf16[2080,128]{1,0:T(8,128)(2,1)S(1)} %get-tuple-element.97), channel_id=1, source_target_pairs={{0,2},{1,3},{2,0},{3,1},{4,6},{5,7},{6,4},{7,5},{8,10},{9,11},{10,... | collective-permute-start | bytes 1597448 | tf_op jit(solution)/shard_map/ppermute | solution.py:915
  6.0 4.0 %collective-permute-start = (bf16[2,80,128]{2,1,0:T(8,128)(2,1)S(1)}, bf16[2,80,128]{2,1,0:T(8,128)(2,1)S(1)}, u32[]{:S(2)}, u32[]{:S(2)}) collective-permute-start(bf16[2,80,128]{2,1,0:T(8,128)(2,1)S(1)} %get-tuple-element.85), channel_id=1, source_target_pairs={{0,4},{4,0},{1,5},{5,1},{2,6},{6,2},{3,7},{7,3},{8,12},{12,8},{9,1... | collective-permute-start | bytes 122888 | tf_op jit(solution)/shard_map/ppermute | solution.py:334
  10.2 6.1 %collective-permute-start.1 = (bf16[3,80,128]{2,1,0:T(8,128)(2,1)S(1)}, bf16[3,80,128]{2,1,0:T(8,128)(2,1)S(1)}, u32[]{:S(2)}, u32[]{:S(2)}) collective-permute-start(bf16[3,80,128]{2,1,0:T(8,128)(2,1)S(1)} %state_third.1), channel_id=1, source_target_pairs={{0,24},{8,16},{16,8},{24,0},{1,25},{9,17},{17,9},{25,1},{2,26},{10... | collective-permute-start | bytes 184328 | tf_op jit(solution)/shard_map/ppermute | solution.py:343
  16.4 3.8 %collective-permute-start.2 = (bf16[1,80,128]{2,1,0:T(8,128)(2,1)S(1)}, bf16[1,80,128]{2,1,0:T(8,128)(2,1)S(1)}, u32[]{:S(2)}, u32[]{:S(2)}) collective-permute-start(bf16[1,80,128]{2,1,0:T(8,128)(2,1)S(1)} %get-tuple-element.94), channel_id=1, source_target_pairs={{0,8},{8,0},{16,24},{24,16},{1,9},{9,1},{17,25},{25,17},{2,10},{10... | collective-permute-start | bytes 61448 | tf_op jit(solution)/shard_map/ppermute | solution.py:351
  20.2 3.6 %collective-permute-start.4 = (bf16[2080,128]{1,0:T(8,128)(2,1)S(1)}, bf16[2080,128]{1,0:T(8,128)(2,1)S(1)}, u32[]{:S(2)}, u32[]{:S(2)}) collective-permute-start(bf16[2080,128]{1,0:T(8,128)(2,1)S(1)} %cotan_relay.1.refs_2_), channel_id=1, source_target_pairs={{0,1},{1,0},{2,3},{3,2},{4,5},{5,4},{6,7},{7,6},{8,9},{9,8},{10,11... | collective-permute-start | bytes 1597448 | tf_op jit(solution)/shard_map/ppermute | solution.py:931
  20.2 6.8 %collective-permute-start.8 = (bf16[1440,128]{1,0:T(8,128)(2,1)S(1)}, bf16[1440,128]{1,0:T(8,128)(2,1)S(1)}, u32[]{:S(2)}, u32[]{:S(2)}) collective-permute-start(bf16[1440,128]{1,0:T(8,128)(2,1)S(1)} %get-tuple-element.92.refs_4_), channel_id=1, source_target_pairs={{0,1},{1,0},{2,3},{3,2},{4,5},{5,4},{6,7},{7,6},{8,9},{9,8},{10,11... | collective-permute-start | bytes 1105928 | tf_op jit(solution)/shard_map/ppermute | solution.py:960
  22.0 4.6 %collective-permute-start.7 = (bf16[4,80,128]{2,1,0:T(8,128)(2,1)S(1)}, bf16[4,80,128]{2,1,0:T(8,128)(2,1)S(1)}, u32[]{:S(2)}, u32[]{:S(2)}) collective-permute-start(bf16[4,80,128]{2,1,0:T(8,128)(2,1)S(1)} %get-tuple-element.100), channel_id=1, source_target_pairs={{0,3},{1,2},{2,1},{3,0},{4,7},{5,6},{6,5},{7,4},{8,11},{9,10},{10,... | collective-permute-start | bytes 245768 | tf_op jit(solution)/shard_map/ppermute | solution.py:946
  22.2 6.7 %collective-permute-start.6 = (bf16[4,80,128]{2,1,0:T(8,128)(2,1)S(1)}, bf16[4,80,128]{2,1,0:T(8,128)(2,1)S(1)}, u32[]{:S(2)}, u32[]{:S(2)}) collective-permute-start(bf16[4,80,128]{2,1,0:T(8,128)(2,1)S(1)} %get-tuple-element.96.refs_5_), channel_id=1, source_target_pairs={{0,2},{1,3},{2,0},{3,1},{4,6},{5,7},{6,4},{7,5},{8,10},{9,11},{10,... | collective-permute-start | bytes 245768 | tf_op jit(solution)/shard_map/ppermute | solution.py:945
  25.1 3.8 %collective-permute-start.5 = (bf16[4,80,128]{2,1,0:T(8,128)(2,1)S(1)}, bf16[4,80,128]{2,1,0:T(8,128)(2,1)S(1)}, u32[]{:S(2)}, u32[]{:S(2)}) collective-permute-start(bf16[4,80,128]{2,1,0:T(8,128)(2,1)S(1)} %get-tuple-element.99), channel_id=1, source_target_pairs={{0,1},{1,0},{2,3},{3,2},{4,5},{5,4},{6,7},{7,6},{8,9},{9,8},{10,11... | collective-permute-start | bytes 245768 | tf_op jit(solution)/shard_map/ppermute | solution.py:944
  25.3 5.4 %collective-permute-start.10 = (bf16[4,80,128]{2,1,0:T(8,128)(2,1)S(1)}, bf16[4,80,128]{2,1,0:T(8,128)(2,1)S(1)}, u32[]{:S(2)}, u32[]{:S(2)}) collective-permute-start(bf16[4,80,128]{2,1,0:T(8,128)(2,1)S(1)} %get-tuple-element.108), channel_id=1, source_target_pairs={{0,2},{1,3},{2,0},{3,1},{4,6},{5,7},{6,4},{7,5},{8,10},{9,11},{10,... | collective-permute-start | bytes 245768 | tf_op jit(solution)/shard_map/ppermute | solution.py:945
  26.6 5.2 %collective-permute-start.11 = (bf16[4,80,128]{2,1,0:T(8,128)(2,1)S(1)}, bf16[4,80,128]{2,1,0:T(8,128)(2,1)S(1)}, u32[]{:S(2)}, u32[]{:S(2)}) collective-permute-start(bf16[4,80,128]{2,1,0:T(8,128)(2,1)S(1)} %get-tuple-element.109), channel_id=1, source_target_pairs={{0,3},{1,2},{2,1},{3,0},{4,7},{5,6},{6,5},{7,4},{8,11},{9,10},{10,... | collective-permute-start | bytes 245768 | tf_op jit(solution)/shard_map/ppermute | solution.py:946
  27.0 4.8 %collective-permute-start.9 = (bf16[4,80,128]{2,1,0:T(8,128)(2,1)S(1)}, bf16[4,80,128]{2,1,0:T(8,128)(2,1)S(1)}, u32[]{:S(2)}, u32[]{:S(2)}) collective-permute-start(bf16[4,80,128]{2,1,0:T(8,128)(2,1)S(1)} %get-tuple-element.107), channel_id=1, source_target_pairs={{0,1},{1,0},{2,3},{3,2},{4,5},{5,4},{6,7},{7,6},{8,9},{9,8},{10,11... | collective-permute-start | bytes 245768 | tf_op jit(solution)/shard_map/ppermute | solution.py:944
  33.5 1.8 %collective-permute-start.14 = (bf16[2,832,128]{2,1,0:T(8,128)(2,1)S(1)}, bf16[2,832,128]{2,1,0:T(8,128)(2,1)S(1)}, u32[]{:S(2)}, u32[]{:S(2)}) collective-permute-start(bf16[2,832,128]{2,1,0:T(8,128)(2,1)S(1)} %get-tuple-element.117), channel_id=1, source_target_pairs={{0,1},{1,0},{2,3},{3,2},{4,5},{5,4},{6,7},{7,6},{8,9},{9,8},{10,11... | collective-permute-start | bytes 1277960 | tf_op jit(solution)/shard_map/ppermute | solution.py:979
  34.2 10.2 %collective-permute-start.13 = (bf16[2,8,80,128]{3,2,1,0:T(8,128)(2,1)S(1)}, bf16[2,8,80,128]{3,2,1,0:T(8,128)(2,1)S(1)}, u32[]{:S(2)}, u32[]{:S(2)}) collective-permute-start(bf16[2,8,80,128]{3,2,1,0:T(8,128)(2,1)S(1)} %gradient_away.1.refs_3_), channel_id=1, source_target_pairs={{0,2},{1,3},{2,0},{3,1},{4,6},{5,7},{6,4},{7,5},{8,10},{9,11},{10,... | collective-permute-start | bytes 983048 | tf_op jit(solution)/shard_map/ppermute | solution.py:997
  35.2 5.0 %collective-permute-start.12 = (bf16[8,80,128]{2,1,0:T(8,128)(2,1)S(1)}, bf16[8,80,128]{2,1,0:T(8,128)(2,1)S(1)}, u32[]{:S(2)}, u32[]{:S(2)}) collective-permute-start(bf16[8,80,128]{2,1,0:T(8,128)(2,1)S(1)} %get-tuple-element.115), channel_id=1, source_target_pairs={{0,1},{1,0},{2,3},{3,2},{4,5},{5,4},{6,7},{7,6},{8,9},{9,8},{10,11... | collective-permute-start | bytes 491528 | tf_op jit(solution)/shard_map/ppermute | solution.py:996
  35.5 6.8 %collective-permute-start.16 = (bf16[2,208,128]{2,1,0:T(8,128)(2,1)S(1)}, bf16[2,208,128]{2,1,0:T(8,128)(2,1)S(1)}, u32[]{:S(2)}, u32[]{:S(2)}) collective-permute-start(bf16[2,208,128]{2,1,0:T(8,128)(2,1)S(1)} %get-tuple-element.120), channel_id=1, source_target_pairs={{0,4},{4,0},{8,12},{12,8},{16,20},{20,16},{24,28},{28,24},{1,5},{5... | collective-permute-start | bytes 319496 | tf_op jit(solution)/shard_map/ppermute | solution.py:1024
  37.1 6.7 %collective-permute-start.17 = (bf16[2,208,128]{2,1,0:T(8,128)(2,1)S(1)}, bf16[2,208,128]{2,1,0:T(8,128)(2,1)S(1)}, u32[]{:S(2)}, u32[]{:S(2)}) collective-permute-start(bf16[2,208,128]{2,1,0:T(8,128)(2,1)S(1)} %get-tuple-element.121), channel_id=1, source_target_pairs={{0,12},{4,8},{8,4},{12,0},{16,28},{20,24},{24,20},{28,16},{1,13},{... | collective-permute-start | bytes 319496 | tf_op jit(solution)/shard_map/ppermute | solution.py:1024
  37.7 6.6 %collective-permute-start.15 = (bf16[2,208,128]{2,1,0:T(8,128)(2,1)S(1)}, bf16[2,208,128]{2,1,0:T(8,128)(2,1)S(1)}, u32[]{:S(2)}, u32[]{:S(2)}) collective-permute-start(bf16[2,208,128]{2,1,0:T(8,128)(2,1)S(1)} %get-tuple-element.119.refs_4_), channel_id=1, source_target_pairs={{0,8},{4,12},{8,0},{12,4},{16,24},{20,28},{24,16},{28,20},{1,9},{5... | collective-permute-start | bytes 319496 | tf_op jit(solution)/shard_map/ppermute | solution.py:1024
  44.5 1.7 %collective-permute-start.18 = (bf16[8,80,128]{2,1,0:T(8,128)(2,1)S(1)}, bf16[8,80,128]{2,1,0:T(8,128)(2,1)S(1)}, u32[]{:S(2)}, u32[]{:S(2)}) collective-permute-start(bf16[8,80,128]{2,1,0:T(8,128)(2,1)S(1)} %grad_half.1), channel_id=1, source_target_pairs={{0,1},{1,0},{2,3},{3,2},{4,5},{5,4},{6,7},{7,6},{8,9},{9,8},{10,11... | collective-permute-start | bytes 491528 | tf_op jit(solution)/shard_map/ppermute | solution.py:1040
  44.5 10.0 %collective-permute-start.22 = (bf16[320,128]{1,0:T(8,128)(2,1)S(1)}, bf16[320,128]{1,0:T(8,128)(2,1)S(1)}, u32[]{:S(2)}, u32[]{:S(2)}) collective-permute-start(bf16[320,128]{1,0:T(8,128)(2,1)S(1)} %get-tuple-element.123.refs_1_), channel_id=1, source_target_pairs={{0,2},{1,3},{2,0},{3,1},{4,6},{5,7},{6,4},{7,5},{8,10},{9,11},{10,... | collective-permute-start | bytes 245768 | tf_op jit(solution)/shard_map/ppermute | solution.py:1056
  46.6 4.1 %collective-permute-start.19 = (bf16[2,80,128]{2,1,0:T(8,128)(2,1)S(1)}, bf16[2,80,128]{2,1,0:T(8,128)(2,1)S(1)}, u32[]{:S(2)}, u32[]{:S(2)}) collective-permute-start(bf16[2,80,128]{2,1,0:T(8,128)(2,1)S(1)} %get-tuple-element.125), channel_id=1, source_target_pairs={{0,4},{4,0},{1,5},{5,1},{2,6},{6,2},{3,7},{7,3},{8,12},{12,8},{9,1... | collective-permute-start | bytes 122888 | tf_op jit(solution)/shard_map/ppermute | solution.py:334
  50.8 6.1 %collective-permute-start.20 = (bf16[3,80,128]{2,1,0:T(8,128)(2,1)S(1)}, bf16[3,80,128]{2,1,0:T(8,128)(2,1)S(1)}, u32[]{:S(2)}, u32[]{:S(2)}) collective-permute-start(bf16[3,80,128]{2,1,0:T(8,128)(2,1)S(1)} %grad_third.1), channel_id=1, source_target_pairs={{0,24},{8,16},{16,8},{24,0},{1,25},{9,17},{17,9},{25,1},{2,26},{10... | collective-permute-start | bytes 184328 | tf_op jit(solution)/shard_map/ppermute | solution.py:343
  54.5 5.1 %collective-permute-start.23 = (bf16[208,128]{1,0:T(8,128)(2,1)S(1)}, bf16[208,128]{1,0:T(8,128)(2,1)S(1)}, u32[]{:S(2)}, u32[]{:S(2)}) collective-permute-start(bf16[208,128]{1,0:T(8,128)(2,1)S(1)} %add_across.1.refs_0_), channel_id=1, source_target_pairs={{0,16},{8,24},{16,0},{24,8},{1,17},{9,25},{17,1},{25,9},{2,18},{10... | collective-permute-start | bytes 159752 | tf_op jit(solution)/shard_map/ppermute | solution.py:1085
  57.1 6.2 %collective-permute-start.21 = (bf16[4,80,128]{2,1,0:T(8,128)(2,1)S(1)}, bf16[4,80,128]{2,1,0:T(8,128)(2,1)S(1)}, u32[]{:S(2)}, u32[]{:S(2)}) collective-permute-start(bf16[4,80,128]{2,1,0:T(8,128)(2,1)S(1)} %get-tuple-element.131.refs_4_), channel_id=1, source_target_pairs={{0,8},{8,0},{16,24},{24,16},{1,9},{9,1},{17,25},{25,17},{2,10},{10... | collective-permute-start | bytes 245768 | tf_op jit(solution)/shard_map/ppermute | solution.py:351
  59.8 5.9 %collective-permute-start.26 = (bf16[224,128]{1,0:T(8,128)(2,1)S(1)}, bf16[224,128]{1,0:T(8,128)(2,1)S(1)}, u32[]{:S(2)}, u32[]{:S(2)}) collective-permute-start(bf16[224,128]{1,0:T(8,128)(2,1)S(1)} %finish_pieces.1.refs_0_), channel_id=1, source_target_pairs={{0,12},{4,8},{8,4},{12,0},{16,28},{20,24},{24,20},{28,16},{1,13},{... | collective-permute-start | bytes 172040 | tf_op jit(solution)/shard_map/ppermute | solution.py:1024
  60.3 5.4 %collective-permute-start.25 = (bf16[224,128]{1,0:T(8,128)(2,1)S(1)}, bf16[224,128]{1,0:T(8,128)(2,1)S(1)}, u32[]{:S(2)}, u32[]{:S(2)}) collective-permute-start(bf16[224,128]{1,0:T(8,128)(2,1)S(1)} %finish_pieces.1.refs_0_), channel_id=1, source_target_pairs={{0,4},{4,0},{8,12},{12,8},{16,20},{20,16},{24,28},{28,24},{1,5},{5... | collective-permute-start | bytes 172040 | tf_op jit(solution)/shard_map/ppermute | solution.py:1024
  61.4 4.3 %collective-permute-start.24 = (bf16[224,128]{1,0:T(8,128)(2,1)S(1)}, bf16[224,128]{1,0:T(8,128)(2,1)S(1)}, u32[]{:S(2)}, u32[]{:S(2)}) collective-permute-start(bf16[224,128]{1,0:T(8,128)(2,1)S(1)} %finish_pieces.1.refs_0_), channel_id=1, source_target_pairs={{0,8},{4,12},{8,0},{12,4},{16,24},{20,28},{24,16},{28,20},{1,9},{5... | collective-permute-start | bytes 172040 | tf_op jit(solution)/shard_map/ppermute | solution.py:1024
